TPU v7x, 32 devices: a whole 2x2x4 slice. The times are simulated.
32 devices in a mesh: dp: 4 (over y, x), mp: 8 (over z, core).
Axes of the slice: x: 2, y: 2, z: 4, core: 2. Of those that a mesh axis runs over, the one named last changes fastest.
Arguments:
- layer_input: bfloat16 [8192, 2048], P(('dp', 'mp')), may hold values from -6 to 6
- width_choice: int32 [8192, 2], P('dp'), may hold values from 0 to 3
- routed_flag: int32 [8192, 2], P('dp'), may hold values 0 or 1
- mixer_gain: float32 [2048], replicated, may hold values from 0.1 to 1.9
- mixer_router: float32 [2048, 4], replicated, may hold values from -0.09375 to 0.09375
- attention_weight: bfloat16 [2048, 3, 2048], P(None, None, 'mp'), may hold values from -0.125 to 0.125
- output_weight: bfloat16 [2048, 2048], P('mp'), may hold values from -0.75 to 0.75
- hidden_gain: float32 [2048], replicated, may hold values from 0.1 to 1.9
- hidden_router: float32 [2048, 4], replicated, may hold values from -0.09375 to 0.09375
- up_weight: bfloat16 [2048, 8192], P(None, 'mp'), may hold values from -0.125 to 0.125
- down_weight: bfloat16 [8192, 2048], P('mp'), may hold values from -0.0625 to 0.0625
- out_grad: bfloat16 [8192, 2048], P(('dp', 'mp')), may hold values from -6 to 6
Outputs:
- layer_output: bfloat16 [8192, 2048], P(('dp', 'mp'))
- input_grad: bfloat16 [8192, 2048], P(('dp', 'mp'))
- mixer_gain_grad: float32 [2048], replicated
- mixer_router_grad: float32 [2048, 4], replicated
- attention_weight_grad: float32 [2048, 3, 2048], P(None, None, 'mp')
- output_weight_grad: float32 [2048, 2048], P('mp')
- hidden_gain_grad: float32 [2048], replicated
- hidden_router_grad: float32 [2048, 4], replicated
- up_weight_grad: float32 [2048, 8192], P(None, 'mp')
- down_weight_grad: float32 [8192, 2048], P('mp')
All inputs are finite; a program needn't handle non-finite values. No bound on the sum of `routed_flag` on one device may be relied on, other than what follows from the above.
Results may differ from a plain program's by a relative error of at most 0.02.
Values may be sent and summed in bfloat16 or wider, within the bound.
No kernel may reach another device: no remote copies, remote signals or barrier semaphores. Data moves between devices by JAX's collectives and lax.ppermute only.
A program may use at most 192 MiB of HBM per device.

v0:
```python
import math

import jax
import jax.numpy as jnp
from jax import lax
from jax.sharding import PartitionSpec as P

H = 16
HD = 128
FF = 8192
SEQ_LEN = 1024


EPSILON = 1e-05
NEG_LARGE = -1e30
HIGHEST = lax.Precision.HIGHEST


def norm_forward(values, gain_vec):
    row_mean = jnp.mean(values, axis=1, keepdims=True)
    centred = values - row_mean
    row_variance = jnp.mean(centred * centred, axis=1, keepdims=True)
    inverse_scale = lax.rsqrt(row_variance + EPSILON)
    scaled = centred * inverse_scale
    return (scaled * gain_vec[None, :], scaled, inverse_scale)


def norm_backward(normed_grad, scaled, inverse_scale, gain_vec):
    gain_grad = jnp.sum(normed_grad * scaled, axis=0)
    scaled_grad = normed_grad * gain_vec[None, :]
    first_mean = jnp.mean(scaled_grad, axis=1, keepdims=True)
    second_mean = jnp.mean(scaled_grad * scaled, axis=1, keepdims=True)
    return (inverse_scale * (scaled_grad - first_mean - scaled * second_mean), gain_grad)


def gate_forward(normed, router, width_col, routed_col):
    logits = jnp.dot(normed, router, precision=HIGHEST, preferred_element_type=jnp.float32)
    soft_probs = jax.nn.softmax(logits, axis=1)
    one_hot = (width_col[:, None] == jnp.arange(4, dtype=jnp.int32)[None, :]).astype(jnp.float32)
    chosen = jnp.sum(soft_probs * one_hot, axis=1)
    route_flags = routed_col.astype(jnp.float32)
    return (
        route_flags * 4.0 * chosen + (1.0 - route_flags),
        (soft_probs, one_hot, chosen, route_flags),
    )


def gate_backward(normed, router, gate_state, gate_grad):
    soft_probs, one_hot, chosen, route_flags = gate_state
    coefficient = route_flags * 4.0 * chosen * gate_grad
    logit_grad = coefficient[:, None] * (one_hot - soft_probs)
    router_grad = lax.dot_general(
        normed,
        logit_grad,
        (((0,), (0,)), ((), ())),
        precision=HIGHEST,
        preferred_element_type=jnp.float32,
    )
    normed_grad = lax.dot_general(
        logit_grad,
        router,
        (((1,), (1,)), ((), ())),
        precision=HIGHEST,
        preferred_element_type=jnp.float32,
    )
    return (normed_grad, router_grad)


def rope_tables(token_count, head_width):
    positions = jnp.arange(token_count, dtype=jnp.float32)
    frequency = jnp.exp(
        jnp.arange(head_width // 2, dtype=jnp.float32) * (-2.0 * math.log(10000.0) / head_width)
    )
    angles = positions[:, None] * frequency[None, :]
    return (jnp.cos(angles)[:, None, :], jnp.sin(angles)[:, None, :])


def rotate(halves, cosine_table, sine_table):
    half_size = halves.shape[-1] // 2
    first_half = halves[..., :half_size]
    second_half = halves[..., half_size:]
    return jnp.concatenate(
        [
            first_half * cosine_table - second_half * sine_table,
            second_half * cosine_table + first_half * sine_table,
        ],
        axis=-1,
    )


def rotate_back(halves, cosine_table, sine_table):
    half_size = halves.shape[-1] // 2
    first_half = halves[..., :half_size]
    second_half = halves[..., half_size:]
    return jnp.concatenate(
        [
            first_half * cosine_table + second_half * sine_table,
            second_half * cosine_table - first_half * sine_table,
        ],
        axis=-1,
    )


def split_rows(qkv_rows, heads_local, cosine_table, sine_table):
    shaped = qkv_rows.reshape(-1, SEQ_LEN, 3, heads_local, HD)
    queries = rotate(shaped[:, :, 0], cosine_table, sine_table).astype(jnp.bfloat16)
    keys_all = rotate(shaped[:, :, 1], cosine_table, sine_table).astype(jnp.bfloat16)
    values_all = shaped[:, :, 2].astype(jnp.bfloat16)
    return (queries, keys_all, values_all)


def causal_scores(queries, keys_all):
    token_count = queries.shape[0]
    scores = jnp.einsum("qhd,khd->hqk", queries, keys_all, preferred_element_type=jnp.float32) * (
        1.0 / math.sqrt(HD)
    )
    positions = jnp.arange(token_count, dtype=jnp.int32)
    causal = positions[None, :] <= positions[:, None]
    return jnp.where(causal[None, :, :], scores, NEG_LARGE)


def attend_forward(packed):
    queries, keys_all, values_all = packed
    scores = causal_scores(queries, keys_all)
    row_max = jnp.max(scores, axis=2, keepdims=True)
    shifted = jnp.exp(scores - row_max)
    exp_total = jnp.sum(shifted, axis=2, keepdims=True)
    probs_low = (shifted / exp_total).astype(jnp.bfloat16)
    head_mix = jnp.einsum("hqk,khd->qhd", probs_low, values_all, preferred_element_type=jnp.float32)
    return (head_mix, (row_max + jnp.log(exp_total))[:, :, 0])


def attend_backward(packed):
    queries, keys_all, values_all, log_total, heads_grad = packed
    scores = causal_scores(queries, keys_all)
    soft_probs = jnp.exp(scores - log_total[:, :, None])
    probs_low = soft_probs.astype(jnp.bfloat16)
    values_grad = jnp.einsum(
        "hqk,qhd->khd", probs_low, heads_grad, preferred_element_type=jnp.float32
    )
    probs_grad = jnp.einsum(
        "qhd,khd->hqk", heads_grad, values_all, preferred_element_type=jnp.float32
    )
    score_grad = (
        soft_probs * (probs_grad - jnp.sum(soft_probs * probs_grad, axis=2, keepdims=True))
    ).astype(jnp.bfloat16)
    score_scale = 1.0 / math.sqrt(HD)
    queries_grad = (
        jnp.einsum("hqk,khd->qhd", score_grad, keys_all, preferred_element_type=jnp.float32)
        * score_scale
    )
    keys_grad = (
        jnp.einsum("hqk,qhd->khd", score_grad, queries, preferred_element_type=jnp.float32)
        * score_scale
    )
    return (queries_grad, keys_grad, values_grad)


def local(
    layer_input,
    width_choice,
    routed_flag,
    mixer_gain,
    mixer_router,
    attention_weight,
    output_weight,
    hidden_gain,
    hidden_router,
    up_weight,
    down_weight,
    out_grad,
):
    model_rank = lax.axis_index("mp")
    local_rows = layer_input.shape[0]
    row_offset = model_rank * local_rows
    heads_local = output_weight.shape[0] // HD
    cols_local = up_weight.shape[1]
    width_local = lax.dynamic_slice_in_dim(width_choice, row_offset, local_rows, 0)
    routed_local = lax.dynamic_slice_in_dim(routed_flag, row_offset, local_rows, 0)
    head_ids = model_rank * heads_local + jnp.arange(heads_local, dtype=jnp.int32)
    head_mask = (head_ids[None, :] * 4 < (width_choice[:, 0:1] + 1) * H).astype(jnp.bfloat16)
    col_ids = model_rank * cols_local + jnp.arange(cols_local, dtype=jnp.int32)
    col_mask = (col_ids[None, :] * 4 < (width_choice[:, 1:2] + 1) * FF).astype(jnp.bfloat16)
    attention_flat = attention_weight.reshape(attention_weight.shape[0], -1)
    cosine_table, sine_table = rope_tables(SEQ_LEN, HD)
    input_wide = layer_input.astype(jnp.float32)
    normed_one, scaled_one, inverse_one = norm_forward(input_wide, mixer_gain)
    gate_one, state_one = gate_forward(
        normed_one, mixer_router, width_local[:, 0], routed_local[:, 0]
    )
    gathered_one = lax.all_gather(normed_one.astype(jnp.bfloat16), "mp", axis=0, tiled=True)
    group_rows = gathered_one.shape[0]
    qkv_rows = jnp.dot(gathered_one, attention_flat, preferred_element_type=jnp.float32)
    queries, keys_all, values_all = split_rows(qkv_rows, heads_local, cosine_table, sine_table)
    head_mix, log_total = lax.map(attend_forward, (queries, keys_all, values_all))
    heads_out = (
        (head_mix.reshape(group_rows, heads_local, HD) * head_mask[:, :, None])
        .reshape(group_rows, heads_local * HD)
        .astype(jnp.bfloat16)
    )
    mixer_branch = lax.psum_scatter(
        jnp.dot(heads_out, output_weight, preferred_element_type=jnp.float32),
        "mp",
        scatter_dimension=0,
        tiled=True,
    )
    middle = input_wide + gate_one[:, None] * mixer_branch
    normed_two, scaled_two, inverse_two = norm_forward(middle, hidden_gain)
    gate_two, state_two = gate_forward(
        normed_two, hidden_router, width_local[:, 1], routed_local[:, 1]
    )
    gathered_two = lax.all_gather(normed_two.astype(jnp.bfloat16), "mp", axis=0, tiled=True)
    pre_act = jnp.dot(gathered_two, up_weight, preferred_element_type=jnp.float32)
    relu_act = jax.nn.relu(pre_act)
    hidden = (relu_act * relu_act * col_mask).astype(jnp.bfloat16)
    hidden_branch = lax.psum_scatter(
        jnp.dot(hidden, down_weight, preferred_element_type=jnp.float32).astype(jnp.bfloat16),
        "mp",
        scatter_dimension=0,
        tiled=True,
    ).astype(jnp.float32)
    layer_output = (middle + gate_two[:, None] * hidden_branch).astype(jnp.bfloat16)
    grad_top = out_grad.astype(jnp.float32)
    branch_grad_two = (gate_two[:, None] * grad_top).astype(jnp.bfloat16)
    gate_grad_two = jnp.sum(grad_top * hidden_branch, axis=1)
    stored = lax.optimization_barrier((middle, grad_top))
    normed_again = norm_forward(stored[0], hidden_gain)[0]
    inputs_two = lax.all_gather(normed_again.astype(jnp.bfloat16), "mp", axis=0, tiled=True)
    grads_two = lax.all_gather(branch_grad_two, "mp", axis=0, tiled=True)
    pre_again = jnp.dot(inputs_two, up_weight, preferred_element_type=jnp.float32)
    relu_again = jax.nn.relu(pre_again)
    hidden_again = (relu_again * relu_again * col_mask).astype(jnp.bfloat16)
    down_weight_grad = jnp.einsum(
        "rf,rd->fd", hidden_again, grads_two, preferred_element_type=jnp.float32
    )
    hidden_grad = jnp.einsum(
        "rd,fd->rf", grads_two, down_weight, preferred_element_type=jnp.float32
    )
    pre_grad = (hidden_grad * col_mask * 2.0 * relu_again).astype(jnp.bfloat16)
    up_weight_grad = jnp.einsum(
        "rd,rf->df", inputs_two, pre_grad, preferred_element_type=jnp.float32
    )
    normed_grad_two = lax.psum_scatter(
        jnp.einsum("rf,df->rd", pre_grad, up_weight, preferred_element_type=jnp.float32),
        "mp",
        scatter_dimension=0,
        tiled=True,
    )
    router_part_two, hidden_router_grad = gate_backward(
        normed_two, hidden_router, state_two, gate_grad_two
    )
    middle_part, hidden_gain_grad = norm_backward(
        normed_grad_two + router_part_two, scaled_two, inverse_two, hidden_gain
    )
    middle_grad = grad_top + middle_part
    branch_grad_one = (gate_one[:, None] * middle_grad).astype(jnp.bfloat16)
    gate_grad_one = jnp.sum(middle_grad * mixer_branch, axis=1)
    stored_one = lax.optimization_barrier((input_wide, middle_grad))
    normed_redo = norm_forward(stored_one[0], mixer_gain)[0]
    inputs_one = lax.all_gather(normed_redo.astype(jnp.bfloat16), "mp", axis=0, tiled=True)
    grads_one = lax.all_gather(branch_grad_one, "mp", axis=0, tiled=True)
    output_weight_grad = jnp.einsum(
        "rc,rd->cd", heads_out, grads_one, preferred_element_type=jnp.float32
    )
    heads_rows = jnp.einsum(
        "rd,cd->rc", grads_one, output_weight, preferred_element_type=jnp.float32
    ).astype(jnp.bfloat16)
    heads_grad = (heads_rows.reshape(group_rows, heads_local, HD) * head_mask[:, :, None]).reshape(
        -1, SEQ_LEN, heads_local, HD
    )
    qkv_redo = jnp.dot(inputs_one, attention_flat, preferred_element_type=jnp.float32)
    queries, keys_all, values_all = split_rows(qkv_redo, heads_local, cosine_table, sine_table)
    queries_grad, keys_grad, values_grad = lax.map(
        attend_backward, (queries, keys_all, values_all, log_total, heads_grad)
    )
    qkv_grad = (
        jnp.stack(
            [
                rotate_back(queries_grad, cosine_table, sine_table),
                rotate_back(keys_grad, cosine_table, sine_table),
                values_grad,
            ],
            axis=2,
        )
        .reshape(group_rows, -1)
        .astype(jnp.bfloat16)
    )
    attention_weight_grad = jnp.einsum(
        "rd,rc->dc", inputs_one, qkv_grad, preferred_element_type=jnp.float32
    ).reshape(attention_weight.shape)
    normed_grad_one = lax.psum_scatter(
        jnp.einsum(
            "rc,dc->rd", qkv_grad, attention_flat, preferred_element_type=jnp.float32
        ).astype(jnp.bfloat16),
        "mp",
        scatter_dimension=0,
        tiled=True,
    ).astype(jnp.float32)
    router_part_one, mixer_router_grad = gate_backward(
        normed_one, mixer_router, state_one, gate_grad_one
    )
    input_part, mixer_gain_grad = norm_backward(
        normed_grad_one + router_part_one, scaled_one, inverse_one, mixer_gain
    )
    input_grad = (middle_grad + input_part).astype(jnp.bfloat16)
    attention_sum, output_sum, up_sum, down_sum = (
        lax.psum(attention_weight_grad.astype(jnp.bfloat16), "dp").astype(jnp.float32),
        lax.psum(output_weight_grad.astype(jnp.bfloat16), "dp").astype(jnp.float32),
        lax.psum(up_weight_grad.astype(jnp.bfloat16), "dp").astype(jnp.float32),
        lax.psum(down_weight_grad.astype(jnp.bfloat16), "dp").astype(jnp.float32),
    )
    mixer_gain_sum, mixer_router_sum, hidden_gain_sum, hidden_router_sum = lax.psum(
        (mixer_gain_grad, mixer_router_grad, hidden_gain_grad, hidden_router_grad), ("dp", "mp")
    )
    return (
        layer_output,
        input_grad,
        mixer_gain_sum,
        mixer_router_sum,
        attention_sum,
        output_sum,
        hidden_gain_sum,
        hidden_router_sum,
        up_sum,
        down_sum,
    )


def solution(mesh):
    return jax.shard_map(
        local,
        mesh=mesh,
        in_specs=(
            P(("dp", "mp"), None),
            P("dp", None),
            P("dp", None),
            P(),
            P(),
            P(None, None, "mp"),
            P("mp", None),
            P(),
            P(),
            P(None, "mp"),
            P("mp", None),
            P(("dp", "mp"), None),
        ),
        out_specs=(
            P(("dp", "mp"), None),
            P(("dp", "mp"), None),
            P(),
            P(),
            P(None, None, "mp"),
            P("mp", None),
            P(),
            P(),
            P(None, "mp"),
            P("mp", None),
        ),
        check_vma=False,
    )
```

profile of v0, /device:TPU:0, one launch (start us, length us, event | category | flops | bytes accessed | tf_op | source)
XLA Modules:
  0.0 1611.2 jit_solution(16401282207134468683)
XLA Ops:
  22.1 75.9 %all-gather.7.cloned.1.call-done = bf16[2048,2048]{1,0:T(8,128)(2,1)} async-done(((bf16[256,2048]{1,0:T(8,128)(2,1)}), bf16[2048,2048]{1,0:T(8,128)(2,1)}) %all-gather.7.cloned.1.call-update) | async-done | bytes 8388624 | tf_op jit(solution)/shard_map/all_gather | solution.py:191
  98.0 10.1 fusion.123
  112.1 22.2 %while.26 = (s32[]{:T(128)}, f32[2,1024,2,128]{3,2,1,0:T(2,128)}, f32[2,2,1024]{2,1,0:T(2,128)S(1)}, bf16[2,1024,2,128]{1,3,2,0:T(8,128)(2,1)}, bf16[2,1024,2,12...) while((s32[]{:T(128)}, f32[2,1024,2,128]{3,2,1,0:T(2,128)}, ...), condition=%wide.region_8.9_spmd, body=%wide.region_5.8_spmd.sunk | while | flops 1099954176 | bytes 36242528 | solution.py:195
  153.6 162.4 %reduce-scatter.5.cloned.1.call-done = f32[256,2048]{1,0:T(8,128)} async-done(((f32[2048,2048]{1,0:T(8,128)}), f32[256,2048]{1,0:T(8,128)}) %reduce-scatter.5.cloned.1.call-update) | async-done | bytes 2097168 | tf_op jit(solution)/shard_map/reduce_scatter | solution.py:201
  321.3 80.5 %all-gather.9.cloned.1.call-done = bf16[2048,2048]{1,0:T(8,128)(2,1)} async-done(((bf16[256,2048]{1,0:T(8,128)(2,1)}), bf16[2048,2048]{1,0:T(8,128)(2,1)}) %all-gather.9.cloned.1.call-update) | async-done | bytes 8388624 | tf_op jit(solution)/shard_map/all_gather | solution.py:212
  401.8 24.9 %convolution_convert_fusion.1 = bf16[2048,2048]{1,0:T(8,128)(2,1)} fusion(bf16[1024,2048]{1,0:T(8,128)(2,1)} %param.26, bf16[2048,2048]{1,0:T(8,128)(2,1)} %all-gather.9.cloned.1.call-done, bf16[2048,1024]{1,0:T(8,128)(2,1)} %param.25, s32[1024]{0:T(1024)S(1)} %add_multiply_fusion.2, s32[2048]{0:T(1024)S(1)} %bitcast.226), kind=kOutput, calls=%fused_computation.72 | convolution fusion | flops 17198743552 | bytes 25178112 | tf_op jit(solution)/shard_map/dot_general | solution.py:217
  430.2 84.8 %reduce-scatter.7.cloned.1.call-done = bf16[256,2048]{1,0:T(8,128)(2,1)} async-done(((bf16[2048,2048]{1,0:T(8,128)(2,1)}), bf16[256,2048]{1,0:T(8,128)(2,1)}) %reduce-scatter.7.cloned.1.call-update) | async-done | bytes 1048592 | tf_op jit(solution)/shard_map/reduce_scatter | solution.py:216
  518.1 79.4 %all-gather.13.cloned.1.call-done = bf16[2048,2048]{1,0:T(8,128)(2,1)} async-done(((bf16[256,2048]{1,0:T(8,128)(2,1)}), bf16[2048,2048]{1,0:T(8,128)(2,1)}) %all-gather.13.cloned.1.call-update) | async-done | bytes 8388624 | tf_op jit(solution)/shard_map/all_gather | solution.py:228
  597.5 14.6 fusion.125
  612.1 68.0 %all-gather.11.cloned.1.call-done = bf16[2048,2048]{1,0:T(8,128)(2,1)} async-done(((bf16[256,2048]{1,0:T(8,128)(2,1)}), bf16[2048,2048]{1,0:T(8,128)(2,1)}) %all-gather.11.cloned.1.call-update) | async-done | bytes 8388624 | tf_op jit(solution)/shard_map/all_gather | solution.py:229
  680.1 15.7 fusion.55
  697.9 11.8 fusion.126
  713.3 163.3 %reduce-scatter.9.cloned.1.call-done = f32[256,2048]{1,0:T(8,128)} async-done(((f32[2048,2048]{1,0:T(8,128)}), f32[256,2048]{1,0:T(8,128)}) %reduce-scatter.9.cloned.1.call-update) | async-done | bytes 2097168 | tf_op jit(solution)/shard_map/reduce_scatter | solution.py:243
  892.3 14.7 convolution_convert_fusion.2
  907.0 16.0 fusion.67
  922.9 46.3 %all-gather.15.cloned.1.call-done = bf16[2048,2048]{1,0:T(8,128)(2,1)} async-done(((bf16[256,2048]{1,0:T(8,128)(2,1)}), bf16[2048,2048]{1,0:T(8,128)(2,1)}) %all-gather.15.cloned.1.call-update) | async-done | bytes 8388624 | tf_op jit(solution)/shard_map/all_gather | solution.py:260
  969.2 10.3 fusion.127
  982.4 69.1 %all-gather.17.cloned.1.call-done = bf16[2048,2048]{1,0:T(8,128)(2,1)} async-done(((bf16[256,2048]{1,0:T(8,128)(2,1)}), bf16[2048,2048]{1,0:T(8,128)(2,1)}) %all-gather.17.cloned.1.call-update) | async-done | bytes 8388624 | tf_op jit(solution)/shard_map/all_gather | solution.py:261
  1065.4 29.6 %while.27 = (s32[]{:T(128)}, f32[2,1024,2,128]{1,3,2,0:T(8,128)}, f32[2,1024,2,128]{1,3,2,0:T(8,128)}, bf16[2,1024,2,128]{1,3,2,0:T(8,128)(2,1)}, bf16[2,1024,2,...) while((s32[]{:T(128)}, f32[2,1024,2,128]{1,3,2,0:T(8,128)}, ...), condition=%wide.region_26.27_spmd, body=%wide.region_24.26_spmd.sunk | while | flops 2717382656 | bytes 124319072 | solution.py:273
  1129.8 10.5 fusion.70
  1140.4 11.4 convolution_convert_fusion
  1160.1 220.6 %all-reduce.7.cloned.1.call-done = (bf16[2048,3,256]{2,0,1:T(8,128)(2,1)}, bf16[256,2048]{1,0:T(8,128)(2,1)}, bf16[2048,1024]{1,0:T(8,128)(2,1)}, bf16[1024,2048]{1,0:T(8,128)(2,1)}) async-done(((bf16[2048,3,256]{2,0,1:T(8,128)(2,1)}, bf16[256,2048]{1,0:T(8,128)(2,1)}, bf16[2048,1024]{1,0:T(8,128)(2,1)}, bf16[1024,2048]{1,0:T(8,128)(2,1)}), (bf16[2048,3,256]{2,0,1:T(8,128)(2,1)}, ...) | async-done | bytes 12582928 | tf_op jit(solution)/shard_map/psum | solution.py:307
  1396.5 76.1 %reduce-scatter.11.cloned.1.call-done = bf16[256,2048]{1,0:T(8,128)(2,1)} async-done(((bf16[2048,2048]{1,0:T(8,128)(2,1)}), bf16[256,2048]{1,0:T(8,128)(2,1)}) %reduce-scatter.11.cloned.1.call-update) | async-done | bytes 1048592 | tf_op jit(solution)/shard_map/reduce_scatter | solution.py:291
  1482.3 116.3 %all-reduce.5.cloned.1.call-done = (f32[2048]{0:T(1024)}, f32[2048,4]{0,1:T(4,128)}, f32[2048]{0:T(1024)}, f32[2048,4]{0,1:T(4,128)}) async-done(((f32[2048]{0:T(1024)}, f32[2048,4]{0,1:T(4,128)}, f32[2048]{0:T(1024)}, f32[2048,4]{0,1:T(4,128)}), (f32[2048]{0:T(1024)}, f32[2048,4]{0,1:T(4,128)}, f32[2048]{0:T(1024)}, f32[2048,4]{0,1:T(4,128)})) %all-reduce.5.cloned.1.call-update) | async-done | bytes 81936 | tf_op jit(solution)/shard_map/psum | solution.py:312
  (288 shorter events, 213.1 us)
Async XLA Ops:
  7.2 133.8 %copy-start = (bf16[256,2048]{1,0:T(8,128)(2,1)S(1)}, bf16[256,2048]{1,0:T(8,128)(2,1)}, u32[]{:S(2)}) copy-start(bf16[256,2048]{1,0:T(8,128)(2,1)} %param.22) | copy-start | bytes 3145732
  7.2 90.8 %all-gather.7.cloned.1.call-start = ((), (), s32[]{:S(2)}) async-start(), calls=%async_computation.4 | async-start | bytes 9437184 | tf_op jit(solution)/shard_map/all_gather | solution.py:191
  8.8 140.5 %copy-start.46 = (f32[256]{0:T(256)}, f32[256]{0:T(256)S(1)}, u32[]{:S(2)}) copy-start(f32[256]{0:T(256)S(1)} %broadcast_multiply_fusion.7) | copy-start | bytes 3076
  10.4 138.8 %copy-start.52 = (f32[256]{0:T(256)}, f32[256]{0:T(256)S(1)}, u32[]{:S(2)}) copy-start(f32[256]{0:T(256)S(1)} %add_rsqrt_fusion.3) | copy-start | bytes 3076
  13.1 303.0 %reduce-scatter.5.cloned.1.call-start = ((), (), s32[]{:S(2)}) async-start(), calls=%async_computation.5 | async-start | bytes 18874368 | tf_op jit(solution)/shard_map/reduce_scatter | solution.py:201
  22.1 87.7 %copy-start.16 = (f32[1024,64]{0,1:T(8,128)}, f32[1024,64]{0,1:T(8,128)S(1)}, u32[]{:S(2)}) copy-start(f32[1024,64]{0,1:T(8,128)S(1)} %get-tuple-element.234) | copy-start | bytes 786436
  149.1 252.7 %all-gather.9.cloned.1.call-start = ((), (), s32[]{:S(2)}) async-start(), calls=%async_computation.6 | async-start | bytes 9437184 | tf_op jit(solution)/shard_map/all_gather | solution.py:212
  150.3 165.7 %copy-start.56 = (s32[256,1]{0,1:T(1,128)}, s32[256,1]{0,1:T(1,128)S(1)}, u32[]{:S(2)}) copy-start(s32[256,1]{0,1:T(1,128)S(1)} %get-tuple-element.230) | copy-start | bytes 3076
  150.3 726.3 %copy-start.44 = (s32[256,1]{0,1:T(1,128)}, s32[256,1]{0,1:T(1,128)S(1)}, u32[]{:S(2)}) copy-start(s32[256,1]{0,1:T(1,128)S(1)} %get-tuple-element.229) | copy-start | bytes 3076
  152.9 165.6 %copy-start.50 = (f32[256]{0:T(256)}, f32[256]{0:T(256)S(1)}, u32[]{:S(2)}) copy-start(f32[256]{0:T(256)S(1)} %get-tuple-element.198) | copy-start | bytes 3076
  318.3 563.2 %copy-start.1 = (f32[256,2048]{1,0:T(8,128)}, f32[256,2048]{1,0:T(8,128)S(1)}, u32[]{:S(2)}) copy-start(f32[256,2048]{1,0:T(8,128)S(1)} %get-tuple-element.95) | copy-start | bytes 6291460
  318.4 563.2 %copy-start.36 = (f32[256]{0:T(256)}, f32[256]{0:T(256)S(1)}, u32[]{:S(2)}) copy-start(f32[256]{0:T(256)S(1)} %broadcast_multiply_fusion.6) | copy-start | bytes 3076
  319.3 562.3 %copy-start.38 = (f32[256]{0:T(256)}, f32[256]{0:T(256)S(1)}, u32[]{:S(2)}) copy-start(f32[256]{0:T(256)S(1)} %add_rsqrt_fusion.2) | copy-start | bytes 3076
  321.3 193.8 %reduce-scatter.7.cloned.1.call-start = ((), (), s32[]{:S(2)}) async-start(), calls=%async_computation.7 | async-start | bytes 9437184 | tf_op jit(solution)/shard_map/reduce_scatter | solution.py:216
  426.7 170.8 %all-gather.13.cloned.1.call-start = ((), (), s32[]{:S(2)}) async-start(), calls=%async_computation.9 | async-start | bytes 9437184 | tf_op jit(solution)/shard_map/all_gather | solution.py:228
  427.3 252.8 %all-gather.11.cloned.1.call-start = ((), (), s32[]{:S(2)}) async-start(), calls=%async_computation.8 | async-start | bytes 9437184 | tf_op jit(solution)/shard_map/all_gather | solution.py:229
  429.4 447.2 %copy-start.40 = (f32[256,4]{0,1:T(4,128)}, f32[256,4]{0,1:T(4,128)S(1)}, u32[]{:S(2)}) copy-start(f32[256,4]{0,1:T(4,128)S(1)} %get-tuple-element.195) | copy-start | bytes 12292
  518.1 358.5 %reduce-scatter.9.cloned.1.call-start = ((), (), s32[]{:S(2)}) async-start(), calls=%async_computation.10 | async-start | bytes 18874368 | tf_op jit(solution)/shard_map/reduce_scatter | solution.py:243
  709.7 259.6 %all-gather.15.cloned.1.call-start = ((), (), s32[]{:S(2)}) async-start(), calls=%async_computation.11 | async-start | bytes 9437184 | tf_op jit(solution)/shard_map/all_gather | solution.py:260
  713.3 168.3 %copy-start.48 = (f32[256,1]{0,1:T(1,128)}, f32[256,1]{0,1:T(1,128)S(1)}, u32[]{:S(2)}) copy-start(f32[256,1]{0,1:T(1,128)S(1)} %fusion.112) | copy-start | bytes 3076
  888.9 162.6 %all-gather.17.cloned.1.call-start = ((), (), s32[]{:S(2)}) async-start(), calls=%async_computation.12 | async-start | bytes 9437184 | tf_op jit(solution)/shard_map/all_gather | solution.py:261
  891.7 489.0 %all-reduce.7.cloned.1.call-start = ((), (), s32[]{:S(2)}) async-start(), calls=%async_computation.15 | async-start | bytes 25165824 | tf_op jit(solution)/shard_map/psum | solution.py:307
  1140.3 332.3 %reduce-scatter.11.cloned.1.call-start = ((), (), s32[]{:S(2)}) async-start(), calls=%async_computation.13 | async-start | bytes 9437184 | tf_op jit(solution)/shard_map/reduce_scatter | solution.py:291
  1151.9 446.7 %all-reduce.5.cloned.1.call-start = ((), (), s32[]{:S(2)}) async-start(), calls=%async_computation.14 | async-start | bytes 163840 | tf_op jit(solution)/shard_map/psum | solution.py:312
  (60 other events, 433.4 us)
Sparse Core Ops, SparseCore 0:
  13.2 84.7 all-gather.6
  149.2 166.7 reduce-scatter.4
  321.4 80.3 all-gather.8
  426.8 88.1 reduce-scatter.6
  517.1 80.3 all-gather.12
  599.5 80.5 all-gather.10
  709.8 166.7 reduce-scatter.8
  889.0 80.1 all-gather.14
  970.8 80.5 all-gather.16
  1140.4 240.1 all-reduce.6
  1383.0 89.5 reduce-scatter.10
  1479.1 119.4 all-reduce.4
where the time goes:
time: 1620 us; the launch traced here: 1610 us
  waiting for transfers between devices  1240 us (77%)
  matrix products  215 us (13%)
  other arithmetic  74.7 us (5%)
  local copies, waits for them, and re-layouts  61.5 us (4%)
    psum x1, waiting for transfers between devices, local(): lax.psum(attention_weight_grad.astype(jnp.bfloat16), 'dp')  221 us
    reduce_scatter x1, waiting for transfers between devices, local(): lax.psum_scatter(jnp.einsum('rf,df->rd', pre_grad, up_weight, preferred_e...  163 us
    reduce_scatter x1, waiting for transfers between devices, local(): lax.psum_scatter(jnp.dot(heads_out, output_weight, preferred_element_type...  162 us
    psum x1, waiting for transfers between devices, local(): lax.psum((mixer_gain_grad, mixer_router_grad, hidden_gain_grad, hidden_ro...  116 us
    reduce_scatter x1, waiting for transfers between devices, local(): lax.psum_scatter(jnp.dot(hidden, down_weight, preferred_element_type=jnp....  84.8 us
    all_gather x1, waiting for transfers between devices, local(): lax.all_gather(normed_two.astype(jnp.bfloat16), 'mp', axis=0, tiled=True)  80.5 us
    all_gather x1, waiting for transfers between devices, local(): lax.all_gather(normed_again.astype(jnp.bfloat16), 'mp', axis=0, tiled=True)  79.4 us
    reduce_scatter x1, waiting for transfers between devices, local(): lax.psum_scatter(jnp.einsum('rc,dc->rd', qkv_grad, attention_flat, prefer...  76.1 us
  transfers between devices with their start and end apart: 12, of which 12 were waited for; matrix products, arithmetic and copies ran while one was open for 7% of the time, Pallas kernels for 0%

commit v1 on v0

v1 whole, which is shorter than its diff:
```python
import math

import jax
import jax.numpy as jnp
from jax import lax
from jax.experimental import pallas as pl
from jax.experimental.pallas import tpu as pltpu
from jax.sharding import PartitionSpec as P

H = 16
HD = 128
FF = 8192
SEQ_LEN = 1024


EPSILON = 1e-05
NEG_LARGE = -1e30
HIGHEST = lax.Precision.HIGHEST


def norm_forward(values, gain_vec):
    row_mean = jnp.mean(values, axis=1, keepdims=True)
    centred = values - row_mean
    row_variance = jnp.mean(centred * centred, axis=1, keepdims=True)
    inverse_scale = lax.rsqrt(row_variance + EPSILON)
    scaled = centred * inverse_scale
    return (scaled * gain_vec[None, :], scaled, inverse_scale)


def norm_backward(normed_grad, scaled, inverse_scale, gain_vec):
    gain_grad = jnp.sum(normed_grad * scaled, axis=0)
    scaled_grad = normed_grad * gain_vec[None, :]
    first_mean = jnp.mean(scaled_grad, axis=1, keepdims=True)
    second_mean = jnp.mean(scaled_grad * scaled, axis=1, keepdims=True)
    return (inverse_scale * (scaled_grad - first_mean - scaled * second_mean), gain_grad)


def gate_forward(normed, router, width_col, routed_col):
    logits = jnp.dot(normed, router, precision=HIGHEST, preferred_element_type=jnp.float32)
    soft_probs = jax.nn.softmax(logits, axis=1)
    one_hot = (width_col[:, None] == jnp.arange(4, dtype=jnp.int32)[None, :]).astype(jnp.float32)
    chosen = jnp.sum(soft_probs * one_hot, axis=1)
    route_flags = routed_col.astype(jnp.float32)
    return (
        route_flags * 4.0 * chosen + (1.0 - route_flags),
        (soft_probs, one_hot, chosen, route_flags),
    )


def gate_backward(normed, router, gate_state, gate_grad):
    soft_probs, one_hot, chosen, route_flags = gate_state
    coefficient = route_flags * 4.0 * chosen * gate_grad
    logit_grad = coefficient[:, None] * (one_hot - soft_probs)
    router_grad = lax.dot_general(
        normed,
        logit_grad,
        (((0,), (0,)), ((), ())),
        precision=HIGHEST,
        preferred_element_type=jnp.float32,
    )
    normed_grad = lax.dot_general(
        logit_grad,
        router,
        (((1,), (1,)), ((), ())),
        precision=HIGHEST,
        preferred_element_type=jnp.float32,
    )
    return (normed_grad, router_grad)


Q_BLOCK = 256


def rope_tables(token_count, head_width):
    positions = jnp.arange(token_count, dtype=jnp.float32)
    frequency = jnp.exp(
        jnp.arange(head_width // 2, dtype=jnp.float32) * (-2.0 * math.log(10000.0) / head_width)
    )
    angles = positions[:, None] * frequency[None, :]
    cosine, sine = jnp.cos(angles), jnp.sin(angles)
    return jnp.concatenate([cosine, cosine], axis=1), jnp.concatenate([-sine, sine], axis=1)


def wide(x):
    return x.astype(jnp.float32)


def narrow(x):
    return x.astype(jnp.bfloat16)


def product(a, b, dims):
    return lax.dot_general(a, b, ((dims[:1], dims[1:]), ((), ())), preferred_element_type=jnp.float32)


def block_scores(queries, keys_all, start):
    scores = product(queries, keys_all, (1, 1)) * (1.0 / math.sqrt(HD))
    row = lax.broadcasted_iota(jnp.int32, scores.shape, 0) + start
    col = lax.broadcasted_iota(jnp.int32, scores.shape, 1)
    return jnp.where(col <= row, scores, NEG_LARGE)


def forward_kernel(x_ref, w_ref, cos_ref, sin_ref, mask_ref, qkv_ref, heads_ref, log_ref):
    tokens, heads = x_ref.shape[0], mask_ref.shape[1]
    block = min(Q_BLOCK, tokens)
    for start in range(0, tokens, block):
        here, end = slice(start, start + block), start + block
        x = x_ref[here, :]
        cos, sin = cos_ref[here, :], sin_ref[here, :]
        for part in range(3):
            rows = product(x, w_ref[part], (1, 0))
            for head in range(heads):
                lanes = slice(head * HD, (head + 1) * HD)
                value = rows[:, lanes]
                if part < 2:
                    value = value * cos + pltpu.roll(value, HD // 2, 1) * sin
                qkv_ref[part, here, lanes] = narrow(value)
        for head in range(heads):
            lanes = slice(head * HD, (head + 1) * HD)
            scores = block_scores(qkv_ref[0, here, lanes], qkv_ref[1, :end, lanes], start)
            row_max = jnp.max(scores, axis=1, keepdims=True)
            shifted = jnp.exp(scores - row_max)
            total = jnp.sum(shifted, axis=1, keepdims=True)
            mix = product(narrow(shifted / total), qkv_ref[2, :end, lanes], (1, 0))
            heads_ref[here, lanes] = narrow(mix * mask_ref[here, head : head + 1])
            log_ref[here, head : head + 1] = row_max + jnp.log(total)


def backward_kernel(g_ref, w_ref, qkv_ref, log_ref, cos_ref, sin_ref, mask_ref, out_ref, keys_acc, values_acc):
    tokens, heads = g_ref.shape[0], mask_ref.shape[1]
    block = min(Q_BLOCK, tokens)
    scale = 1.0 / math.sqrt(HD)
    for start in range(0, tokens, block):
        here, end = slice(start, start + block), start + block
        cos, sin = cos_ref[here, :], sin_ref[here, :]
        rows = narrow(product(g_ref[here, :], w_ref[0], (1, 0)))
        for head in range(heads):
            lanes = slice(head * HD, (head + 1) * HD)
            heads_grad = rows[:, lanes] * narrow(mask_ref[here, head : head + 1])
            queries, keys_all = qkv_ref[0, here, lanes], qkv_ref[1, :end, lanes]
            scores = block_scores(queries, keys_all, start)
            probs = jnp.exp(scores - log_ref[here, head : head + 1])
            values_part = product(narrow(probs), heads_grad, (0, 0))
            probs_grad = product(heads_grad, qkv_ref[2, :end, lanes], (1, 1))
            centre = jnp.sum(probs * probs_grad, axis=1, keepdims=True)
            score_grad = narrow(probs * (probs_grad - centre))
            queries_grad = product(score_grad, keys_all, (1, 0)) * scale
            keys_part = product(score_grad, queries, (0, 0)) * scale
            turned = queries_grad * cos - pltpu.roll(queries_grad, HD // 2, 1) * sin
            out_ref[0, here, lanes] = narrow(turned)
            if start:
                values_acc[:start, lanes] += values_part[:start]
                keys_acc[:start, lanes] += keys_part[:start]
            values_acc[here, lanes] = values_part[start:]
            keys_acc[here, lanes] = keys_part[start:]
    for start in range(0, tokens, block):
        here = slice(start, start + block)
        cos, sin = cos_ref[here, :], sin_ref[here, :]
        out_ref[2, here, :] = narrow(values_acc[here, :])
        for head in range(heads):
            lanes = slice(head * HD, (head + 1) * HD)
            value = keys_acc[here, lanes]
            out_ref[1, here, lanes] = narrow(value * cos - pltpu.roll(value, HD // 2, 1) * sin)


VMEM_LIMIT = 56 * 1024 * 1024


def whole_specs(count):
    return [pl.BlockSpec(memory_space=pltpu.VMEM)] * count


def attend_forward(x, w, cos, sin, mask):
    tokens, heads = mask.shape
    dim, width = w.shape[1:]
    flops = 2 * tokens * dim * width * 3 + 2 * tokens * tokens * width
    return pl.pallas_call(
        forward_kernel,
        out_shape=(
            jax.ShapeDtypeStruct((3, tokens, width), jnp.bfloat16),
            jax.ShapeDtypeStruct((tokens, width), jnp.bfloat16),
            jax.ShapeDtypeStruct((tokens, heads), jnp.float32),
        ),
        in_specs=whole_specs(5),
        out_specs=tuple(whole_specs(3)),
        compiler_params=pltpu.CompilerParams(vmem_limit_bytes=VMEM_LIMIT),
        cost_estimate=pl.CostEstimate(flops=flops, bytes_accessed=12 << 20, transcendentals=tokens * tokens * heads // 2),
        name="attend_forward",
    )(x, w, cos, sin, mask)


def attend_backward(g, w, qkv, log_total, cos, sin, mask):
    tokens, heads = mask.shape
    dim, width = w.shape[1:]
    flops = 2 * tokens * dim * width + 5 * tokens * tokens * width
    fixed = whole_specs(1)[0]
    return pl.pallas_call(
        backward_kernel,
        grid=(1,),
        out_shape=jax.ShapeDtypeStruct((3, tokens, width), jnp.bfloat16),
        in_specs=[fixed, pl.BlockSpec((1, dim, width), lambda i: (3, 0, 0))] + [fixed] * 5,
        out_specs=fixed,
        scratch_shapes=[pltpu.VMEM((tokens, width), jnp.float32)] * 2,
        compiler_params=pltpu.CompilerParams(vmem_limit_bytes=VMEM_LIMIT),
        cost_estimate=pl.CostEstimate(flops=flops, bytes_accessed=8 << 20, transcendentals=tokens * tokens * heads // 2),
        name="attend_backward",
    )(g, w, qkv, log_total, cos, sin, mask)


def swap_pairs(size, bit):
    return [(i, i ^ bit) for i in range(size)]


def shift_pairs(size, shift):
    return [(i, (i - shift) % size) for i in range(size)]


def bits_of(size):
    return [1 << i for i in range(size.bit_length() - 1)]


def pick(x, index, axis=0):
    return lax.dynamic_index_in_dim(x, index, axis, keepdims=False)


def after(x, *others):
    return lax.optimization_barrier((x,) + others)[0]


def xor_gather(x, axis, size, bits):
    held = {0: x}
    for bit in bits:
        for far in list(held):
            held[far ^ bit] = lax.ppermute(held[far], axis, swap_pairs(size, bit))
    return held


def by_index(held, index, axis=0):
    shape = held[0].shape
    out = jnp.zeros(shape[:axis] + (len(held),) + shape[axis:], held[0].dtype)
    for far, block in held.items():
        out = lax.dynamic_update_index_in_dim(out, block, index ^ far, axis)
    return out


def xor_scatter(blocks, axis_name, size, bits, steps, index, axis):
    count = blocks.shape[axis].bit_length() - 1
    blocks = blocks.reshape(blocks.shape[:axis] + (2,) * count + blocks.shape[axis + 1 :])
    left = [1 << (count - 1 - i) for i in range(count)]
    for bit, step in zip(bits, steps):
        at = axis + left.index(step)
        left.remove(step)
        side = (index // step) % 2
        got = lax.ppermute(narrow(pick(blocks, 1 - side, at)), axis_name, swap_pairs(size, bit))
        blocks = wide(pick(blocks, side, at)) + wide(got)
    return blocks


def column_gather(x, size, column):
    bits, half = bits_of(size), x.shape[1] // 2
    parts = [
        by_index(xor_gather(x[:, :half], "dp", size, bits), column, 1),
        by_index(xor_gather(x[:, half:], "dp", size, bits[::-1]), column, 1),
    ]
    return jnp.concatenate(parts, axis=2).reshape(x.shape[0], -1, x.shape[2])


def column_scatter(x, size, column):
    bits = bits_of(size)
    blocks = x.reshape(x.shape[0], size, -1, x.shape[2])
    half = blocks.shape[2] // 2
    return jnp.concatenate(
        [
            narrow(xor_scatter(blocks[:, :, :half], "dp", size, bits, bits, column, 1)),
            narrow(xor_scatter(blocks[:, :, half:], "dp", size, bits[::-1], bits[::-1], column, 1)),
        ],
        axis=1,
    )


def all_sum(x, sizes):
    for axis, size in sizes.items():
        for bit in bits_of(size):
            x = x + lax.ppermute(x, axis, swap_pairs(size, bit))
    return x


def make_local(columns, ranks):
    def local(
        layer_input, width_choice, routed_flag, mixer_gain, mixer_router, attention_weight,
        output_weight, hidden_gain, hidden_router, up_weight, down_weight, out_grad,
    ):
        column, rank = lax.axis_index("dp"), lax.axis_index("mp")
        rows, dim = layer_input.shape
        core = rank % 2
        group = SEQ_LEN // rows
        sequences = ranks // group
        place, sequence = rank % group, rank // group
        pair_bits = [b for b in bits_of(group) if b > 1]
        own_heads = output_weight.shape[0] // HD
        cols_local = up_weight.shape[1]
        width_own = lax.dynamic_slice_in_dim(width_choice, rank * rows, rows, 0)
        routed_own = lax.dynamic_slice_in_dim(routed_flag, rank * rows, rows, 0)
        cos, sin = rope_tables(SEQ_LEN, HD)

        def to_sequence(x):
            held = xor_gather(x, "mp", ranks, pair_bits + [1])
            return by_index(held, place).reshape(SEQ_LEN, -1), held

        def from_sequence(x):
            blocks = x.reshape(group // 2, 2, -1, x.shape[1])
            got = lax.ppermute(narrow(pick(blocks, 1 - core, 1)), "mp", swap_pairs(ranks, 1))
            blocks = wide(pick(blocks, core, 1)) + wide(got)
            bits = pair_bits[::-1]
            return xor_scatter(blocks, "mp", ranks, bits, [b // 2 for b in bits], place // 2, 0)

        planes = jnp.concatenate([attention_weight.transpose(1, 0, 2), output_weight.T[None]], axis=0)
        plane_rows = dim // columns
        chunk = lax.dynamic_slice_in_dim(planes, column * plane_rows, plane_rows, 1)
        weights, fetched = [planes], []
        for k in range(1, sequences):
            got = lax.ppermute(chunk, "mp", shift_pairs(ranks, k * group))
            fetched.append(got)
            weights.append(column_gather(got, columns, column))

        input_wide = wide(layer_input)
        normed_one, scaled_one, inverse_one = norm_forward(input_wide, mixer_gain)
        inputs_one, held_one = to_sequence(narrow(normed_one))
        gate_one, state_one = gate_forward(normed_one, mixer_router, width_own[:, 0], routed_own[:, 0])
        grads_all = lax.all_gather(after(out_grad, *fetched), "mp", axis=0, tiled=True)

        sequence_width = lax.dynamic_slice_in_dim(width_choice[:, 0], sequence * SEQ_LEN, SEQ_LEN, 0)
        kept = []
        branch = None
        for k in range(sequences):
            heads = ((rank + k * group) % ranks) * own_heads + jnp.arange(own_heads, dtype=jnp.int32)
            mask = (heads[None, :] * 4 < (sequence_width[:, None] + 1) * H).astype(jnp.float32)
            qkv, heads_out, log_total = attend_forward(inputs_one, weights[k], cos, sin, mask)
            kept.append((qkv, heads_out, log_total, mask))
            share = product(heads_out, weights[k][3], (1, 1))
            branch = share if branch is None else branch + share
        mixer_branch = from_sequence(branch)

        middle = input_wide + gate_one[:, None] * mixer_branch
        normed_two, scaled_two, inverse_two = norm_forward(middle, hidden_gain)
        gate_two, state_two = gate_forward(normed_two, hidden_router, width_own[:, 1], routed_own[:, 1])
        inputs_two = lax.all_gather(narrow(normed_two), "mp", axis=0, tiled=True)
        gates = by_index(xor_gather(gate_two.reshape(-1, 128), "mp", ranks, bits_of(ranks)), rank).reshape(-1)

        col_ids = rank * cols_local + jnp.arange(cols_local, dtype=jnp.int32)
        col_mask = (col_ids[None, :] * 4 < (width_choice[:, 1:2] + 1) * FF).astype(jnp.float32)
        top_down = product(grads_all, down_weight, (1, 1))
        pre = product(inputs_two, up_weight, (1, 0))
        relu_act = jax.nn.relu(pre)
        hidden = narrow(relu_act * relu_act * col_mask)
        pre_grad = narrow(top_down * gates[:, None] * col_mask * 2.0 * relu_act)
        normed_grad_two = wide(
            lax.psum_scatter(narrow(product(pre_grad, up_weight, (1, 1))), "mp", scatter_dimension=0, tiled=True)
        )
        dots = jnp.sum(wide(hidden) * top_down, axis=1).reshape(-1, 128)
        gate_grad_two = lax.dynamic_slice_in_dim(all_sum(dots, {"mp": ranks}).reshape(-1), rank * rows, rows, 0)
        router_part, router_two = gate_backward(normed_two, hidden_router, state_two, gate_grad_two)
        middle_part, gain_two = norm_backward(normed_grad_two + router_part, scaled_two, inverse_two, hidden_gain)
        middle_grad = wide(out_grad) + middle_part
        gated = narrow(gates[:, None] * wide(grads_all))
        down_grad = narrow(product(hidden, gated, (0, 0)))
        up_grad = narrow(product(inputs_two, pre_grad, (0, 0)))

        def column_total(x):
            return wide(column_gather(column_scatter(x[None], columns, column), columns, column)[0])

        down_sum = column_total(down_grad)
        up_sum = column_total(up_grad)

        grads_one, held_grads = to_sequence(narrow(gate_one[:, None] * middle_grad))
        share = narrow(product(hidden, down_weight, (1, 0)))
        share = after(share, *held_grads.values())
        hidden_branch = wide(lax.psum_scatter(share, "mp", scatter_dimension=0, tiled=True))
        layer_output = narrow(middle + gate_two[:, None] * hidden_branch)

        gate_grad_one = jnp.sum(middle_grad * mixer_branch, axis=1)
        share_one = None
        plane_grads = [None] * sequences
        for k in range(sequences)[::-1]:
            qkv, heads_out, log_total, mask = kept[k]
            qkv_grad = attend_backward(grads_one, weights[k], qkv, log_total, cos, sin, mask)
            in_grads = [product(inputs_one, qkv_grad[p], (0, 0)) for p in range(3)]
            plane_grads[k] = jnp.stack([narrow(x) for x in in_grads] + [narrow(product(grads_one, heads_out, (0, 0)))])
            for p in range(3):
                share = product(qkv_grad[p], weights[k][p], (1, 1))
                share_one = share if share_one is None else share_one + share
        normed_grad_one = from_sequence(share_one)

        piece = wide(column_scatter(plane_grads[0], columns, column))
        for k in range(1, sequences):
            there = column_scatter(plane_grads[k], columns, column)
            piece = piece + wide(lax.ppermute(there, "mp", shift_pairs(ranks, -k * group)))
        plane_sum = wide(column_gather(narrow(piece), columns, column))
        attention_sum = plane_sum[:3].transpose(1, 0, 2)
        output_sum = plane_sum[3].T

        router_part_one, router_one = gate_backward(normed_one, mixer_router, state_one, gate_grad_one)
        input_part, gain_one = norm_backward(normed_grad_one + router_part_one, scaled_one, inverse_one, mixer_gain)
        input_grad = narrow(middle_grad + input_part)

        sizes = {"mp": ranks, "dp": columns}

        def small_total(gain, router):
            packed = jnp.concatenate([gain.reshape(-1, 128), router.T.reshape(-1, 128)], axis=0)
            packed = all_sum(packed, sizes)
            cut = dim // 128
            return packed[:cut].reshape(dim), packed[cut:].reshape(-1, dim).T

        hidden_gain_sum, hidden_router_sum = small_total(gain_two, router_two)
        mixer_gain_sum, mixer_router_sum = small_total(gain_one, router_one)
        return (
            layer_output, input_grad, mixer_gain_sum, mixer_router_sum, attention_sum, output_sum,
            hidden_gain_sum, hidden_router_sum, up_sum, down_sum,
        )

    return local


def solution(mesh):
    return jax.shard_map(
        make_local(mesh.shape["dp"], mesh.shape["mp"]),
        mesh=mesh,
        in_specs=(
            P(("dp", "mp"), None),
            P("dp", None),
            P("dp", None),
            P(),
            P(),
            P(None, None, "mp"),
            P("mp", None),
            P(),
            P(),
            P(None, "mp"),
            P("mp", None),
            P(("dp", "mp"), None),
        ),
        out_specs=(
            P(("dp", "mp"), None),
            P(("dp", "mp"), None),
            P(),
            P(),
            P(None, None, "mp"),
            P("mp", None),
            P(),
            P(),
            P(None, "mp"),
            P("mp", None),
        ),
        check_vma=False,
    )
```

time: 1620 us -> 910 us (0.56)
  waiting for transfers between devices: 1240 us -> 433 us
  starting transfers between devices: 1.15 us -> 68.4 us
  Pallas kernels: 0 us -> 52.7 us
  matrix products: 215 us -> 179 us
    reduce_scatter x4 -> x2, waiting for transfers between devices: 487 us -> 0.01 us  [the longest x1 0.01 us: local(): lax.psum_scatter(narrow(product(pre_grad, up_weight, (1, 1))), 'mp', scat...]
    psum x2 -> x0, waiting for transfers between devices: 337 us -> none  [the longest x1 221 us: local(): lax.psum(attention_weight_grad.astype(jnp.bfloat16), 'dp')]
    ppermute x0 -> x72, waiting for transfers between devices: none -> 301 us  [the longest x37 94.8 us: xor_gather(): held[far ^ bit] = lax.ppermute(held[far], axis, swap_pairs(size, bit))]
    all_gather x6 -> x2, waiting for transfers between devices: 419 us -> 132 us  [the longest x1 67.3 us: local(): lax.all_gather(after(out_grad, *fetched), 'mp', axis=0, tiled=True)]
    ppermute x0 -> x72, starting transfers between devices: none -> 68.3 us  [the longest x37 38.1 us: xor_gather(): held[far ^ bit] = lax.ppermute(held[far], axis, swap_pairs(size, bit))]
    pallas_call x0 -> x4, Pallas kernels: none -> 52.7 us  [the longest x2 26.9 us: attend_backward(): pl.pallas_call(backward_kernel, grid=(1,), out_shape=jax.ShapeDtypeStruct...]
    dot_general x27 -> x22, matrix products: 195 us -> 165 us  [product(): lax.dot_general(a, b, ((dims[:1], dims[1:]), ((), ())), preferred_element...]
    dynamic_update_slice x4 -> x42, local copies, waits for them, and re-layouts: 3.25 us -> 22.5 us  [by_index(): out = lax.dynamic_update_index_in_dim(out, block, index ^ far, axis)]
  transfers between devices with their start and end apart: 12 -> 76, of which waited for: 12 -> 36; matrix products, arithmetic and copies ran while one was open for 7% -> 28% of each run, Pallas kernels for 0% -> 2%
where the time goes in v1:
time: 910 us; the launch traced here: 904 us
  waiting for transfers between devices  433 us (48%)
  matrix products  179 us (20%)
  other arithmetic  78.7 us (9%)
  local copies, waits for them, and re-layouts  76.8 us (8%)
  starting transfers between devices  68.4 us (8%)
  Pallas kernels  52.7 us (6%)
  between operations  15.5 us (2%)
    dot_general x22, matrix products, product(): lax.dot_general(a, b, ((dims[:1], dims[1:]), ((), ())), preferred_element...  165 us
    ppermute x37, waiting for transfers between devices, xor_gather(): held[far ^ bit] = lax.ppermute(held[far], axis, swap_pairs(size, bit))  94.8 us
    ppermute x18, waiting for transfers between devices, xor_scatter(): lax.ppermute(narrow(pick(blocks, 1 - side, at)), axis_name, swap_pairs(si...  90.3 us
    all_gather x1, waiting for transfers between devices, local(): lax.all_gather(after(out_grad, *fetched), 'mp', axis=0, tiled=True)  67.3 us
    all_gather x1, waiting for transfers between devices, local(): inputs_two = lax.all_gather(narrow(normed_two), 'mp', axis=0, tiled=True)  64.6 us
    ppermute x1, waiting for transfers between devices, local(): lax.ppermute(there, 'mp', shift_pairs(ranks, -k * group))  43.7 us
    ppermute x37, starting transfers between devices, xor_gather(): held[far ^ bit] = lax.ppermute(held[far], axis, swap_pairs(size, bit))  38.1 us
    ppermute x1, waiting for transfers between devices, local(): got = lax.ppermute(chunk, 'mp', shift_pairs(ranks, k * group))  35.3 us
  transfers between devices with their start and end apart: 76, of which 36 were waited for; matrix products, arithmetic and copies ran while one was open for 28% of the time, Pallas kernels for 2%

profile of v1, /device:TPU:0, one launch (start us, length us, event | category | flops | bytes accessed | tf_op | source)
XLA Modules:
  0.0 904.1 jit_solution(14865607014076410568)
XLA Ops:
  34.4 35.3 %collective-permute-done.3 = bf16[4,512,256]{2,1,0:T(8,128)(2,1)S(1)} collective-permute-done((bf16[4,512,256]{2,1,0:T(8,128)(2,1)}, bf16[4,512,256]{2,1,0:T(8,128)(2,1)S(1)}, u32[]{:S(2)}, u32[]{:S(2)}) %collective-permute-start.3) | collective-permute-done | bytes 1048608 | tf_op jit(solution)/shard_map/ppermute | solution.py:322
  86.1 11.2 %collective-permute-done.7 = bf16[4,256,256]{2,1,0:T(8,128)(2,1)S(1)} collective-permute-done((bf16[4,256,256]{2,1,0:T(8,128)(2,1)S(1)}, bf16[4,256,256]{2,1,0:T(8,128)(2,1)S(1)}, u32[]{:S(2)}, u32[]{:S(2)}) %collective-permute-start.7) | collective-permute-done | bytes 524320 | tf_op jit(solution)/shard_map/ppermute | solution.py:234
  113.6 12.9 %attend_forward.2 = (bf16[3,1024,256]{2,1,0:T(8,128)(2,1)}, bf16[1024,256]{1,0:T(8,128)(2,1)}, f32[1024,2]{1,0:T(8,128)}) custom-call(bf16[1024,2048]{1,0:T(8,128)(2,1)} %bitcast.7.x_ref, bf16[4,2048,256]{2,1,0:T(8,128)(2,1)} %pad_maximum_fusion.1.w_ref, f32[1024,128]{1,0:T(8,128)} %get-tuple-element.91.cos_ref, f32[1024,128]{1,0:T(8,128)} %get-tuple-element.92.sin_ref, ...), custom_call_target="tpu_custom_call" | custom-call | flops 3758096384 | bytes 12582912 | tf_op jit(solution)/shard_map/attend_forward/pallas_call | solution.py:177
  132.2 12.9 %attend_forward.3 = (bf16[3,1024,256]{2,1,0:T(8,128)(2,1)}, bf16[1024,256]{1,0:T(8,128)(2,1)}, f32[1024,2]{1,0:T(8,128)}) custom-call(bf16[1024,2048]{1,0:T(8,128)(2,1)} %bitcast.7.x_ref, bf16[4,2048,256]{2,1,0:T(8,128)(2,1)} %bitcast.394, f32[1024,128]{1,0:T(8,128)} %get-tuple-element.91.cos_ref, f32[1024,128]{1,0:T(8,128)} %get-tuple-element.92.sin_ref, ...), custom_call_target="tpu_custom_call" | custom-call | flops 3758096384 | bytes 12582912 | tf_op jit(solution)/shard_map/attend_forward/pallas_call | solution.py:177
  167.6 21.3 %collective-permute-done.11 = bf16[256,2048]{1,0:T(8,128)(2,1)S(1)} collective-permute-done((bf16[256,2048]{1,0:T(8,128)(2,1)S(1)}, bf16[256,2048]{1,0:T(8,128)(2,1)S(1)}, u32[]{:S(2)}, u32[]{:S(2)}) %collective-permute-start.11) | collective-permute-done | bytes 1048608 | tf_op jit(solution)/shard_map/ppermute | solution.py:254
  211.3 64.6 %all-gather.3.cloned.1.call-done = bf16[2048,2048]{1,0:T(8,128)(2,1)} async-done(((bf16[256,2048]{1,0:T(8,128)(2,1)}), bf16[2048,2048]{1,0:T(8,128)(2,1)}) %all-gather.3.cloned.1.call-update) | async-done | bytes 8388624 | tf_op jit(solution)/shard_map/all_gather | solution.py:347
  275.9 14.8 %fusion.111 = f32[2048,1024]{0,1:T(8,128)} fusion(bf16[2048,2048]{1,0:T(8,128)(2,1)} %all-gather.3.cloned.1.call-done, bf16[2048,1024]{1,0:T(8,128)(2,1)} %param.21), kind=kOutput, calls=%fused_computation.299 | convolution fusion | flops 8589934592 | bytes 20971520 | tf_op jit(solution)/shard_map/dot_general | solution.py:93
  290.8 67.3 %all-gather.5.cloned.1.call-done = bf16[2048,2048]{1,0:T(8,128)(2,1)} async-done(((bf16[256,2048]{1,0:T(8,128)(2,1)}), bf16[2048,2048]{1,0:T(8,128)(2,1)}) %all-gather.5.cloned.1.call-update) | async-done | bytes 8388624 | tf_op jit(solution)/shard_map/all_gather | solution.py:330
  358.1 16.9 %multiply_reduce_fusion = (f32[2048]{0:T(1024)S(1)}, bf16[2048,1024]{0,1:T(8,128)(2,1)}, bf16[2048,1024]{0,1:T(8,128)(2,1)S(1)}) fusion(f32[2048,1024]{0,1:T(8,128)} %fusion.111, s32[2048]{0:T(1024)S(1)} %bitcast.453, s32[1024]{0:T(1024)S(1)} %add_multiply_fusion.1, f32[2048]{0:T(1024)S(1)} %bitcast.451, ...), kind=kOutput, calls=%fused_computation.10 | convolution fusion | flops 8617195520 | bytes 29388800 | tf_op jit(solution)/shard_map/dot_general | solution.py:93
  377.0 11.8 %convolution_convert_fusion = bf16[2048,2048]{1,0:T(8,128)(2,1)} fusion(bf16[2048,1024]{0,1:T(8,128)(2,1)S(1)} %get-tuple-element.57, bf16[2048,1024]{1,0:T(8,128)(2,1)S(1)} %copy-done.51), kind=kOutput, calls=%fused_computation.11 | convolution fusion | flops 8594128896 | bytes 16777216 | tf_op jit(solution)/shard_map/dot_general | solution.py:93
  388.9 12.7 %fusion.6 = bf16[1024,2048]{1,0:T(8,128)(2,1)S(1)} fusion(bf16[2048,1024]{0,1:T(8,128)(2,1)} %get-tuple-element.48, bf16[2048,2048]{1,0:T(8,128)(2,1)} %all-gather.5.cloned.1.call-done, f32[2048]{0:T(1024)S(1)} %bitcast.452), kind=kOutput, calls=%fused_computation.37 | convolution fusion | flops 8604614656 | bytes 16785408 | tf_op jit(solution)/shard_map/dot_general | solution.py:93
  405.7 11.4 %convolution_convert_fusion.2 = bf16[2048,1024]{1,0:T(8,128)(2,1)S(1)} fusion(bf16[2048,2048]{1,0:T(8,128)(2,1)} %all-gather.3.cloned.1.call-done, bf16[2048,1024]{0,1:T(8,128)(2,1)S(1)} %copy-done.56), kind=kOutput, calls=%fused_computation.38 | convolution fusion | flops 8592031744 | bytes 16777216 | tf_op jit(solution)/shard_map/dot_general | solution.py:93
  422.2 11.4 %convolution_convert_fusion.1 = bf16[2048,2048]{1,0:T(8,128)(2,1)} fusion(bf16[2048,1024]{0,1:T(8,128)(2,1)S(1)} %copy-done.57, bf16[1024,2048]{1,0:T(8,128)(2,1)S(1)} %copy-done.52), kind=kOutput, calls=%fused_computation.12 | convolution fusion | flops 8594128896 | bytes 16777216 | tf_op jit(solution)/shard_map/dot_general | solution.py:93
  448.1 14.2 %collective-permute-done.52 = bf16[1,2,256,1024]{3,2,1,0:T(8,128)(2,1)S(1)} collective-permute-done((bf16[1,2,256,1024]{3,2,1,0:T(8,128)(2,1)}, bf16[1,2,256,1024]{3,2,1,0:T(8,128)(2,1)S(1)}, u32[]{:S(2)}, u32[]{:S(2)}) %collective-permute-start.52) | collective-permute-done | bytes 1048608 | tf_op jit(solution)/shard_map/ppermute | solution.py:254
  472.2 12.7 %collective-permute-done.62 = bf16[1,2,128,2048]{3,2,1,0:T(8,128)(2,1)} collective-permute-done((bf16[1,2,128,2048]{3,2,1,0:T(8,128)(2,1)}, bf16[1,2,128,2048]{3,2,1,0:T(8,128)(2,1)}, u32[]{:S(2)}, u32[]{:S(2)}) %collective-permute-start.62) | collective-permute-done | bytes 1048608 | tf_op jit(solution)/shard_map/ppermute | solution.py:254
  518.6 10.2 %collective-permute-done.64 = bf16[1,128,2048]{2,1,0:T(8,128)(2,1)S(1)} collective-permute-done((bf16[1,128,2048]{2,1,0:T(8,128)(2,1)S(1)}, bf16[1,128,2048]{2,1,0:T(8,128)(2,1)S(1)}, u32[]{:S(2)}, u32[]{:S(2)}) %collective-permute-start.64) | collective-permute-done | bytes 524320 | tf_op jit(solution)/shard_map/ppermute | solution.py:234
  538.7 9.7 %collective-permute-done.69 = bf16[1,128,2048]{2,1,0:T(8,128)(2,1)S(1)} collective-permute-done((bf16[1,128,2048]{2,1,0:T(8,128)(2,1)S(1)}, bf16[1,128,2048]{2,1,0:T(8,128)(2,1)S(1)}, u32[]{:S(2)}, u32[]{:S(2)}) %collective-permute-start.69) | collective-permute-done | bytes 524320 | tf_op jit(solution)/shard_map/ppermute | solution.py:234
  561.8 18.2 %collective-permute-done.56 = bf16[1,256,1024]{2,1,0:T(8,128)(2,1)S(1)} collective-permute-done((bf16[1,256,1024]{2,1,0:T(8,128)(2,1)S(1)}, bf16[1,256,1024]{2,1,0:T(8,128)(2,1)S(1)}, u32[]{:S(2)}, u32[]{:S(2)}) %collective-permute-start.56) | collective-permute-done | bytes 524320 | tf_op jit(solution)/shard_map/ppermute | solution.py:234
  607.9 17.1 %collective-permute-done.49 = f32[80,128]{1,0:T(8,128)S(1)} collective-permute-done((f32[80,128]{1,0:T(8,128)S(1)}, f32[80,128]{1,0:T(8,128)S(1)}, u32[]{:S(2)}, u32[]{:S(2)}) %collective-permute-start.49) | collective-permute-done | bytes 40992 | tf_op jit(solution)/shard_map/ppermute | solution.py:284
  645.9 13.1 %attend_backward.2 = bf16[3,1024,256]{2,1,0:T(8,128)(2,1)} custom-call(bf16[1024,2048]{1,0:T(8,128)(2,1)} %bitcast.54.g_ref, bf16[4,2048,256]{2,1,0:T(8,128)(2,1)} %bitcast.395, bf16[3,1024,256]{2,1,0:T(8,128)(2,1)} %get-tuple-element.22.qkv_ref, f32[1024,2]{1,0:T(8,128)} %get-tuple-element.23.log_ref, f32[1024,128]{1,0:T(8,128)} %get-tuple-element.91.cos_ref, ...), custom_call_target="tpu_custom_call" | custom-call | flops 2415919104 | bytes 8388608 | tf_op jit(solution)/shard_map/attend_backward/pallas_call | solution.py:197
  678.1 13.8 %attend_backward.3 = bf16[3,1024,256]{2,1,0:T(8,128)(2,1)} custom-call(bf16[1024,2048]{1,0:T(8,128)(2,1)} %bitcast.54.g_ref, bf16[4,2048,256]{2,1,0:T(8,128)(2,1)} %pad_maximum_fusion.1.w_ref, bf16[3,1024,256]{2,1,0:T(8,128)(2,1)} %get-tuple-element.24.qkv_ref, f32[1024,2]{1,0:T(8,128)} %get-tuple-element.25.log_ref, f32[1024,128]{1,0:T(8,128)} %get-tuple-element.91.cos_ref, ...), custom_call_target="tpu_custom_call" | custom-call | flops 2415919104 | bytes 8388608 | tf_op jit(solution)/shard_map/attend_backward/pallas_call | solution.py:197
  739.8 19.5 %add_add_fusion = f32[1024,2048]{1,0:T(8,128)} fusion(f32[1024,2048]{1,0:T(8,128)} %fusion.39, f32[1024,2048]{1,0:T(8,128)} %fusion.40, f32[1024,2048]{1,0:T(8,128)} %fusion.69, f32[1024,2048]{1,0:T(8,128)} %fusion.67, f32[1024,2048]{1,0:T(8,128)} %fusion.68, bf16[3,2048,256]{2,1,0:T(8,128)(2,1)} %bitcast.385, bf16[3,1024,256]{2,1,0:T(8,128)(2,1)} %attend_backward.3), kind=kOutput, calls=%fused_computation.9 | convolution fusion | flops 1084227584 | bytes 51904512 | tf_op jit(solution)/shard_map/dot_general | solution.py:93
  773.2 16.0 %collective-permute-done.37 = bf16[4,256,256]{2,1,0:T(8,128)(2,1)S(1)} collective-permute-done((bf16[4,256,256]{2,1,0:T(8,128)(2,1)S(1)}, bf16[4,256,256]{2,1,0:T(8,128)(2,1)S(1)}, u32[]{:S(2)}, u32[]{:S(2)}) %collective-permute-start.37) | collective-permute-done | bytes 524320 | tf_op jit(solution)/shard_map/ppermute | solution.py:254
  794.3 43.7 %collective-permute-done.40 = bf16[4,512,256]{2,1,0:T(8,128)(2,1)S(1)} collective-permute-done((bf16[4,512,256]{2,1,0:T(8,128)(2,1)S(1)}, bf16[4,512,256]{2,1,0:T(8,128)(2,1)S(1)}, u32[]{:S(2)}, u32[]{:S(2)}) %collective-permute-start.40) | collective-permute-done | bytes 1048608 | tf_op jit(solution)/shard_map/ppermute | solution.py:397
  (463 shorter events, 395.8 us)
Async XLA Ops:
  7.2 268.7 %all-gather.3.cloned.1.call-start = ((), (), s32[]{:S(2)}) async-start(), calls=%async_computation.2 | async-start | bytes 9437184 | tf_op jit(solution)/shard_map/all_gather | solution.py:347
  14.7 58.6 %collective-permute-start = (bf16[256,2048]{1,0:T(8,128)(2,1)}, bf16[256,2048]{1,0:T(8,128)(2,1)}, u32[]{:S(2)}, u32[]{:S(2)}) collective-permute-start(bf16[256,2048]{1,0:T(8,128)(2,1)} %get-tuple-element.56), channel_id=1, source_target_pairs={{0,2},{1,3},{2,0},{3,1},{4,6},{5,7},{6,4},{7,5},{8,10},{9,11},{10,... | collective-permute-start | bytes 3145736 | tf_op jit(solution)/shard_map/ppermute | solution.py:234
  17.7 58.4 %collective-permute-start.1 = (bf16[256,2048]{1,0:T(8,128)(2,1)}, bf16[256,2048]{1,0:T(8,128)(2,1)}, u32[]{:S(2)}, u32[]{:S(2)}) collective-permute-start(bf16[256,2048]{1,0:T(8,128)(2,1)} %get-tuple-element.56), channel_id=1, source_target_pairs={{0,1},{1,0},{2,3},{3,2},{4,5},{5,4},{6,7},{7,6},{8,9},{9,8},{10,11... | collective-permute-start | bytes 3145736 | tf_op jit(solution)/shard_map/ppermute | solution.py:234
  20.4 49.2 %collective-permute-start.3 = (bf16[4,512,256]{2,1,0:T(8,128)(2,1)}, bf16[4,512,256]{2,1,0:T(8,128)(2,1)S(1)}, u32[]{:S(2)}, u32[]{:S(2)}) collective-permute-start(bf16[4,512,256]{2,1,0:T(8,128)(2,1)} %fusion.34), channel_id=1, source_target_pairs={{0,4},{1,5},{2,6},{3,7},{4,0},{5,1},{6,2},{7,3},{8,12},{9,13},{10,... | collective-permute-start | bytes 3145736 | tf_op jit(solution)/shard_map/ppermute | solution.py:322
  76.1 36.3 %collective-permute-start.2 = (bf16[256,2048]{1,0:T(8,128)(2,1)}, bf16[256,2048]{1,0:T(8,128)(2,1)S(1)}, u32[]{:S(2)}, u32[]{:S(2)}) collective-permute-start(bf16[256,2048]{1,0:T(8,128)(2,1)} %collective-permute-done), channel_id=1, source_target_pairs={{0,1},{1,0},{2,3},{3,2},{4,5},{5,4},{6,7},{7,6},{8,9},{9,8},{10,11... | collective-permute-start | bytes 3145736 | tf_op jit(solution)/shard_map/ppermute | solution.py:234
  194.4 163.7 %all-gather.5.cloned.1.call-start = ((), (), s32[]{:S(2)}) async-start(), calls=%async_computation.3 | async-start | bytes 9437184 | tf_op jit(solution)/shard_map/all_gather | solution.py:330
  195.2 393.0 %reduce-scatter.3.cloned.1.call-start = ((), (), s32[]{:S(2)}) async-start(), calls=%async_computation.4 | async-start | bytes 9437184 | tf_op jit(solution)/shard_map/reduce_scatter | solution.py:358
  375.0 62.6 %collective-permute-start.19 = (f32[16,128]{1,0:T(8,128)S(1)}, f32[16,128]{1,0:T(8,128)S(1)}, u32[]{:S(2)}, u32[]{:S(2)}) collective-permute-start(f32[16,128]{1,0:T(8,128)S(1)} %bitcast.434), channel_id=1, source_target_pairs={{0,1},{1,0},{2,3},{3,2},{4,5},{5,4},{6,7},{7,6},{8,9},{9,8},{10,11... | collective-permute-start | bytes 24584 | tf_op jit(solution)/shard_map/ppermute | solution.py:284
  388.9 506.0 %reduce-scatter.5.cloned.1.call-start = ((), (), s32[]{:S(2)}) async-start(), calls=%async_computation.5 | async-start | bytes 9437184 | tf_op jit(solution)/shard_map/reduce_scatter | solution.py:378
  444.9 40.0 %collective-permute-start.62 = (bf16[1,2,128,2048]{3,2,1,0:T(8,128)(2,1)}, bf16[1,2,128,2048]{3,2,1,0:T(8,128)(2,1)}, u32[]{:S(2)}, u32[]{:S(2)}) collective-permute-start(bf16[1,2,128,2048]{3,2,1,0:T(8,128)(2,1)} %dynamic-slice_bitcast_fusion.1), channel_id=1, source_target_pairs={{0,8},{8,0},{16,24},{24,16},{1,9},{9,1},{17,25},{25,17},{2,10},{10... | collective-permute-start | bytes 3145736 | tf_op jit(solution)/shard_map/ppermute | solution.py:254
  445.4 46.8 %collective-permute-start.67 = (bf16[1,2,128,2048]{3,2,1,0:T(8,128)(2,1)}, bf16[1,2,128,2048]{3,2,1,0:T(8,128)(2,1)}, u32[]{:S(2)}, u32[]{:S(2)}) collective-permute-start(bf16[1,2,128,2048]{3,2,1,0:T(8,128)(2,1)} %dynamic-slice_bitcast_fusion), channel_id=1, source_target_pairs={{0,16},{8,24},{16,0},{24,8},{1,17},{9,25},{17,1},{25,9},{2,18},{10... | collective-permute-start | bytes 3145736 | tf_op jit(solution)/shard_map/ppermute | solution.py:254
  464.0 39.4 %collective-permute-start.53 = (bf16[1,256,1024]{2,1,0:T(8,128)(2,1)S(1)}, bf16[1,256,1024]{2,1,0:T(8,128)(2,1)S(1)}, u32[]{:S(2)}, u32[]{:S(2)}) collective-permute-start(bf16[1,256,1024]{2,1,0:T(8,128)(2,1)S(1)} %fusion.61), channel_id=1, source_target_pairs={{0,16},{8,24},{16,0},{24,8},{1,17},{9,25},{17,1},{25,9},{2,18},{10... | collective-permute-start | bytes 1572872 | tf_op jit(solution)/shard_map/ppermute | solution.py:254
  471.5 46.0 %collective-permute-start.58 = (bf16[1,256,1024]{2,1,0:T(8,128)(2,1)S(1)}, bf16[1,256,1024]{2,1,0:T(8,128)(2,1)S(1)}, u32[]{:S(2)}, u32[]{:S(2)}) collective-permute-start(bf16[1,256,1024]{2,1,0:T(8,128)(2,1)S(1)} %fusion.62), channel_id=1, source_target_pairs={{0,8},{8,0},{16,24},{24,16},{1,9},{9,1},{17,25},{25,17},{2,10},{10... | collective-permute-start | bytes 1572872 | tf_op jit(solution)/shard_map/ppermute | solution.py:254
  503.9 45.1 %collective-permute-start.54 = (bf16[1,256,1024]{2,1,0:T(8,128)(2,1)S(1)}, bf16[1,256,1024]{2,1,0:T(8,128)(2,1)S(1)}, u32[]{:S(2)}, u32[]{:S(2)}) collective-permute-start(bf16[1,256,1024]{2,1,0:T(8,128)(2,1)S(1)} %get-tuple-element.37), channel_id=1, source_target_pairs={{0,8},{8,0},{16,24},{24,16},{1,9},{9,1},{17,25},{25,17},{2,10},{10... | collective-permute-start | bytes 1572872 | tf_op jit(solution)/shard_map/ppermute | solution.py:234
  504.5 55.7 %collective-permute-start.55 = (bf16[1,256,1024]{2,1,0:T(8,128)(2,1)S(1)}, bf16[1,256,1024]{2,1,0:T(8,128)(2,1)S(1)}, u32[]{:S(2)}, u32[]{:S(2)}) collective-permute-start(bf16[1,256,1024]{2,1,0:T(8,128)(2,1)S(1)} %get-tuple-element.37), channel_id=1, source_target_pairs={{0,16},{8,24},{16,0},{24,8},{1,17},{9,25},{17,1},{25,9},{2,18},{10... | collective-permute-start | bytes 1572872 | tf_op jit(solution)/shard_map/ppermute | solution.py:234
  549.0 33.7 %collective-permute-start.66 = (bf16[1,128,2048]{2,1,0:T(8,128)(2,1)S(1)}, bf16[1,128,2048]{2,1,0:T(8,128)(2,1)S(1)}, u32[]{:S(2)}, u32[]{:S(2)}) collective-permute-start(bf16[1,128,2048]{2,1,0:T(8,128)(2,1)S(1)} %collective-permute-done.64), channel_id=1, source_target_pairs={{0,16},{8,24},{16,0},{24,8},{1,17},{9,25},{17,1},{25,9},{2,18},{10... | collective-permute-start | bytes 1572872 | tf_op jit(solution)/shard_map/ppermute | solution.py:234
  599.6 33.5 %collective-permute-start.22 = (bf16[256,2048]{1,0:T(8,128)(2,1)}, bf16[256,2048]{1,0:T(8,128)(2,1)}, u32[]{:S(2)}, u32[]{:S(2)}) collective-permute-start(bf16[256,2048]{1,0:T(8,128)(2,1)} %get-tuple-element.43), channel_id=1, source_target_pairs={{0,2},{1,3},{2,0},{3,1},{4,6},{5,7},{6,4},{7,5},{8,10},{9,11},{10,... | collective-permute-start | bytes 3145736 | tf_op jit(solution)/shard_map/ppermute | solution.py:234
  708.9 53.1 %collective-permute-start.32 = (bf16[4,2,256,256]{3,2,1,0:T(8,128)(2,1)}, bf16[4,2,256,256]{3,2,1,0:T(8,128)(2,1)}, u32[]{:S(2)}, u32[]{:S(2)}) collective-permute-start(bf16[4,2,256,256]{3,2,1,0:T(8,128)(2,1)} %dynamic-slice_bitcast_fusion.6), channel_id=1, source_target_pairs={{0,8},{8,0},{16,24},{24,16},{1,9},{9,1},{17,25},{25,17},{2,10},{10... | collective-permute-start | bytes 3145736 | tf_op jit(solution)/shard_map/ppermute | solution.py:254
  709.4 55.1 %collective-permute-start.36 = (bf16[4,2,256,256]{3,2,0,1:T(8,128)(2,1)}, bf16[4,2,256,256]{3,2,0,1:T(8,128)(2,1)}, u32[]{:S(2)}, u32[]{:S(2)}) collective-permute-start(bf16[4,2,256,256]{3,2,0,1:T(8,128)(2,1)} %bitcast.382), channel_id=1, source_target_pairs={{0,8},{8,0},{16,24},{24,16},{1,9},{9,1},{17,25},{25,17},{2,10},{10... | collective-permute-start | bytes 3145736 | tf_op jit(solution)/shard_map/ppermute | solution.py:254
  712.3 57.7 %collective-permute-start.34 = (bf16[4,2,256,256]{3,2,0,1:T(8,128)(2,1)}, bf16[4,2,256,256]{3,2,0,1:T(8,128)(2,1)}, u32[]{:S(2)}, u32[]{:S(2)}) collective-permute-start(bf16[4,2,256,256]{3,2,0,1:T(8,128)(2,1)} %dynamic-slice_bitcast_fusion.5), channel_id=1, source_target_pairs={{0,16},{8,24},{16,0},{24,8},{1,17},{9,25},{17,1},{25,9},{2,18},{10... | collective-permute-start | bytes 3145736 | tf_op jit(solution)/shard_map/ppermute | solution.py:254
  714.9 52.8 %collective-permute-start.38 = (bf16[4,2,256,256]{3,2,0,1:T(8,128)(2,1)}, bf16[4,2,256,256]{3,2,0,1:T(8,128)(2,1)}, u32[]{:S(2)}, u32[]{:S(2)}) collective-permute-start(bf16[4,2,256,256]{3,2,0,1:T(8,128)(2,1)} %dynamic-slice_bitcast_fusion.4), channel_id=1, source_target_pairs={{0,16},{8,24},{16,0},{24,8},{1,17},{9,25},{17,1},{25,9},{2,18},{10... | collective-permute-start | bytes 3145736 | tf_op jit(solution)/shard_map/ppermute | solution.py:254
  789.6 48.5 %collective-permute-start.40 = (bf16[4,512,256]{2,1,0:T(8,128)(2,1)S(1)}, bf16[4,512,256]{2,1,0:T(8,128)(2,1)S(1)}, u32[]{:S(2)}, u32[]{:S(2)}) collective-permute-start(bf16[4,512,256]{2,1,0:T(8,128)(2,1)S(1)} %pad_maximum_fusion.6), channel_id=1, source_target_pairs={{0,4},{1,5},{2,6},{3,7},{4,0},{5,1},{6,2},{7,3},{8,12},{9,13},{10,... | collective-permute-start | bytes 3145736 | tf_op jit(solution)/shard_map/ppermute | solution.py:397
  794.1 53.2 %collective-permute-start.26 = (bf16[256,2048]{1,0:T(8,128)(2,1)S(1)}, bf16[256,2048]{1,0:T(8,128)(2,1)S(1)}, u32[]{:S(2)}, u32[]{:S(2)}) collective-permute-start(bf16[256,2048]{1,0:T(8,128)(2,1)S(1)} %fusion.33), channel_id=1, source_target_pairs={{0,2},{1,3},{2,0},{3,1},{4,6},{5,7},{6,4},{7,5},{8,10},{9,11},{10,... | collective-permute-start | bytes 3145736 | tf_op jit(solution)/shard_map/ppermute | solution.py:254
  841.4 34.9 %collective-permute-start.45 = (bf16[4,256,256]{2,1,0:T(8,128)(2,1)S(1)}, bf16[4,256,256]{2,1,0:T(8,128)(2,1)S(1)}, u32[]{:S(2)}, u32[]{:S(2)}) collective-permute-start(bf16[4,256,256]{2,1,0:T(8,128)(2,1)S(1)} %get-tuple-element.73), channel_id=1, source_target_pairs={{0,8},{8,0},{16,24},{24,16},{1,9},{9,1},{17,25},{25,17},{2,10},{10... | collective-permute-start | bytes 1572872 | tf_op jit(solution)/shard_map/ppermute | solution.py:234
  (112 other events, 1920.5 us)
Sparse Core Ops, SparseCore 0:
  194.5 81.3 all-gather.2
  277.5 80.5 all-gather.4
  389.0 88.4 reduce-scatter.2
  673.0 89.7 reduce-scatter.4

commit v2 on v1

--- a/solution.py
+++ b/solution.py
@@ -1,3 +1,4 @@
+import functools
 import math
 
 import jax
@@ -100,54 +101,70 @@
     return jnp.where(col <= row, scores, NEG_LARGE)
 
 
-def forward_kernel(x_ref, w_ref, cos_ref, sin_ref, mask_ref, qkv_ref, heads_ref, log_ref):
+def forward_kernel(earlier, *refs):
+    x_ref, w_ref, cos_ref, sin_ref, mask_ref = refs[:5]
+    others = refs[5 : 5 + 2 * earlier]
+    qkv_ref, heads_ref, log_ref, *share_ref = refs[5 + 2 * earlier :]
     tokens, heads = x_ref.shape[0], mask_ref.shape[1]
+    width = heads * HD
     block = min(Q_BLOCK, tokens)
     for start in range(0, tokens, block):
         here, end = slice(start, start + block), start + block
         x = x_ref[here, :]
         cos, sin = cos_ref[here, :], sin_ref[here, :]
         for part in range(3):
-            rows = product(x, w_ref[part], (1, 0))
+            rows = product(x, w_ref[:, part * width : (part + 1) * width], (1, 0))
             for head in range(heads):
-                lanes = slice(head * HD, (head + 1) * HD)
-                value = rows[:, lanes]
+                value = rows[:, head * HD : (head + 1) * HD]
                 if part < 2:
                     value = value * cos + pltpu.roll(value, HD // 2, 1) * sin
-                qkv_ref[part, here, lanes] = narrow(value)
+                at = part * width + head * HD
+                qkv_ref[here, at : at + HD] = narrow(value)
         for head in range(heads):
-            lanes = slice(head * HD, (head + 1) * HD)
-            scores = block_scores(qkv_ref[0, here, lanes], qkv_ref[1, :end, lanes], start)
+            at = head * HD
+            lanes, key_lanes, value_lanes = (slice(at + p * width, at + p * width + HD) for p in range(3))
+            scores = block_scores(qkv_ref[here, lanes], qkv_ref[:end, key_lanes], start)
             row_max = jnp.max(scores, axis=1, keepdims=True)
             shifted = jnp.exp(scores - row_max)
             total = jnp.sum(shifted, axis=1, keepdims=True)
-            mix = product(narrow(shifted / total), qkv_ref[2, :end, lanes], (1, 0))
+            mix = product(narrow(shifted / total), qkv_ref[:end, value_lanes], (1, 0))
             heads_ref[here, lanes] = narrow(mix * mask_ref[here, head : head + 1])
             log_ref[here, head : head + 1] = row_max + jnp.log(total)
-
-
-def backward_kernel(g_ref, w_ref, qkv_ref, log_ref, cos_ref, sin_ref, mask_ref, out_ref, keys_acc, values_acc):
+        if share_ref:
+            share = product(heads_ref[here, :], w_ref[:, 3 * width :], (1, 1))
+            for k in range(earlier):
+                share = share + product(others[2 * k][here, :], others[2 * k + 1][:, 3 * width :], (1, 1))
+            share_ref[0][here, :] = narrow(share)
+
+
+def backward_kernel(earlier, *refs):
+    g_ref, w_ref, qkv_ref, log_ref, cos_ref, sin_ref, mask_ref = refs[:7]
+    others = refs[7 : 7 + 2 * earlier]
+    *outs, keys_acc, values_acc = refs[7 + 2 * earlier :]
+    out_ref = outs[0]
     tokens, heads = g_ref.shape[0], mask_ref.shape[1]
+    width = heads * HD
     block = min(Q_BLOCK, tokens)
     scale = 1.0 / math.sqrt(HD)
     for start in range(0, tokens, block):
         here, end = slice(start, start + block), start + block
         cos, sin = cos_ref[here, :], sin_ref[here, :]
-        rows = narrow(product(g_ref[here, :], w_ref[0], (1, 0)))
+        rows = narrow(product(g_ref[here, :], w_ref[:, 3 * width :], (1, 0)))
         for head in range(heads):
-            lanes = slice(head * HD, (head + 1) * HD)
+            at = head * HD
+            lanes, key_lanes, value_lanes = (slice(at + p * width, at + p * width + HD) for p in range(3))
             heads_grad = rows[:, lanes] * narrow(mask_ref[here, head : head + 1])
-            queries, keys_all = qkv_ref[0, here, lanes], qkv_ref[1, :end, lanes]
+            queries, keys_all = qkv_ref[here, lanes], qkv_ref[:end, key_lanes]
             scores = block_scores(queries, keys_all, start)
             probs = jnp.exp(scores - log_ref[here, head : head + 1])
             values_part = product(narrow(probs), heads_grad, (0, 0))
-            probs_grad = product(heads_grad, qkv_ref[2, :end, lanes], (1, 1))
+            probs_grad = product(heads_grad, qkv_ref[:end, value_lanes], (1, 1))
             centre = jnp.sum(probs * probs_grad, axis=1, keepdims=True)
             score_grad = narrow(probs * (probs_grad - centre))
             queries_grad = product(score_grad, keys_all, (1, 0)) * scale
             keys_part = product(score_grad, queries, (0, 0)) * scale
             turned = queries_grad * cos - pltpu.roll(queries_grad, HD // 2, 1) * sin
-            out_ref[0, here, lanes] = narrow(turned)
+            out_ref[here, lanes] = narrow(turned)
             if start:
                 values_acc[:start, lanes] += values_part[:start]
                 keys_acc[:start, lanes] += keys_part[:start]
@@ -156,11 +173,48 @@
     for start in range(0, tokens, block):
         here = slice(start, start + block)
         cos, sin = cos_ref[here, :], sin_ref[here, :]
-        out_ref[2, here, :] = narrow(values_acc[here, :])
+        out_ref[here, 2 * width :] = narrow(values_acc[here, :])
         for head in range(heads):
-            lanes = slice(head * HD, (head + 1) * HD)
-            value = keys_acc[here, lanes]
-            out_ref[1, here, lanes] = narrow(value * cos - pltpu.roll(value, HD // 2, 1) * sin)
+            at = head * HD
+            value = keys_acc[here, at : at + HD]
+            out_ref[here, width + at : width + at + HD] = narrow(value * cos - pltpu.roll(value, HD // 2, 1) * sin)
+        if outs[1:]:
+            share = product(out_ref[here, :], w_ref[:, : 3 * width], (1, 1))
+            for k in range(earlier):
+                share = share + product(others[2 * k][here, :], others[2 * k + 1][:, : 3 * width], (1, 1))
+            outs[1][here, :] = narrow(share)
+
+
+def weight_kernel(x_ref, q_ref, g_ref, h_ref, *outs):
+    width = h_ref.shape[1]
+    half = x_ref.shape[1] // 2
+    for lane, out_ref in enumerate(outs):
+        here = slice(lane * half, (lane + 1) * half)
+        out_ref[0, :, : 3 * width] = narrow(product(x_ref[:, here], q_ref[...], (0, 0)))
+        out_ref[0, :, 3 * width :] = narrow(product(g_ref[:, here], h_ref[...], (0, 0)))
+
+
+def place_kernel(count, widths, turned, at_ref, *refs):
+    blocks, outs = refs[: 2 * count], refs[2 * count :]
+    half = blocks[0].shape[0]
+    for far in range(count):
+
+        @pl.when((pl.program_id(0) ^ at_ref[0]) == far)
+        def _():
+            for lane in range(2):
+                here = slice(lane * half, (lane + 1) * half)
+                block = blocks[lane * count + far]
+                start = 0
+                for out_ref, width, turn in zip(outs, widths, turned):
+                    for part in range(out_ref.shape[0] if len(out_ref.shape) == 3 else 1):
+                        value = block[:, start : start + width].astype(out_ref.dtype)
+                        start += width
+                        if turn:
+                            out_ref[:, here] = value.T
+                        elif len(out_ref.shape) == 3:
+                            out_ref[part, here, :] = value
+                        else:
+                            out_ref[here, :] = value
 
 
 VMEM_LIMIT = 56 * 1024 * 1024
@@ -170,41 +224,102 @@
     return [pl.BlockSpec(memory_space=pltpu.VMEM)] * count
 
 
-def attend_forward(x, w, cos, sin, mask):
+def attend_forward(x, w, cos, sin, mask, earlier, last):
     tokens, heads = mask.shape
-    dim, width = w.shape[1:]
+    dim, width = w.shape[0], heads * HD
     flops = 2 * tokens * dim * width * 3 + 2 * tokens * tokens * width
+    out = [
+        jax.ShapeDtypeStruct((tokens, 3 * width), jnp.bfloat16),
+        jax.ShapeDtypeStruct((tokens, width), jnp.bfloat16),
+        jax.ShapeDtypeStruct((tokens, heads), jnp.float32),
+    ]
+    given = [a for pair in earlier for a in pair] if last else []
+    if last:
+        out.append(jax.ShapeDtypeStruct((tokens, dim), jnp.bfloat16))
+        flops += 2 * tokens * dim * width * (1 + len(earlier))
     return pl.pallas_call(
-        forward_kernel,
-        out_shape=(
-            jax.ShapeDtypeStruct((3, tokens, width), jnp.bfloat16),
-            jax.ShapeDtypeStruct((tokens, width), jnp.bfloat16),
-            jax.ShapeDtypeStruct((tokens, heads), jnp.float32),
-        ),
-        in_specs=whole_specs(5),
-        out_specs=tuple(whole_specs(3)),
+        functools.partial(forward_kernel, len(given) // 2),
+        out_shape=out,
+        in_specs=whole_specs(5 + len(given)),
+        out_specs=whole_specs(len(out)),
         compiler_params=pltpu.CompilerParams(vmem_limit_bytes=VMEM_LIMIT),
         cost_estimate=pl.CostEstimate(flops=flops, bytes_accessed=12 << 20, transcendentals=tokens * tokens * heads // 2),
         name="attend_forward",
-    )(x, w, cos, sin, mask)
-
-
-def attend_backward(g, w, qkv, log_total, cos, sin, mask):
+    )(x, w, cos, sin, mask, *given)
+
+
+def attend_backward(g, w, qkv, log_total, cos, sin, mask, earlier, last):
     tokens, heads = mask.shape
-    dim, width = w.shape[1:]
+    dim, width = w.shape[0], heads * HD
     flops = 2 * tokens * dim * width + 5 * tokens * tokens * width
-    fixed = whole_specs(1)[0]
+    out = [jax.ShapeDtypeStruct((tokens, 3 * width), jnp.bfloat16)]
+    given = [a for pair in earlier for a in pair] if last else []
+    if last:
+        out.append(jax.ShapeDtypeStruct((tokens, dim), jnp.bfloat16))
+        flops += 6 * tokens * dim * width * (1 + len(earlier))
     return pl.pallas_call(
-        backward_kernel,
-        grid=(1,),
-        out_shape=jax.ShapeDtypeStruct((3, tokens, width), jnp.bfloat16),
-        in_specs=[fixed, pl.BlockSpec((1, dim, width), lambda i: (3, 0, 0))] + [fixed] * 5,
-        out_specs=fixed,
+        functools.partial(backward_kernel, len(given) // 2),
+        out_shape=out,
+        in_specs=whole_specs(7 + len(given)),
+        out_specs=whole_specs(len(out)),
         scratch_shapes=[pltpu.VMEM((tokens, width), jnp.float32)] * 2,
         compiler_params=pltpu.CompilerParams(vmem_limit_bytes=VMEM_LIMIT),
-        cost_estimate=pl.CostEstimate(flops=flops, bytes_accessed=8 << 20, transcendentals=tokens * tokens * heads // 2),
+        cost_estimate=pl.CostEstimate(flops=flops, bytes_accessed=12 << 20, transcendentals=tokens * tokens * heads // 2),
         name="attend_backward",
-    )(g, w, qkv, log_total, cos, sin, mask)
+    )(g, w, qkv, log_total, cos, sin, mask, *given)
+
+
+def weight_grads(x, qkv_grad, g, heads_out, count):
+    tokens, dim = x.shape
+    width = heads_out.shape[1]
+    block = dim // count
+    out = jax.ShapeDtypeStruct((count, block // 2, 4 * width), jnp.bfloat16)
+    return pl.pallas_call(
+        weight_kernel,
+        grid=(count,),
+        out_shape=[out, out],
+        in_specs=[
+            pl.BlockSpec((tokens, block), lambda i: (0, i)),
+            pl.BlockSpec((tokens, 3 * width), lambda i: (0, 0)),
+            pl.BlockSpec((tokens, block), lambda i: (0, i)),
+            pl.BlockSpec((tokens, width), lambda i: (0, 0)),
+        ],
+        out_specs=[pl.BlockSpec((1, block // 2, 4 * width), lambda i: (i, 0, 0))] * 2,
+        compiler_params=pltpu.CompilerParams(vmem_limit_bytes=VMEM_LIMIT),
+        cost_estimate=pl.CostEstimate(flops=8 * tokens * dim * width, bytes_accessed=14 << 20, transcendentals=0),
+        name="weight_grads",
+    )(x, qkv_grad, g, heads_out)
+
+
+def place_blocks(lanes, index, outs):
+    count = len(lanes[0])
+    half, total = lanes[0][0].shape
+    rows = 2 * half
+    shapes, specs = [], []
+    for planes, width, kind, turned in outs:
+        if turned:
+            shapes.append(jax.ShapeDtypeStruct((width, rows * count), kind))
+            specs.append(pl.BlockSpec((width, rows), lambda i, at: (0, i)))
+        elif planes > 1:
+            shapes.append(jax.ShapeDtypeStruct((planes, rows * count, width), kind))
+            specs.append(pl.BlockSpec((planes, rows, width), lambda i, at: (0, i, 0)))
+        else:
+            shapes.append(jax.ShapeDtypeStruct((rows * count, width), kind))
+            specs.append(pl.BlockSpec((rows, width), lambda i, at: (i, 0)))
+    given = [held[far] for held in lanes for far in range(count)]
+    return pl.pallas_call(
+        functools.partial(place_kernel, count, [o[1] for o in outs], [o[3] for o in outs]),
+        grid_spec=pltpu.PrefetchScalarGridSpec(
+            num_scalar_prefetch=1,
+            grid=(count,),
+            in_specs=[pl.BlockSpec((half, total), lambda i, at: (0, 0))] * len(given),
+            out_specs=specs,
+        ),
+        out_shape=shapes,
+        compiler_params=pltpu.CompilerParams(vmem_limit_bytes=VMEM_LIMIT),
+        cost_estimate=pl.CostEstimate(flops=0, bytes_accessed=12 << 20, transcendentals=0),
+        name="place_blocks",
+    )(index.astype(jnp.int32).reshape(1), *given)
 
 
 def swap_pairs(size, bit):
@@ -228,7 +343,7 @@
 
 
 def xor_gather(x, axis, size, bits):
-    held = {0: x}
+    held = dict(x) if isinstance(x, dict) else {0: x}
     for bit in bits:
         for far in list(held):
             held[far ^ bit] = lax.ppermute(held[far], axis, swap_pairs(size, bit))
@@ -256,26 +371,28 @@
     return blocks
 
 
-def column_gather(x, size, column):
-    bits, half = bits_of(size), x.shape[1] // 2
-    parts = [
-        by_index(xor_gather(x[:, :half], "dp", size, bits), column, 1),
-        by_index(xor_gather(x[:, half:], "dp", size, bits[::-1]), column, 1),
-    ]
-    return jnp.concatenate(parts, axis=2).reshape(x.shape[0], -1, x.shape[2])
-
-
-def column_scatter(x, size, column):
-    bits = bits_of(size)
-    blocks = x.reshape(x.shape[0], size, -1, x.shape[2])
-    half = blocks.shape[2] // 2
-    return jnp.concatenate(
-        [
-            narrow(xor_scatter(blocks[:, :, :half], "dp", size, bits, bits, column, 1)),
-            narrow(xor_scatter(blocks[:, :, half:], "dp", size, bits[::-1], bits[::-1], column, 1)),
-        ],
-        axis=1,
-    )
+def lane_bits(size):
+    return bits_of(size), bits_of(size)[::-1]
+
+
+def column_gather(lanes, size, cut=None, start=None):
+    return [xor_gather(x, "dp", size, bits[start:cut]) for x, bits in zip(lanes, lane_bits(size))]
+
+
+def gate_lanes(lanes, *gates):
+    flat = [held[far] for held in lanes for far in held]
+    flat = lax.optimization_barrier((*flat, *gates))
+    flat = iter(flat)
+    return [{far: next(flat) for far in held} for held in lanes]
+
+
+def column_scatter(lanes, size, column):
+    return [narrow(xor_scatter(x, "dp", size, bits, bits, column, 0)) for x, bits in zip(lanes, lane_bits(size))]
+
+
+def two_lanes(x, size):
+    blocks = x.reshape(size, 2, -1, x.shape[1])
+    return [blocks[:, 0], blocks[:, 1]]
 
 
 def all_sum(x, sizes):
@@ -314,32 +431,39 @@
             bits = pair_bits[::-1]
             return xor_scatter(blocks, "mp", ranks, bits, [b // 2 for b in bits], place // 2, 0)
 
-        planes = jnp.concatenate([attention_weight.transpose(1, 0, 2), output_weight.T[None]], axis=0)
-        plane_rows = dim // columns
-        chunk = lax.dynamic_slice_in_dim(planes, column * plane_rows, plane_rows, 1)
-        weights, fetched = [planes], []
-        for k in range(1, sequences):
-            got = lax.ppermute(chunk, "mp", shift_pairs(ranks, k * group))
-            fetched.append(got)
-            weights.append(column_gather(got, columns, column))
-
+        width = own_heads * HD
+        packed = jnp.concatenate([attention_weight[:, p] for p in range(3)] + [output_weight.T], axis=1)
+        chunk_rows = dim // columns
+        chunks = [
+            lax.dynamic_slice_in_dim(packed, column * chunk_rows + at, chunk_rows // 2, 0)
+            for at in (0, chunk_rows // 2)
+        ]
         input_wide = wide(layer_input)
         normed_one, scaled_one, inverse_one = norm_forward(input_wide, mixer_gain)
         inputs_one, held_one = to_sequence(narrow(normed_one))
+        fetched = [
+            lax.ppermute(lane, "mp", shift_pairs(ranks, k * group)) for k in range(1, sequences) for lane in chunks
+        ]
+        inputs_one, *fetched = lax.optimization_barrier((inputs_one, *fetched))
+        weights = [packed]
+        for k in range(1, sequences):
+            held = column_gather(fetched[2 * k - 2 : 2 * k], columns)
+            weights += place_blocks(held, column, [(1, packed.shape[1], jnp.bfloat16, False)])
         gate_one, state_one = gate_forward(normed_one, mixer_router, width_own[:, 0], routed_own[:, 0])
         grads_all = lax.all_gather(after(out_grad, *fetched), "mp", axis=0, tiled=True)
 
         sequence_width = lax.dynamic_slice_in_dim(width_choice[:, 0], sequence * SEQ_LEN, SEQ_LEN, 0)
-        kept = []
-        branch = None
+        kept, earlier = [], []
         for k in range(sequences):
             heads = ((rank + k * group) % ranks) * own_heads + jnp.arange(own_heads, dtype=jnp.int32)
             mask = (heads[None, :] * 4 < (sequence_width[:, None] + 1) * H).astype(jnp.float32)
-            qkv, heads_out, log_total = attend_forward(inputs_one, weights[k], cos, sin, mask)
+            last = k == sequences - 1
+            qkv, heads_out, log_total, *share = attend_forward(inputs_one, weights[k], cos, sin, mask, earlier, last)
             kept.append((qkv, heads_out, log_total, mask))
-            share = product(heads_out, weights[k][3], (1, 1))
-            branch = share if branch is None else branch + share
-        mixer_branch = from_sequence(branch)
+            earlier.append((heads_out, weights[k]))
+        mixer_branch = from_sequence(share[0])
+        top_down = product(grads_all, down_weight, (1, 1))
+        mixer_branch, top_down = lax.optimization_barrier((mixer_branch, top_down))
 
         middle = input_wide + gate_one[:, None] * mixer_branch
         normed_two, scaled_two, inverse_two = norm_forward(middle, hidden_gain)
@@ -349,55 +473,62 @@
 
         col_ids = rank * cols_local + jnp.arange(cols_local, dtype=jnp.int32)
         col_mask = (col_ids[None, :] * 4 < (width_choice[:, 1:2] + 1) * FF).astype(jnp.float32)
-        top_down = product(grads_all, down_weight, (1, 1))
         pre = product(inputs_two, up_weight, (1, 0))
         relu_act = jax.nn.relu(pre)
         hidden = narrow(relu_act * relu_act * col_mask)
         pre_grad = narrow(top_down * gates[:, None] * col_mask * 2.0 * relu_act)
-        normed_grad_two = wide(
-            lax.psum_scatter(narrow(product(pre_grad, up_weight, (1, 1))), "mp", scatter_dimension=0, tiled=True)
-        )
         dots = jnp.sum(wide(hidden) * top_down, axis=1).reshape(-1, 128)
+        share = narrow(product(pre_grad, up_weight, (1, 1)))
+        share, hidden, pre_grad = lax.optimization_barrier((share, hidden, pre_grad))
+        normed_grad_two = wide(lax.psum_scatter(share, "mp", scatter_dimension=0, tiled=True))
         gate_grad_two = lax.dynamic_slice_in_dim(all_sum(dots, {"mp": ranks}).reshape(-1), rank * rows, rows, 0)
+        gated = narrow(gates[:, None] * wide(grads_all))
+        down_piece = column_scatter(two_lanes(narrow(product(hidden, gated, (0, 0))), columns), columns, column)
+        up_piece = column_scatter(two_lanes(narrow(product(inputs_two, pre_grad, (0, 0))), columns), columns, column)
+        hidden_share = narrow(product(hidden, down_weight, (1, 0)))
+
         router_part, router_two = gate_backward(normed_two, hidden_router, state_two, gate_grad_two)
         middle_part, gain_two = norm_backward(normed_grad_two + router_part, scaled_two, inverse_two, hidden_gain)
         middle_grad = wide(out_grad) + middle_part
-        gated = narrow(gates[:, None] * wide(grads_all))
-        down_grad = narrow(product(hidden, gated, (0, 0)))
-        up_grad = narrow(product(inputs_two, pre_grad, (0, 0)))
-
-        def column_total(x):
-            return wide(column_gather(column_scatter(x[None], columns, column), columns, column)[0])
-
-        down_sum = column_total(down_grad)
-        up_sum = column_total(up_grad)
-
         grads_one, held_grads = to_sequence(narrow(gate_one[:, None] * middle_grad))
-        share = narrow(product(hidden, down_weight, (1, 0)))
-        share = after(share, *held_grads.values())
-        hidden_branch = wide(lax.psum_scatter(share, "mp", scatter_dimension=0, tiled=True))
+        grads_one, hidden_share = lax.optimization_barrier((grads_one, hidden_share))
+        hidden_branch = wide(lax.psum_scatter(hidden_share, "mp", scatter_dimension=0, tiled=True))
         layer_output = narrow(middle + gate_two[:, None] * hidden_branch)
 
         gate_grad_one = jnp.sum(middle_grad * mixer_branch, axis=1)
-        share_one = None
-        plane_grads = [None] * sequences
+        down_held = column_gather(down_piece, columns, cut=1)
+        up_held = column_gather(up_piece, columns, cut=1)
+        earlier, weight_parts = [], [None] * sequences
+        grads_now = grads_one
         for k in range(sequences)[::-1]:
             qkv, heads_out, log_total, mask = kept[k]
-            qkv_grad = attend_backward(grads_one, weights[k], qkv, log_total, cos, sin, mask)
-            in_grads = [product(inputs_one, qkv_grad[p], (0, 0)) for p in range(3)]
-            plane_grads[k] = jnp.stack([narrow(x) for x in in_grads] + [narrow(product(grads_one, heads_out, (0, 0)))])
-            for p in range(3):
-                share = product(qkv_grad[p], weights[k][p], (1, 1))
-                share_one = share if share_one is None else share_one + share
-        normed_grad_one = from_sequence(share_one)
-
-        piece = wide(column_scatter(plane_grads[0], columns, column))
+            qkv_grad, *share = attend_backward(
+                grads_now, weights[k], qkv, log_total, cos, sin, mask, earlier, k == 0
+            )
+            earlier.append((qkv_grad, weights[k]))
+            weight_parts[k] = weight_grads(inputs_one, qkv_grad, grads_one, heads_out, columns)
+            if k:
+                grads_now, *weight_parts[k] = lax.optimization_barrier((grads_now, *weight_parts[k]))
+        down_held = gate_lanes(down_held, earlier[0][0])
+        up_held = gate_lanes(up_held, earlier[0][0])
+        normed_grad_one = from_sequence(share[0])
+
+        down_held = column_gather(down_held, columns, start=1)
+        up_held = column_gather(up_held, columns, start=1)
+        down_sum, = place_blocks(down_held, column, [(1, dim, jnp.float32, False)])
+        up_sum, = place_blocks(up_held, column, [(1, cols_local, jnp.float32, False)])
+
+        pieces = column_scatter(weight_parts[0], columns, column)
         for k in range(1, sequences):
-            there = column_scatter(plane_grads[k], columns, column)
-            piece = piece + wide(lax.ppermute(there, "mp", shift_pairs(ranks, -k * group)))
-        plane_sum = wide(column_gather(narrow(piece), columns, column))
-        attention_sum = plane_sum[:3].transpose(1, 0, 2)
-        output_sum = plane_sum[3].T
+            there = column_scatter(weight_parts[k], columns, column)
+            back = shift_pairs(ranks, -k * group)
+            pieces = [narrow(wide(p) + wide(lax.ppermute(t, "mp", back))) for p, t in zip(pieces, there)]
+        attention_sum, output_sum = place_blocks(
+            column_gather(pieces, columns),
+            column,
+            [(3, width, jnp.float32, False), (1, width, jnp.float32, True)],
+        )
+        attention_sum = attention_sum.transpose(1, 0, 2)
 
         router_part_one, router_one = gate_backward(normed_one, mixer_router, state_one, gate_grad_one)
         input_part, gain_one = norm_backward(normed_grad_one + router_part_one, scaled_one, inverse_one, mixer_gain)
@@ -405,14 +536,14 @@
 
         sizes = {"mp": ranks, "dp": columns}
 
-        def small_total(gain, router):
-            packed = jnp.concatenate([gain.reshape(-1, 128), router.T.reshape(-1, 128)], axis=0)
-            packed = all_sum(packed, sizes)
-            cut = dim // 128
-            return packed[:cut].reshape(dim), packed[cut:].reshape(-1, dim).T
-
-        hidden_gain_sum, hidden_router_sum = small_total(gain_two, router_two)
-        mixer_gain_sum, mixer_router_sum = small_total(gain_one, router_one)
+        smalls = [gain_two, gain_one, router_two.T, router_one.T]
+        small_sum = all_sum(jnp.concatenate([x.reshape(-1, 128) for x in smalls], axis=0), sizes)
+        cuts = [dim // 128, 2 * dim // 128, (2 * dim + router_two.size) // 128]
+        hidden_gain_sum, mixer_gain_sum, hidden_router_sum, mixer_router_sum = (
+            x.reshape(-1, dim) for x in jnp.split(small_sum, cuts)
+        )
+        hidden_gain_sum, mixer_gain_sum = hidden_gain_sum[0], mixer_gain_sum[0]
+        hidden_router_sum, mixer_router_sum = hidden_router_sum.T, mixer_router_sum.T
         return (
             layer_output, input_grad, mixer_gain_sum, mixer_router_sum, attention_sum, output_sum,
             hidden_gain_sum, hidden_router_sum, up_sum, down_sum,

time: 910 us -> 831 us (0.913)
  matrix products: 179 us -> 86.7 us
  Pallas kernels: 52.7 us -> 108 us
  local copies, waits for them, and re-layouts: 76.8 us -> 49.9 us
  other arithmetic: 78.7 us -> 57.9 us
    dot_general x22 -> x6, matrix products: 165 us -> 72.6 us  [product(): lax.dot_general(a, b, ((dims[:1], dims[1:]), ((), ())), preferred_element...]
    reduce_scatter x1, waiting for transfers between devices: 0.01 us -> 78.6 us  [local(): lax.psum_scatter(share, 'mp', scatter_dimension=0, tiled=True)]
    all_gather x1, waiting for transfers between devices: 67.3 us -> 0.02 us  [local(): lax.all_gather(after(out_grad, *fetched), 'mp', axis=0, tiled=True)]
    pallas_call x4 -> x10, Pallas kernels: 52.7 us -> 108 us  [the longest x2 36.9 us: attend_backward(): pl.pallas_call(functools.partial(backward_kernel, len(given) // 2), out_s...]
    ppermute x18, waiting for transfers between devices: 90.3 us -> 127 us  [xor_scatter(): lax.ppermute(narrow(pick(blocks, 1 - side, at)), axis_name, swap_pairs(si...]
    ppermute x2 -> x4, waiting for transfers between devices: 79 us -> 56.1 us  [the longest x2 40.7 us: local(): lax.ppermute(lane, 'mp', shift_pairs(ranks, k * group))]
    ppermute x13 -> x8, waiting for transfers between devices: 32.3 us -> 17.4 us  [all_sum(): x = x + lax.ppermute(x, axis, swap_pairs(size, bit))]
    convert_element_type x3 -> x0, other arithmetic: 12.6 us -> none  [wide(): return x.astype(jnp.float32)]
  transfers between devices with their start and end apart: 76 -> 73, of which waited for: 36 -> 33; matrix products, arithmetic and copies ran while one was open for 28% -> 14% of each run, Pallas kernels for 2% -> 13%
where the time goes in v2:
time: 831 us; the launch traced here: 828 us
  waiting for transfers between devices  436 us (52%)
  Pallas kernels  108 us (13%)
  matrix products  86.7 us (10%)
  starting transfers between devices  74 us (9%)
  other arithmetic  57.9 us (7%)
  local copies, waits for them, and re-layouts  49.9 us (6%)
  between operations  15.2 us (2%)
    ppermute x18, waiting for transfers between devices, xor_scatter(): lax.ppermute(narrow(pick(blocks, 1 - side, at)), axis_name, swap_pairs(si...  127 us
    ppermute x37, waiting for transfers between devices, xor_gather(): held[far ^ bit] = lax.ppermute(held[far], axis, swap_pairs(size, bit))  86.9 us
    reduce_scatter x1, waiting for transfers between devices, local(): lax.psum_scatter(share, 'mp', scatter_dimension=0, tiled=True)  78.6 us
    dot_general x6, matrix products, product(): lax.dot_general(a, b, ((dims[:1], dims[1:]), ((), ())), preferred_element...  72.6 us
    all_gather x1, waiting for transfers between devices, local(): inputs_two = lax.all_gather(narrow(normed_two), 'mp', axis=0, tiled=True)  65.3 us
    ppermute x2, waiting for transfers between devices, local(): lax.ppermute(lane, 'mp', shift_pairs(ranks, k * group))  40.7 us
    ppermute x37, starting transfers between devices, xor_gather(): held[far ^ bit] = lax.ppermute(held[far], axis, swap_pairs(size, bit))  37.3 us
    pallas_call x2, Pallas kernels, attend_backward(): pl.pallas_call(functools.partial(backward_kernel, len(given) // 2), out_s...  36.9 us
  transfers between devices with their start and end apart: 73, of which 33 were waited for; matrix products, arithmetic and copies ran while one was open for 14% of the time, Pallas kernels for 13%

profile of v2, /device:TPU:0, one launch (start us, length us, event | category | flops | bytes accessed | tf_op | source)
XLA Modules:
  0.0 827.5 jit_solution(8562527528470679584)
XLA Ops:
  22.6 18.6 %collective-permute-done = bf16[256,2048]{1,0:T(8,128)(2,1)} collective-permute-done((bf16[256,2048]{1,0:T(8,128)(2,1)}, bf16[256,2048]{1,0:T(8,128)(2,1)}, u32[]{:S(2)}, u32[]{:S(2)}) %collective-permute-start) | collective-permute-done | bytes 1048608 | tf_op jit(solution)/shard_map/ppermute | solution.py:349
  50.7 29.6 %collective-permute-done.3.refs_0_ = bf16[256,1024]{1,0:T(8,128)(2,1)S(1)} collective-permute-done((bf16[256,1024]{1,0:T(8,128)(2,1)}, bf16[256,1024]{1,0:T(8,128)(2,1)S(1)}, u32[]{:S(2)}, u32[]{:S(2)}) %collective-permute-start.3) | collective-permute-done | bytes 524320 | tf_op jit(solution)/shard_map/ppermute | solution.py:445
  80.3 11.1 %collective-permute-done.4.refs_4_ = bf16[256,1024]{1,0:T(8,128)(2,1)} collective-permute-done((bf16[256,1024]{1,0:T(8,128)(2,1)S(1)}, bf16[256,1024]{1,0:T(8,128)(2,1)}, u32[]{:S(2)}, u32[]{:S(2)}) %collective-permute-start.4) | collective-permute-done | bytes 524320 | tf_op jit(solution)/shard_map/ppermute | solution.py:445
  112.5 12.9 %attend_forward.2 = (bf16[1024,768]{1,0:T(8,128)(2,1)}, bf16[1024,256]{1,0:T(8,128)(2,1)}, f32[1024,2]{1,0:T(8,128)}) custom-call(bf16[1024,2048]{1,0:T(8,128)(2,1)} %bitcast.7.refs_0_.x_ref, bf16[2048,1024]{1,0:T(8,128)(2,1)} %copy-done.15, f32[1024,128]{1,0:T(8,128)} %get-tuple-element.138.refs_2_.refs_4_, f32[1024,128]{1,0:T(8,128)} %get-tuple-element.139.refs_3_.refs_5_, ...), custom_call_target="tpu_custom_call" | custom-call | flops 3758096384 | bytes 12582912 | tf_op jit(solution)/shard_map/attend_forward/pallas_call | solution.py:240
  134.1 17.8 %attend_forward.3 = (bf16[1024,768]{1,0:T(8,128)(2,1)}, bf16[1024,256]{1,0:T(8,128)(2,1)}, f32[1024,2]{1,0:T(8,128)}, bf16[1024,2048]{1,0:T(8,128)(2,1)}) custom-call(bf16[1024,2048]{1,0:T(8,128)(2,1)} %bitcast.7.refs_0_.x_ref, bf16[2048,1024]{1,0:T(8,128)(2,1)} %place_blocks.4.refs_1_.refs_8_, f32[1024,128]{1,0:T(8,128)} %get-tuple-element.138.refs_2_.refs_4_, ...), custom_call_target="tpu_custom_call" | custom-call | flops 5905580032 | bytes 12582912 | tf_op jit(solution)/shard_map/attend_forward/pallas_call | solution.py:240
  167.5 26.2 %collective-permute-done.12 = bf16[256,2048]{1,0:T(8,128)(2,1)} collective-permute-done((bf16[256,2048]{1,0:T(8,128)(2,1)S(1)}, bf16[256,2048]{1,0:T(8,128)(2,1)}, u32[]{:S(2)}, u32[]{:S(2)}) %collective-permute-start.12) | collective-permute-done | bytes 1048608 | tf_op jit(solution)/shard_map/ppermute | solution.py:369
  196.5 14.6 %fusion.91 = f32[2048,1024]{1,0:T(8,128)} fusion(bf16[2048,2048]{1,0:T(8,128)(2,1)} %all-gather.3.cloned.1.call-done, bf16[1024,2048]{1,0:T(8,128)(2,1)} %param.22), kind=kOutput, calls=%fused_computation.213 | convolution fusion | flops 8589934592 | bytes 20971520 | tf_op jit(solution)/shard_map/dot_general | solution.py:94
  231.9 65.3 %all-gather.5.cloned.1.call-done = bf16[2048,2048]{1,0:T(8,128)(2,1)} async-done(((bf16[256,2048]{1,0:T(8,128)(2,1)}), bf16[2048,2048]{1,0:T(8,128)(2,1)}) %all-gather.5.cloned.1.call-update) | async-done | bytes 8388624 | tf_op jit(solution)/shard_map/all_gather | solution.py:471
  297.2 12.6 %fusion.92 = f32[2048,1024]{1,0:T(8,128)S(1)} fusion(bf16[2048,2048]{1,0:T(8,128)(2,1)} %all-gather.5.cloned.1.call-done, bf16[2048,1024]{1,0:T(8,128)(2,1)} %param.21), kind=kOutput, calls=%fused_computation.214 | convolution fusion | flops 8589934592 | bytes 20971520 | tf_op jit(solution)/shard_map/dot_general | solution.py:94
  318.7 10.9 %convolution_convert_fusion.1 = bf16[2048,2048]{1,0:T(8,128)(2,1)} fusion(bf16[2048,1024]{1,0:T(8,128)(2,1)S(1)} %get-tuple-element.75, bf16[2048,1024]{1,0:T(8,128)(2,1)S(1)} %copy-done.68), kind=kOutput, calls=%fused_computation.11 | convolution fusion | flops 8594128896 | bytes 16777216 | tf_op jit(solution)/shard_map/dot_general | solution.py:94
  339.4 78.6 %reduce-scatter.3.cloned.1.call-done = bf16[256,2048]{1,0:T(8,128)(2,1)} async-done(((bf16[2048,2048]{1,0:T(8,128)(2,1)}), bf16[256,2048]{1,0:T(8,128)(2,1)}) %reduce-scatter.3.cloned.1.call-update) | async-done | bytes 1048592 | tf_op jit(solution)/shard_map/reduce_scatter | solution.py:483
  428.4 11.8 %fusion.6 = bf16[1024,2048]{1,0:T(8,128)(2,1)} fusion(bf16[2048,1024]{1,0:T(8,128)(2,1)S(1)} %copy-done.20, bf16[2048,2048]{1,0:T(8,128)(2,1)S(1)} %bitcast.303, f32[2048]{0:T(1024)S(1)} %bitcast.279), kind=kOutput, calls=%fused_computation.15 | convolution fusion | flops 8604614656 | bytes 16785408 | tf_op jit(solution)/shard_map/dot_general | solution.py:94
  440.3 11.2 %collective-permute-done.23 = bf16[256,2048]{1,0:T(8,128)(2,1)} collective-permute-done((bf16[256,2048]{1,0:T(8,128)(2,1)}, bf16[256,2048]{1,0:T(8,128)(2,1)}, u32[]{:S(2)}, u32[]{:S(2)}) %collective-permute-start.23) | collective-permute-done | bytes 1048608 | tf_op jit(solution)/shard_map/ppermute | solution.py:349
  451.5 10.9 %convolution_convert_fusion = bf16[2048,2048]{1,0:T(8,128)(2,1)} fusion(bf16[2048,1024]{1,0:T(8,128)(2,1)S(1)} %copy-done.20, bf16[1024,2048]{1,0:T(8,128)(2,1)S(1)} %copy-done.69), kind=kOutput, calls=%fused_computation.10 | convolution fusion | flops 8594128896 | bytes 16777216 | tf_op jit(solution)/shard_map/dot_general | solution.py:94
  477.3 11.8 %convolution_convert_fusion.2 = bf16[2048,1024]{1,0:T(8,128)(2,1)S(1)} fusion(bf16[2048,2048]{1,0:T(8,128)(2,1)} %all-gather.5.cloned.1.call-done, bf16[2048,1024]{1,0:T(8,128)(2,1)S(1)} %copy-done.19), kind=kOutput, calls=%fused_computation.16 | convolution fusion | flops 8592031744 | bytes 16777216 | tf_op jit(solution)/shard_map/dot_general | solution.py:94
  506.3 15.6 %collective-permute-done.52 = bf16[2,256,1024]{2,1,0:T(8,128)(2,1)} collective-permute-done((bf16[2,256,1024]{2,1,0:T(8,128)(2,1)}, bf16[2,256,1024]{2,1,0:T(8,128)(2,1)}, u32[]{:S(2)}, u32[]{:S(2)}) %collective-permute-start.52) | collective-permute-done | bytes 1048608 | tf_op jit(solution)/shard_map/ppermute | solution.py:369
  549.0 13.9 %attend_backward.2.q_ref.refs_7_ = bf16[1024,768]{1,0:T(8,128)(2,1)} custom-call(bf16[1024,2048]{1,0:T(8,128)(2,1)} %bitcast.241, bf16[2048,1024]{1,0:T(8,128)(2,1)} %place_blocks.4.refs_1_.refs_8_, bf16[1024,768]{1,0:T(8,128)(2,1)} %get-tuple-element.59.refs_2_, f32[1024,2]{1,0:T(8,128)} %get-tuple-element.60.refs_3_, ...), custom_call_target="tpu_custom_call" | custom-call | flops 2415919104 | bytes 12582912 | tf_op jit(solution)/shard_map/attend_backward/pallas_call | solution.py:260
  572.2 23.0 %attend_backward.3 = (bf16[1024,768]{1,0:T(8,128)(2,1)}, bf16[1024,2048]{1,0:T(8,128)(2,1)}) custom-call(bf16[1024,2048]{1,0:T(8,128)(2,1)} %bitcast.243, bf16[2048,1024]{1,0:T(8,128)(2,1)} %copy-done.15, bf16[1024,768]{1,0:T(8,128)(2,1)} %get-tuple-element.65.refs_2_, f32[1024,2]{1,0:T(8,128)} %get-tuple-element.66.refs_3_, ...), custom_call_target="tpu_custom_call" | custom-call | flops 8858370048 | bytes 12582912 | tf_op jit(solution)/shard_map/attend_backward/pallas_call | solution.py:260
  621.1 14.7 %collective-permute-done.41 = bf16[2,256,1024]{2,1,0:T(8,128)(2,1)} collective-permute-done((bf16[2,256,1024]{2,1,0:T(8,128)(2,1)}, bf16[2,256,1024]{2,1,0:T(8,128)(2,1)}, u32[]{:S(2)}, u32[]{:S(2)}) %collective-permute-start.41) | collective-permute-done | bytes 1048608 | tf_op jit(solution)/shard_map/ppermute | solution.py:369
  639.0 19.4 %collective-permute-done.43 = bf16[2,256,1024]{2,1,0:T(8,128)(2,1)} collective-permute-done((bf16[2,256,1024]{2,1,0:T(8,128)(2,1)}, bf16[2,256,1024]{2,1,0:T(8,128)(2,1)}, u32[]{:S(2)}, u32[]{:S(2)}) %collective-permute-start.43) | collective-permute-done | bytes 1048608 | tf_op jit(solution)/shard_map/ppermute | solution.py:369
  668.5 16.5 %collective-permute-done.35 = bf16[2,256,1024]{2,1,0:T(8,128)(2,1)S(1)} collective-permute-done((bf16[2,256,1024]{2,1,0:T(8,128)(2,1)S(1)}, bf16[2,256,1024]{2,1,0:T(8,128)(2,1)S(1)}, u32[]{:S(2)}, u32[]{:S(2)}) %collective-permute-start.35) | collective-permute-done | bytes 1048608 | tf_op jit(solution)/shard_map/ppermute | solution.py:369
  687.1 9.9 %collective-permute-done.44 = bf16[256,1024]{1,0:T(8,128)(2,1)S(1)} collective-permute-done((bf16[256,1024]{1,0:T(8,128)(2,1)S(1)}, bf16[256,1024]{1,0:T(8,128)(2,1)S(1)}, u32[]{:S(2)}, u32[]{:S(2)}) %collective-permute-start.44) | collective-permute-done | bytes 524320 | tf_op jit(solution)/shard_map/ppermute | solution.py:369
  712.0 11.1 %collective-permute-done.66.refs_3_ = bf16[128,2048]{1,0:T(8,128)(2,1)S(1)} collective-permute-done((bf16[128,2048]{1,0:T(8,128)(2,1)}, bf16[128,2048]{1,0:T(8,128)(2,1)S(1)}, u32[]{:S(2)}, u32[]{:S(2)}) %collective-permute-start.66) | collective-permute-done | bytes 524320 | tf_op jit(solution)/shard_map/ppermute | solution.py:349
  761.3 10.5 %collective-permute-done.58.refs_7_ = bf16[256,1024]{1,0:T(8,128)(2,1)} collective-permute-done((bf16[256,1024]{1,0:T(8,128)(2,1)S(1)}, bf16[256,1024]{1,0:T(8,128)(2,1)}, u32[]{:S(2)}, u32[]{:S(2)}) %collective-permute-start.58) | collective-permute-done | bytes 524320 | tf_op jit(solution)/shard_map/ppermute | solution.py:349
  (407 shorter events, 333.8 us)
Async XLA Ops:
  7.2 189.3 %all-gather.3.cloned.1.call-start = ((), (), s32[]{:S(2)}) async-start(), calls=%async_computation.2 | async-start | bytes 9437184 | tf_op jit(solution)/shard_map/all_gather | solution.py:453
  42.0 38.3 %collective-permute-start.3 = (bf16[256,1024]{1,0:T(8,128)(2,1)}, bf16[256,1024]{1,0:T(8,128)(2,1)S(1)}, u32[]{:S(2)}, u32[]{:S(2)}) collective-permute-start(bf16[256,1024]{1,0:T(8,128)(2,1)} %get-tuple-element.114), channel_id=1, source_target_pairs={{0,4},{1,5},{2,6},{3,7},{4,0},{5,1},{6,2},{7,3},{8,12},{9,13},{10,... | collective-permute-start | bytes 1572872 | tf_op jit(solution)/shard_map/ppermute | solution.py:445
  44.8 46.6 %collective-permute-start.4 = (bf16[256,1024]{1,0:T(8,128)(2,1)S(1)}, bf16[256,1024]{1,0:T(8,128)(2,1)}, u32[]{:S(2)}, u32[]{:S(2)}) collective-permute-start(bf16[256,1024]{1,0:T(8,128)(2,1)S(1)} %get-tuple-element.113), channel_id=1, source_target_pairs={{0,4},{1,5},{2,6},{3,7},{4,0},{5,1},{6,2},{7,3},{8,12},{9,13},{10,... | collective-permute-start | bytes 1572872 | tf_op jit(solution)/shard_map/ppermute | solution.py:445
  91.4 205.7 %all-gather.5.cloned.1.call-start = ((), (), s32[]{:S(2)}) async-start(), calls=%async_computation.3 | async-start | bytes 9437184 | tf_op jit(solution)/shard_map/all_gather | solution.py:471
  214.4 203.6 %reduce-scatter.3.cloned.1.call-start = ((), (), s32[]{:S(2)}) async-start(), calls=%async_computation.4 | async-start | bytes 9437184 | tf_op jit(solution)/shard_map/reduce_scatter | solution.py:483
  329.6 486.2 %reduce-scatter.5.cloned.1.call-start = ((), (), s32[]{:S(2)}) async-start(), calls=%async_computation.5 | async-start | bytes 9437184 | tf_op jit(solution)/shard_map/reduce_scatter | solution.py:495
  492.7 32.5 %collective-permute-start.49 = (bf16[2,256,1024]{2,1,0:T(8,128)(2,1)}, bf16[2,256,1024]{2,1,0:T(8,128)(2,1)}, u32[]{:S(2)}, u32[]{:S(2)}) collective-permute-start(bf16[2,256,1024]{2,1,0:T(8,128)(2,1)} %dynamic-slice_bitcast_fusion.5), channel_id=1, source_target_pairs={{0,8},{8,0},{16,24},{24,16},{1,9},{9,1},{17,25},{25,17},{2,10},{10... | collective-permute-start | bytes 3145736 | tf_op jit(solution)/shard_map/ppermute | solution.py:369
  501.5 34.2 %collective-permute-start.63 = (bf16[128,2048]{1,0:T(8,128)(2,1)S(1)}, bf16[128,2048]{1,0:T(8,128)(2,1)S(1)}, u32[]{:S(2)}, u32[]{:S(2)}) collective-permute-start(bf16[128,2048]{1,0:T(8,128)(2,1)S(1)} %fusion.55), channel_id=1, source_target_pairs={{0,8},{8,0},{16,24},{24,16},{1,9},{9,1},{17,25},{25,17},{2,10},{10... | collective-permute-start | bytes 1572872 | tf_op jit(solution)/shard_map/ppermute | solution.py:369
  535.8 78.6 %collective-permute-start.64 = (bf16[128,2048]{1,0:T(8,128)(2,1)S(1)}, bf16[128,2048]{1,0:T(8,128)(2,1)S(1)}, u32[]{:S(2)}, u32[]{:S(2)}) collective-permute-start(bf16[128,2048]{1,0:T(8,128)(2,1)S(1)} %fusion.32.refs_4_), channel_id=1, source_target_pairs={{0,16},{8,24},{16,0},{24,8},{1,17},{9,25},{17,1},{25,9},{2,18},{10... | collective-permute-start | bytes 1572872 | tf_op jit(solution)/shard_map/ppermute | solution.py:349
  537.7 82.4 %collective-permute-start.61 = (bf16[128,2048]{1,0:T(8,128)(2,1)}, bf16[128,2048]{1,0:T(8,128)(2,1)}, u32[]{:S(2)}, u32[]{:S(2)}) collective-permute-start(bf16[128,2048]{1,0:T(8,128)(2,1)} %fusion.33.refs_0_), channel_id=1, source_target_pairs={{0,8},{8,0},{16,24},{24,16},{1,9},{9,1},{17,25},{25,17},{2,10},{10... | collective-permute-start | bytes 1572872 | tf_op jit(solution)/shard_map/ppermute | solution.py:349
  598.3 65.7 %collective-permute-start.26 = (bf16[2,256,2048]{2,1,0:T(8,128)(2,1)}, bf16[2,256,2048]{2,1,0:T(8,128)(2,1)}, u32[]{:S(2)}, u32[]{:S(2)}) collective-permute-start(bf16[2,256,2048]{2,1,0:T(8,128)(2,1)} %dynamic-slice_bitcast_fusion), channel_id=1, source_target_pairs={{0,1},{1,0},{2,3},{3,2},{4,5},{5,4},{6,7},{7,6},{8,9},{9,8},{10,11... | collective-permute-start | bytes 6291464 | tf_op jit(solution)/shard_map/ppermute | solution.py:429
  612.2 46.1 %collective-permute-start.43 = (bf16[2,256,1024]{2,1,0:T(8,128)(2,1)}, bf16[2,256,1024]{2,1,0:T(8,128)(2,1)}, u32[]{:S(2)}, u32[]{:S(2)}) collective-permute-start(bf16[2,256,1024]{2,1,0:T(8,128)(2,1)} %dynamic-slice_bitcast_fusion.6), channel_id=1, source_target_pairs={{0,16},{8,24},{16,0},{24,8},{1,17},{9,25},{17,1},{25,9},{2,18},{10... | collective-permute-start | bytes 3145736 | tf_op jit(solution)/shard_map/ppermute | solution.py:369
  615.3 45.5 %collective-permute-start.33 = (bf16[2,256,1024]{2,1,0:T(8,128)(2,1)}, bf16[2,256,1024]{2,1,0:T(8,128)(2,1)}, u32[]{:S(2)}, u32[]{:S(2)}) collective-permute-start(bf16[2,256,1024]{2,1,0:T(8,128)(2,1)} %dynamic-slice_bitcast_fusion.9), channel_id=1, source_target_pairs={{0,8},{8,0},{16,24},{24,16},{1,9},{9,1},{17,25},{25,17},{2,10},{10... | collective-permute-start | bytes 3145736 | tf_op jit(solution)/shard_map/ppermute | solution.py:369
  620.1 78.0 %collective-permute-start.54 = (bf16[256,1024]{1,0:T(8,128)(2,1)}, bf16[256,1024]{1,0:T(8,128)(2,1)S(1)}, u32[]{:S(2)}, u32[]{:S(2)}) collective-permute-start(bf16[256,1024]{1,0:T(8,128)(2,1)} %fusion.34.refs_4_), channel_id=1, source_target_pairs={{0,16},{8,24},{16,0},{24,8},{1,17},{9,25},{17,1},{25,9},{2,18},{10... | collective-permute-start | bytes 1572872 | tf_op jit(solution)/shard_map/ppermute | solution.py:349
  635.9 63.4 %collective-permute-start.51 = (bf16[256,1024]{1,0:T(8,128)(2,1)}, bf16[256,1024]{1,0:T(8,128)(2,1)S(1)}, u32[]{:S(2)}, u32[]{:S(2)}) collective-permute-start(bf16[256,1024]{1,0:T(8,128)(2,1)} %fusion.35.refs_0_), channel_id=1, source_target_pairs={{0,8},{8,0},{16,24},{24,16},{1,9},{9,1},{17,25},{25,17},{2,10},{10... | collective-permute-start | bytes 1572872 | tf_op jit(solution)/shard_map/ppermute | solution.py:349
  658.3 46.9 %collective-permute-start.65 = (bf16[128,2048]{1,0:T(8,128)(2,1)}, bf16[128,2048]{1,0:T(8,128)(2,1)S(1)}, u32[]{:S(2)}, u32[]{:S(2)}) collective-permute-start(bf16[128,2048]{1,0:T(8,128)(2,1)} %fusion.33.refs_0_), channel_id=1, source_target_pairs={{0,16},{8,24},{16,0},{24,8},{1,17},{9,25},{17,1},{25,9},{2,18},{10... | collective-permute-start | bytes 1572872 | tf_op jit(solution)/shard_map/ppermute | solution.py:349
  666.6 34.0 %collective-permute-start.27 = (bf16[256,2048]{1,0:T(8,128)(2,1)S(1)}, bf16[256,2048]{1,0:T(8,128)(2,1)S(1)}, u32[]{:S(2)}, u32[]{:S(2)}) collective-permute-start(bf16[256,2048]{1,0:T(8,128)(2,1)S(1)} %fusion.31), channel_id=1, source_target_pairs={{0,2},{1,3},{2,0},{3,1},{4,6},{5,7},{6,4},{7,5},{8,10},{9,11},{10,... | collective-permute-start | bytes 3145736 | tf_op jit(solution)/shard_map/ppermute | solution.py:369
  700.6 34.9 %collective-permute-start.45 = (bf16[256,1024]{1,0:T(8,128)(2,1)S(1)}, bf16[256,1024]{1,0:T(8,128)(2,1)S(1)}, u32[]{:S(2)}, u32[]{:S(2)}) collective-permute-start(bf16[256,1024]{1,0:T(8,128)(2,1)S(1)} %fusion.36), channel_id=1, source_target_pairs={{0,4},{1,5},{2,6},{3,7},{4,0},{5,1},{6,2},{7,3},{8,12},{9,13},{10,... | collective-permute-start | bytes 1572872 | tf_op jit(solution)/shard_map/ppermute | solution.py:525
  705.3 32.3 %collective-permute-start.34 = (bf16[256,1024]{1,0:T(8,128)(2,1)S(1)}, bf16[256,1024]{1,0:T(8,128)(2,1)S(1)}, u32[]{:S(2)}, u32[]{:S(2)}) collective-permute-start(bf16[256,1024]{1,0:T(8,128)(2,1)S(1)} %fusion.48), channel_id=1, source_target_pairs={{0,16},{8,24},{16,0},{24,8},{1,17},{9,25},{17,1},{25,9},{2,18},{10... | collective-permute-start | bytes 1572872 | tf_op jit(solution)/shard_map/ppermute | solution.py:369
  749.7 33.2 %collective-permute-start.38 = (bf16[256,1024]{1,0:T(8,128)(2,1)S(1)}, bf16[256,1024]{1,0:T(8,128)(2,1)S(1)}, u32[]{:S(2)}, u32[]{:S(2)}) collective-permute-start(bf16[256,1024]{1,0:T(8,128)(2,1)S(1)} %add_convert_fusion.2.refs_0_), channel_id=1, source_target_pairs={{0,8},{8,0},{16,24},{24,16},{1,9},{9,1},{17,25},{25,17},{2,10},{10... | collective-permute-start | bytes 1572872 | tf_op jit(solution)/shard_map/ppermute | solution.py:349
  757.6 38.5 %collective-permute-start.30 = (f32[160,128]{1,0:T(8,128)S(1)}, f32[160,128]{1,0:T(8,128)S(1)}, u32[]{:S(2)}, u32[]{:S(2)}) collective-permute-start(f32[160,128]{1,0:T(8,128)S(1)} %add.420), channel_id=1, source_target_pairs={{0,4},{1,5},{2,6},{3,7},{4,0},{5,1},{6,2},{7,3},{8,12},{9,13},{10,... | collective-permute-start | bytes 245768 | tf_op jit(solution)/shard_map/ppermute | solution.py:401
  760.5 45.7 %collective-permute-start.46 = (bf16[256,1024]{1,0:T(8,128)(2,1)S(1)}, bf16[256,1024]{1,0:T(8,128)(2,1)S(1)}, u32[]{:S(2)}, u32[]{:S(2)}) collective-permute-start(bf16[256,1024]{1,0:T(8,128)(2,1)S(1)} %add_convert_fusion.1.refs_4_), channel_id=1, source_target_pairs={{0,8},{8,0},{16,24},{24,16},{1,9},{9,1},{17,25},{25,17},{2,10},{10... | collective-permute-start | bytes 1572872 | tf_op jit(solution)/shard_map/ppermute | solution.py:349
  771.8 34.3 %collective-permute-start.39 = (bf16[256,1024]{1,0:T(8,128)(2,1)S(1)}, bf16[256,1024]{1,0:T(8,128)(2,1)S(1)}, u32[]{:S(2)}, u32[]{:S(2)}) collective-permute-start(bf16[256,1024]{1,0:T(8,128)(2,1)S(1)} %add_convert_fusion.2.refs_0_), channel_id=1, source_target_pairs={{0,16},{8,24},{16,0},{24,8},{1,17},{9,25},{17,1},{25,9},{2,18},{10... | collective-permute-start | bytes 1572872 | tf_op jit(solution)/shard_map/ppermute | solution.py:349
  773.0 33.2 %collective-permute-start.48 = (bf16[256,1024]{1,0:T(8,128)(2,1)S(1)}, bf16[256,1024]{1,0:T(8,128)(2,1)S(1)}, u32[]{:S(2)}, u32[]{:S(2)}) collective-permute-start(bf16[256,1024]{1,0:T(8,128)(2,1)S(1)} %collective-permute-done.47.refs_6_), channel_id=1, source_target_pairs={{0,8},{8,0},{16,24},{24,16},{1,9},{9,1},{17,25},{25,17},{2,10},{10... | collective-permute-start | bytes 1572872 | tf_op jit(solution)/shard_map/ppermute | solution.py:349
  (121 other events, 2369.8 us)
Sparse Core Ops, SparseCore 0:
  91.6 83.1 all-gather.2
  214.5 82.6 all-gather.4
  329.8 88.2 reduce-scatter.2
  469.4 89.7 reduce-scatter.4

commit v3 on v2

--- a/solution.py
+++ b/solution.py
@@ -195,13 +195,14 @@
 
 
 def place_kernel(count, widths, turned, at_ref, *refs):
-    blocks, outs = refs[: 2 * count], refs[2 * count :]
+    lanes = (len(refs) - len(widths)) // count
+    blocks, outs = refs[: lanes * count], refs[lanes * count :]
     half = blocks[0].shape[0]
     for far in range(count):
 
         @pl.when((pl.program_id(0) ^ at_ref[0]) == far)
         def _():
-            for lane in range(2):
+            for lane in range(lanes):
                 here = slice(lane * half, (lane + 1) * half)
                 block = blocks[lane * count + far]
                 start = 0
@@ -294,7 +295,7 @@
 def place_blocks(lanes, index, outs):
     count = len(lanes[0])
     half, total = lanes[0][0].shape
-    rows = 2 * half
+    rows = len(lanes) * half
     shapes, specs = [], []
     for planes, width, kind, turned in outs:
         if turned:
@@ -358,17 +359,18 @@
     return out
 
 
-def xor_scatter(blocks, axis_name, size, bits, steps, index, axis):
-    count = blocks.shape[axis].bit_length() - 1
-    blocks = blocks.reshape(blocks.shape[:axis] + (2,) * count + blocks.shape[axis + 1 :])
-    left = [1 << (count - 1 - i) for i in range(count)]
+def xor_scatter(blocks, axis_name, size, bits, steps, index, axis, all_steps=None):
+    all_steps = list(all_steps or steps)
+    left = sorted(all_steps[all_steps.index(steps[0]) :], reverse=True)
+    blocks = blocks.reshape(blocks.shape[:axis] + (2,) * len(left) + blocks.shape[axis + 1 :])
     for bit, step in zip(bits, steps):
         at = axis + left.index(step)
         left.remove(step)
         side = (index // step) % 2
         got = lax.ppermute(narrow(pick(blocks, 1 - side, at)), axis_name, swap_pairs(size, bit))
         blocks = wide(pick(blocks, side, at)) + wide(got)
-    return blocks
+    tail = blocks.shape[axis + len(left) :]
+    return blocks.reshape(blocks.shape[:axis] + ((2 ** len(left),) if left else ()) + tail)
 
 
 def lane_bits(size):
@@ -386,13 +388,11 @@
     return [{far: next(flat) for far in held} for held in lanes]
 
 
-def column_scatter(lanes, size, column):
-    return [narrow(xor_scatter(x, "dp", size, bits, bits, column, 0)) for x, bits in zip(lanes, lane_bits(size))]
-
-
-def two_lanes(x, size):
-    blocks = x.reshape(size, 2, -1, x.shape[1])
-    return [blocks[:, 0], blocks[:, 1]]
+def column_scatter(lanes, size, column, cut=None, start=None):
+    return [
+        xor_scatter(x, "dp", size, bits[start:cut], bits[start:cut], column, 0, bits)
+        for x, bits in zip(lanes, lane_bits(size))
+    ]
 
 
 def all_sum(x, sizes):
@@ -445,25 +445,25 @@
             lax.ppermute(lane, "mp", shift_pairs(ranks, k * group)) for k in range(1, sequences) for lane in chunks
         ]
         inputs_one, *fetched = lax.optimization_barrier((inputs_one, *fetched))
-        weights = [packed]
-        for k in range(1, sequences):
-            held = column_gather(fetched[2 * k - 2 : 2 * k], columns)
-            weights += place_blocks(held, column, [(1, packed.shape[1], jnp.bfloat16, False)])
+        helds = [column_gather(fetched[2 * k - 2 : 2 * k], columns, cut=1) for k in range(1, sequences)]
         gate_one, state_one = gate_forward(normed_one, mixer_router, width_own[:, 0], routed_own[:, 0])
         grads_all = lax.all_gather(after(out_grad, *fetched), "mp", axis=0, tiled=True)
 
         sequence_width = lax.dynamic_slice_in_dim(width_choice[:, 0], sequence * SEQ_LEN, SEQ_LEN, 0)
-        kept, earlier = [], []
+        weights, kept, earlier = [packed], [], []
         for k in range(sequences):
             heads = ((rank + k * group) % ranks) * own_heads + jnp.arange(own_heads, dtype=jnp.int32)
             mask = (heads[None, :] * 4 < (sequence_width[:, None] + 1) * H).astype(jnp.float32)
             last = k == sequences - 1
+            if k:
+                held = column_gather(gate_lanes(helds[k - 1], kept[0][0]), columns, start=1)
+                weights += place_blocks(held, column, [(1, packed.shape[1], jnp.bfloat16, False)])
             qkv, heads_out, log_total, *share = attend_forward(inputs_one, weights[k], cos, sin, mask, earlier, last)
             kept.append((qkv, heads_out, log_total, mask))
             earlier.append((heads_out, weights[k]))
         mixer_branch = from_sequence(share[0])
+        mixer_branch, grads_all = lax.optimization_barrier((mixer_branch, grads_all))
         top_down = product(grads_all, down_weight, (1, 1))
-        mixer_branch, top_down = lax.optimization_barrier((mixer_branch, top_down))
 
         middle = input_wide + gate_one[:, None] * mixer_branch
         normed_two, scaled_two, inverse_two = norm_forward(middle, hidden_gain)
@@ -473,6 +473,7 @@
 
         col_ids = rank * cols_local + jnp.arange(cols_local, dtype=jnp.int32)
         col_mask = (col_ids[None, :] * 4 < (width_choice[:, 1:2] + 1) * FF).astype(jnp.float32)
+        inputs_two, top_down = lax.optimization_barrier((inputs_two, top_down))
         pre = product(inputs_two, up_weight, (1, 0))
         relu_act = jax.nn.relu(pre)
         hidden = narrow(relu_act * relu_act * col_mask)
@@ -483,21 +484,23 @@
         normed_grad_two = wide(lax.psum_scatter(share, "mp", scatter_dimension=0, tiled=True))
         gate_grad_two = lax.dynamic_slice_in_dim(all_sum(dots, {"mp": ranks}).reshape(-1), rank * rows, rows, 0)
         gated = narrow(gates[:, None] * wide(grads_all))
-        down_piece = column_scatter(two_lanes(narrow(product(hidden, gated, (0, 0))), columns), columns, column)
-        up_piece = column_scatter(two_lanes(narrow(product(inputs_two, pre_grad, (0, 0))), columns), columns, column)
+        lanes = [narrow(product(hidden, gated, (0, 0))), narrow(product(inputs_two, pre_grad, (0, 0)))]
+        lanes = [x.reshape(columns, -1, x.shape[1]) for x in lanes]
+        lanes = column_scatter(lanes, columns, column, cut=1)
         hidden_share = narrow(product(hidden, down_weight, (1, 0)))
+        normed_grad_two, hidden_share, *lanes = lax.optimization_barrier((normed_grad_two, hidden_share, *lanes))
+        lanes = [narrow(x) for x in column_scatter(lanes, columns, column, start=1)]
 
         router_part, router_two = gate_backward(normed_two, hidden_router, state_two, gate_grad_two)
         middle_part, gain_two = norm_backward(normed_grad_two + router_part, scaled_two, inverse_two, hidden_gain)
         middle_grad = wide(out_grad) + middle_part
         grads_one, held_grads = to_sequence(narrow(gate_one[:, None] * middle_grad))
-        grads_one, hidden_share = lax.optimization_barrier((grads_one, hidden_share))
+        grads_one, hidden_share, *lanes = lax.optimization_barrier((grads_one, hidden_share, *lanes))
         hidden_branch = wide(lax.psum_scatter(hidden_share, "mp", scatter_dimension=0, tiled=True))
         layer_output = narrow(middle + gate_two[:, None] * hidden_branch)
 
         gate_grad_one = jnp.sum(middle_grad * mixer_branch, axis=1)
-        down_held = column_gather(down_piece, columns, cut=1)
-        up_held = column_gather(up_piece, columns, cut=1)
+        helds = column_gather(lanes, columns, cut=1)
         earlier, weight_parts = [], [None] * sequences
         grads_now = grads_one
         for k in range(sequences)[::-1]:
@@ -506,23 +509,27 @@
                 grads_now, weights[k], qkv, log_total, cos, sin, mask, earlier, k == 0
             )
             earlier.append((qkv_grad, weights[k]))
+            if k == 0:
+                helds = column_gather(helds, columns, start=1)
+                flat = [held[far] for held in helds for far in held]
+                qkv_grad, *flat = lax.optimization_barrier((qkv_grad, *flat))
+                helds = [dict(zip(held, flat[i * columns :])) for i, held in enumerate(helds)]
             weight_parts[k] = weight_grads(inputs_one, qkv_grad, grads_one, heads_out, columns)
-            if k:
-                grads_now, *weight_parts[k] = lax.optimization_barrier((grads_now, *weight_parts[k]))
-        down_held = gate_lanes(down_held, earlier[0][0])
-        up_held = gate_lanes(up_held, earlier[0][0])
+            if k == sequences - 1:
+                flat = [held[far] for held in helds for far in held]
+                grads_now, *rest = lax.optimization_barrier((grads_now, *weight_parts[k], *flat))
+                weight_parts[k], flat = rest[:2], rest[2:]
+                helds = [dict(zip(held, flat[i * 2 :])) for i, held in enumerate(helds)]
         normed_grad_one = from_sequence(share[0])
 
-        down_held = column_gather(down_held, columns, start=1)
-        up_held = column_gather(up_held, columns, start=1)
-        down_sum, = place_blocks(down_held, column, [(1, dim, jnp.float32, False)])
-        up_sum, = place_blocks(up_held, column, [(1, cols_local, jnp.float32, False)])
+        down_sum, = place_blocks(helds[:1], column, [(1, dim, jnp.float32, False)])
+        up_sum, = place_blocks(helds[1:], column, [(1, cols_local, jnp.float32, False)])
 
         pieces = column_scatter(weight_parts[0], columns, column)
         for k in range(1, sequences):
-            there = column_scatter(weight_parts[k], columns, column)
+            there = [narrow(x) for x in column_scatter(weight_parts[k], columns, column)]
             back = shift_pairs(ranks, -k * group)
-            pieces = [narrow(wide(p) + wide(lax.ppermute(t, "mp", back))) for p, t in zip(pieces, there)]
+            pieces = [narrow(p + wide(lax.ppermute(t, "mp", back))) for p, t in zip(pieces, there)]
         attention_sum, output_sum = place_blocks(
             column_gather(pieces, columns),
             column,

time: 831 us -> 680 us (0.82)
  waiting for transfers between devices: 436 us -> 297 us
  starting transfers between devices: 74 us -> 58.4 us
  matrix products: 86.7 us -> 95.6 us
    reduce_scatter x1, waiting for transfers between devices: 78.6 us -> 2.47 us  [local(): lax.psum_scatter(share, 'mp', scatter_dimension=0, tiled=True)]
    ppermute x18 -> x14, waiting for transfers between devices: 127 us -> 98.8 us  [xor_scatter(): lax.ppermute(narrow(pick(blocks, 1 - side, at)), axis_name, swap_pairs(si...]
    all_gather x1, waiting for transfers between devices: 65.3 us -> 49.7 us  [local(): inputs_two = lax.all_gather(narrow(normed_two), 'mp', axis=0, tiled=True)]
    ppermute x2, waiting for transfers between devices: 15.4 us -> 0.01 us  [local(): lax.ppermute(t, 'mp', back)]
    ppermute x37 -> x31, waiting for transfers between devices: 86.9 us -> 74.7 us  [xor_gather(): held[far ^ bit] = lax.ppermute(held[far], axis, swap_pairs(size, bit))]
    ppermute x18 -> x14, starting transfers between devices: 24.3 us -> 15 us  [xor_scatter(): lax.ppermute(narrow(pick(blocks, 1 - side, at)), axis_name, swap_pairs(si...]
    ppermute x8, waiting for transfers between devices: 17.4 us -> 26.6 us  [all_sum(): x = x + lax.ppermute(x, axis, swap_pairs(size, bit))]
    dot_general x6, matrix products: 72.6 us -> 80.9 us  [product(): lax.dot_general(a, b, ((dims[:1], dims[1:]), ((), ())), preferred_element...]
  transfers between devices with their start and end apart: 73 -> 63, of which waited for: 33 -> 28; matrix products, arithmetic and copies ran while one was open for 14% -> 19% of each run, Pallas kernels for 13% -> 16%
where the time goes in v3:
time: 680 us; the launch traced here: 677 us
  waiting for transfers between devices  297 us (44%)
  Pallas kernels  109 us (16%)
  matrix products  95.6 us (14%)
  starting transfers between devices  58.4 us (9%)
  other arithmetic  57.2 us (8%)
  local copies, waits for them, and re-layouts  44 us (6%)
  between operations  14.9 us (2%)
    ppermute x14, waiting for transfers between devices, xor_scatter(): lax.ppermute(narrow(pick(blocks, 1 - side, at)), axis_name, swap_pairs(si...  98.8 us
    dot_general x6, matrix products, product(): lax.dot_general(a, b, ((dims[:1], dims[1:]), ((), ())), preferred_element...  80.9 us
    ppermute x31, waiting for transfers between devices, xor_gather(): held[far ^ bit] = lax.ppermute(held[far], axis, swap_pairs(size, bit))  74.7 us
    all_gather x1, waiting for transfers between devices, local(): inputs_two = lax.all_gather(narrow(normed_two), 'mp', axis=0, tiled=True)  49.7 us
    ppermute x2, waiting for transfers between devices, local(): lax.ppermute(lane, 'mp', shift_pairs(ranks, k * group))  40.7 us
    pallas_call x2, Pallas kernels, attend_backward(): pl.pallas_call(functools.partial(backward_kernel, len(given) // 2), out_s...  37.4 us
    ppermute x31, starting transfers between devices, xor_gather(): held[far ^ bit] = lax.ppermute(held[far], axis, swap_pairs(size, bit))  33.8 us
    pallas_call x2, Pallas kernels, attend_forward(): pl.pallas_call(functools.partial(forward_kernel, len(given) // 2), out_sh...  31.7 us
  transfers between devices with their start and end apart: 63, of which 28 were waited for; matrix products, arithmetic and copies ran while one was open for 19% of the time, Pallas kernels for 16%

profile of v3, /device:TPU:0, one launch (start us, length us, event | category | flops | bytes accessed | tf_op | source)
XLA Modules:
  0.0 676.6 jit_solution(14757651894671847361)
XLA Ops:
  22.5 18.6 %collective-permute-done = bf16[256,2048]{1,0:T(8,128)(2,1)} collective-permute-done((bf16[256,2048]{1,0:T(8,128)(2,1)}, bf16[256,2048]{1,0:T(8,128)(2,1)}, u32[]{:S(2)}, u32[]{:S(2)}) %collective-permute-start) | collective-permute-done | bytes 1048608 | tf_op jit(solution)/shard_map/ppermute | solution.py:350
  50.8 29.7 %collective-permute-done.3.refs_0_ = bf16[256,1024]{1,0:T(8,128)(2,1)S(1)} collective-permute-done((bf16[256,1024]{1,0:T(8,128)(2,1)}, bf16[256,1024]{1,0:T(8,128)(2,1)S(1)}, u32[]{:S(2)}, u32[]{:S(2)}) %collective-permute-start.3) | collective-permute-done | bytes 524320 | tf_op jit(solution)/shard_map/ppermute | solution.py:445
  80.5 11.0 %collective-permute-done.4.refs_4_ = bf16[256,1024]{1,0:T(8,128)(2,1)S(1)} collective-permute-done((bf16[256,1024]{1,0:T(8,128)(2,1)}, bf16[256,1024]{1,0:T(8,128)(2,1)S(1)}, u32[]{:S(2)}, u32[]{:S(2)}) %collective-permute-start.4) | collective-permute-done | bytes 524320 | tf_op jit(solution)/shard_map/ppermute | solution.py:445
  99.5 13.9 %attend_forward.2 = (bf16[1024,768]{1,0:T(8,128)(2,1)}, bf16[1024,256]{1,0:T(8,128)(2,1)}, f32[1024,2]{1,0:T(8,128)}) custom-call(bf16[1024,2048]{1,0:T(8,128)(2,1)} %bitcast.7.refs_0_.x_ref, bf16[2048,1024]{1,0:T(8,128)(2,1)} %copy-done.7, f32[1024,128]{1,0:T(8,128)} %get-tuple-element.168.refs_2_.refs_4_, f32[1024,128]{1,0:T(8,128)} %get-tuple-element.169.refs_3_.refs_5_, ...), custom_call_target="tpu_custom_call" | custom-call | flops 3758096384 | bytes 12582912 | tf_op jit(solution)/shard_map/attend_forward/pallas_call | solution.py:241
  117.5 10.9 %collective-permute-done.10.refs_7_ = bf16[256,1024]{1,0:T(8,128)(2,1)} collective-permute-done((bf16[256,1024]{1,0:T(8,128)(2,1)S(1)}, bf16[256,1024]{1,0:T(8,128)(2,1)}, u32[]{:S(2)}, u32[]{:S(2)}) %collective-permute-start.10) | collective-permute-done | bytes 524320 | tf_op jit(solution)/shard_map/ppermute | solution.py:350
  143.0 17.8 %attend_forward.3 = (bf16[1024,768]{1,0:T(8,128)(2,1)}, bf16[1024,256]{1,0:T(8,128)(2,1)}, f32[1024,2]{1,0:T(8,128)}, bf16[1024,2048]{1,0:T(8,128)(2,1)}) custom-call(bf16[1024,2048]{1,0:T(8,128)(2,1)} %bitcast.7.refs_0_.x_ref, bf16[2048,1024]{1,0:T(8,128)(2,1)} %place_blocks.4.refs_1_.refs_8_, f32[1024,128]{1,0:T(8,128)} %get-tuple-element.168.refs_2_.refs_4_, ...), custom_call_target="tpu_custom_call" | custom-call | flops 5905580032 | bytes 12582912 | tf_op jit(solution)/shard_map/attend_forward/pallas_call | solution.py:241
  175.7 22.0 %collective-permute-done.12 = bf16[256,2048]{1,0:T(8,128)(2,1)} collective-permute-done((bf16[256,2048]{1,0:T(8,128)(2,1)S(1)}, bf16[256,2048]{1,0:T(8,128)(2,1)}, u32[]{:S(2)}, u32[]{:S(2)}) %collective-permute-start.12) | collective-permute-done | bytes 1048608 | tf_op jit(solution)/shard_map/ppermute | solution.py:370
  212.4 15.2 %fusion.88 = f32[2048,1024]{1,0:T(8,128)} fusion(bf16[2048,2048]{1,0:T(8,128)(2,1)} %all-gather.3.cloned.1.call-done, bf16[1024,2048]{1,0:T(8,128)(2,1)} %param.22), kind=kOutput, calls=%fused_computation.199 | convolution fusion | flops 8589934592 | bytes 20971520 | tf_op jit(solution)/shard_map/dot_general | solution.py:94
  236.6 49.7 %all-gather.5.cloned.1.call-done = bf16[2048,2048]{1,0:T(8,128)(2,1)} async-done(((bf16[256,2048]{1,0:T(8,128)(2,1)}), bf16[2048,2048]{1,0:T(8,128)(2,1)}) %all-gather.5.cloned.1.call-update) | async-done | bytes 8388624 | tf_op jit(solution)/shard_map/all_gather | solution.py:471
  286.3 18.3 %multiply_reduce_fusion = (f32[2048]{0:T(1024)S(1)}, bf16[2048,1024]{1,0:T(8,128)(2,1)}, bf16[2048,1024]{1,0:T(8,128)(2,1)S(1)}) fusion(f32[2048,1024]{1,0:T(8,128)} %fusion.88, s32[2048]{0:T(1024)S(1)} %bitcast.251, s32[1024]{0:T(1024)S(1)} %add_multiply_fusion.1, f32[2048]{0:T(1024)S(1)} %bitcast.249, bf16[2048,2048]{1,0:T(8,128)(2,1)} %all-gather.5.cloned.1.call-done, ...), kind=kOutput, calls=%fused_computation.8 | convolution fusion | flops 8617195520 | bytes 29388800 | tf_op jit(solution)/shard_map/dot_general | solution.py:94
  306.7 10.9 %convolution_convert_fusion.1 = bf16[2048,2048]{1,0:T(8,128)(2,1)} fusion(bf16[2048,1024]{1,0:T(8,128)(2,1)S(1)} %get-tuple-element.81, bf16[2048,1024]{1,0:T(8,128)(2,1)S(1)} %copy-done.33), kind=kOutput, calls=%fused_computation.11 | convolution fusion | flops 8594128896 | bytes 16777216 | tf_op jit(solution)/shard_map/dot_general | solution.py:94
  317.8 13.1 %convolution_convert_fusion.2 = bf16[2048,1024]{1,0:T(8,128)(2,1)S(1)} fusion(bf16[2048,2048]{1,0:T(8,128)(2,1)} %all-gather.5.cloned.1.call-done, bf16[2048,1024]{1,0:T(8,128)(2,1)} %copy-done.36), kind=kOutput, calls=%fused_computation.18 | convolution fusion | flops 8592031744 | bytes 16777216 | tf_op jit(solution)/shard_map/dot_general | solution.py:94
  335.5 12.3 %fusion.6 = bf16[1024,2048]{1,0:T(8,128)(2,1)S(1)} fusion(bf16[2048,1024]{1,0:T(8,128)(2,1)S(1)} %copy-done.35, bf16[2048,2048]{1,0:T(8,128)(2,1)} %all-gather.3.cloned.1.call-done, f32[2048]{0:T(1024)S(1)} %bitcast.250), kind=kOutput, calls=%fused_computation.17 | convolution fusion | flops 8604614656 | bytes 16785408 | tf_op jit(solution)/shard_map/dot_general | solution.py:94
  352.9 11.1 %convolution_convert_fusion = bf16[2048,2048]{1,0:T(8,128)(2,1)} fusion(bf16[2048,1024]{1,0:T(8,128)(2,1)S(1)} %copy-done.35, bf16[1024,2048]{1,0:T(8,128)(2,1)S(1)} %copy-done.34), kind=kOutput, calls=%fused_computation.10 | convolution fusion | flops 8594128896 | bytes 16777216 | tf_op jit(solution)/shard_map/dot_general | solution.py:94
  367.4 14.7 %collective-permute-done.21 = bf16[2,512,1024]{2,1,0:T(8,128)(2,1)} collective-permute-done((bf16[2,512,1024]{2,1,0:T(8,128)(2,1)}, bf16[2,512,1024]{2,1,0:T(8,128)(2,1)}, u32[]{:S(2)}, u32[]{:S(2)}) %collective-permute-start.21) | collective-permute-done | bytes 2097184 | tf_op jit(solution)/shard_map/ppermute | solution.py:370
  387.2 12.1 %collective-permute-done.20 = bf16[2,256,2048]{2,1,0:T(8,128)(2,1)} collective-permute-done((bf16[2,256,2048]{2,1,0:T(8,128)(2,1)}, bf16[2,256,2048]{2,1,0:T(8,128)(2,1)}, u32[]{:S(2)}, u32[]{:S(2)}) %collective-permute-start.20) | collective-permute-done | bytes 2097184 | tf_op jit(solution)/shard_map/ppermute | solution.py:370
  419.7 19.4 %collective-permute-done.25 = bf16[256,2048]{1,0:T(8,128)(2,1)S(1)} collective-permute-done((bf16[256,2048]{1,0:T(8,128)(2,1)S(1)}, bf16[256,2048]{1,0:T(8,128)(2,1)S(1)}, u32[]{:S(2)}, u32[]{:S(2)}) %collective-permute-start.25) | collective-permute-done | bytes 1048608 | tf_op jit(solution)/shard_map/ppermute | solution.py:350
  454.5 14.2 %attend_backward.2.q_ref.refs_7_ = bf16[1024,768]{1,0:T(8,128)(2,1)} custom-call(bf16[1024,2048]{1,0:T(8,128)(2,1)} %bitcast.50.refs_0_.g_ref, bf16[2048,1024]{1,0:T(8,128)(2,1)} %place_blocks.4.refs_1_.refs_8_, bf16[1024,768]{1,0:T(8,128)(2,1)} %get-tuple-element.88.refs_2_, f32[1024,2]{1,0:T(8,128)} %get-tuple-element.89.refs_3_, ...), custom_call_target="tpu_custom_call" | custom-call | flops 2415919104 | bytes 12582912 | tf_op jit(solution)/shard_map/attend_backward/pallas_call | solution.py:261
  484.8 23.1 %attend_backward.3 = (bf16[1024,768]{1,0:T(8,128)(2,1)}, bf16[1024,2048]{1,0:T(8,128)(2,1)}) custom-call(bf16[1024,2048]{1,0:T(8,128)(2,1)} %bitcast.50.refs_0_.g_ref, bf16[2048,1024]{1,0:T(8,128)(2,1)} %copy-done.7, bf16[1024,768]{1,0:T(8,128)(2,1)} %get-tuple-element.67.refs_2_, f32[1024,2]{1,0:T(8,128)} %get-tuple-element.96.refs_3_, ...), custom_call_target="tpu_custom_call" | custom-call | flops 8858370048 | bytes 12582912 | tf_op jit(solution)/shard_map/attend_backward/pallas_call | solution.py:261
  515.1 11.3 %collective-permute-done.40.refs_3_ = bf16[256,2048]{1,0:T(8,128)(2,1)S(1)} collective-permute-done((bf16[256,2048]{1,0:T(8,128)(2,1)}, bf16[256,2048]{1,0:T(8,128)(2,1)S(1)}, u32[]{:S(2)}, u32[]{:S(2)}) %collective-permute-start.40) | collective-permute-done | bytes 1048608 | tf_op jit(solution)/shard_map/ppermute | solution.py:350
  538.5 10.4 %collective-permute-done.53 = bf16[2,256,1024]{2,1,0:T(8,128)(2,1)} collective-permute-done((bf16[2,256,1024]{2,1,0:T(8,128)(2,1)}, bf16[2,256,1024]{2,1,0:T(8,128)(2,1)}, u32[]{:S(2)}, u32[]{:S(2)}) %collective-permute-start.53) | collective-permute-done | bytes 1048608 | tf_op jit(solution)/shard_map/ppermute | solution.py:370
  555.5 10.1 %collective-permute-done.54 = bf16[256,1024]{1,0:T(8,128)(2,1)S(1)} collective-permute-done((bf16[256,1024]{1,0:T(8,128)(2,1)S(1)}, bf16[256,1024]{1,0:T(8,128)(2,1)S(1)}, u32[]{:S(2)}, u32[]{:S(2)}) %collective-permute-start.54) | collective-permute-done | bytes 524320 | tf_op jit(solution)/shard_map/ppermute | solution.py:370
  595.9 11.8 %collective-permute-done.33 = bf16[256,2048]{1,0:T(8,128)(2,1)S(1)} collective-permute-done((bf16[256,2048]{1,0:T(8,128)(2,1)S(1)}, bf16[256,2048]{1,0:T(8,128)(2,1)S(1)}, u32[]{:S(2)}, u32[]{:S(2)}) %collective-permute-start.33) | collective-permute-done | bytes 1048608 | tf_op jit(solution)/shard_map/ppermute | solution.py:370
  635.1 12.3 %collective-permute-done.37 = f32[160,128]{1,0:T(8,128)S(1)} collective-permute-done((f32[160,128]{1,0:T(8,128)S(1)}, f32[160,128]{1,0:T(8,128)S(1)}, u32[]{:S(2)}, u32[]{:S(2)}) %collective-permute-start.37) | collective-permute-done | bytes 81952 | tf_op jit(solution)/shard_map/ppermute | solution.py:401
  (307 shorter events, 268.0 us)
Async XLA Ops:
  7.2 192.9 %all-gather.3.cloned.1.call-start = ((), (), s32[]{:S(2)}) async-start(), calls=%async_computation.2 | async-start | bytes 9437184 | tf_op jit(solution)/shard_map/all_gather | solution.py:450
  17.7 29.8 %collective-permute-start.1 = (bf16[256,2048]{1,0:T(8,128)(2,1)}, bf16[256,2048]{1,0:T(8,128)(2,1)}, u32[]{:S(2)}, u32[]{:S(2)}) collective-permute-start(bf16[256,2048]{1,0:T(8,128)(2,1)} %get-tuple-element.142), channel_id=1, source_target_pairs={{0,1},{1,0},{2,3},{3,2},{4,5},{5,4},{6,7},{7,6},{8,9},{9,8},{10,11... | collective-permute-start | bytes 3145736 | tf_op jit(solution)/shard_map/ppermute | solution.py:350
  42.2 38.3 %collective-permute-start.3 = (bf16[256,1024]{1,0:T(8,128)(2,1)}, bf16[256,1024]{1,0:T(8,128)(2,1)S(1)}, u32[]{:S(2)}, u32[]{:S(2)}) collective-permute-start(bf16[256,1024]{1,0:T(8,128)(2,1)} %get-tuple-element.145), channel_id=1, source_target_pairs={{0,4},{1,5},{2,6},{3,7},{4,0},{5,1},{6,2},{7,3},{8,12},{9,13},{10,... | collective-permute-start | bytes 1572872 | tf_op jit(solution)/shard_map/ppermute | solution.py:445
  45.0 46.5 %collective-permute-start.4 = (bf16[256,1024]{1,0:T(8,128)(2,1)}, bf16[256,1024]{1,0:T(8,128)(2,1)S(1)}, u32[]{:S(2)}, u32[]{:S(2)}) collective-permute-start(bf16[256,1024]{1,0:T(8,128)(2,1)} %get-tuple-element.144), channel_id=1, source_target_pairs={{0,4},{1,5},{2,6},{3,7},{4,0},{5,1},{6,2},{7,3},{8,12},{9,13},{10,... | collective-permute-start | bytes 1572872 | tf_op jit(solution)/shard_map/ppermute | solution.py:445
  91.5 194.8 %all-gather.5.cloned.1.call-start = ((), (), s32[]{:S(2)}) async-start(), calls=%async_computation.3 | async-start | bytes 9437184 | tf_op jit(solution)/shard_map/all_gather | solution.py:471
  203.4 202.8 %reduce-scatter.3.cloned.1.call-start = ((), (), s32[]{:S(2)}) async-start(), calls=%async_computation.4 | async-start | bytes 9437184 | tf_op jit(solution)/shard_map/reduce_scatter | solution.py:484
  317.7 347.4 %reduce-scatter.5.cloned.1.call-start = ((), (), s32[]{:S(2)}) async-start(), calls=%async_computation.5 | async-start | bytes 9437184 | tf_op jit(solution)/shard_map/reduce_scatter | solution.py:499
  334.0 48.1 %collective-permute-start.21 = (bf16[2,512,1024]{2,1,0:T(8,128)(2,1)}, bf16[2,512,1024]{2,1,0:T(8,128)(2,1)}, u32[]{:S(2)}, u32[]{:S(2)}) collective-permute-start(bf16[2,512,1024]{2,1,0:T(8,128)(2,1)} %dynamic-slice_bitcast_fusion.1), channel_id=1, source_target_pairs={{0,16},{8,24},{16,0},{24,8},{1,17},{9,25},{17,1},{25,9},{2,18},{10... | collective-permute-start | bytes 6291464 | tf_op jit(solution)/shard_map/ppermute | solution.py:370
  350.9 48.4 %collective-permute-start.20 = (bf16[2,256,2048]{2,1,0:T(8,128)(2,1)}, bf16[2,256,2048]{2,1,0:T(8,128)(2,1)}, u32[]{:S(2)}, u32[]{:S(2)}) collective-permute-start(bf16[2,256,2048]{2,1,0:T(8,128)(2,1)} %dynamic-slice_bitcast_fusion.2), channel_id=1, source_target_pairs={{0,8},{8,0},{16,24},{24,16},{1,9},{9,1},{17,25},{25,17},{2,10},{10... | collective-permute-start | bytes 6291464 | tf_op jit(solution)/shard_map/ppermute | solution.py:370
  449.5 28.2 %collective-permute-start.30 = (bf16[256,2048]{1,0:T(8,128)(2,1)}, bf16[256,2048]{1,0:T(8,128)(2,1)}, u32[]{:S(2)}, u32[]{:S(2)}) collective-permute-start(bf16[256,2048]{1,0:T(8,128)(2,1)} %fusion.27.refs_0_), channel_id=1, source_target_pairs={{0,8},{8,0},{16,24},{24,16},{1,9},{9,1},{17,25},{25,17},{2,10},{10... | collective-permute-start | bytes 3145736 | tf_op jit(solution)/shard_map/ppermute | solution.py:350
  451.0 26.7 %collective-permute-start.31 = (bf16[512,1024]{1,0:T(8,128)(2,1)}, bf16[512,1024]{1,0:T(8,128)(2,1)}, u32[]{:S(2)}, u32[]{:S(2)}) collective-permute-start(bf16[512,1024]{1,0:T(8,128)(2,1)} %fusion.26.refs_0_), channel_id=1, source_target_pairs={{0,16},{8,24},{16,0},{24,8},{1,17},{9,25},{17,1},{25,9},{2,18},{10... | collective-permute-start | bytes 3145736 | tf_op jit(solution)/shard_map/ppermute | solution.py:350
  477.7 33.4 %collective-permute-start.39 = (bf16[256,2048]{1,0:T(8,128)(2,1)S(1)}, bf16[256,2048]{1,0:T(8,128)(2,1)S(1)}, u32[]{:S(2)}, u32[]{:S(2)}) collective-permute-start(bf16[256,2048]{1,0:T(8,128)(2,1)S(1)} %copy-done.8), channel_id=1, source_target_pairs={{0,16},{8,24},{16,0},{24,8},{1,17},{9,25},{17,1},{25,9},{2,18},{10... | collective-permute-start | bytes 3145736 | tf_op jit(solution)/shard_map/ppermute | solution.py:350
  478.5 47.8 %collective-permute-start.40 = (bf16[256,2048]{1,0:T(8,128)(2,1)}, bf16[256,2048]{1,0:T(8,128)(2,1)S(1)}, u32[]{:S(2)}, u32[]{:S(2)}) collective-permute-start(bf16[256,2048]{1,0:T(8,128)(2,1)} %collective-permute-done.30.refs_1_), channel_id=1, source_target_pairs={{0,16},{8,24},{16,0},{24,8},{1,17},{9,25},{17,1},{25,9},{2,18},{10... | collective-permute-start | bytes 3145736 | tf_op jit(solution)/shard_map/ppermute | solution.py:350
  479.8 47.2 %collective-permute-start.41 = (bf16[512,1024]{1,0:T(8,128)(2,1)S(1)}, bf16[512,1024]{1,0:T(8,128)(2,1)}, u32[]{:S(2)}, u32[]{:S(2)}) collective-permute-start(bf16[512,1024]{1,0:T(8,128)(2,1)S(1)} %copy-done.9), channel_id=1, source_target_pairs={{0,8},{8,0},{16,24},{24,16},{1,9},{9,1},{17,25},{25,17},{2,10},{10... | collective-permute-start | bytes 3145736 | tf_op jit(solution)/shard_map/ppermute | solution.py:350
  480.5 46.5 %collective-permute-start.42 = (bf16[512,1024]{1,0:T(8,128)(2,1)}, bf16[512,1024]{1,0:T(8,128)(2,1)}, u32[]{:S(2)}, u32[]{:S(2)}) collective-permute-start(bf16[512,1024]{1,0:T(8,128)(2,1)} %collective-permute-done.31.refs_2_), channel_id=1, source_target_pairs={{0,8},{8,0},{16,24},{24,16},{1,9},{9,1},{17,25},{25,17},{2,10},{10... | collective-permute-start | bytes 3145736 | tf_op jit(solution)/shard_map/ppermute | solution.py:350
  484.1 64.8 %collective-permute-start.53 = (bf16[2,256,1024]{2,1,0:T(8,128)(2,1)}, bf16[2,256,1024]{2,1,0:T(8,128)(2,1)}, u32[]{:S(2)}, u32[]{:S(2)}) collective-permute-start(bf16[2,256,1024]{2,1,0:T(8,128)(2,1)} %dynamic-slice_bitcast_fusion.4), channel_id=1, source_target_pairs={{0,16},{8,24},{16,0},{24,8},{1,17},{9,25},{17,1},{25,9},{2,18},{10... | collective-permute-start | bytes 3145736 | tf_op jit(solution)/shard_map/ppermute | solution.py:370
  512.2 55.5 %collective-permute-start.32 = (bf16[2,256,2048]{2,1,0:T(8,128)(2,1)}, bf16[2,256,2048]{2,1,0:T(8,128)(2,1)}, u32[]{:S(2)}, u32[]{:S(2)}) collective-permute-start(bf16[2,256,2048]{2,1,0:T(8,128)(2,1)} %dynamic-slice_bitcast_fusion), channel_id=1, source_target_pairs={{0,1},{1,0},{2,3},{3,2},{4,5},{5,4},{6,7},{7,6},{8,9},{9,8},{10,11... | collective-permute-start | bytes 6291464 | tf_op jit(solution)/shard_map/ppermute | solution.py:429
  537.7 33.7 %collective-permute-start.51 = (bf16[2,256,1024]{2,1,0:T(8,128)(2,1)S(1)}, bf16[2,256,1024]{2,1,0:T(8,128)(2,1)S(1)}, u32[]{:S(2)}, u32[]{:S(2)}) collective-permute-start(bf16[2,256,1024]{2,1,0:T(8,128)(2,1)S(1)} %dynamic-slice_bitcast_fusion.5), channel_id=1, source_target_pairs={{0,16},{8,24},{16,0},{24,8},{1,17},{9,25},{17,1},{25,9},{2,18},{10... | collective-permute-start | bytes 3145736 | tf_op jit(solution)/shard_map/ppermute | solution.py:370
  551.5 36.2 %collective-permute-start.43 = (bf16[2,256,1024]{2,1,0:T(8,128)(2,1)S(1)}, bf16[2,256,1024]{2,1,0:T(8,128)(2,1)S(1)}, u32[]{:S(2)}, u32[]{:S(2)}) collective-permute-start(bf16[2,256,1024]{2,1,0:T(8,128)(2,1)S(1)} %dynamic-slice_bitcast_fusion.7), channel_id=1, source_target_pairs={{0,8},{8,0},{16,24},{24,16},{1,9},{9,1},{17,25},{25,17},{2,10},{10... | collective-permute-start | bytes 3145736 | tf_op jit(solution)/shard_map/ppermute | solution.py:370
  570.3 37.4 %collective-permute-start.33 = (bf16[256,2048]{1,0:T(8,128)(2,1)S(1)}, bf16[256,2048]{1,0:T(8,128)(2,1)S(1)}, u32[]{:S(2)}, u32[]{:S(2)}) collective-permute-start(bf16[256,2048]{1,0:T(8,128)(2,1)S(1)} %fusion.35), channel_id=1, source_target_pairs={{0,2},{1,3},{2,0},{3,1},{4,6},{5,7},{6,4},{7,5},{8,10},{9,11},{10,... | collective-permute-start | bytes 3145736 | tf_op jit(solution)/shard_map/ppermute | solution.py:370
  580.2 29.8 %collective-permute-start.47 = (bf16[256,1024]{1,0:T(8,128)(2,1)S(1)}, bf16[256,1024]{1,0:T(8,128)(2,1)S(1)}, u32[]{:S(2)}, u32[]{:S(2)}) collective-permute-start(bf16[256,1024]{1,0:T(8,128)(2,1)S(1)} %fusion.39), channel_id=1, source_target_pairs={{0,4},{1,5},{2,6},{3,7},{4,0},{5,1},{6,2},{7,3},{8,12},{9,13},{10,... | collective-permute-start | bytes 1572872 | tf_op jit(solution)/shard_map/ppermute | solution.py:532
  594.4 38.3 %collective-permute-start.57 = (bf16[256,1024]{1,0:T(8,128)(2,1)}, bf16[256,1024]{1,0:T(8,128)(2,1)}, u32[]{:S(2)}, u32[]{:S(2)}) collective-permute-start(bf16[256,1024]{1,0:T(8,128)(2,1)} %fusion.38.refs_4_), channel_id=1, source_target_pairs={{0,16},{8,24},{16,0},{24,8},{1,17},{9,25},{17,1},{25,9},{2,18},{10... | collective-permute-start | bytes 1572872 | tf_op jit(solution)/shard_map/ppermute | solution.py:350
  630.6 28.5 %collective-permute-start.56 = (bf16[256,1024]{1,0:T(8,128)(2,1)}, bf16[256,1024]{1,0:T(8,128)(2,1)}, u32[]{:S(2)}, u32[]{:S(2)}) collective-permute-start(bf16[256,1024]{1,0:T(8,128)(2,1)} %fusion.38.refs_4_), channel_id=1, source_target_pairs={{0,8},{8,0},{16,24},{24,16},{1,9},{9,1},{17,25},{25,17},{2,10},{10... | collective-permute-start | bytes 1572872 | tf_op jit(solution)/shard_map/ppermute | solution.py:350
  630.9 28.2 %collective-permute-start.49 = (bf16[256,1024]{1,0:T(8,128)(2,1)}, bf16[256,1024]{1,0:T(8,128)(2,1)}, u32[]{:S(2)}, u32[]{:S(2)}) collective-permute-start(bf16[256,1024]{1,0:T(8,128)(2,1)} %fusion.41.refs_0_), channel_id=1, source_target_pairs={{0,16},{8,24},{16,0},{24,8},{1,17},{9,25},{17,1},{25,9},{2,18},{10... | collective-permute-start | bytes 1572872 | tf_op jit(solution)/shard_map/ppermute | solution.py:350
  (76 other events, 1189.2 us)
Sparse Core Ops, SparseCore 0:
  91.6 83.2 all-gather.2
  203.6 82.6 all-gather.4
  317.8 88.4 reduce-scatter.2
  446.8 89.3 reduce-scatter.4

commit v4 on v3

--- a/solution.py
+++ b/solution.py
@@ -99,6 +99,13 @@
     row = lax.broadcasted_iota(jnp.int32, scores.shape, 0) + start
     col = lax.broadcasted_iota(jnp.int32, scores.shape, 1)
     return jnp.where(col <= row, scores, NEG_LARGE)
+
+
+def store_share(refs, start, value):
+    rows, parts = refs[0].shape[2], len(refs)
+    for at in range(0, value.shape[0], rows):
+        device, part = divmod((start + at) // rows, parts)
+        refs[part][device % 2, device // 2] = value[at : at + rows]
 
 
 def forward_kernel(earlier, *refs):
@@ -134,7 +141,7 @@
             share = product(heads_ref[here, :], w_ref[:, 3 * width :], (1, 1))
             for k in range(earlier):
                 share = share + product(others[2 * k][here, :], others[2 * k + 1][:, 3 * width :], (1, 1))
-            share_ref[0][here, :] = narrow(share)
+            store_share(share_ref, start, narrow(share))
 
 
 def backward_kernel(earlier, *refs):
@@ -182,7 +189,7 @@
             share = product(out_ref[here, :], w_ref[:, : 3 * width], (1, 1))
             for k in range(earlier):
                 share = share + product(others[2 * k][here, :], others[2 * k + 1][:, : 3 * width], (1, 1))
-            outs[1][here, :] = narrow(share)
+            store_share(outs[1:], start, narrow(share))
 
 
 def weight_kernel(x_ref, q_ref, g_ref, h_ref, *outs):
@@ -225,7 +232,7 @@
     return [pl.BlockSpec(memory_space=pltpu.VMEM)] * count
 
 
-def attend_forward(x, w, cos, sin, mask, earlier, last):
+def attend_forward(x, w, cos, sin, mask, earlier, share):
     tokens, heads = mask.shape
     dim, width = w.shape[0], heads * HD
     flops = 2 * tokens * dim * width * 3 + 2 * tokens * tokens * width
@@ -234,9 +241,9 @@
         jax.ShapeDtypeStruct((tokens, width), jnp.bfloat16),
         jax.ShapeDtypeStruct((tokens, heads), jnp.float32),
     ]
-    given = [a for pair in earlier for a in pair] if last else []
-    if last:
-        out.append(jax.ShapeDtypeStruct((tokens, dim), jnp.bfloat16))
+    given = [a for pair in earlier for a in pair] if share else []
+    if share:
+        out += [jax.ShapeDtypeStruct(share[1:], jnp.bfloat16)] * share[0]
         flops += 2 * tokens * dim * width * (1 + len(earlier))
     return pl.pallas_call(
         functools.partial(forward_kernel, len(given) // 2),
@@ -249,14 +256,14 @@
     )(x, w, cos, sin, mask, *given)
 
 
-def attend_backward(g, w, qkv, log_total, cos, sin, mask, earlier, last):
+def attend_backward(g, w, qkv, log_total, cos, sin, mask, earlier, share):
     tokens, heads = mask.shape
     dim, width = w.shape[0], heads * HD
     flops = 2 * tokens * dim * width + 5 * tokens * tokens * width
     out = [jax.ShapeDtypeStruct((tokens, 3 * width), jnp.bfloat16)]
-    given = [a for pair in earlier for a in pair] if last else []
-    if last:
-        out.append(jax.ShapeDtypeStruct((tokens, dim), jnp.bfloat16))
+    given = [a for pair in earlier for a in pair] if share else []
+    if share:
+        out += [jax.ShapeDtypeStruct(share[1:], jnp.bfloat16)] * share[0]
         flops += 6 * tokens * dim * width * (1 + len(earlier))
     return pl.pallas_call(
         functools.partial(backward_kernel, len(given) // 2),
@@ -373,6 +380,12 @@
     return blocks.reshape(blocks.shape[:axis] + ((2 ** len(left),) if left else ()) + tail)
 
 
+def chain_step(up, down, step, chips):
+    up_pairs = [(z * 2 + c, z * 2 + 2 + c) for z in range(step - 1, chips - 1) for c in (0, 1)]
+    down_pairs = [(z * 2 + c, z * 2 - 2 + c) for z in range(1, chips - step + 1) for c in (0, 1)]
+    return lax.ppermute(up, "mp", up_pairs), lax.ppermute(down, "mp", down_pairs)
+
+
 def lane_bits(size):
     return bits_of(size), bits_of(size)[::-1]
 
@@ -420,14 +433,13 @@
         routed_own = lax.dynamic_slice_in_dim(routed_flag, rank * rows, rows, 0)
         cos, sin = rope_tables(SEQ_LEN, HD)
 
-        def to_sequence(x):
-            held = xor_gather(x, "mp", ranks, pair_bits + [1])
-            return by_index(held, place).reshape(SEQ_LEN, -1), held
-
-        def from_sequence(x):
-            blocks = x.reshape(group // 2, 2, -1, x.shape[1])
-            got = lax.ppermute(narrow(pick(blocks, 1 - core, 1)), "mp", swap_pairs(ranks, 1))
-            blocks = wide(pick(blocks, core, 1)) + wide(got)
+        parts = 2
+        part_rows = rows // parts
+        chips, chip = ranks // 2, rank // 2
+
+        def from_sequence(blocks):
+            got = lax.ppermute(pick(blocks, 1 - core), "mp", swap_pairs(ranks, 1))
+            blocks = wide(pick(blocks, core)) + wide(got)
             bits = pair_bits[::-1]
             return xor_scatter(blocks, "mp", ranks, bits, [b // 2 for b in bits], place // 2, 0)
 
@@ -440,11 +452,13 @@
         ]
         input_wide = wide(layer_input)
         normed_one, scaled_one, inverse_one = norm_forward(input_wide, mixer_gain)
-        inputs_one, held_one = to_sequence(narrow(normed_one))
+        held = xor_gather(narrow(normed_one), "mp", ranks, pair_bits)
         fetched = [
             lax.ppermute(lane, "mp", shift_pairs(ranks, k * group)) for k in range(1, sequences) for lane in chunks
         ]
-        inputs_one, *fetched = lax.optimization_barrier((inputs_one, *fetched))
+        held, fetched = lax.optimization_barrier((held, fetched))
+        inputs_one = by_index(xor_gather(held, "mp", ranks, [1]), place).reshape(SEQ_LEN, -1)
+        inputs_one, fetched = lax.optimization_barrier((inputs_one, fetched))
         helds = [column_gather(fetched[2 * k - 2 : 2 * k], columns, cut=1) for k in range(1, sequences)]
         gate_one, state_one = gate_forward(normed_one, mixer_router, width_own[:, 0], routed_own[:, 0])
         grads_all = lax.all_gather(after(out_grad, *fetched), "mp", axis=0, tiled=True)
@@ -454,49 +468,124 @@
         for k in range(sequences):
             heads = ((rank + k * group) % ranks) * own_heads + jnp.arange(own_heads, dtype=jnp.int32)
             mask = (heads[None, :] * 4 < (sequence_width[:, None] + 1) * H).astype(jnp.float32)
-            last = k == sequences - 1
+            share_shape = (parts, 2, group // 2, part_rows, dim) if k == sequences - 1 else None
             if k:
                 held = column_gather(gate_lanes(helds[k - 1], kept[0][0]), columns, start=1)
                 weights += place_blocks(held, column, [(1, packed.shape[1], jnp.bfloat16, False)])
-            qkv, heads_out, log_total, *share = attend_forward(inputs_one, weights[k], cos, sin, mask, earlier, last)
+            qkv, heads_out, log_total, *share = attend_forward(inputs_one, weights[k], cos, sin, mask, earlier, share_shape)
             kept.append((qkv, heads_out, log_total, mask))
             earlier.append((heads_out, weights[k]))
-        mixer_branch = from_sequence(share[0])
-        mixer_branch, grads_all = lax.optimization_barrier((mixer_branch, grads_all))
-        top_down = product(grads_all, down_weight, (1, 1))
-
-        middle = input_wide + gate_one[:, None] * mixer_branch
-        normed_two, scaled_two, inverse_two = norm_forward(middle, hidden_gain)
-        gate_two, state_two = gate_forward(normed_two, hidden_router, width_own[:, 1], routed_own[:, 1])
-        inputs_two = lax.all_gather(narrow(normed_two), "mp", axis=0, tiled=True)
-        gates = by_index(xor_gather(gate_two.reshape(-1, 128), "mp", ranks, bits_of(ranks)), rank).reshape(-1)
-
+        mixer_branches = [from_sequence(share[j]) for j in range(parts)]
         col_ids = rank * cols_local + jnp.arange(cols_local, dtype=jnp.int32)
-        col_mask = (col_ids[None, :] * 4 < (width_choice[:, 1:2] + 1) * FF).astype(jnp.float32)
-        inputs_two, top_down = lax.optimization_barrier((inputs_two, top_down))
-        pre = product(inputs_two, up_weight, (1, 0))
-        relu_act = jax.nn.relu(pre)
-        hidden = narrow(relu_act * relu_act * col_mask)
-        pre_grad = narrow(top_down * gates[:, None] * col_mask * 2.0 * relu_act)
-        dots = jnp.sum(wide(hidden) * top_down, axis=1).reshape(-1, 128)
-        share = narrow(product(pre_grad, up_weight, (1, 1)))
-        share, hidden, pre_grad = lax.optimization_barrier((share, hidden, pre_grad))
-        normed_grad_two = wide(lax.psum_scatter(share, "mp", scatter_dimension=0, tiled=True))
-        gate_grad_two = lax.dynamic_slice_in_dim(all_sum(dots, {"mp": ranks}).reshape(-1), rank * rows, rows, 0)
-        gated = narrow(gates[:, None] * wide(grads_all))
-        lanes = [narrow(product(hidden, gated, (0, 0))), narrow(product(inputs_two, pre_grad, (0, 0)))]
+        widths = width_choice[:, 1].reshape(ranks, parts, part_rows)
+        fronts = []
+        for j in range(parts):
+            here = slice(j * part_rows, (j + 1) * part_rows)
+            if j == 0:
+                mixer_branches[j], grads_all = lax.optimization_barrier((mixer_branches[j], grads_all))
+            middle = input_wide[here] + gate_one[here, None] * mixer_branches[j]
+            normed_two, scaled_two, inverse_two = norm_forward(middle, hidden_gain)
+            gate_two, state_two = gate_forward(normed_two, hidden_router, width_own[here, 1], routed_own[here, 1])
+            high = lax.optimization_barrier(narrow(gate_two))
+            low = narrow(gate_two - wide(high))
+            tail = jnp.pad(jnp.stack([high, low]), ((0, 14), (0, dim - part_rows)))
+            block = jnp.concatenate([narrow(normed_two), tail], axis=0)
+            first = chain_step(block, block, 1, chips)
+            other = lax.ppermute(block, "mp", swap_pairs(ranks, 1))
+            if j < parts - 1:
+                mixer_branches[j + 1], other = lax.optimization_barrier((mixer_branches[j + 1], other))
+            fronts.append((middle, normed_two, scaled_two, inverse_two, gate_two, state_two, block, first, other))
+
+        starts = [f[-1] for f in fronts]
+        inputs_parts, gates_parts = [], []
+        for j in range(parts):
+            block, (up, down), other = fronts[j][-3:]
+            if j < parts - 1:
+                up, down, starts[j + 1] = lax.optimization_barrier((up, down, starts[j + 1]))
+            ups, downs = [up], [down]
+            for step in range(2, chips):
+                up, down = chain_step(up, down, step, chips)
+                ups.append(up)
+                downs.append(down)
+            inputs_two = jnp.zeros((chips, 2, part_rows, dim), jnp.bfloat16)
+            gates = jnp.zeros((chips, 2, 2, part_rows), jnp.bfloat16)
+            for k in range(chips):
+                if k:
+                    block = jnp.where(chip + k < chips, downs[k - 1], ups[chips - k - 1])
+                    other = lax.ppermute(block, "mp", swap_pairs(ranks, 1))
+                else:
+                    other = starts[j]
+                for value, side in ((block, core), (other, 1 - core)):
+                    at = ((chip + k) % chips, side, 0, 0)
+                    inputs_two = lax.dynamic_update_slice(inputs_two, value[None, None, :part_rows], at)
+                    gates = lax.dynamic_update_slice(
+                        gates, value[None, None, part_rows : part_rows + 2, :part_rows], at
+                    )
+            inputs_parts.append(inputs_two.reshape(-1, dim))
+            gates_parts.append(jnp.sum(wide(gates), axis=2).reshape(-1))
+
+        tops = [grads_all.reshape(ranks, parts, part_rows, dim)[:, j].reshape(-1, dim) for j in range(parts)]
+        top_downs = [product(top, down_weight, (1, 1)) for top in tops]
+        hiddens, pre_grads, sums, dots = [], [], [], []
+        for j in range(parts):
+            inputs_two, gates = inputs_parts[j], gates_parts[j]
+            if j:
+                inputs_two, shared = lax.optimization_barrier((inputs_two, shared))
+            else:
+                inputs_two, top_downs = lax.optimization_barrier((inputs_two, top_downs))
+            inputs_parts[j] = inputs_two
+            col_mask = (col_ids[None, :] * 4 < (widths[:, j].reshape(-1)[:, None] + 1) * FF).astype(jnp.float32)
+            pre = product(inputs_two, up_weight, (1, 0))
+            relu_act = jax.nn.relu(pre)
+            hidden = narrow(relu_act * relu_act * col_mask)
+            pre_grad = narrow(top_downs[j] * gates[:, None] * col_mask * 2.0 * relu_act)
+            dots.append(jnp.sum(wide(hidden) * top_downs[j], axis=1))
+            shared = narrow(product(pre_grad, up_weight, (1, 1)))
+            shared, hidden, pre_grad = lax.optimization_barrier((shared, hidden, pre_grad))
+            hiddens.append(hidden)
+            pre_grads.append(pre_grad)
+            sums.append(shared)
+        last_sum, hiddens, pre_grads = lax.optimization_barrier((sums[-1], hiddens, pre_grads))
+        sums = sums[:-1] + [last_sum]
+        normed_grads = []
+        for x in sums:
+            x = after(x, *normed_grads)
+            normed_grads.append(lax.psum_scatter(x, "mp", scatter_dimension=0, tiled=True))
+        dots = all_sum(jnp.concatenate(dots).reshape(-1, 128), {"mp": ranks}).reshape(parts, ranks, part_rows)
+        gate_grad_two = pick(dots, rank, 1)
+
+        lanes = [
+            narrow(sum(product(a, narrow(f[:, None] * wide(t)), (0, 0)) for a, f, t in zip(hiddens, gates_parts, tops))),
+            narrow(sum(product(a, b, (0, 0)) for a, b in zip(inputs_parts, pre_grads))),
+        ]
         lanes = [x.reshape(columns, -1, x.shape[1]) for x in lanes]
         lanes = column_scatter(lanes, columns, column, cut=1)
-        hidden_share = narrow(product(hidden, down_weight, (1, 0)))
-        normed_grad_two, hidden_share, *lanes = lax.optimization_barrier((normed_grad_two, hidden_share, *lanes))
+        hidden_share = [narrow(product(x, down_weight, (1, 0))) for x in hiddens]
+        normed_grads[-1], hidden_share, lanes = lax.optimization_barrier((normed_grads[-1], hidden_share, lanes))
         lanes = [narrow(x) for x in column_scatter(lanes, columns, column, start=1)]
 
-        router_part, router_two = gate_backward(normed_two, hidden_router, state_two, gate_grad_two)
-        middle_part, gain_two = norm_backward(normed_grad_two + router_part, scaled_two, inverse_two, hidden_gain)
-        middle_grad = wide(out_grad) + middle_part
-        grads_one, held_grads = to_sequence(narrow(gate_one[:, None] * middle_grad))
-        grads_one, hidden_share, *lanes = lax.optimization_barrier((grads_one, hidden_share, *lanes))
-        hidden_branch = wide(lax.psum_scatter(hidden_share, "mp", scatter_dimension=0, tiled=True))
+        middle_grads, gain_two, router_two = [], 0.0, 0.0
+        grads_one = jnp.zeros((group, parts, part_rows, dim), jnp.bfloat16)
+        for j in range(parts):
+            here = slice(j * part_rows, (j + 1) * part_rows)
+            _, normed_two, scaled_two, inverse_two, _, state_two = fronts[j][:6]
+            router_part, router_grad = gate_backward(normed_two, hidden_router, state_two, gate_grad_two[j])
+            middle_part, gain_grad = norm_backward(
+                wide(normed_grads[j]) + router_part, scaled_two, inverse_two, hidden_gain
+            )
+            middle_grads.append(wide(out_grad[here]) + middle_part)
+            gain_two, router_two = gain_two + gain_grad, router_two + router_grad
+            held = xor_gather(narrow(gate_one[here, None] * middle_grads[j]), "mp", ranks, pair_bits + [1])
+            for far, block in held.items():
+                grads_one = lax.dynamic_update_slice(grads_one, block[None, None], (place ^ far, j, 0, 0))
+        grads_one = grads_one.reshape(SEQ_LEN, dim)
+        middle_grad = jnp.concatenate(middle_grads)
+        middle = jnp.concatenate([f[0] for f in fronts])
+        gate_two = jnp.concatenate([f[4] for f in fronts])
+        mixer_branch = jnp.concatenate(mixer_branches)
+        grads_one, hidden_share, lanes = lax.optimization_barrier((grads_one, hidden_share, lanes))
+        hidden_branch = [lax.psum_scatter(x, "mp", scatter_dimension=0, tiled=True) for x in hidden_share]
+        hidden_branch = wide(jnp.concatenate(hidden_branch))
         layer_output = narrow(middle + gate_two[:, None] * hidden_branch)
 
         gate_grad_one = jnp.sum(middle_grad * mixer_branch, axis=1)
@@ -506,7 +595,8 @@
         for k in range(sequences)[::-1]:
             qkv, heads_out, log_total, mask = kept[k]
             qkv_grad, *share = attend_backward(
-                grads_now, weights[k], qkv, log_total, cos, sin, mask, earlier, k == 0
+                grads_now, weights[k], qkv, log_total, cos, sin, mask, earlier,
+                None if k else (1, 2, group // 2, rows, dim),
             )
             earlier.append((qkv_grad, weights[k]))
             if k == 0:
@@ -525,7 +615,11 @@
         down_sum, = place_blocks(helds[:1], column, [(1, dim, jnp.float32, False)])
         up_sum, = place_blocks(helds[1:], column, [(1, cols_local, jnp.float32, False)])
 
-        pieces = column_scatter(weight_parts[0], columns, column)
+        pieces = column_scatter(weight_parts[0], columns, column, cut=1)
+        pieces, normed_grad_one, down_sum, up_sum = lax.optimization_barrier(
+            (pieces, normed_grad_one, down_sum, up_sum)
+        )
+        pieces = column_scatter(pieces, columns, column, start=1)
         for k in range(1, sequences):
             there = [narrow(x) for x in column_scatter(weight_parts[k], columns, column)]
             back = shift_pairs(ranks, -k * group)

time: 680 us -> 749 us (1.10)
  waiting for transfers between devices: 297 us -> 316 us
  starting transfers between devices: 58.4 us -> 75.9 us
  local copies, waits for them, and re-layouts: 44 us -> 60.9 us
  other arithmetic: 57.2 us -> 72.8 us
    all_gather x1 -> x0, waiting for transfers between devices: 49.7 us -> none  [local(): inputs_two = lax.all_gather(narrow(normed_two), 'mp', axis=0, tiled=True)]
    ppermute x2 -> x23, waiting for transfers between devices: 4.23 us -> 48.8 us  [the longest x6 35.5 us: chain_step(): lax.ppermute(down, 'mp', down_pairs)]
    reduce_scatter x2 -> x4, waiting for transfers between devices: 2.47 us -> 24.5 us  [local(): lax.psum_scatter(x, 'mp', scatter_dimension=0, tiled=True)]
    ppermute x2 -> x23, starting transfers between devices: 0.07 us -> 21.5 us  [the longest x6 11.1 us: chain_step(): lax.ppermute(up, 'mp', up_pairs)]
    ppermute x8, waiting for transfers between devices: 26.6 us -> 12.8 us  [all_sum(): x = x + lax.ppermute(x, axis, swap_pairs(size, bit))]
    ppermute x31 -> x27, waiting for transfers between devices: 74.7 us -> 85.2 us  [xor_gather(): held[far ^ bit] = lax.ppermute(held[far], axis, swap_pairs(size, bit))]
    ppermute x31 -> x27, starting transfers between devices: 33.8 us -> 26.2 us  [xor_gather(): held[far ^ bit] = lax.ppermute(held[far], axis, swap_pairs(size, bit))]
    squeeze x8 -> x9, local copies, waits for them, and re-layouts: 12.7 us -> 19 us  [pick(): return lax.dynamic_index_in_dim(x, index, axis, keepdims=False)]
  transfers between devices with their start and end apart: 63 -> 82, of which waited for: 28 -> 36; matrix products, arithmetic and copies ran while one was open for 19% -> 26% of each run, Pallas kernels for 16% -> 15%
where the time goes in v4:
time: 749 us; the launch traced here: 745 us
  waiting for transfers between devices  316 us (42%)
  Pallas kernels  109 us (15%)
  matrix products  94.6 us (13%)
  starting transfers between devices  75.9 us (10%)
  other arithmetic  72.8 us (10%)
  local copies, waits for them, and re-layouts  60.9 us (8%)
  between operations  15.9 us (2%)
    ppermute x15, waiting for transfers between devices, xor_scatter(): lax.ppermute(narrow(pick(blocks, 1 - side, at)), axis_name, swap_pairs(si...  99.5 us
    ppermute x27, waiting for transfers between devices, xor_gather(): held[far ^ bit] = lax.ppermute(held[far], axis, swap_pairs(size, bit))  85.2 us
    dot_general x12, matrix products, product(): lax.dot_general(a, b, ((dims[:1], dims[1:]), ((), ())), preferred_element...  80.3 us
    ppermute x2, waiting for transfers between devices, local(): lax.ppermute(lane, 'mp', shift_pairs(ranks, k * group))  45.1 us
    pallas_call x2, Pallas kernels, attend_backward(): pl.pallas_call(functools.partial(backward_kernel, len(given) // 2), out_s...  37 us
    ppermute x6, waiting for transfers between devices, chain_step(): lax.ppermute(down, 'mp', down_pairs)  35.5 us
    pallas_call x2, Pallas kernels, attend_forward(): pl.pallas_call(functools.partial(forward_kernel, len(given) // 2), out_sh...  31.3 us
    ppermute x27, starting transfers between devices, xor_gather(): held[far ^ bit] = lax.ppermute(held[far], axis, swap_pairs(size, bit))  26.2 us
  transfers between devices with their start and end apart: 82, of which 36 were waited for; matrix products, arithmetic and copies ran while one was open for 26% of the time, Pallas kernels for 15%

profile of v4, /device:TPU:0, one launch (start us, length us, event | category | flops | bytes accessed | tf_op | source)
XLA Modules:
  0.0 745.2 jit_solution(14764005698794754891)
XLA Ops:
  25.2 24.9 %collective-permute-done.2.refs_4_ = bf16[256,1024]{1,0:T(8,128)(2,1)S(1)} collective-permute-done((bf16[256,1024]{1,0:T(8,128)(2,1)S(1)}, bf16[256,1024]{1,0:T(8,128)(2,1)S(1)}, u32[]{:S(2)}, u32[]{:S(2)}) %collective-permute-start.2) | collective-permute-done | bytes 524320 | tf_op jit(solution)/shard_map/ppermute | solution.py:457
  50.1 20.2 %collective-permute-done.1.refs_0_ = bf16[256,1024]{1,0:T(8,128)(2,1)S(1)} collective-permute-done((bf16[256,1024]{1,0:T(8,128)(2,1)S(1)}, bf16[256,1024]{1,0:T(8,128)(2,1)S(1)}, u32[]{:S(2)}, u32[]{:S(2)}) %collective-permute-start.1) | collective-permute-done | bytes 524320 | tf_op jit(solution)/shard_map/ppermute | solution.py:457
  86.8 13.6 %attend_forward.2 = (bf16[1024,768]{1,0:T(8,128)(2,1)}, bf16[1024,256]{1,0:T(8,128)(2,1)}, f32[1024,2]{1,0:T(8,128)}) custom-call(bf16[1024,2048]{1,0:T(8,128)(2,1)} %bitcast.11.refs_0_.x_ref, bf16[2048,1024]{1,0:T(8,128)(2,1)} %copy-done.11, f32[1024,128]{1,0:T(8,128)} %get-tuple-element.256.refs_2_.refs_4_, ...), custom_call_target="tpu_custom_call" | custom-call | flops 3758096384 | bytes 12582912 | tf_op jit(solution)/shard_map/attend_forward/pallas_call | solution.py:248
  107.2 8.1 %collective-permute-done.7.refs_2_ = bf16[256,1024]{1,0:T(8,128)(2,1)S(1)} collective-permute-done((bf16[256,1024]{1,0:T(8,128)(2,1)S(1)}, bf16[256,1024]{1,0:T(8,128)(2,1)S(1)}, u32[]{:S(2)}, u32[]{:S(2)}) %collective-permute-start.7) | collective-permute-done | bytes 524320 | tf_op jit(solution)/shard_map/ppermute | solution.py:357
  115.4 10.0 %collective-permute-done.8.refs_3_ = bf16[256,1024]{1,0:T(8,128)(2,1)S(1)} collective-permute-done((bf16[256,1024]{1,0:T(8,128)(2,1)S(1)}, bf16[256,1024]{1,0:T(8,128)(2,1)S(1)}, u32[]{:S(2)}, u32[]{:S(2)}) %collective-permute-start.8) | collective-permute-done | bytes 524320 | tf_op jit(solution)/shard_map/ppermute | solution.py:357
  132.7 17.7 %attend_forward.3 = (bf16[1024,768]{1,0:T(8,128)(2,1)}, bf16[1024,256]{1,0:T(8,128)(2,1)}, f32[1024,2]{1,0:T(8,128)}, bf16[2,2,128,2048]{3,2,1,0:T(8,128)(2,1)}, bf16[2,2,128,2048]{3,2,1,0:T(8,128)(2,1)}) custom-call(bf16[1024,2048]{1,0:T(8,128)(2,1)} %bitcast.11.refs_0_.x_ref, bf16[2048,1024]{1,0:T(8,128)(2,1)} %place_blocks.4.refs_1_.refs_8_, ...), custom_call_target="tpu_custom_call" | custom-call | flops 5905580032 | bytes 12582912 | tf_op jit(solution)/shard_map/attend_forward/pallas_call | solution.py:248
  165.4 9.5 %collective-permute-done.14 = bf16[128,2048]{1,0:T(8,128)(2,1)} collective-permute-done((bf16[128,2048]{1,0:T(8,128)(2,1)}, bf16[128,2048]{1,0:T(8,128)(2,1)}, u32[]{:S(2)}, u32[]{:S(2)}) %collective-permute-start.14) | collective-permute-done | bytes 524320 | tf_op jit(solution)/shard_map/ppermute | solution.py:377
  176.4 8.9 %collective-permute-done.12 = bf16[128,2048]{1,0:T(8,128)(2,1)} collective-permute-done((bf16[128,2048]{1,0:T(8,128)(2,1)S(1)}, bf16[128,2048]{1,0:T(8,128)(2,1)}, u32[]{:S(2)}, u32[]{:S(2)}) %collective-permute-start.12) | collective-permute-done | bytes 524320 | tf_op jit(solution)/shard_map/ppermute | solution.py:377
  220.8 9.3 %collective-permute-done.27 = bf16[144,2048]{1,0:T(8,128)(2,1)S(1)} collective-permute-done((bf16[144,2048]{1,0:T(8,128)(2,1)S(1)}, bf16[144,2048]{1,0:T(8,128)(2,1)S(1)}, u32[]{:S(2)}, u32[]{:S(2)}) %collective-permute-start.27) | collective-permute-done | bytes 589856 | tf_op jit(solution)/shard_map/ppermute | solution.py:386
  236.9 11.3 %collective-permute-done.22 = bf16[144,2048]{1,0:T(8,128)(2,1)S(1)} collective-permute-done((bf16[144,2048]{1,0:T(8,128)(2,1)S(1)}, bf16[144,2048]{1,0:T(8,128)(2,1)S(1)}, u32[]{:S(2)}, u32[]{:S(2)}) %collective-permute-start.22) | collective-permute-done | bytes 589856 | tf_op jit(solution)/shard_map/ppermute | solution.py:386
  251.9 9.1 %collective-permute-done.31 = bf16[144,2048]{1,0:T(8,128)(2,1)} collective-permute-done((bf16[144,2048]{1,0:T(8,128)(2,1)S(1)}, bf16[144,2048]{1,0:T(8,128)(2,1)}, u32[]{:S(2)}, u32[]{:S(2)}) %collective-permute-start.31) | collective-permute-done | bytes 589856 | tf_op jit(solution)/shard_map/ppermute | solution.py:386
  262.2 11.2 %collective-permute-done.24 = bf16[144,2048]{1,0:T(8,128)(2,1)S(1)} collective-permute-done((bf16[144,2048]{1,0:T(8,128)(2,1)S(1)}, bf16[144,2048]{1,0:T(8,128)(2,1)S(1)}, u32[]{:S(2)}, u32[]{:S(2)}) %collective-permute-start.24) | collective-permute-done | bytes 589856 | tf_op jit(solution)/shard_map/ppermute | solution.py:386
  314.2 24.5 %reduce-scatter.5.cloned.1.call-done = bf16[128,2048]{1,0:T(8,128)(2,1)} async-done(((bf16[1024,2048]{1,0:T(8,128)(2,1)}), bf16[128,2048]{1,0:T(8,128)(2,1)}) %reduce-scatter.5.cloned.1.call-update) | async-done | bytes 524304 | tf_op jit(solution)/shard_map/reduce_scatter | solution.py:553
  338.8 11.1 %fusion.8 = f32[1024,2048]{1,0:T(8,128)} fusion(bf16[1024,1024]{1,0:T(8,128)(2,1)} %get-tuple-element.127, bf16[1024,2048]{1,0:T(8,128)(2,1)} %bitcast.376, f32[1024]{0:T(1024)S(1)} %bitcast.396), kind=kOutput, calls=%fused_computation.16 | convolution fusion | flops 4301258752 | bytes 14684160 | tf_op jit(solution)/shard_map/dot_general | solution.py:94
  388.8 9.4 %convolution_convert_fusion.1 = bf16[1024,2048]{1,0:T(8,128)(2,1)} fusion(bf16[1024,1024]{1,0:T(8,128)(2,1)} %get-tuple-element.127, bf16[1024,2048]{1,0:T(8,128)(2,1)} %param.22), kind=kOutput, calls=%fused_computation.27 | convolution fusion | flops 4297064448 | bytes 10485760 | tf_op jit(solution)/shard_map/dot_general | solution.py:94
  399.0 26.7 %collective-permute-done.42 = bf16[2,512,1024]{2,1,0:T(8,128)(2,1)} collective-permute-done((bf16[2,512,1024]{2,1,0:T(8,128)(2,1)}, bf16[2,512,1024]{2,1,0:T(8,128)(2,1)}, u32[]{:S(2)}, u32[]{:S(2)}) %collective-permute-start.42) | collective-permute-done | bytes 2097184 | tf_op jit(solution)/shard_map/ppermute | solution.py:377
  449.1 9.5 %collective-permute-done.38 = bf16[128,2048]{1,0:T(8,128)(2,1)S(1)} collective-permute-done((bf16[128,2048]{1,0:T(8,128)(2,1)S(1)}, bf16[128,2048]{1,0:T(8,128)(2,1)S(1)}, u32[]{:S(2)}, u32[]{:S(2)}) %collective-permute-start.38) | collective-permute-done | bytes 524320 | tf_op jit(solution)/shard_map/ppermute | solution.py:357
  486.3 13.9 %attend_backward.2.q_ref.refs_7_ = bf16[1024,768]{1,0:T(8,128)(2,1)} custom-call(bf16[1024,2048]{1,0:T(8,128)(2,1)} %bitcast.97.refs_0_.g_ref, bf16[2048,1024]{1,0:T(8,128)(2,1)} %place_blocks.4.refs_1_.refs_8_, bf16[1024,768]{1,0:T(8,128)(2,1)} %get-tuple-element.139.refs_2_, f32[1024,2]{1,0:T(8,128)} %get-tuple-element.140.refs_3_, ...), custom_call_target="tpu_custom_call" | custom-call | flops 2415919104 | bytes 12582912 | tf_op jit(solution)/shard_map/attend_backward/pallas_call | solution.py:268
  500.2 9.1 %weight_grads.2 = (bf16[4,256,1024]{2,1,0:T(8,128)(2,1)}, bf16[4,256,1024]{2,1,0:T(8,128)(2,1)}) custom-call(bf16[1024,2048]{1,0:T(8,128)(2,1)} %bitcast.11.refs_0_.x_ref, bf16[1024,768]{1,0:T(8,128)(2,1)} %attend_backward.2.q_ref.refs_7_, bf16[1024,2048]{1,0:T(8,128)(2,1)} %bitcast.97.refs_0_.g_ref, bf16[1024,256]{1,0:T(8,128)(2,1)} %get-tuple-element.141.h_ref), custom_call_target="tpu_custom_call" | custom-call | flops 4294967296 | bytes 14680064 | tf_op jit(solution)/shard_map/weight_grads/pallas_call | solution.py:285
  516.2 23.1 %attend_backward.3 = (bf16[1024,768]{1,0:T(8,128)(2,1)}, bf16[2,2,256,2048]{3,2,1,0:T(8,128)(2,1)}) custom-call(bf16[1024,2048]{1,0:T(8,128)(2,1)} %bitcast.97.refs_0_.g_ref, bf16[2048,1024]{1,0:T(8,128)(2,1)} %copy-done.11, bf16[1024,768]{1,0:T(8,128)(2,1)} %get-tuple-element.99.refs_2_, f32[1024,2]{1,0:T(8,128)} %get-tuple-element.147.refs_3_, ...), custom_call_target="tpu_custom_call" | custom-call | flops 8858370048 | bytes 12582912 | tf_op jit(solution)/shard_map/attend_backward/pallas_call | solution.py:268
  556.9 13.6 %collective-permute-done.50.refs_2_ = bf16[256,2048]{1,0:T(8,128)(2,1)} collective-permute-done((bf16[256,2048]{1,0:T(8,128)(2,1)}, bf16[256,2048]{1,0:T(8,128)(2,1)}, u32[]{:S(2)}, u32[]{:S(2)}) %collective-permute-start.50) | collective-permute-done | bytes 1048608 | tf_op jit(solution)/shard_map/ppermute | solution.py:357
  571.3 21.3 %collective-permute-done.51.refs_3_ = bf16[256,2048]{1,0:T(8,128)(2,1)} collective-permute-done((bf16[256,2048]{1,0:T(8,128)(2,1)}, bf16[256,2048]{1,0:T(8,128)(2,1)}, u32[]{:S(2)}, u32[]{:S(2)}) %collective-permute-start.51) | collective-permute-done | bytes 1048608 | tf_op jit(solution)/shard_map/ppermute | solution.py:357
  595.1 8.8 %weight_grads.3 = (bf16[4,256,1024]{2,1,0:T(8,128)(2,1)}, bf16[4,256,1024]{2,1,0:T(8,128)(2,1)}) custom-call(bf16[1024,2048]{1,0:T(8,128)(2,1)} %bitcast.11.refs_0_.x_ref, bf16[1024,768]{1,0:T(8,128)(2,1)} %get-tuple-element.153.q_ref, bf16[1024,2048]{1,0:T(8,128)(2,1)} %bitcast.97.refs_0_.g_ref, bf16[1024,256]{1,0:T(8,128)(2,1)} %get-tuple-element.104.refs_5_.h_ref), custom_call_target="tpu_custom_call" | custom-call | flops 4294967296 | bytes 14680064 | tf_op jit(solution)/shard_map/weight_grads/pallas_call | solution.py:285
  635.0 35.2 %collective-permute-done.57 = bf16[256,2048]{1,0:T(8,128)(2,1)S(1)} collective-permute-done((bf16[256,2048]{1,0:T(8,128)(2,1)S(1)}, bf16[256,2048]{1,0:T(8,128)(2,1)S(1)}, u32[]{:S(2)}, u32[]{:S(2)}) %collective-permute-start.57) | collective-permute-done | bytes 1048608 | tf_op jit(solution)/shard_map/ppermute | solution.py:377
  (499 shorter events, 369.2 us)
Async XLA Ops:
  7.2 179.7 %all-gather.2.cloned.1.call-start = ((), (), s32[]{:S(2)}) async-start(), calls=%async_computation.4 | async-start | bytes 9437184 | tf_op jit(solution)/shard_map/all_gather | solution.py:464
  12.1 58.2 %collective-permute-start = (bf16[256,2048]{1,0:T(8,128)(2,1)S(1)}, bf16[256,2048]{1,0:T(8,128)(2,1)}, u32[]{:S(2)}, u32[]{:S(2)}) collective-permute-start(bf16[256,2048]{1,0:T(8,128)(2,1)S(1)} %multiply_convert_fusion.6), channel_id=1, source_target_pairs={{0,2},{1,3},{2,0},{3,1},{4,6},{5,7},{6,4},{7,5},{8,10},{9,11},{10,... | collective-permute-start | bytes 3145736 | tf_op jit(solution)/shard_map/ppermute | solution.py:357
  24.9 45.4 %collective-permute-start.1 = (bf16[256,1024]{1,0:T(8,128)(2,1)S(1)}, bf16[256,1024]{1,0:T(8,128)(2,1)S(1)}, u32[]{:S(2)}, u32[]{:S(2)}) collective-permute-start(bf16[256,1024]{1,0:T(8,128)(2,1)S(1)} %get-tuple-element.221), channel_id=1, source_target_pairs={{0,4},{1,5},{2,6},{3,7},{4,0},{5,1},{6,2},{7,3},{8,12},{9,13},{10,... | collective-permute-start | bytes 1572872 | tf_op jit(solution)/shard_map/ppermute | solution.py:457
  78.9 259.9 %reduce-scatter.5.cloned.1.call-start = ((), (), s32[]{:S(2)}) async-start(), calls=%async_computation.5 | async-start | bytes 4718592 | tf_op jit(solution)/shard_map/reduce_scatter | solution.py:553
  218.8 29.4 %collective-permute-start.22 = (bf16[144,2048]{1,0:T(8,128)(2,1)S(1)}, bf16[144,2048]{1,0:T(8,128)(2,1)S(1)}, u32[]{:S(2)}, u32[]{:S(2)}) collective-permute-start(bf16[144,2048]{1,0:T(8,128)(2,1)S(1)} %collective-permute-done.17), channel_id=1, source_target_pairs={{2,0},{3,1},{4,2},{5,3},{10,8},{11,9},{12,10},{13,11},{18,16},{19,... | collective-permute-start | bytes 1769480 | tf_op jit(solution)/shard_map/ppermute | solution.py:386
  250.3 43.6 %collective-permute-start.29 = (bf16[144,2048]{1,0:T(8,128)(2,1)}, bf16[144,2048]{1,0:T(8,128)(2,1)}, u32[]{:S(2)}, u32[]{:S(2)}) collective-permute-start(bf16[144,2048]{1,0:T(8,128)(2,1)} %collective-permute-done.28), channel_id=1, source_target_pairs={{4,6},{5,7},{12,14},{13,15},{20,22},{21,23},{28,30},{29,31}} | collective-permute-start | bytes 1769480 | tf_op jit(solution)/shard_map/ppermute | solution.py:386
  260.9 34.7 %collective-permute-start.33 = (bf16[144,2048]{1,0:T(8,128)(2,1)}, bf16[144,2048]{1,0:T(8,128)(2,1)}, u32[]{:S(2)}, u32[]{:S(2)}) collective-permute-start(bf16[144,2048]{1,0:T(8,128)(2,1)} %collective-permute-done.31), channel_id=1, source_target_pairs={{2,0},{3,1},{10,8},{11,9},{18,16},{19,17},{26,24},{27,25}} | collective-permute-start | bytes 1769480 | tf_op jit(solution)/shard_map/ppermute | solution.py:386
  292.0 145.3 %reduce-scatter.7.cloned.1.call-start = ((), (), s32[]{:S(2)}) async-start(), calls=%async_computation.6 | async-start | bytes 4718592 | tf_op jit(solution)/shard_map/reduce_scatter | solution.py:553
  306.8 75.2 %collective-permute-start.35 = (f32[16,128]{1,0:T(8,128)S(1)}, f32[16,128]{1,0:T(8,128)S(1)}, u32[]{:S(2)}, u32[]{:S(2)}) collective-permute-start(f32[16,128]{1,0:T(8,128)S(1)} %pad_maximum_fusion.5), channel_id=1, source_target_pairs={{0,1},{1,0},{2,3},{3,2},{4,5},{5,4},{6,7},{7,6},{8,9},{9,8},{10,11... | collective-permute-start | bytes 24584 | tf_op jit(solution)/shard_map/ppermute | solution.py:414
  338.8 397.2 %reduce-scatter.9.cloned.1.call-start = ((), (), s32[]{:S(2)}) async-start(), calls=%async_computation.7 | async-start | bytes 4718592 | tf_op jit(solution)/shard_map/reduce_scatter | solution.py:587
  361.4 69.5 %collective-permute-start.41 = (bf16[2,256,2048]{2,1,0:T(8,128)(2,1)}, bf16[2,256,2048]{2,1,0:T(8,128)(2,1)}, u32[]{:S(2)}, u32[]{:S(2)}) collective-permute-start(bf16[2,256,2048]{2,1,0:T(8,128)(2,1)} %dynamic-slice_bitcast_fusion.2), channel_id=1, source_target_pairs={{0,8},{8,0},{16,24},{24,16},{1,9},{9,1},{17,25},{25,17},{2,10},{10... | collective-permute-start | bytes 6291464 | tf_op jit(solution)/shard_map/ppermute | solution.py:377
  380.5 45.2 %collective-permute-start.42 = (bf16[2,512,1024]{2,1,0:T(8,128)(2,1)}, bf16[2,512,1024]{2,1,0:T(8,128)(2,1)}, u32[]{:S(2)}, u32[]{:S(2)}) collective-permute-start(bf16[2,512,1024]{2,1,0:T(8,128)(2,1)} %dynamic-slice_bitcast_fusion.1), channel_id=1, source_target_pairs={{0,16},{8,24},{16,0},{24,8},{1,17},{9,25},{17,1},{25,9},{2,18},{10... | collective-permute-start | bytes 6291464 | tf_op jit(solution)/shard_map/ppermute | solution.py:377
  479.9 256.0 %reduce-scatter.11.cloned.1.call-start = ((), (), s32[]{:S(2)}) async-start(), calls=%async_computation.8 | async-start | bytes 4718592 | tf_op jit(solution)/shard_map/reduce_scatter | solution.py:587
  513.9 32.4 %collective-permute-start.71 = (bf16[2,256,1024]{2,1,0:T(8,128)(2,1)}, bf16[2,256,1024]{2,1,0:T(8,128)(2,1)}, u32[]{:S(2)}, u32[]{:S(2)}) collective-permute-start(bf16[2,256,1024]{2,1,0:T(8,128)(2,1)} %dynamic-slice_bitcast_fusion.3), channel_id=1, source_target_pairs={{0,16},{8,24},{16,0},{24,8},{1,17},{9,25},{17,1},{25,9},{2,18},{10... | collective-permute-start | bytes 3145736 | tf_op jit(solution)/shard_map/ppermute | solution.py:377
  514.9 32.1 %collective-permute-start.64 = (bf16[2,256,1024]{2,1,0:T(8,128)(2,1)}, bf16[2,256,1024]{2,1,0:T(8,128)(2,1)}, u32[]{:S(2)}, u32[]{:S(2)}) collective-permute-start(bf16[2,256,1024]{2,1,0:T(8,128)(2,1)} %dynamic-slice_bitcast_fusion.4), channel_id=1, source_target_pairs={{0,8},{8,0},{16,24},{24,16},{1,9},{9,1},{17,25},{25,17},{2,10},{10... | collective-permute-start | bytes 3145736 | tf_op jit(solution)/shard_map/ppermute | solution.py:377
  542.6 79.5 %collective-permute-start.56 = (bf16[2,256,2048]{2,1,0:T(8,128)(2,1)}, bf16[2,256,2048]{2,1,0:T(8,128)(2,1)}, u32[]{:S(2)}, u32[]{:S(2)}) collective-permute-start(bf16[2,256,2048]{2,1,0:T(8,128)(2,1)} %dynamic-slice_bitcast_fusion), channel_id=1, source_target_pairs={{0,1},{1,0},{2,3},{3,2},{4,5},{5,4},{6,7},{7,6},{8,9},{9,8},{10,11... | collective-permute-start | bytes 6291464 | tf_op jit(solution)/shard_map/ppermute | solution.py:441
  545.3 47.3 %collective-permute-start.51 = (bf16[256,2048]{1,0:T(8,128)(2,1)}, bf16[256,2048]{1,0:T(8,128)(2,1)}, u32[]{:S(2)}, u32[]{:S(2)}) collective-permute-start(bf16[256,2048]{1,0:T(8,128)(2,1)} %collective-permute-done.48.refs_1_), channel_id=1, source_target_pairs={{0,16},{8,24},{16,0},{24,8},{1,17},{9,25},{17,1},{25,9},{2,18},{10... | collective-permute-start | bytes 3145736 | tf_op jit(solution)/shard_map/ppermute | solution.py:357
  546.3 47.4 %collective-permute-start.52 = (bf16[512,1024]{1,0:T(8,128)(2,1)}, bf16[512,1024]{1,0:T(8,128)(2,1)}, u32[]{:S(2)}, u32[]{:S(2)}) collective-permute-start(bf16[512,1024]{1,0:T(8,128)(2,1)} %fusion.14.refs_0_), channel_id=1, source_target_pairs={{0,8},{8,0},{16,24},{24,16},{1,9},{9,1},{17,25},{25,17},{2,10},{10... | collective-permute-start | bytes 3145736 | tf_op jit(solution)/shard_map/ppermute | solution.py:357
  547.0 48.1 %collective-permute-start.53 = (bf16[512,1024]{1,0:T(8,128)(2,1)}, bf16[512,1024]{1,0:T(8,128)(2,1)}, u32[]{:S(2)}, u32[]{:S(2)}) collective-permute-start(bf16[512,1024]{1,0:T(8,128)(2,1)} %collective-permute-done.49.refs_2_), channel_id=1, source_target_pairs={{0,8},{8,0},{16,24},{24,16},{1,9},{9,1},{17,25},{25,17},{2,10},{10... | collective-permute-start | bytes 3145736 | tf_op jit(solution)/shard_map/ppermute | solution.py:357
  570.5 56.8 %collective-permute-start.72 = (bf16[256,1024]{1,0:T(8,128)(2,1)}, bf16[256,1024]{1,0:T(8,128)(2,1)S(1)}, u32[]{:S(2)}, u32[]{:S(2)}) collective-permute-start(bf16[256,1024]{1,0:T(8,128)(2,1)} %fusion.51), channel_id=1, source_target_pairs={{0,8},{8,0},{16,24},{24,16},{1,9},{9,1},{17,25},{25,17},{2,10},{10... | collective-permute-start | bytes 1572872 | tf_op jit(solution)/shard_map/ppermute | solution.py:377
  592.6 37.1 %collective-permute-start.65 = (bf16[256,1024]{1,0:T(8,128)(2,1)}, bf16[256,1024]{1,0:T(8,128)(2,1)}, u32[]{:S(2)}, u32[]{:S(2)}) collective-permute-start(bf16[256,1024]{1,0:T(8,128)(2,1)} %fusion.49), channel_id=1, source_target_pairs={{0,16},{8,24},{16,0},{24,8},{1,17},{9,25},{17,1},{25,9},{2,18},{10... | collective-permute-start | bytes 1572872 | tf_op jit(solution)/shard_map/ppermute | solution.py:377
  625.5 44.7 %collective-permute-start.57 = (bf16[256,2048]{1,0:T(8,128)(2,1)S(1)}, bf16[256,2048]{1,0:T(8,128)(2,1)S(1)}, u32[]{:S(2)}, u32[]{:S(2)}) collective-permute-start(bf16[256,2048]{1,0:T(8,128)(2,1)S(1)} %fusion.24), channel_id=1, source_target_pairs={{0,2},{1,3},{2,0},{3,1},{4,6},{5,7},{6,4},{7,5},{8,10},{9,11},{10,... | collective-permute-start | bytes 3145736 | tf_op jit(solution)/shard_map/ppermute | solution.py:377
  627.5 46.9 %collective-permute-start.73 = (bf16[256,1024]{1,0:T(8,128)(2,1)S(1)}, bf16[256,1024]{1,0:T(8,128)(2,1)S(1)}, u32[]{:S(2)}, u32[]{:S(2)}) collective-permute-start(bf16[256,1024]{1,0:T(8,128)(2,1)S(1)} %fusion.25), channel_id=1, source_target_pairs={{0,4},{1,5},{2,6},{3,7},{4,0},{5,1},{6,2},{7,3},{8,12},{9,13},{10,... | collective-permute-start | bytes 1572872 | tf_op jit(solution)/shard_map/ppermute | solution.py:626
  630.9 53.1 %collective-permute-start.66 = (bf16[256,1024]{1,0:T(8,128)(2,1)S(1)}, bf16[256,1024]{1,0:T(8,128)(2,1)S(1)}, u32[]{:S(2)}, u32[]{:S(2)}) collective-permute-start(bf16[256,1024]{1,0:T(8,128)(2,1)S(1)} %fusion.28), channel_id=1, source_target_pairs={{0,4},{1,5},{2,6},{3,7},{4,0},{5,1},{6,2},{7,3},{8,12},{9,13},{10,... | collective-permute-start | bytes 1572872 | tf_op jit(solution)/shard_map/ppermute | solution.py:626
  (134 other events, 2083.9 us)
Sparse Core Ops, SparseCore 0:
  79.0 82.1 all-gather.1
  292.1 46.6 reduce-scatter.4
  341.1 48.3 reduce-scatter.6
  480.0 50.0 reduce-scatter.8
  532.3 48.1 reduce-scatter.10

commit v5 on v3

--- a/solution.py
+++ b/solution.py
@@ -101,10 +101,7 @@
     return jnp.where(col <= row, scores, NEG_LARGE)
 
 
-def forward_kernel(earlier, *refs):
-    x_ref, w_ref, cos_ref, sin_ref, mask_ref = refs[:5]
-    others = refs[5 : 5 + 2 * earlier]
-    qkv_ref, heads_ref, log_ref, *share_ref = refs[5 + 2 * earlier :]
+def forward_kernel(x_ref, w_ref, cos_ref, sin_ref, mask_ref, qkv_ref, heads_ref, log_ref):
     tokens, heads = x_ref.shape[0], mask_ref.shape[1]
     width = heads * HD
     block = min(Q_BLOCK, tokens)
@@ -130,18 +127,9 @@
             mix = product(narrow(shifted / total), qkv_ref[:end, value_lanes], (1, 0))
             heads_ref[here, lanes] = narrow(mix * mask_ref[here, head : head + 1])
             log_ref[here, head : head + 1] = row_max + jnp.log(total)
-        if share_ref:
-            share = product(heads_ref[here, :], w_ref[:, 3 * width :], (1, 1))
-            for k in range(earlier):
-                share = share + product(others[2 * k][here, :], others[2 * k + 1][:, 3 * width :], (1, 1))
-            share_ref[0][here, :] = narrow(share)
-
-
-def backward_kernel(earlier, *refs):
-    g_ref, w_ref, qkv_ref, log_ref, cos_ref, sin_ref, mask_ref = refs[:7]
-    others = refs[7 : 7 + 2 * earlier]
-    *outs, keys_acc, values_acc = refs[7 + 2 * earlier :]
-    out_ref = outs[0]
+
+
+def backward_kernel(g_ref, w_ref, qkv_ref, log_ref, cos_ref, sin_ref, mask_ref, out_ref, keys_acc, values_acc):
     tokens, heads = g_ref.shape[0], mask_ref.shape[1]
     width = heads * HD
     block = min(Q_BLOCK, tokens)
@@ -149,7 +137,7 @@
     for start in range(0, tokens, block):
         here, end = slice(start, start + block), start + block
         cos, sin = cos_ref[here, :], sin_ref[here, :]
-        rows = narrow(product(g_ref[here, :], w_ref[:, 3 * width :], (1, 0)))
+        rows = narrow(product(g_ref[here, :], w_ref[...], (1, 0)))
         for head in range(heads):
             at = head * HD
             lanes, key_lanes, value_lanes = (slice(at + p * width, at + p * width + HD) for p in range(3))
@@ -178,11 +166,14 @@
             at = head * HD
             value = keys_acc[here, at : at + HD]
             out_ref[here, width + at : width + at + HD] = narrow(value * cos - pltpu.roll(value, HD // 2, 1) * sin)
-        if outs[1:]:
-            share = product(out_ref[here, :], w_ref[:, : 3 * width], (1, 1))
-            for k in range(earlier):
-                share = share + product(others[2 * k][here, :], others[2 * k + 1][:, : 3 * width], (1, 1))
-            outs[1][here, :] = narrow(share)
+
+
+def share_kernel(*refs):
+    *given, out_ref = refs
+    total = product(given[0][...], given[1][...], (1, 1))
+    for a_ref, w_ref in zip(given[2::2], given[3::2]):
+        total = total + product(a_ref[...], w_ref[...], (1, 1))
+    out_ref[0, 0] = narrow(total)
 
 
 def weight_kernel(x_ref, q_ref, g_ref, h_ref, *outs):
@@ -225,49 +216,66 @@
     return [pl.BlockSpec(memory_space=pltpu.VMEM)] * count
 
 
-def attend_forward(x, w, cos, sin, mask, earlier, last):
+def attend_forward(x, w, cos, sin, mask):
     tokens, heads = mask.shape
     dim, width = w.shape[0], heads * HD
-    flops = 2 * tokens * dim * width * 3 + 2 * tokens * tokens * width
-    out = [
-        jax.ShapeDtypeStruct((tokens, 3 * width), jnp.bfloat16),
-        jax.ShapeDtypeStruct((tokens, width), jnp.bfloat16),
-        jax.ShapeDtypeStruct((tokens, heads), jnp.float32),
-    ]
-    given = [a for pair in earlier for a in pair] if last else []
-    if last:
-        out.append(jax.ShapeDtypeStruct((tokens, dim), jnp.bfloat16))
-        flops += 2 * tokens * dim * width * (1 + len(earlier))
     return pl.pallas_call(
-        functools.partial(forward_kernel, len(given) // 2),
-        out_shape=out,
-        in_specs=whole_specs(5 + len(given)),
-        out_specs=whole_specs(len(out)),
+        forward_kernel,
+        out_shape=[
+            jax.ShapeDtypeStruct((tokens, 3 * width), jnp.bfloat16),
+            jax.ShapeDtypeStruct((tokens, width), jnp.bfloat16),
+            jax.ShapeDtypeStruct((tokens, heads), jnp.float32),
+        ],
+        in_specs=whole_specs(5),
+        out_specs=whole_specs(3),
         compiler_params=pltpu.CompilerParams(vmem_limit_bytes=VMEM_LIMIT),
-        cost_estimate=pl.CostEstimate(flops=flops, bytes_accessed=12 << 20, transcendentals=tokens * tokens * heads // 2),
+        cost_estimate=pl.CostEstimate(
+            flops=6 * tokens * dim * width + 2 * tokens * tokens * width,
+            bytes_accessed=12 << 20,
+            transcendentals=tokens * tokens * heads // 2,
+        ),
         name="attend_forward",
-    )(x, w, cos, sin, mask, *given)
-
-
-def attend_backward(g, w, qkv, log_total, cos, sin, mask, earlier, last):
+    )(x, w, cos, sin, mask)
+
+
+def attend_backward(g, w, qkv, log_total, cos, sin, mask):
     tokens, heads = mask.shape
     dim, width = w.shape[0], heads * HD
-    flops = 2 * tokens * dim * width + 5 * tokens * tokens * width
-    out = [jax.ShapeDtypeStruct((tokens, 3 * width), jnp.bfloat16)]
-    given = [a for pair in earlier for a in pair] if last else []
-    if last:
-        out.append(jax.ShapeDtypeStruct((tokens, dim), jnp.bfloat16))
-        flops += 6 * tokens * dim * width * (1 + len(earlier))
     return pl.pallas_call(
-        functools.partial(backward_kernel, len(given) // 2),
-        out_shape=out,
-        in_specs=whole_specs(7 + len(given)),
-        out_specs=whole_specs(len(out)),
+        backward_kernel,
+        out_shape=jax.ShapeDtypeStruct((tokens, 3 * width), jnp.bfloat16),
+        in_specs=whole_specs(7),
+        out_specs=whole_specs(1)[0],
         scratch_shapes=[pltpu.VMEM((tokens, width), jnp.float32)] * 2,
         compiler_params=pltpu.CompilerParams(vmem_limit_bytes=VMEM_LIMIT),
-        cost_estimate=pl.CostEstimate(flops=flops, bytes_accessed=12 << 20, transcendentals=tokens * tokens * heads // 2),
+        cost_estimate=pl.CostEstimate(
+            flops=2 * tokens * dim * width + 5 * tokens * tokens * width,
+            bytes_accessed=12 << 20,
+            transcendentals=tokens * tokens * heads // 2,
+        ),
         name="attend_backward",
-    )(g, w, qkv, log_total, cos, sin, mask, *given)
+    )(g, w, qkv, log_total, cos, sin, mask)
+
+
+def share_of(pairs, rows):
+    tokens, depth = pairs[0][0].shape
+    dim = pairs[0][1].shape[0]
+    specs = [
+        pl.BlockSpec((rows, depth), lambda i: (i, 0)),
+        pl.BlockSpec((dim, depth), lambda i: (0, 0)),
+    ] * len(pairs)
+    return pl.pallas_call(
+        share_kernel,
+        grid=(tokens // rows,),
+        out_shape=jax.ShapeDtypeStruct((2, tokens // rows // 2, rows, dim), jnp.bfloat16),
+        in_specs=specs,
+        out_specs=pl.BlockSpec((1, 1, rows, dim), lambda i: (i % 2, i // 2, 0, 0)),
+        compiler_params=pltpu.CompilerParams(vmem_limit_bytes=VMEM_LIMIT),
+        cost_estimate=pl.CostEstimate(
+            flops=2 * tokens * dim * depth * len(pairs), bytes_accessed=12 << 20, transcendentals=0
+        ),
+        name="share_of",
+    )(*[x for pair in pairs for x in pair])
 
 
 def weight_grads(x, qkv_grad, g, heads_out, count):
@@ -420,48 +428,65 @@
         routed_own = lax.dynamic_slice_in_dim(routed_flag, rank * rows, rows, 0)
         cos, sin = rope_tables(SEQ_LEN, HD)
 
-        def to_sequence(x):
-            held = xor_gather(x, "mp", ranks, pair_bits + [1])
-            return by_index(held, place).reshape(SEQ_LEN, -1), held
-
-        def from_sequence(x):
-            blocks = x.reshape(group // 2, 2, -1, x.shape[1])
-            got = lax.ppermute(narrow(pick(blocks, 1 - core, 1)), "mp", swap_pairs(ranks, 1))
-            blocks = wide(pick(blocks, core, 1)) + wide(got)
+        def place_sequence(held):
+            return by_index(held, place).reshape(SEQ_LEN, -1)
+
+        def from_sequence(blocks):
+            got = lax.ppermute(pick(blocks, 1 - core), "mp", swap_pairs(ranks, 1))
+            blocks = wide(pick(blocks, core)) + wide(got)
             bits = pair_bits[::-1]
             return xor_scatter(blocks, "mp", ranks, bits, [b // 2 for b in bits], place // 2, 0)
 
         width = own_heads * HD
-        packed = jnp.concatenate([attention_weight[:, p] for p in range(3)] + [output_weight.T], axis=1)
         chunk_rows = dim // columns
-        chunks = [
-            lax.dynamic_slice_in_dim(packed, column * chunk_rows + at, chunk_rows // 2, 0)
-            for at in (0, chunk_rows // 2)
+        half_rows = chunk_rows // 2
+
+        def in_slice(w):
+            return jnp.concatenate([w[:, p] for p in range(3)], axis=1)
+
+        lanes_in = [
+            in_slice(lax.dynamic_slice_in_dim(attention_weight, column * chunk_rows + at, half_rows, 0))
+            for at in (0, half_rows)
+        ]
+        lanes_out = [
+            lax.dynamic_slice_in_dim(output_weight, column * chunk_rows + at, half_rows, 1).T
+            for at in (0, half_rows)
         ]
         input_wide = wide(layer_input)
         normed_one, scaled_one, inverse_one = norm_forward(input_wide, mixer_gain)
-        inputs_one, held_one = to_sequence(narrow(normed_one))
-        fetched = [
-            lax.ppermute(lane, "mp", shift_pairs(ranks, k * group)) for k in range(1, sequences) for lane in chunks
+        low_one = narrow(normed_one)
+        low_one, lanes_in, lanes_out = lax.optimization_barrier((low_one, lanes_in, lanes_out))
+        held = xor_gather(low_one, "mp", ranks, pair_bits)
+        fetched_in, fetched_out = [
+            [[lax.ppermute(x, "mp", shift_pairs(ranks, k * group)) for x in lanes] for k in range(1, sequences)]
+            for lanes in (lanes_in, lanes_out)
         ]
-        inputs_one, *fetched = lax.optimization_barrier((inputs_one, *fetched))
-        helds = [column_gather(fetched[2 * k - 2 : 2 * k], columns, cut=1) for k in range(1, sequences)]
-        gate_one, state_one = gate_forward(normed_one, mixer_router, width_own[:, 0], routed_own[:, 0])
-        grads_all = lax.all_gather(after(out_grad, *fetched), "mp", axis=0, tiled=True)
-
         sequence_width = lax.dynamic_slice_in_dim(width_choice[:, 0], sequence * SEQ_LEN, SEQ_LEN, 0)
-        weights, kept, earlier = [packed], [], []
+        masks = []
         for k in range(sequences):
             heads = ((rank + k * group) % ranks) * own_heads + jnp.arange(own_heads, dtype=jnp.int32)
-            mask = (heads[None, :] * 4 < (sequence_width[:, None] + 1) * H).astype(jnp.float32)
-            last = k == sequences - 1
+            masks.append((heads[None, :] * 4 < (sequence_width[:, None] + 1) * H).astype(jnp.float32))
+        weights_in, weights_out = [in_slice(attention_weight)], [output_weight.T]
+        held, fetched_in, masks, weights_in, weights_out, cos, sin = lax.optimization_barrier(
+            (held, fetched_in, masks, weights_in, weights_out, cos, sin)
+        )
+        inputs_one = place_sequence(xor_gather(held, "mp", ranks, [1]))
+        grads_all = lax.all_gather(after(out_grad, *[x for lanes in fetched_in for x in lanes]), "mp", axis=0, tiled=True)
+        steps_in = [column_gather(x, columns, cut=1) for x in fetched_in]
+        inputs_one, fetched_out = lax.optimization_barrier((inputs_one, fetched_out))
+        gate_one, state_one = gate_forward(normed_one, mixer_router, width_own[:, 0], routed_own[:, 0])
+
+        kept = []
+        for k in range(sequences):
+            mask = masks[k]
             if k:
-                held = column_gather(gate_lanes(helds[k - 1], kept[0][0]), columns, start=1)
-                weights += place_blocks(held, column, [(1, packed.shape[1], jnp.bfloat16, False)])
-            qkv, heads_out, log_total, *share = attend_forward(inputs_one, weights[k], cos, sin, mask, earlier, last)
-            kept.append((qkv, heads_out, log_total, mask))
-            earlier.append((heads_out, weights[k]))
-        mixer_branch = from_sequence(share[0])
+                steps, fetched, _ = lax.optimization_barrier((steps_in[k - 1], fetched_out[k - 1], kept[0][0]))
+                held = column_gather(steps, columns, start=1)
+                held_out = column_gather(fetched, columns)
+                weights_in += place_blocks(held, column, [(1, 3 * width, jnp.bfloat16, False)])
+                weights_out += place_blocks(held_out, column, [(1, width, jnp.bfloat16, False)])
+            kept.append((*attend_forward(inputs_one, weights_in[k], cos, sin, mask), mask))
+        mixer_branch = from_sequence(share_of([(x[1], w) for x, w in zip(kept, weights_out)], rows))
         mixer_branch, grads_all = lax.optimization_barrier((mixer_branch, grads_all))
         top_down = product(grads_all, down_weight, (1, 1))
 
@@ -494,38 +519,35 @@
         router_part, router_two = gate_backward(normed_two, hidden_router, state_two, gate_grad_two)
         middle_part, gain_two = norm_backward(normed_grad_two + router_part, scaled_two, inverse_two, hidden_gain)
         middle_grad = wide(out_grad) + middle_part
-        grads_one, held_grads = to_sequence(narrow(gate_one[:, None] * middle_grad))
-        grads_one, hidden_share, *lanes = lax.optimization_barrier((grads_one, hidden_share, *lanes))
+        grads_one = place_sequence(
+            xor_gather(narrow(gate_one[:, None] * middle_grad), "mp", ranks, pair_bits + [1])
+        )
+        helds = column_gather(lanes, columns, cut=1)
+        grads_one, hidden_share, lanes = lax.optimization_barrier((grads_one, hidden_share, lanes))
         hidden_branch = wide(lax.psum_scatter(hidden_share, "mp", scatter_dimension=0, tiled=True))
         layer_output = narrow(middle + gate_two[:, None] * hidden_branch)
 
         gate_grad_one = jnp.sum(middle_grad * mixer_branch, axis=1)
-        helds = column_gather(lanes, columns, cut=1)
-        earlier, weight_parts = [], [None] * sequences
+        weight_parts, pairs = [None] * sequences, []
         grads_now = grads_one
         for k in range(sequences)[::-1]:
             qkv, heads_out, log_total, mask = kept[k]
-            qkv_grad, *share = attend_backward(
-                grads_now, weights[k], qkv, log_total, cos, sin, mask, earlier, k == 0
-            )
-            earlier.append((qkv_grad, weights[k]))
-            if k == 0:
-                helds = column_gather(helds, columns, start=1)
-                flat = [held[far] for held in helds for far in held]
-                qkv_grad, *flat = lax.optimization_barrier((qkv_grad, *flat))
-                helds = [dict(zip(held, flat[i * columns :])) for i, held in enumerate(helds)]
+            qkv_grad = attend_backward(grads_now, weights_out[k], qkv, log_total, cos, sin, mask)
+            pairs.append((qkv_grad, weights_in[k]))
             weight_parts[k] = weight_grads(inputs_one, qkv_grad, grads_one, heads_out, columns)
             if k == sequences - 1:
-                flat = [held[far] for held in helds for far in held]
-                grads_now, *rest = lax.optimization_barrier((grads_now, *weight_parts[k], *flat))
-                weight_parts[k], flat = rest[:2], rest[2:]
-                helds = [dict(zip(held, flat[i * 2 :])) for i, held in enumerate(helds)]
-        normed_grad_one = from_sequence(share[0])
-
+                grads_now, weight_parts[k], helds = lax.optimization_barrier((grads_now, weight_parts[k], helds))
+        helds = column_gather(helds, columns, start=1)
+        pieces = column_scatter(weight_parts[0], columns, column, cut=1)
+        pairs, helds, _ = lax.optimization_barrier((pairs, helds, weight_parts[0]))
+        normed_grad_one = from_sequence(share_of(pairs, rows))
         down_sum, = place_blocks(helds[:1], column, [(1, dim, jnp.float32, False)])
         up_sum, = place_blocks(helds[1:], column, [(1, cols_local, jnp.float32, False)])
 
-        pieces = column_scatter(weight_parts[0], columns, column)
+        pieces, normed_grad_one, down_sum, up_sum = lax.optimization_barrier(
+            (pieces, normed_grad_one, down_sum, up_sum)
+        )
+        pieces = column_scatter(pieces, columns, column, start=1)
         for k in range(1, sequences):
             there = [narrow(x) for x in column_scatter(weight_parts[k], columns, column)]
             back = shift_pairs(ranks, -k * group)

time: 680 us -> 710 us (1.044)
  starting transfers between devices: 58.4 us -> 80.5 us
    ppermute x2, waiting for transfers between devices: 0.01 us -> 20.9 us  [local(): lax.ppermute(t, 'mp', back)]
    ppermute x8, waiting for transfers between devices: 26.6 us -> 13.1 us  [all_sum(): x = x + lax.ppermute(x, axis, swap_pairs(size, bit))]
    ppermute x14, waiting for transfers between devices: 98.8 us -> 87.3 us  [xor_scatter(): lax.ppermute(narrow(pick(blocks, 1 - side, at)), axis_name, swap_pairs(si...]
    ppermute x14, starting transfers between devices: 15 us -> 25.1 us  [xor_scatter(): lax.ppermute(narrow(pick(blocks, 1 - side, at)), axis_name, swap_pairs(si...]
    ppermute x31 -> x37, waiting for transfers between devices: 74.7 us -> 82.9 us  [xor_gather(): held[far ^ bit] = lax.ppermute(held[far], axis, swap_pairs(size, bit))]
    ppermute x31 -> x37, starting transfers between devices: 33.8 us -> 41.2 us  [xor_gather(): held[far ^ bit] = lax.ppermute(held[far], axis, swap_pairs(size, bit))]
    add x7 -> x8, other arithmetic: 16.1 us -> 18.6 us  [xor_scatter(): blocks = wide(pick(blocks, side, at)) + wide(got)]
    pallas_call x4 -> x5, Pallas kernels: 22.5 us -> 24.5 us  [place_blocks(): pl.pallas_call(functools.partial(place_kernel, count, [o[1] for o in outs...]
  transfers between devices with their start and end apart: 63 -> 71, of which waited for: 28 -> 38; matrix products, arithmetic and copies ran while one was open for 19% -> 19% of each run, Pallas kernels for 16% -> 16%
where the time goes in v5:
time: 710 us; the launch traced here: 706 us
  waiting for transfers between devices  301 us (42%)
  Pallas kernels  112 us (16%)
  matrix products  94.1 us (13%)
  starting transfers between devices  80.5 us (11%)
  other arithmetic  58.8 us (8%)
  local copies, waits for them, and re-layouts  43.5 us (6%)
  between operations  15.2 us (2%)
    ppermute x14, waiting for transfers between devices, xor_scatter(): lax.ppermute(narrow(pick(blocks, 1 - side, at)), axis_name, swap_pairs(si...  87.3 us
    ppermute x37, waiting for transfers between devices, xor_gather(): held[far ^ bit] = lax.ppermute(held[far], axis, swap_pairs(size, bit))  82.9 us
    dot_general x6, matrix products, product(): lax.dot_general(a, b, ((dims[:1], dims[1:]), ((), ())), preferred_element...  81.1 us
    all_gather x1, waiting for transfers between devices, local(): inputs_two = lax.all_gather(narrow(normed_two), 'mp', axis=0, tiled=True)  48.5 us
    ppermute x4, waiting for transfers between devices, local(): lax.ppermute(x, 'mp', shift_pairs(ranks, k * group))  41.5 us
    ppermute x37, starting transfers between devices, xor_gather(): held[far ^ bit] = lax.ppermute(held[far], axis, swap_pairs(size, bit))  41.2 us
    pallas_call x2, Pallas kernels, attend_backward(): pl.pallas_call(backward_kernel, out_shape=jax.ShapeDtypeStruct((tokens, 3...  26.4 us
    pallas_call x2, Pallas kernels, attend_forward(): pl.pallas_call(forward_kernel, out_shape=[jax.ShapeDtypeStruct((tokens, 3...  25.3 us
  transfers between devices with their start and end apart: 71, of which 38 were waited for; matrix products, arithmetic and copies ran while one was open for 19% of the time, Pallas kernels for 16%

profile of v5, /device:TPU:0, one launch (start us, length us, event | category | flops | bytes accessed | tf_op | source)
XLA Modules:
  0.0 705.8 jit_solution(10771232791268267837)
XLA Ops:
  28.5 19.5 %collective-permute-done.1.refs_0_ = bf16[256,768]{1,0:T(8,128)(2,1)} collective-permute-done((bf16[256,768]{1,0:T(8,128)(2,1)}, bf16[256,768]{1,0:T(8,128)(2,1)}, u32[]{:S(2)}, u32[]{:S(2)}) %collective-permute-start.1) | collective-permute-done | bytes 393248 | tf_op jit(solution)/shard_map/ppermute | solution.py:461
  69.5 10.0 %collective-permute-done.6.refs_4_ = bf16[256,256]{1,0:T(8,128)(2,1)S(1)} collective-permute-done((bf16[256,256]{1,0:T(8,128)(2,1)}, bf16[256,256]{1,0:T(8,128)(2,1)S(1)}, u32[]{:S(2)}, u32[]{:S(2)}) %collective-permute-start.6) | collective-permute-done | bytes 131104 | tf_op jit(solution)/shard_map/ppermute | solution.py:461
  79.6 12.7 %attend_forward.2 = (bf16[1024,768]{1,0:T(8,128)(2,1)}, bf16[1024,256]{1,0:T(8,128)(2,1)}, f32[1024,2]{1,0:T(8,128)}) custom-call(bf16[1024,2048]{1,0:T(8,128)(2,1)} %bitcast.214, bf16[2048,768]{1,0:T(8,128)(2,1)} %pad_maximum_fusion.w_ref.refs_3_, f32[1024,128]{1,0:T(8,128)} %get-tuple-element.93.cos_ref, f32[1024,128]{1,0:T(8,128)} %get-tuple-element.94.sin_ref, ...), custom_call_target="tpu_custom_call" | custom-call | flops 3758096384 | bytes 12582912 | tf_op jit(solution)/shard_map/attend_forward/pallas_call | solution.py:222
  105.5 12.1 %collective-permute-done.15.refs_3_ = bf16[256,256]{1,0:T(8,128)(2,1)S(1)} collective-permute-done((bf16[256,256]{1,0:T(8,128)(2,1)S(1)}, bf16[256,256]{1,0:T(8,128)(2,1)S(1)}, u32[]{:S(2)}, u32[]{:S(2)}) %collective-permute-start.15) | collective-permute-done | bytes 131104 | tf_op jit(solution)/shard_map/ppermute | solution.py:358
  131.3 12.6 %attend_forward.3 = (bf16[1024,768]{1,0:T(8,128)(2,1)}, bf16[1024,256]{1,0:T(8,128)(2,1)}, f32[1024,2]{1,0:T(8,128)}) custom-call(bf16[1024,2048]{1,0:T(8,128)(2,1)} %bitcast.215, bf16[2048,768]{1,0:T(8,128)(2,1)} %place_blocks.5.w_ref.refs_1_, f32[1024,128]{1,0:T(8,128)} %get-tuple-element.93.cos_ref, f32[1024,128]{1,0:T(8,128)} %get-tuple-element.94.sin_ref, ...), custom_call_target="tpu_custom_call" | custom-call | flops 3758096384 | bytes 12582912 | tf_op jit(solution)/shard_map/attend_forward/pallas_call | solution.py:222
  161.8 9.7 %collective-permute-start.20 = (bf16[256,2048]{1,0:T(8,128)(2,1)S(1)}, bf16[256,2048]{1,0:T(8,128)(2,1)}, u32[]{:S(2)}, u32[]{:S(2)}) collective-permute-start(bf16[256,2048]{1,0:T(8,128)(2,1)S(1)} %fusion.31), channel_id=1, source_target_pairs={{0,2},{1,3},{2,0},{3,1},{4,6},{5,7},{6,4},{7,5},{8,10},{9,11},{10,... | collective-permute-start | bytes 3145736 | tf_op jit(solution)/shard_map/ppermute | solution.py:378
  174.9 20.2 %collective-permute-done.20 = bf16[256,2048]{1,0:T(8,128)(2,1)} collective-permute-done((bf16[256,2048]{1,0:T(8,128)(2,1)S(1)}, bf16[256,2048]{1,0:T(8,128)(2,1)}, u32[]{:S(2)}, u32[]{:S(2)}) %collective-permute-start.20) | collective-permute-done | bytes 1048608 | tf_op jit(solution)/shard_map/ppermute | solution.py:378
  213.2 15.6 %fusion.85 = f32[2048,1024]{1,0:T(8,128)} fusion(bf16[2048,2048]{1,0:T(8,128)(2,1)} %all-gather.3.cloned.1.call-done, bf16[1024,2048]{1,0:T(8,128)(2,1)} %param.22), kind=kOutput, calls=%fused_computation.206 | convolution fusion | flops 8589934592 | bytes 20971520 | tf_op jit(solution)/shard_map/dot_general | solution.py:94
  238.6 48.5 %all-gather.5.cloned.1.call-done = bf16[2048,2048]{1,0:T(8,128)(2,1)} async-done(((bf16[256,2048]{1,0:T(8,128)(2,1)}), bf16[2048,2048]{1,0:T(8,128)(2,1)}) %all-gather.5.cloned.1.call-update) | async-done | bytes 8388624 | tf_op jit(solution)/shard_map/all_gather | solution.py:496
  287.1 18.2 %multiply_reduce_fusion = (f32[2048]{0:T(1024)S(1)}, bf16[2048,1024]{1,0:T(8,128)(2,1)}, bf16[2048,1024]{1,0:T(8,128)(2,1)S(1)}) fusion(f32[2048,1024]{1,0:T(8,128)} %fusion.85, s32[2048]{0:T(1024)S(1)} %bitcast.259, s32[1024]{0:T(1024)S(1)} %add_multiply_fusion.1, f32[2048]{0:T(1024)S(1)} %bitcast.257, bf16[2048,2048]{1,0:T(8,128)(2,1)} %all-gather.5.cloned.1.call-done, ...), kind=kOutput, calls=%fused_computation.8 | convolution fusion | flops 8617195520 | bytes 29388800 | tf_op jit(solution)/shard_map/dot_general | solution.py:94
  307.4 10.9 %convolution_convert_fusion.1 = bf16[2048,2048]{1,0:T(8,128)(2,1)} fusion(bf16[2048,1024]{1,0:T(8,128)(2,1)S(1)} %get-tuple-element.118, bf16[2048,1024]{1,0:T(8,128)(2,1)S(1)} %copy-done.56), kind=kOutput, calls=%fused_computation.11 | convolution fusion | flops 8594128896 | bytes 16777216 | tf_op jit(solution)/shard_map/dot_general | solution.py:94
  318.4 12.9 %convolution_convert_fusion.2 = bf16[2048,1024]{1,0:T(8,128)(2,1)S(1)} fusion(bf16[2048,2048]{1,0:T(8,128)(2,1)} %all-gather.5.cloned.1.call-done, bf16[2048,1024]{1,0:T(8,128)(2,1)} %copy-done.59), kind=kOutput, calls=%fused_computation.17 | convolution fusion | flops 8592031744 | bytes 16777216 | tf_op jit(solution)/shard_map/dot_general | solution.py:94
  335.9 12.3 %fusion.6 = bf16[1024,2048]{1,0:T(8,128)(2,1)S(1)} fusion(bf16[2048,1024]{1,0:T(8,128)(2,1)S(1)} %copy-done.58, bf16[2048,2048]{1,0:T(8,128)(2,1)} %all-gather.3.cloned.1.call-done, f32[2048]{0:T(1024)S(1)} %bitcast.258), kind=kOutput, calls=%fused_computation.16 | convolution fusion | flops 8604614656 | bytes 16785408 | tf_op jit(solution)/shard_map/dot_general | solution.py:94
  353.3 11.3 %convolution_convert_fusion = bf16[2048,2048]{1,0:T(8,128)(2,1)} fusion(bf16[2048,1024]{1,0:T(8,128)(2,1)S(1)} %copy-done.58, bf16[1024,2048]{1,0:T(8,128)(2,1)S(1)} %copy-done.57), kind=kOutput, calls=%fused_computation.10 | convolution fusion | flops 8594128896 | bytes 16777216 | tf_op jit(solution)/shard_map/dot_general | solution.py:94
  367.9 14.6 %collective-permute-done.29 = bf16[2,512,1024]{2,1,0:T(8,128)(2,1)} collective-permute-done((bf16[2,512,1024]{2,1,0:T(8,128)(2,1)}, bf16[2,512,1024]{2,1,0:T(8,128)(2,1)}, u32[]{:S(2)}, u32[]{:S(2)}) %collective-permute-start.29) | collective-permute-done | bytes 2097184 | tf_op jit(solution)/shard_map/ppermute | solution.py:378
  387.7 12.0 %collective-permute-done.28 = bf16[2,256,2048]{2,1,0:T(8,128)(2,1)} collective-permute-done((bf16[2,256,2048]{2,1,0:T(8,128)(2,1)}, bf16[2,256,2048]{2,1,0:T(8,128)(2,1)}, u32[]{:S(2)}, u32[]{:S(2)}) %collective-permute-start.28) | collective-permute-done | bytes 2097184 | tf_op jit(solution)/shard_map/ppermute | solution.py:378
  420.4 19.3 %collective-permute-done.33 = bf16[256,2048]{1,0:T(8,128)(2,1)S(1)} collective-permute-done((bf16[256,2048]{1,0:T(8,128)(2,1)S(1)}, bf16[256,2048]{1,0:T(8,128)(2,1)S(1)}, u32[]{:S(2)}, u32[]{:S(2)}) %collective-permute-start.33) | collective-permute-done | bytes 1048608 | tf_op jit(solution)/shard_map/ppermute | solution.py:358
  449.4 13.4 %attend_backward.2.q_ref.refs_0_ = bf16[1024,768]{1,0:T(8,128)(2,1)} custom-call(bf16[1024,2048]{1,0:T(8,128)(2,1)} %bitcast.57.g_ref, bf16[2048,256]{1,0:T(8,128)(2,1)} %place_blocks.6.refs_3_.w_ref, bf16[1024,768]{1,0:T(8,128)(2,1)} %get-tuple-element.125.qkv_ref, f32[1024,2]{1,0:T(8,128)} %get-tuple-element.126.log_ref, ...), custom_call_target="tpu_custom_call" | custom-call | flops 2415919104 | bytes 12582912 | tf_op jit(solution)/shard_map/attend_backward/pallas_call | solution.py:244
  477.2 13.0 %attend_backward.3.q_ref.refs_2_ = bf16[1024,768]{1,0:T(8,128)(2,1)} custom-call(bf16[1024,2048]{1,0:T(8,128)(2,1)} %bitcast.57.g_ref, bf16[2048,256]{1,0:T(8,128)(2,1)} %bitcast.213, bf16[1024,768]{1,0:T(8,128)(2,1)} %get-tuple-element.102.qkv_ref, f32[1024,2]{1,0:T(8,128)} %get-tuple-element.130.log_ref, f32[1024,128]{1,0:T(8,128)} %get-tuple-element.93.cos_ref, ...), custom_call_target="tpu_custom_call" | custom-call | flops 2415919104 | bytes 12582912 | tf_op jit(solution)/shard_map/attend_backward/pallas_call | solution.py:244
  499.1 18.2 %collective-permute-done.43.refs_3_ = bf16[256,2048]{1,0:T(8,128)(2,1)} collective-permute-done((bf16[256,2048]{1,0:T(8,128)(2,1)}, bf16[256,2048]{1,0:T(8,128)(2,1)}, u32[]{:S(2)}, u32[]{:S(2)}) %collective-permute-start.43) | collective-permute-done | bytes 1048608 | tf_op jit(solution)/shard_map/ppermute | solution.py:358
  519.0 11.7 %share_of.3 = bf16[2,2,256,2048]{3,2,1,0:T(8,128)(2,1)} custom-call(bf16[1024,768]{1,0:T(8,128)(2,1)} %attend_backward.2.q_ref.refs_0_, bf16[2048,768]{1,0:T(8,128)(2,1)} %place_blocks.5.w_ref.refs_1_, bf16[1024,768]{1,0:T(8,128)(2,1)} %attend_backward.3.q_ref.refs_2_, bf16[2048,768]{1,0:T(8,128)(2,1)} %pad_maximum_fusion.w_ref.refs_3_), custom_call_target="tpu_custom_call" | custom-call | flops 6442450944 | bytes 12582912 | tf_op jit(solution)/shard_map/share_of/pallas_call | solution.py:267
  547.8 13.6 %collective-permute-done.61 = bf16[2,256,1024]{2,1,0:T(8,128)(2,1)} collective-permute-done((bf16[2,256,1024]{2,1,0:T(8,128)(2,1)}, bf16[2,256,1024]{2,1,0:T(8,128)(2,1)}, u32[]{:S(2)}, u32[]{:S(2)}) %collective-permute-start.61) | collective-permute-done | bytes 1048608 | tf_op jit(solution)/shard_map/ppermute | solution.py:378
  602.4 16.3 %collective-permute-done.47 = bf16[256,2048]{1,0:T(8,128)(2,1)S(1)} collective-permute-done((bf16[256,2048]{1,0:T(8,128)(2,1)S(1)}, bf16[256,2048]{1,0:T(8,128)(2,1)S(1)}, u32[]{:S(2)}, u32[]{:S(2)}) %collective-permute-start.47) | collective-permute-done | bytes 1048608 | tf_op jit(solution)/shard_map/ppermute | solution.py:378
  623.2 13.2 %collective-permute-done.63 = bf16[256,1024]{1,0:T(8,128)(2,1)S(1)} collective-permute-done((bf16[256,1024]{1,0:T(8,128)(2,1)S(1)}, bf16[256,1024]{1,0:T(8,128)(2,1)S(1)}, u32[]{:S(2)}, u32[]{:S(2)}) %collective-permute-start.63) | collective-permute-done | bytes 524320 | tf_op jit(solution)/shard_map/ppermute | solution.py:554
  (376 shorter events, 318.8 us)
Async XLA Ops:
  7.2 190.1 %all-gather.3.cloned.1.call-start = ((), (), s32[]{:S(2)}) async-start(), calls=%async_computation.2 | async-start | bytes 9437184 | tf_op jit(solution)/shard_map/all_gather | solution.py:474
  12.9 43.1 %collective-permute-start = (bf16[256,2048]{1,0:T(8,128)(2,1)S(1)}, bf16[256,2048]{1,0:T(8,128)(2,1)}, u32[]{:S(2)}, u32[]{:S(2)}) collective-permute-start(bf16[256,2048]{1,0:T(8,128)(2,1)S(1)} %fusion.15), channel_id=1, source_target_pairs={{0,2},{1,3},{2,0},{3,1},{4,6},{5,7},{6,4},{7,5},{8,10},{9,11},{10,... | collective-permute-start | bytes 3145736 | tf_op jit(solution)/shard_map/ppermute | solution.py:358
  15.9 32.1 %collective-permute-start.1 = (bf16[256,768]{1,0:T(8,128)(2,1)}, bf16[256,768]{1,0:T(8,128)(2,1)}, u32[]{:S(2)}, u32[]{:S(2)}) collective-permute-start(bf16[256,768]{1,0:T(8,128)(2,1)} %get-tuple-element.85), channel_id=1, source_target_pairs={{0,4},{1,5},{2,6},{3,7},{4,0},{5,1},{6,2},{7,3},{8,12},{9,13},{10,... | collective-permute-start | bytes 1179656 | tf_op jit(solution)/shard_map/ppermute | solution.py:461
  18.5 36.8 %collective-permute-start.2 = (bf16[256,768]{1,0:T(8,128)(2,1)}, bf16[256,768]{1,0:T(8,128)(2,1)}, u32[]{:S(2)}, u32[]{:S(2)}) collective-permute-start(bf16[256,768]{1,0:T(8,128)(2,1)} %get-tuple-element.86), channel_id=1, source_target_pairs={{0,4},{1,5},{2,6},{3,7},{4,0},{5,1},{6,2},{7,3},{8,12},{9,13},{10,... | collective-permute-start | bytes 1179656 | tf_op jit(solution)/shard_map/ppermute | solution.py:461
  56.0 231.1 %all-gather.5.cloned.1.call-start = ((), (), s32[]{:S(2)}) async-start(), calls=%async_computation.3 | async-start | bytes 9437184 | tf_op jit(solution)/shard_map/all_gather | solution.py:496
  59.3 33.0 %collective-permute-start.7 = (bf16[256,768]{1,0:T(8,128)(2,1)}, bf16[256,768]{1,0:T(8,128)(2,1)}, u32[]{:S(2)}, u32[]{:S(2)}) collective-permute-start(bf16[256,768]{1,0:T(8,128)(2,1)} %collective-permute-done.1.refs_0_), channel_id=1, source_target_pairs={{0,8},{8,0},{16,24},{24,16},{1,9},{9,1},{17,25},{25,17},{2,10},{10... | collective-permute-start | bytes 1179656 | tf_op jit(solution)/shard_map/ppermute | solution.py:358
  63.0 29.3 %collective-permute-start.8 = (bf16[256,768]{1,0:T(8,128)(2,1)}, bf16[256,768]{1,0:T(8,128)(2,1)S(1)}, u32[]{:S(2)}, u32[]{:S(2)}) collective-permute-start(bf16[256,768]{1,0:T(8,128)(2,1)} %collective-permute-done.2.refs_4_), channel_id=1, source_target_pairs={{0,16},{8,24},{16,0},{24,8},{1,17},{9,25},{17,1},{25,9},{2,18},{10... | collective-permute-start | bytes 1179656 | tf_op jit(solution)/shard_map/ppermute | solution.py:358
  96.4 29.8 %collective-permute-start.10 = (bf16[256,768]{1,0:T(8,128)(2,1)}, bf16[256,768]{1,0:T(8,128)(2,1)S(1)}, u32[]{:S(2)}, u32[]{:S(2)}) collective-permute-start(bf16[256,768]{1,0:T(8,128)(2,1)} %collective-permute-done.7.refs_1_), channel_id=1, source_target_pairs={{0,16},{8,24},{16,0},{24,8},{1,17},{9,25},{17,1},{25,9},{2,18},{10... | collective-permute-start | bytes 1179656 | tf_op jit(solution)/shard_map/ppermute | solution.py:358
  161.8 33.2 %collective-permute-start.20 = (bf16[256,2048]{1,0:T(8,128)(2,1)S(1)}, bf16[256,2048]{1,0:T(8,128)(2,1)}, u32[]{:S(2)}, u32[]{:S(2)}) collective-permute-start(bf16[256,2048]{1,0:T(8,128)(2,1)S(1)} %fusion.31), channel_id=1, source_target_pairs={{0,2},{1,3},{2,0},{3,1},{4,6},{5,7},{6,4},{7,5},{8,10},{9,11},{10,... | collective-permute-start | bytes 3145736 | tf_op jit(solution)/shard_map/ppermute | solution.py:378
  200.7 206.1 %reduce-scatter.3.cloned.1.call-start = ((), (), s32[]{:S(2)}) async-start(), calls=%async_computation.4 | async-start | bytes 9437184 | tf_op jit(solution)/shard_map/reduce_scatter | solution.py:509
  318.3 375.8 %reduce-scatter.5.cloned.1.call-start = ((), (), s32[]{:S(2)}) async-start(), calls=%async_computation.5 | async-start | bytes 9437184 | tf_op jit(solution)/shard_map/reduce_scatter | solution.py:527
  334.4 48.1 %collective-permute-start.29 = (bf16[2,512,1024]{2,1,0:T(8,128)(2,1)}, bf16[2,512,1024]{2,1,0:T(8,128)(2,1)}, u32[]{:S(2)}, u32[]{:S(2)}) collective-permute-start(bf16[2,512,1024]{2,1,0:T(8,128)(2,1)} %dynamic-slice_bitcast_fusion.1), channel_id=1, source_target_pairs={{0,16},{8,24},{16,0},{24,8},{1,17},{9,25},{17,1},{25,9},{2,18},{10... | collective-permute-start | bytes 6291464 | tf_op jit(solution)/shard_map/ppermute | solution.py:378
  351.2 48.4 %collective-permute-start.28 = (bf16[2,256,2048]{2,1,0:T(8,128)(2,1)}, bf16[2,256,2048]{2,1,0:T(8,128)(2,1)}, u32[]{:S(2)}, u32[]{:S(2)}) collective-permute-start(bf16[2,256,2048]{2,1,0:T(8,128)(2,1)} %dynamic-slice_bitcast_fusion.2), channel_id=1, source_target_pairs={{0,8},{8,0},{16,24},{24,16},{1,9},{9,1},{17,25},{25,17},{2,10},{10... | collective-permute-start | bytes 6291464 | tf_op jit(solution)/shard_map/ppermute | solution.py:378
  473.1 44.2 %collective-permute-start.43 = (bf16[256,2048]{1,0:T(8,128)(2,1)}, bf16[256,2048]{1,0:T(8,128)(2,1)}, u32[]{:S(2)}, u32[]{:S(2)}) collective-permute-start(bf16[256,2048]{1,0:T(8,128)(2,1)} %collective-permute-done.38.refs_1_), channel_id=1, source_target_pairs={{0,16},{8,24},{16,0},{24,8},{1,17},{9,25},{17,1},{25,9},{2,18},{10... | collective-permute-start | bytes 3145736 | tf_op jit(solution)/shard_map/ppermute | solution.py:358
  474.0 43.4 %collective-permute-start.44 = (bf16[512,1024]{1,0:T(8,128)(2,1)}, bf16[512,1024]{1,0:T(8,128)(2,1)}, u32[]{:S(2)}, u32[]{:S(2)}) collective-permute-start(bf16[512,1024]{1,0:T(8,128)(2,1)} %fusion.25.refs_0_), channel_id=1, source_target_pairs={{0,8},{8,0},{16,24},{24,16},{1,9},{9,1},{17,25},{25,17},{2,10},{10... | collective-permute-start | bytes 3145736 | tf_op jit(solution)/shard_map/ppermute | solution.py:358
  474.9 44.1 %collective-permute-start.45 = (bf16[512,1024]{1,0:T(8,128)(2,1)}, bf16[512,1024]{1,0:T(8,128)(2,1)}, u32[]{:S(2)}, u32[]{:S(2)}) collective-permute-start(bf16[512,1024]{1,0:T(8,128)(2,1)} %collective-permute-done.39.refs_2_), channel_id=1, source_target_pairs={{0,8},{8,0},{16,24},{24,16},{1,9},{9,1},{17,25},{25,17},{2,10},{10... | collective-permute-start | bytes 3145736 | tf_op jit(solution)/shard_map/ppermute | solution.py:358
  534.0 46.8 %collective-permute-start.46 = (bf16[2,256,2048]{2,1,0:T(8,128)(2,1)}, bf16[2,256,2048]{2,1,0:T(8,128)(2,1)}, u32[]{:S(2)}, u32[]{:S(2)}) collective-permute-start(bf16[2,256,2048]{2,1,0:T(8,128)(2,1)} %dynamic-slice_bitcast_fusion), channel_id=1, source_target_pairs={{0,1},{1,0},{2,3},{3,2},{4,5},{5,4},{6,7},{7,6},{8,9},{9,8},{10,11... | collective-permute-start | bytes 6291464 | tf_op jit(solution)/shard_map/ppermute | solution.py:435
  544.3 41.6 %collective-permute-start.41 = (bf16[2,256,1024]{2,1,0:T(8,128)(2,1)}, bf16[2,256,1024]{2,1,0:T(8,128)(2,1)}, u32[]{:S(2)}, u32[]{:S(2)}) collective-permute-start(bf16[2,256,1024]{2,1,0:T(8,128)(2,1)} %dynamic-slice_bitcast_fusion.6), channel_id=1, source_target_pairs={{0,16},{8,24},{16,0},{24,8},{1,17},{9,25},{17,1},{25,9},{2,18},{10... | collective-permute-start | bytes 3145736 | tf_op jit(solution)/shard_map/ppermute | solution.py:378
  546.5 41.0 %collective-permute-start.40 = (bf16[2,256,1024]{2,1,0:T(8,128)(2,1)}, bf16[2,256,1024]{2,1,0:T(8,128)(2,1)}, u32[]{:S(2)}, u32[]{:S(2)}) collective-permute-start(bf16[2,256,1024]{2,1,0:T(8,128)(2,1)} %dynamic-slice_bitcast_fusion.7), channel_id=1, source_target_pairs={{0,8},{8,0},{16,24},{24,16},{1,9},{9,1},{17,25},{25,17},{2,10},{10... | collective-permute-start | bytes 3145736 | tf_op jit(solution)/shard_map/ppermute | solution.py:378
  563.9 33.1 %collective-permute-start.62 = (bf16[256,1024]{1,0:T(8,128)(2,1)}, bf16[256,1024]{1,0:T(8,128)(2,1)S(1)}, u32[]{:S(2)}, u32[]{:S(2)}) collective-permute-start(bf16[256,1024]{1,0:T(8,128)(2,1)} %fusion.52), channel_id=1, source_target_pairs={{0,8},{8,0},{16,24},{24,16},{1,9},{9,1},{17,25},{25,17},{2,10},{10... | collective-permute-start | bytes 1572872 | tf_op jit(solution)/shard_map/ppermute | solution.py:378
  568.5 32.6 %collective-permute-start.55 = (bf16[256,1024]{1,0:T(8,128)(2,1)}, bf16[256,1024]{1,0:T(8,128)(2,1)}, u32[]{:S(2)}, u32[]{:S(2)}) collective-permute-start(bf16[256,1024]{1,0:T(8,128)(2,1)} %fusion.50), channel_id=1, source_target_pairs={{0,16},{8,24},{16,0},{24,8},{1,17},{9,25},{17,1},{25,9},{2,18},{10... | collective-permute-start | bytes 1572872 | tf_op jit(solution)/shard_map/ppermute | solution.py:378
  584.1 34.6 %collective-permute-start.47 = (bf16[256,2048]{1,0:T(8,128)(2,1)S(1)}, bf16[256,2048]{1,0:T(8,128)(2,1)S(1)}, u32[]{:S(2)}, u32[]{:S(2)}) collective-permute-start(bf16[256,2048]{1,0:T(8,128)(2,1)S(1)} %fusion.34), channel_id=1, source_target_pairs={{0,2},{1,3},{2,0},{3,1},{4,6},{5,7},{6,4},{7,5},{8,10},{9,11},{10,... | collective-permute-start | bytes 3145736 | tf_op jit(solution)/shard_map/ppermute | solution.py:378
  597.1 39.3 %collective-permute-start.63 = (bf16[256,1024]{1,0:T(8,128)(2,1)S(1)}, bf16[256,1024]{1,0:T(8,128)(2,1)S(1)}, u32[]{:S(2)}, u32[]{:S(2)}) collective-permute-start(bf16[256,1024]{1,0:T(8,128)(2,1)S(1)} %fusion.35), channel_id=1, source_target_pairs={{0,4},{1,5},{2,6},{3,7},{4,0},{5,1},{6,2},{7,3},{8,12},{9,13},{10,... | collective-permute-start | bytes 1572872 | tf_op jit(solution)/shard_map/ppermute | solution.py:554
  602.3 44.0 %collective-permute-start.56 = (bf16[256,1024]{1,0:T(8,128)(2,1)S(1)}, bf16[256,1024]{1,0:T(8,128)(2,1)S(1)}, u32[]{:S(2)}, u32[]{:S(2)}) collective-permute-start(bf16[256,1024]{1,0:T(8,128)(2,1)S(1)} %fusion.38), channel_id=1, source_target_pairs={{0,4},{1,5},{2,6},{3,7},{4,0},{5,1},{6,2},{7,3},{8,12},{9,13},{10,... | collective-permute-start | bytes 1572872 | tf_op jit(solution)/shard_map/ppermute | solution.py:554
  (107 other events, 1769.5 us)
Sparse Core Ops, SparseCore 0:
  56.2 85.1 all-gather.2
  200.8 86.2 all-gather.4
  318.4 88.3 reduce-scatter.2
  447.4 88.8 reduce-scatter.4

commit v6 on v5

--- a/solution.py
+++ b/solution.py
@@ -431,9 +431,11 @@
         def place_sequence(held):
             return by_index(held, place).reshape(SEQ_LEN, -1)
 
-        def from_sequence(blocks):
+        def core_sum(blocks):
             got = lax.ppermute(pick(blocks, 1 - core), "mp", swap_pairs(ranks, 1))
-            blocks = wide(pick(blocks, core)) + wide(got)
+            return wide(pick(blocks, core)) + wide(got)
+
+        def chip_sum(blocks):
             bits = pair_bits[::-1]
             return xor_scatter(blocks, "mp", ranks, bits, [b // 2 for b in bits], place // 2, 0)
 
@@ -473,7 +475,6 @@
         inputs_one = place_sequence(xor_gather(held, "mp", ranks, [1]))
         grads_all = lax.all_gather(after(out_grad, *[x for lanes in fetched_in for x in lanes]), "mp", axis=0, tiled=True)
         steps_in = [column_gather(x, columns, cut=1) for x in fetched_in]
-        inputs_one, fetched_out = lax.optimization_barrier((inputs_one, fetched_out))
         gate_one, state_one = gate_forward(normed_one, mixer_router, width_own[:, 0], routed_own[:, 0])
 
         kept = []
@@ -482,11 +483,13 @@
             if k:
                 steps, fetched, _ = lax.optimization_barrier((steps_in[k - 1], fetched_out[k - 1], kept[0][0]))
                 held = column_gather(steps, columns, start=1)
-                held_out = column_gather(fetched, columns)
+                held_out = column_gather(fetched, columns, cut=1)
+                held, held_out = lax.optimization_barrier((held, held_out))
+                held_out = column_gather(held_out, columns, start=1)
                 weights_in += place_blocks(held, column, [(1, 3 * width, jnp.bfloat16, False)])
                 weights_out += place_blocks(held_out, column, [(1, width, jnp.bfloat16, False)])
             kept.append((*attend_forward(inputs_one, weights_in[k], cos, sin, mask), mask))
-        mixer_branch = from_sequence(share_of([(x[1], w) for x, w in zip(kept, weights_out)], rows))
+        mixer_branch = chip_sum(core_sum(share_of([(x[1], w) for x, w in zip(kept, weights_out)], rows)))
         mixer_branch, grads_all = lax.optimization_barrier((mixer_branch, grads_all))
         top_down = product(grads_all, down_weight, (1, 1))
 
@@ -528,32 +531,40 @@
         layer_output = narrow(middle + gate_two[:, None] * hidden_branch)
 
         gate_grad_one = jnp.sum(middle_grad * mixer_branch, axis=1)
-        weight_parts, pairs = [None] * sequences, []
+        pairs, sent = [], []
         grads_now = grads_one
         for k in range(sequences)[::-1]:
             qkv, heads_out, log_total, mask = kept[k]
             qkv_grad = attend_backward(grads_now, weights_out[k], qkv, log_total, cos, sin, mask)
+            if sent:
+                qkv_grad, sent[-1] = lax.optimization_barrier((qkv_grad, sent[-1]))
             pairs.append((qkv_grad, weights_in[k]))
-            weight_parts[k] = weight_grads(inputs_one, qkv_grad, grads_one, heads_out, columns)
-            if k == sequences - 1:
-                grads_now, weight_parts[k], helds = lax.optimization_barrier((grads_now, weight_parts[k], helds))
+            part = weight_grads(inputs_one, qkv_grad, grads_one, heads_out, columns)
+            if k:
+                grads_now, part, helds = lax.optimization_barrier((grads_now, part, helds))
+                sent.append(column_scatter(part, columns, column, cut=1))
+        sent = [[narrow(x) for x in column_scatter(lanes, columns, column, start=1)] for lanes in sent]
+        pairs, sent, part = lax.optimization_barrier((pairs, sent, part))
+        there = [
+            [lax.ppermute(x, "mp", shift_pairs(ranks, -k * group)) for x in lanes]
+            for k, lanes in zip(range(1, sequences)[::-1], sent)
+        ]
+        helds, sent = lax.optimization_barrier((helds, sent))
         helds = column_gather(helds, columns, start=1)
-        pieces = column_scatter(weight_parts[0], columns, column, cut=1)
-        pairs, helds, _ = lax.optimization_barrier((pairs, helds, weight_parts[0]))
-        normed_grad_one = from_sequence(share_of(pairs, rows))
+        pieces = column_scatter(part, columns, column, cut=1)
+        blocks = core_sum(share_of(pairs, rows))
+        blocks, pieces = lax.optimization_barrier((blocks, pieces))
+        normed_grad_one = chip_sum(blocks)
+        pieces = column_scatter(pieces, columns, column, start=1)
+        for lanes in there:
+            pieces = [p + wide(t) for p, t in zip(pieces, lanes)]
+        spread = column_gather([narrow(p) for p in pieces], columns, cut=1)
+        spread, helds = lax.optimization_barrier((spread, helds))
+        spread = column_gather(spread, columns, start=1)
         down_sum, = place_blocks(helds[:1], column, [(1, dim, jnp.float32, False)])
         up_sum, = place_blocks(helds[1:], column, [(1, cols_local, jnp.float32, False)])
-
-        pieces, normed_grad_one, down_sum, up_sum = lax.optimization_barrier(
-            (pieces, normed_grad_one, down_sum, up_sum)
-        )
-        pieces = column_scatter(pieces, columns, column, start=1)
-        for k in range(1, sequences):
-            there = [narrow(x) for x in column_scatter(weight_parts[k], columns, column)]
-            back = shift_pairs(ranks, -k * group)
-            pieces = [narrow(p + wide(lax.ppermute(t, "mp", back))) for p, t in zip(pieces, there)]
         attention_sum, output_sum = place_blocks(
-            column_gather(pieces, columns),
+            spread,
             column,
             [(3, width, jnp.float32, False), (1, width, jnp.float32, True)],
         )

time: 710 us -> 724 us (1.020)
  waiting for transfers between devices: 301 us -> 316 us
    ppermute x14, waiting for transfers between devices: 87.3 us -> 117 us  [xor_scatter(): lax.ppermute(narrow(pick(blocks, 1 - side, at)), axis_name, swap_pairs(si...]
    ppermute x4, waiting for transfers between devices: 25.1 us -> 7.83 us  [the longest x2 4.23 us: core_sum(): got = lax.ppermute(pick(blocks, 1 - core), 'mp', swap_pairs(ranks, 1))]
    ppermute x4, waiting for transfers between devices: 41.5 us -> 26.8 us  [local(): lax.ppermute(x, 'mp', shift_pairs(ranks, k * group))]
    ppermute x8, waiting for transfers between devices: 13.1 us -> 23.4 us  [all_sum(): x = x + lax.ppermute(x, axis, swap_pairs(size, bit))]
    unnamed x121 -> x137, local copies, waits for them, and re-layouts: 13.3 us -> 17.6 us
    add x8 -> x7, other arithmetic: 18.6 us -> 17.3 us  [xor_scatter(): blocks = wide(pick(blocks, side, at)) + wide(got)]
  transfers between devices with their start and end apart: 71 -> 71, of which waited for: 38 -> 28; matrix products, arithmetic and copies ran while one was open for 19% -> 18% of each run, Pallas kernels for 16% -> 16%
where the time goes in v6:
time: 724 us; the launch traced here: 720 us
  waiting for transfers between devices  316 us (44%)
  Pallas kernels  113 us (16%)
  matrix products  97.8 us (14%)
  starting transfers between devices  77.4 us (11%)
  other arithmetic  54 us (7%)
  local copies, waits for them, and re-layouts  46.5 us (6%)
  between operations  15.3 us (2%)
    ppermute x14, waiting for transfers between devices, xor_scatter(): lax.ppermute(narrow(pick(blocks, 1 - side, at)), axis_name, swap_pairs(si...  117 us
    ppermute x37, waiting for transfers between devices, xor_gather(): held[far ^ bit] = lax.ppermute(held[far], axis, swap_pairs(size, bit))  88.5 us
    dot_general x6, matrix products, product(): lax.dot_general(a, b, ((dims[:1], dims[1:]), ((), ())), preferred_element...  80.9 us
    all_gather x1, waiting for transfers between devices, local(): inputs_two = lax.all_gather(narrow(normed_two), 'mp', axis=0, tiled=True)  49.6 us
    ppermute x37, starting transfers between devices, xor_gather(): held[far ^ bit] = lax.ppermute(held[far], axis, swap_pairs(size, bit))  40.5 us
    ppermute x4, waiting for transfers between devices, local(): lax.ppermute(x, 'mp', shift_pairs(ranks, k * group))  26.8 us
    pallas_call x2, Pallas kernels, attend_backward(): pl.pallas_call(backward_kernel, out_shape=jax.ShapeDtypeStruct((tokens, 3...  26.7 us
    pallas_call x2, Pallas kernels, attend_forward(): pl.pallas_call(forward_kernel, out_shape=[jax.ShapeDtypeStruct((tokens, 3...  25.4 us
  transfers between devices with their start and end apart: 71, of which 28 were waited for; matrix products, arithmetic and copies ran while one was open for 18% of the time, Pallas kernels for 16%

profile of v6, /device:TPU:0, one launch (start us, length us, event | category | flops | bytes accessed | tf_op | source)
XLA Modules:
  0.0 719.7 jit_solution(4747881747524745200)
XLA Ops:
  28.5 19.5 %collective-permute-done.1.refs_0_ = bf16[256,768]{1,0:T(8,128)(2,1)} collective-permute-done((bf16[256,768]{1,0:T(8,128)(2,1)}, bf16[256,768]{1,0:T(8,128)(2,1)}, u32[]{:S(2)}, u32[]{:S(2)}) %collective-permute-start.1) | collective-permute-done | bytes 393248 | tf_op jit(solution)/shard_map/ppermute | solution.py:463
  66.8 12.9 %attend_forward.2 = (bf16[1024,768]{1,0:T(8,128)(2,1)}, bf16[1024,256]{1,0:T(8,128)(2,1)}, f32[1024,2]{1,0:T(8,128)}) custom-call(bf16[1024,2048]{1,0:T(8,128)(2,1)} %bitcast.216, bf16[2048,768]{1,0:T(8,128)(2,1)} %pad_maximum_fusion.w_ref.refs_3_, f32[1024,128]{1,0:T(8,128)} %get-tuple-element.112.cos_ref, f32[1024,128]{1,0:T(8,128)} %get-tuple-element.113.sin_ref, ...), custom_call_target="tpu_custom_call" | custom-call | flops 3758096384 | bytes 12582912 | tf_op jit(solution)/shard_map/attend_forward/pallas_call | solution.py:222
  85.5 17.7 %collective-permute-done.13.refs_1_ = bf16[256,256]{1,0:T(8,128)(2,1)S(1)} collective-permute-done((bf16[256,256]{1,0:T(8,128)(2,1)S(1)}, bf16[256,256]{1,0:T(8,128)(2,1)S(1)}, u32[]{:S(2)}, u32[]{:S(2)}) %collective-permute-start.13) | collective-permute-done | bytes 131104 | tf_op jit(solution)/shard_map/ppermute | solution.py:358
  116.6 12.5 %attend_forward.3 = (bf16[1024,768]{1,0:T(8,128)(2,1)}, bf16[1024,256]{1,0:T(8,128)(2,1)}, f32[1024,2]{1,0:T(8,128)}) custom-call(bf16[1024,2048]{1,0:T(8,128)(2,1)} %bitcast.217, bf16[2048,768]{1,0:T(8,128)(2,1)} %place_blocks.5.w_ref.refs_1_, f32[1024,128]{1,0:T(8,128)} %get-tuple-element.112.cos_ref, f32[1024,128]{1,0:T(8,128)} %get-tuple-element.113.sin_ref, ...), custom_call_target="tpu_custom_call" | custom-call | flops 3758096384 | bytes 12582912 | tf_op jit(solution)/shard_map/attend_forward/pallas_call | solution.py:222
  161.6 20.2 %collective-permute-done.20 = bf16[256,2048]{1,0:T(8,128)(2,1)} collective-permute-done((bf16[256,2048]{1,0:T(8,128)(2,1)S(1)}, bf16[256,2048]{1,0:T(8,128)(2,1)}, u32[]{:S(2)}, u32[]{:S(2)}) %collective-permute-start.20) | collective-permute-done | bytes 1048608 | tf_op jit(solution)/shard_map/ppermute | solution.py:378
  199.3 15.4 %fusion.86 = f32[2048,1024]{1,0:T(8,128)} fusion(bf16[2048,2048]{1,0:T(8,128)(2,1)} %all-gather.3.cloned.1.call-done, bf16[1024,2048]{1,0:T(8,128)(2,1)} %param.22), kind=kOutput, calls=%fused_computation.207 | convolution fusion | flops 8589934592 | bytes 20971520 | tf_op jit(solution)/shard_map/dot_general | solution.py:94
  223.3 49.6 %all-gather.5.cloned.1.call-done = bf16[2048,2048]{1,0:T(8,128)(2,1)} async-done(((bf16[256,2048]{1,0:T(8,128)(2,1)}), bf16[2048,2048]{1,0:T(8,128)(2,1)}) %all-gather.5.cloned.1.call-update) | async-done | bytes 8388624 | tf_op jit(solution)/shard_map/all_gather | solution.py:499
  273.0 18.2 %multiply_reduce_fusion = (f32[2048]{0:T(1024)S(1)}, bf16[2048,1024]{1,0:T(8,128)(2,1)}, bf16[2048,1024]{1,0:T(8,128)(2,1)S(1)}) fusion(f32[2048,1024]{1,0:T(8,128)} %fusion.86, s32[2048]{0:T(1024)S(1)} %bitcast.258, s32[1024]{0:T(1024)S(1)} %add_multiply_fusion.1, f32[2048]{0:T(1024)S(1)} %bitcast.256, bf16[2048,2048]{1,0:T(8,128)(2,1)} %all-gather.5.cloned.1.call-done, ...), kind=kOutput, calls=%fused_computation.8 | convolution fusion | flops 8617195520 | bytes 29388800 | tf_op jit(solution)/shard_map/dot_general | solution.py:94
  293.2 10.9 %convolution_convert_fusion.1 = bf16[2048,2048]{1,0:T(8,128)(2,1)} fusion(bf16[2048,1024]{1,0:T(8,128)(2,1)S(1)} %get-tuple-element.149, bf16[2048,1024]{1,0:T(8,128)(2,1)S(1)} %copy-done.64), kind=kOutput, calls=%fused_computation.11 | convolution fusion | flops 8594128896 | bytes 16777216 | tf_op jit(solution)/shard_map/dot_general | solution.py:94
  304.2 12.9 %convolution_convert_fusion.2 = bf16[2048,1024]{1,0:T(8,128)(2,1)S(1)} fusion(bf16[2048,2048]{1,0:T(8,128)(2,1)} %all-gather.5.cloned.1.call-done, bf16[2048,1024]{1,0:T(8,128)(2,1)} %copy-done.67), kind=kOutput, calls=%fused_computation.17 | convolution fusion | flops 8592031744 | bytes 16777216 | tf_op jit(solution)/shard_map/dot_general | solution.py:94
  321.8 12.3 %fusion.6 = bf16[1024,2048]{1,0:T(8,128)(2,1)S(1)} fusion(bf16[2048,1024]{1,0:T(8,128)(2,1)S(1)} %copy-done.66, bf16[2048,2048]{1,0:T(8,128)(2,1)} %all-gather.3.cloned.1.call-done, f32[2048]{0:T(1024)S(1)} %bitcast.257), kind=kOutput, calls=%fused_computation.16 | convolution fusion | flops 8604614656 | bytes 16785408 | tf_op jit(solution)/shard_map/dot_general | solution.py:94
  339.2 11.3 %convolution_convert_fusion = bf16[2048,2048]{1,0:T(8,128)(2,1)} fusion(bf16[2048,1024]{1,0:T(8,128)(2,1)S(1)} %copy-done.66, bf16[1024,2048]{1,0:T(8,128)(2,1)S(1)} %copy-done.65), kind=kOutput, calls=%fused_computation.10 | convolution fusion | flops 8594128896 | bytes 16777216 | tf_op jit(solution)/shard_map/dot_general | solution.py:94
  353.8 14.5 %collective-permute-done.29 = bf16[2,512,1024]{2,1,0:T(8,128)(2,1)} collective-permute-done((bf16[2,512,1024]{2,1,0:T(8,128)(2,1)}, bf16[2,512,1024]{2,1,0:T(8,128)(2,1)}, u32[]{:S(2)}, u32[]{:S(2)}) %collective-permute-start.29) | collective-permute-done | bytes 2097184 | tf_op jit(solution)/shard_map/ppermute | solution.py:378
  373.5 12.1 %collective-permute-done.28 = bf16[2,256,2048]{2,1,0:T(8,128)(2,1)} collective-permute-done((bf16[2,256,2048]{2,1,0:T(8,128)(2,1)}, bf16[2,256,2048]{2,1,0:T(8,128)(2,1)}, u32[]{:S(2)}, u32[]{:S(2)}) %collective-permute-start.28) | collective-permute-done | bytes 2097184 | tf_op jit(solution)/shard_map/ppermute | solution.py:378
  406.2 19.4 %collective-permute-done.33 = bf16[256,2048]{1,0:T(8,128)(2,1)S(1)} collective-permute-done((bf16[256,2048]{1,0:T(8,128)(2,1)S(1)}, bf16[256,2048]{1,0:T(8,128)(2,1)S(1)}, u32[]{:S(2)}, u32[]{:S(2)}) %collective-permute-start.33) | collective-permute-done | bytes 1048608 | tf_op jit(solution)/shard_map/ppermute | solution.py:358
  435.3 13.5 %attend_backward.2.q_ref.refs_0_ = bf16[1024,768]{1,0:T(8,128)(2,1)} custom-call(bf16[1024,2048]{1,0:T(8,128)(2,1)} %bitcast.57.g_ref, bf16[2048,256]{1,0:T(8,128)(2,1)} %place_blocks.6.refs_3_.w_ref, bf16[1024,768]{1,0:T(8,128)(2,1)} %get-tuple-element.156.qkv_ref, f32[1024,2]{1,0:T(8,128)} %get-tuple-element.157.log_ref, ...), custom_call_target="tpu_custom_call" | custom-call | flops 2415919104 | bytes 12582912 | tf_op jit(solution)/shard_map/attend_backward/pallas_call | solution.py:244
  463.7 13.2 %attend_backward.3.q_ref.refs_2_ = bf16[1024,768]{1,0:T(8,128)(2,1)} custom-call(bf16[1024,2048]{1,0:T(8,128)(2,1)} %bitcast.57.g_ref, bf16[2048,256]{1,0:T(8,128)(2,1)} %bitcast.215, bf16[1024,768]{1,0:T(8,128)(2,1)} %get-tuple-element.121.qkv_ref, f32[1024,2]{1,0:T(8,128)} %get-tuple-element.161.log_ref, f32[1024,128]{1,0:T(8,128)} %get-tuple-element.112.cos_ref, ...), custom_call_target="tpu_custom_call" | custom-call | flops 2415919104 | bytes 12582912 | tf_op jit(solution)/shard_map/attend_backward/pallas_call | solution.py:244
  499.7 11.7 %share_of.3 = bf16[2,2,256,2048]{3,2,1,0:T(8,128)(2,1)} custom-call(bf16[1024,768]{1,0:T(8,128)(2,1)} %attend_backward.2.q_ref.refs_0_, bf16[2048,768]{1,0:T(8,128)(2,1)} %place_blocks.5.w_ref.refs_1_, bf16[1024,768]{1,0:T(8,128)(2,1)} %attend_backward.3.q_ref.refs_2_, bf16[2048,768]{1,0:T(8,128)(2,1)} %pad_maximum_fusion.w_ref.refs_3_), custom_call_target="tpu_custom_call" | custom-call | flops 6442450944 | bytes 12582912 | tf_op jit(solution)/shard_map/share_of/pallas_call | solution.py:267
  516.3 22.8 %collective-permute-done.46 = bf16[2,256,1024]{2,1,0:T(8,128)(2,1)S(1)} collective-permute-done((bf16[2,256,1024]{2,1,0:T(8,128)(2,1)S(1)}, bf16[2,256,1024]{2,1,0:T(8,128)(2,1)S(1)}, u32[]{:S(2)}, u32[]{:S(2)}) %collective-permute-start.46) | collective-permute-done | bytes 1048608 | tf_op jit(solution)/shard_map/ppermute | solution.py:378
  560.8 31.4 %collective-permute-done.47 = bf16[256,2048]{1,0:T(8,128)(2,1)} collective-permute-done((bf16[256,2048]{1,0:T(8,128)(2,1)}, bf16[256,2048]{1,0:T(8,128)(2,1)}, u32[]{:S(2)}, u32[]{:S(2)}) %collective-permute-start.47) | collective-permute-done | bytes 1048608 | tf_op jit(solution)/shard_map/ppermute | solution.py:378
  618.5 16.9 %collective-permute-done.60.refs_3_ = bf16[256,2048]{1,0:T(8,128)(2,1)S(1)} collective-permute-done((bf16[256,2048]{1,0:T(8,128)(2,1)S(1)}, bf16[256,2048]{1,0:T(8,128)(2,1)S(1)}, u32[]{:S(2)}, u32[]{:S(2)}) %collective-permute-start.60) | collective-permute-done | bytes 1048608 | tf_op jit(solution)/shard_map/ppermute | solution.py:358
  635.4 16.7 %collective-permute-done.62.refs_3_ = bf16[512,1024]{1,0:T(8,128)(2,1)S(1)} collective-permute-done((bf16[512,1024]{1,0:T(8,128)(2,1)S(1)}, bf16[512,1024]{1,0:T(8,128)(2,1)S(1)}, u32[]{:S(2)}, u32[]{:S(2)}) %collective-permute-start.62) | collective-permute-done | bytes 1048608 | tf_op jit(solution)/shard_map/ppermute | solution.py:358
  652.2 8.9 %collective-permute-done.55.refs_1_ = bf16[256,1024]{1,0:T(8,128)(2,1)} collective-permute-done((bf16[256,1024]{1,0:T(8,128)(2,1)}, bf16[256,1024]{1,0:T(8,128)(2,1)}, u32[]{:S(2)}, u32[]{:S(2)}) %collective-permute-start.55) | collective-permute-done | bytes 524320 | tf_op jit(solution)/shard_map/ppermute | solution.py:358
  666.3 20.9 %collective-permute-done.51 = f32[160,128]{1,0:T(8,128)S(1)} collective-permute-done((f32[160,128]{1,0:T(8,128)S(1)}, f32[160,128]{1,0:T(8,128)S(1)}, u32[]{:S(2)}, u32[]{:S(2)}) %collective-permute-start.51) | collective-permute-done | bytes 81952 | tf_op jit(solution)/shard_map/ppermute | solution.py:409
  (390 shorter events, 288.9 us)
Async XLA Ops:
  7.2 176.9 %all-gather.3.cloned.1.call-start = ((), (), s32[]{:S(2)}) async-start(), calls=%async_computation.2 | async-start | bytes 9437184 | tf_op jit(solution)/shard_map/all_gather | solution.py:476
  12.9 43.1 %collective-permute-start = (bf16[256,2048]{1,0:T(8,128)(2,1)S(1)}, bf16[256,2048]{1,0:T(8,128)(2,1)}, u32[]{:S(2)}, u32[]{:S(2)}) collective-permute-start(bf16[256,2048]{1,0:T(8,128)(2,1)S(1)} %fusion.15), channel_id=1, source_target_pairs={{0,2},{1,3},{2,0},{3,1},{4,6},{5,7},{6,4},{7,5},{8,10},{9,11},{10,... | collective-permute-start | bytes 3145736 | tf_op jit(solution)/shard_map/ppermute | solution.py:358
  15.9 32.1 %collective-permute-start.1 = (bf16[256,768]{1,0:T(8,128)(2,1)}, bf16[256,768]{1,0:T(8,128)(2,1)}, u32[]{:S(2)}, u32[]{:S(2)}) collective-permute-start(bf16[256,768]{1,0:T(8,128)(2,1)} %get-tuple-element.107), channel_id=1, source_target_pairs={{0,4},{1,5},{2,6},{3,7},{4,0},{5,1},{6,2},{7,3},{8,12},{9,13},{10,... | collective-permute-start | bytes 1179656 | tf_op jit(solution)/shard_map/ppermute | solution.py:463
  18.5 36.8 %collective-permute-start.2 = (bf16[256,768]{1,0:T(8,128)(2,1)}, bf16[256,768]{1,0:T(8,128)(2,1)}, u32[]{:S(2)}, u32[]{:S(2)}) collective-permute-start(bf16[256,768]{1,0:T(8,128)(2,1)} %get-tuple-element.108), channel_id=1, source_target_pairs={{0,4},{1,5},{2,6},{3,7},{4,0},{5,1},{6,2},{7,3},{8,12},{9,13},{10,... | collective-permute-start | bytes 1179656 | tf_op jit(solution)/shard_map/ppermute | solution.py:463
  56.0 216.9 %all-gather.5.cloned.1.call-start = ((), (), s32[]{:S(2)}) async-start(), calls=%async_computation.3 | async-start | bytes 9437184 | tf_op jit(solution)/shard_map/all_gather | solution.py:499
  151.4 30.4 %collective-permute-start.20 = (bf16[256,2048]{1,0:T(8,128)(2,1)S(1)}, bf16[256,2048]{1,0:T(8,128)(2,1)}, u32[]{:S(2)}, u32[]{:S(2)}) collective-permute-start(bf16[256,2048]{1,0:T(8,128)(2,1)S(1)} %fusion.32), channel_id=1, source_target_pairs={{0,2},{1,3},{2,0},{3,1},{4,6},{5,7},{6,4},{7,5},{8,10},{9,11},{10,... | collective-permute-start | bytes 3145736 | tf_op jit(solution)/shard_map/ppermute | solution.py:378
  187.5 205.3 %reduce-scatter.3.cloned.1.call-start = ((), (), s32[]{:S(2)}) async-start(), calls=%async_computation.4 | async-start | bytes 9437184 | tf_op jit(solution)/shard_map/reduce_scatter | solution.py:512
  304.1 403.8 %reduce-scatter.5.cloned.1.call-start = ((), (), s32[]{:S(2)}) async-start(), calls=%async_computation.5 | async-start | bytes 9437184 | tf_op jit(solution)/shard_map/reduce_scatter | solution.py:530
  320.3 48.1 %collective-permute-start.29 = (bf16[2,512,1024]{2,1,0:T(8,128)(2,1)}, bf16[2,512,1024]{2,1,0:T(8,128)(2,1)}, u32[]{:S(2)}, u32[]{:S(2)}) collective-permute-start(bf16[2,512,1024]{2,1,0:T(8,128)(2,1)} %dynamic-slice_bitcast_fusion.1), channel_id=1, source_target_pairs={{0,16},{8,24},{16,0},{24,8},{1,17},{9,25},{17,1},{25,9},{2,18},{10... | collective-permute-start | bytes 6291464 | tf_op jit(solution)/shard_map/ppermute | solution.py:378
  337.2 48.4 %collective-permute-start.28 = (bf16[2,256,2048]{2,1,0:T(8,128)(2,1)}, bf16[2,256,2048]{2,1,0:T(8,128)(2,1)}, u32[]{:S(2)}, u32[]{:S(2)}) collective-permute-start(bf16[2,256,2048]{2,1,0:T(8,128)(2,1)} %dynamic-slice_bitcast_fusion.2), channel_id=1, source_target_pairs={{0,8},{8,0},{16,24},{24,16},{1,9},{9,1},{17,25},{25,17},{2,10},{10... | collective-permute-start | bytes 6291464 | tf_op jit(solution)/shard_map/ppermute | solution.py:378
  547.7 44.4 %collective-permute-start.47 = (bf16[256,2048]{1,0:T(8,128)(2,1)}, bf16[256,2048]{1,0:T(8,128)(2,1)}, u32[]{:S(2)}, u32[]{:S(2)}) collective-permute-start(bf16[256,2048]{1,0:T(8,128)(2,1)} %fusion.35), channel_id=1, source_target_pairs={{0,2},{1,3},{2,0},{3,1},{4,6},{5,7},{6,4},{7,5},{8,10},{9,11},{10,... | collective-permute-start | bytes 3145736 | tf_op jit(solution)/shard_map/ppermute | solution.py:378
  553.1 45.1 %collective-permute-start.57 = (bf16[256,1024]{1,0:T(8,128)(2,1)}, bf16[256,1024]{1,0:T(8,128)(2,1)S(1)}, u32[]{:S(2)}, u32[]{:S(2)}) collective-permute-start(bf16[256,1024]{1,0:T(8,128)(2,1)} %fusion.40), channel_id=1, source_target_pairs={{0,4},{1,5},{2,6},{3,7},{4,0},{5,1},{6,2},{7,3},{8,12},{9,13},{10,... | collective-permute-start | bytes 1572872 | tf_op jit(solution)/shard_map/ppermute | solution.py:549
  557.3 45.5 %collective-permute-start.54 = (bf16[256,1024]{1,0:T(8,128)(2,1)}, bf16[256,1024]{1,0:T(8,128)(2,1)S(1)}, u32[]{:S(2)}, u32[]{:S(2)}) collective-permute-start(bf16[256,1024]{1,0:T(8,128)(2,1)} %fusion.41), channel_id=1, source_target_pairs={{0,4},{1,5},{2,6},{3,7},{4,0},{5,1},{6,2},{7,3},{8,12},{9,13},{10,... | collective-permute-start | bytes 1572872 | tf_op jit(solution)/shard_map/ppermute | solution.py:549
  557.3 56.7 %collective-permute-start.59 = (bf16[256,2048]{1,0:T(8,128)(2,1)}, bf16[256,2048]{1,0:T(8,128)(2,1)S(1)}, u32[]{:S(2)}, u32[]{:S(2)}) collective-permute-start(bf16[256,2048]{1,0:T(8,128)(2,1)} %copy-done.13), channel_id=1, source_target_pairs={{0,16},{8,24},{16,0},{24,8},{1,17},{9,25},{17,1},{25,9},{2,18},{10... | collective-permute-start | bytes 3145736 | tf_op jit(solution)/shard_map/ppermute | solution.py:358
  559.5 44.1 %collective-permute-start.56 = (bf16[256,1024]{1,0:T(8,128)(2,1)S(1)}, bf16[256,1024]{1,0:T(8,128)(2,1)S(1)}, u32[]{:S(2)}, u32[]{:S(2)}) collective-permute-start(bf16[256,1024]{1,0:T(8,128)(2,1)S(1)} %fusion.53), channel_id=1, source_target_pairs={{0,8},{8,0},{16,24},{24,16},{1,9},{9,1},{17,25},{25,17},{2,10},{10... | collective-permute-start | bytes 1572872 | tf_op jit(solution)/shard_map/ppermute | solution.py:378
  602.8 32.6 %collective-permute-start.60 = (bf16[256,2048]{1,0:T(8,128)(2,1)S(1)}, bf16[256,2048]{1,0:T(8,128)(2,1)S(1)}, u32[]{:S(2)}, u32[]{:S(2)}) collective-permute-start(bf16[256,2048]{1,0:T(8,128)(2,1)S(1)} %copy-done.32), channel_id=1, source_target_pairs={{0,16},{8,24},{16,0},{24,8},{1,17},{9,25},{17,1},{25,9},{2,18},{10... | collective-permute-start | bytes 3145736 | tf_op jit(solution)/shard_map/ppermute | solution.py:358
  603.6 31.8 %collective-permute-start.61 = (bf16[512,1024]{1,0:T(8,128)(2,1)S(1)}, bf16[512,1024]{1,0:T(8,128)(2,1)S(1)}, u32[]{:S(2)}, u32[]{:S(2)}) collective-permute-start(bf16[512,1024]{1,0:T(8,128)(2,1)S(1)} %copy-done.14), channel_id=1, source_target_pairs={{0,8},{8,0},{16,24},{24,16},{1,9},{9,1},{17,25},{25,17},{2,10},{10... | collective-permute-start | bytes 3145736 | tf_op jit(solution)/shard_map/ppermute | solution.py:358
  604.8 47.4 %collective-permute-start.62 = (bf16[512,1024]{1,0:T(8,128)(2,1)S(1)}, bf16[512,1024]{1,0:T(8,128)(2,1)S(1)}, u32[]{:S(2)}, u32[]{:S(2)}) collective-permute-start(bf16[512,1024]{1,0:T(8,128)(2,1)S(1)} %copy-done.30), channel_id=1, source_target_pairs={{0,8},{8,0},{16,24},{24,16},{1,9},{9,1},{17,25},{25,17},{2,10},{10... | collective-permute-start | bytes 3145736 | tf_op jit(solution)/shard_map/ppermute | solution.py:358
  614.0 38.2 %collective-permute-start.58 = (bf16[256,1024]{1,0:T(8,128)(2,1)}, bf16[256,1024]{1,0:T(8,128)(2,1)}, u32[]{:S(2)}, u32[]{:S(2)}) collective-permute-start(bf16[256,1024]{1,0:T(8,128)(2,1)} %fusion.37.refs_4_), channel_id=1, source_target_pairs={{0,16},{8,24},{16,0},{24,8},{1,17},{9,25},{17,1},{25,9},{2,18},{10... | collective-permute-start | bytes 1572872 | tf_op jit(solution)/shard_map/ppermute | solution.py:358
  617.4 43.7 %collective-permute-start.55 = (bf16[256,1024]{1,0:T(8,128)(2,1)}, bf16[256,1024]{1,0:T(8,128)(2,1)}, u32[]{:S(2)}, u32[]{:S(2)}) collective-permute-start(bf16[256,1024]{1,0:T(8,128)(2,1)} %fusion.39.refs_0_), channel_id=1, source_target_pairs={{0,8},{8,0},{16,24},{24,16},{1,9},{9,1},{17,25},{25,17},{2,10},{10... | collective-permute-start | bytes 1572872 | tf_op jit(solution)/shard_map/ppermute | solution.py:358
  661.1 41.0 %collective-permute-start.63 = (bf16[256,1024]{1,0:T(8,128)(2,1)}, bf16[256,1024]{1,0:T(8,128)(2,1)}, u32[]{:S(2)}, u32[]{:S(2)}) collective-permute-start(bf16[256,1024]{1,0:T(8,128)(2,1)} %fusion.39.refs_0_), channel_id=1, source_target_pairs={{0,16},{8,24},{16,0},{24,8},{1,17},{9,25},{17,1},{25,9},{2,18},{10... | collective-permute-start | bytes 1572872 | tf_op jit(solution)/shard_map/ppermute | solution.py:358
  662.3 39.8 %collective-permute-start.64 = (bf16[256,1024]{1,0:T(8,128)(2,1)}, bf16[256,1024]{1,0:T(8,128)(2,1)}, u32[]{:S(2)}, u32[]{:S(2)}) collective-permute-start(bf16[256,1024]{1,0:T(8,128)(2,1)} %collective-permute-done.55.refs_1_), channel_id=1, source_target_pairs={{0,16},{8,24},{16,0},{24,8},{1,17},{9,25},{17,1},{25,9},{2,18},{10... | collective-permute-start | bytes 1572872 | tf_op jit(solution)/shard_map/ppermute | solution.py:358
  663.1 39.0 %collective-permute-start.65 = (bf16[256,1024]{1,0:T(8,128)(2,1)}, bf16[256,1024]{1,0:T(8,128)(2,1)}, u32[]{:S(2)}, u32[]{:S(2)}) collective-permute-start(bf16[256,1024]{1,0:T(8,128)(2,1)} %fusion.37.refs_4_), channel_id=1, source_target_pairs={{0,8},{8,0},{16,24},{24,16},{1,9},{9,1},{17,25},{25,17},{2,10},{10... | collective-permute-start | bytes 1572872 | tf_op jit(solution)/shard_map/ppermute | solution.py:358
  664.2 37.9 %collective-permute-start.66 = (bf16[256,1024]{1,0:T(8,128)(2,1)}, bf16[256,1024]{1,0:T(8,128)(2,1)}, u32[]{:S(2)}, u32[]{:S(2)}) collective-permute-start(bf16[256,1024]{1,0:T(8,128)(2,1)} %collective-permute-done.58.refs_6_), channel_id=1, source_target_pairs={{0,8},{8,0},{16,24},{24,16},{1,9},{9,1},{17,25},{25,17},{2,10},{10... | collective-permute-start | bytes 1572872 | tf_op jit(solution)/shard_map/ppermute | solution.py:358
  (115 other events, 2051.4 us)
Sparse Core Ops, SparseCore 0:
  56.2 85.1 all-gather.2
  187.6 85.3 all-gather.4
  304.3 88.4 reduce-scatter.2
  433.3 88.8 reduce-scatter.4

commit v7 on v6

--- a/solution.py
+++ b/solution.py
@@ -124,7 +124,7 @@
             row_max = jnp.max(scores, axis=1, keepdims=True)
             shifted = jnp.exp(scores - row_max)
             total = jnp.sum(shifted, axis=1, keepdims=True)
-            mix = product(narrow(shifted / total), qkv_ref[:end, value_lanes], (1, 0))
+            mix = product(narrow(shifted * (1.0 / total)), qkv_ref[:end, value_lanes], (1, 0))
             heads_ref[here, lanes] = narrow(mix * mask_ref[here, head : head + 1])
             log_ref[here, head : head + 1] = row_max + jnp.log(total)
 
@@ -168,12 +168,12 @@
             out_ref[here, width + at : width + at + HD] = narrow(value * cos - pltpu.roll(value, HD // 2, 1) * sin)
 
 
-def share_kernel(*refs):
+def share_kernel(side_ref, *refs):
     *given, out_ref = refs
     total = product(given[0][...], given[1][...], (1, 1))
     for a_ref, w_ref in zip(given[2::2], given[3::2]):
         total = total + product(a_ref[...], w_ref[...], (1, 1))
-    out_ref[0, 0] = narrow(total)
+    out_ref[0] = narrow(total)
 
 
 def weight_kernel(x_ref, q_ref, g_ref, h_ref, *outs):
@@ -257,25 +257,29 @@
     )(g, w, qkv, log_total, cos, sin, mask)
 
 
-def share_of(pairs, rows):
+def share_of(pairs, rows, side):
     tokens, depth = pairs[0][0].shape
     dim = pairs[0][1].shape[0]
+    chips = tokens // rows // 2
     specs = [
-        pl.BlockSpec((rows, depth), lambda i: (i, 0)),
-        pl.BlockSpec((dim, depth), lambda i: (0, 0)),
+        pl.BlockSpec((rows, depth), lambda i, side: (2 * i + side[0], 0)),
+        pl.BlockSpec((dim, depth), lambda i, side: (0, 0)),
     ] * len(pairs)
     return pl.pallas_call(
         share_kernel,
-        grid=(tokens // rows,),
-        out_shape=jax.ShapeDtypeStruct((2, tokens // rows // 2, rows, dim), jnp.bfloat16),
-        in_specs=specs,
-        out_specs=pl.BlockSpec((1, 1, rows, dim), lambda i: (i % 2, i // 2, 0, 0)),
+        grid_spec=pltpu.PrefetchScalarGridSpec(
+            num_scalar_prefetch=1,
+            grid=(chips,),
+            in_specs=specs,
+            out_specs=pl.BlockSpec((1, rows, dim), lambda i, side: (i, 0, 0)),
+        ),
+        out_shape=jax.ShapeDtypeStruct((chips, rows, dim), jnp.bfloat16),
         compiler_params=pltpu.CompilerParams(vmem_limit_bytes=VMEM_LIMIT),
         cost_estimate=pl.CostEstimate(
-            flops=2 * tokens * dim * depth * len(pairs), bytes_accessed=12 << 20, transcendentals=0
+            flops=tokens * dim * depth * len(pairs), bytes_accessed=12 << 20, transcendentals=0
         ),
         name="share_of",
-    )(*[x for pair in pairs for x in pair])
+    )(side.astype(jnp.int32).reshape(1), *[x for pair in pairs for x in pair])
 
 
 def weight_grads(x, qkv_grad, g, heads_out, count):
@@ -431,9 +435,11 @@
         def place_sequence(held):
             return by_index(held, place).reshape(SEQ_LEN, -1)
 
-        def core_sum(blocks):
-            got = lax.ppermute(pick(blocks, 1 - core), "mp", swap_pairs(ranks, 1))
-            return wide(pick(blocks, core)) + wide(got)
+        def core_sum(pairs):
+            theirs = share_of(pairs, rows, 1 - core)
+            got = lax.ppermute(theirs, "mp", swap_pairs(ranks, 1))
+            pairs, theirs = lax.optimization_barrier((pairs, theirs))
+            return wide(share_of(pairs, rows, core)) + wide(got)
 
         def chip_sum(blocks):
             bits = pair_bits[::-1]
@@ -489,7 +495,7 @@
                 weights_in += place_blocks(held, column, [(1, 3 * width, jnp.bfloat16, False)])
                 weights_out += place_blocks(held_out, column, [(1, width, jnp.bfloat16, False)])
             kept.append((*attend_forward(inputs_one, weights_in[k], cos, sin, mask), mask))
-        mixer_branch = chip_sum(core_sum(share_of([(x[1], w) for x, w in zip(kept, weights_out)], rows)))
+        mixer_branch = chip_sum(core_sum([(x[1], w) for x, w in zip(kept, weights_out)]))
         mixer_branch, grads_all = lax.optimization_barrier((mixer_branch, grads_all))
         top_down = product(grads_all, down_weight, (1, 1))
 
@@ -543,26 +549,25 @@
             if k:
                 grads_now, part, helds = lax.optimization_barrier((grads_now, part, helds))
                 sent.append(column_scatter(part, columns, column, cut=1))
+        helds, sent = lax.optimization_barrier((helds, sent))
         sent = [[narrow(x) for x in column_scatter(lanes, columns, column, start=1)] for lanes in sent]
-        pairs, sent, part = lax.optimization_barrier((pairs, sent, part))
+        helds = column_gather(helds, columns, start=1)
+        pairs, sent, helds, _ = lax.optimization_barrier((pairs, sent, helds, part))
         there = [
             [lax.ppermute(x, "mp", shift_pairs(ranks, -k * group)) for x in lanes]
             for k, lanes in zip(range(1, sequences)[::-1], sent)
         ]
-        helds, sent = lax.optimization_barrier((helds, sent))
-        helds = column_gather(helds, columns, start=1)
         pieces = column_scatter(part, columns, column, cut=1)
-        blocks = core_sum(share_of(pairs, rows))
-        blocks, pieces = lax.optimization_barrier((blocks, pieces))
+        blocks = core_sum(pairs)
+        blocks, pieces, there = lax.optimization_barrier((blocks, pieces, there))
         normed_grad_one = chip_sum(blocks)
         pieces = column_scatter(pieces, columns, column, start=1)
+        down_sum, = place_blocks(helds[:1], column, [(1, dim, jnp.float32, False)])
+        up_sum, = place_blocks(helds[1:], column, [(1, cols_local, jnp.float32, False)])
+        pieces, down_sum, up_sum = lax.optimization_barrier((pieces, down_sum, up_sum))
         for lanes in there:
             pieces = [p + wide(t) for p, t in zip(pieces, lanes)]
-        spread = column_gather([narrow(p) for p in pieces], columns, cut=1)
-        spread, helds = lax.optimization_barrier((spread, helds))
-        spread = column_gather(spread, columns, start=1)
-        down_sum, = place_blocks(helds[:1], column, [(1, dim, jnp.float32, False)])
-        up_sum, = place_blocks(helds[1:], column, [(1, cols_local, jnp.float32, False)])
+        spread = column_gather([narrow(p) for p in pieces], columns)
         attention_sum, output_sum = place_blocks(
             spread,
             column,

time: 724 us -> 701 us (0.968)
  waiting for transfers between devices: 316 us -> 286 us
  other arithmetic: 54 us -> 64.8 us
    ppermute x37, waiting for transfers between devices: 88.5 us -> 52.5 us  [xor_gather(): held[far ^ bit] = lax.ppermute(held[far], axis, swap_pairs(size, bit))]
    ppermute x2, waiting for transfers between devices: 3.6 us -> 23.8 us  [local(): lax.ppermute(x, 'mp', shift_pairs(ranks, -k * group))]
    ppermute x14, waiting for transfers between devices: 117 us -> 107 us  [xor_scatter(): lax.ppermute(narrow(pick(blocks, 1 - side, at)), axis_name, swap_pairs(si...]
    pallas_call x2 -> x4, Pallas kernels: 18.2 us -> 24.5 us  [share_of(): pl.pallas_call(share_kernel, grid_spec=pltpu.PrefetchScalarGridSpec(num_s...]
    add x7 -> x9, other arithmetic: 17.3 us -> 21.4 us  [xor_scatter(): blocks = wide(pick(blocks, side, at)) + wide(got)]
    unnamed x137 -> x129, local copies, waits for them, and re-layouts: 17.6 us -> 14.1 us
  transfers between devices with their start and end apart: 71 -> 71, of which waited for: 28 -> 30; matrix products, arithmetic and copies ran while one was open for 18% -> 19% of each run, Pallas kernels for 16% -> 17%
where the time goes in v7:
time: 701 us; the launch traced here: 697 us
  waiting for transfers between devices  286 us (41%)
  Pallas kernels  119 us (17%)
  matrix products  95.3 us (14%)
  starting transfers between devices  76.8 us (11%)
  other arithmetic  64.8 us (9%)
  local copies, waits for them, and re-layouts  40.5 us (6%)
  between operations  15.2 us (2%)
    ppermute x14, waiting for transfers between devices, xor_scatter(): lax.ppermute(narrow(pick(blocks, 1 - side, at)), axis_name, swap_pairs(si...  107 us
    dot_general x6, matrix products, product(): lax.dot_general(a, b, ((dims[:1], dims[1:]), ((), ())), preferred_element...  81.1 us
    ppermute x37, waiting for transfers between devices, xor_gather(): held[far ^ bit] = lax.ppermute(held[far], axis, swap_pairs(size, bit))  52.5 us
    all_gather x1, waiting for transfers between devices, local(): inputs_two = lax.all_gather(narrow(normed_two), 'mp', axis=0, tiled=True)  48.3 us
    ppermute x37, starting transfers between devices, xor_gather(): held[far ^ bit] = lax.ppermute(held[far], axis, swap_pairs(size, bit))  40.1 us
    ppermute x4, waiting for transfers between devices, local(): lax.ppermute(x, 'mp', shift_pairs(ranks, k * group))  26.8 us
    pallas_call x2, Pallas kernels, attend_backward(): pl.pallas_call(backward_kernel, out_shape=jax.ShapeDtypeStruct((tokens, 3...  26.7 us
    pallas_call x2, Pallas kernels, attend_forward(): pl.pallas_call(forward_kernel, out_shape=[jax.ShapeDtypeStruct((tokens, 3...  25.3 us
  transfers between devices with their start and end apart: 71, of which 30 were waited for; matrix products, arithmetic and copies ran while one was open for 19% of the time, Pallas kernels for 17%

profile of v7, /device:TPU:0, one launch (start us, length us, event | category | flops | bytes accessed | tf_op | source)
XLA Modules:
  0.0 697.0 jit_solution(16929877336222591505)
XLA Ops:
  28.5 19.5 %collective-permute-done.1.refs_0_ = bf16[256,768]{1,0:T(8,128)(2,1)} collective-permute-done((bf16[256,768]{1,0:T(8,128)(2,1)}, bf16[256,768]{1,0:T(8,128)(2,1)}, u32[]{:S(2)}, u32[]{:S(2)}) %collective-permute-start.1) | collective-permute-done | bytes 393248 | tf_op jit(solution)/shard_map/ppermute | solution.py:469
  66.8 12.8 %attend_forward.2 = (bf16[1024,768]{1,0:T(8,128)(2,1)}, bf16[1024,256]{1,0:T(8,128)(2,1)}, f32[1024,2]{1,0:T(8,128)}) custom-call(bf16[1024,2048]{1,0:T(8,128)(2,1)} %bitcast.202, bf16[2048,768]{1,0:T(8,128)(2,1)} %pad_maximum_fusion.w_ref.refs_3_, f32[1024,128]{1,0:T(8,128)} %get-tuple-element.122.cos_ref, f32[1024,128]{1,0:T(8,128)} %get-tuple-element.123.sin_ref, ...), custom_call_target="tpu_custom_call" | custom-call | flops 3758096384 | bytes 12582912 | tf_op jit(solution)/shard_map/attend_forward/pallas_call | solution.py:222
  85.6 17.6 %collective-permute-done.13.refs_1_ = bf16[256,256]{1,0:T(8,128)(2,1)S(1)} collective-permute-done((bf16[256,256]{1,0:T(8,128)(2,1)S(1)}, bf16[256,256]{1,0:T(8,128)(2,1)S(1)}, u32[]{:S(2)}, u32[]{:S(2)}) %collective-permute-start.13) | collective-permute-done | bytes 131104 | tf_op jit(solution)/shard_map/ppermute | solution.py:362
  116.6 12.5 %attend_forward.3 = (bf16[1024,768]{1,0:T(8,128)(2,1)}, bf16[1024,256]{1,0:T(8,128)(2,1)}, f32[1024,2]{1,0:T(8,128)}) custom-call(bf16[1024,2048]{1,0:T(8,128)(2,1)} %bitcast.203, bf16[2048,768]{1,0:T(8,128)(2,1)} %place_blocks.5.w_ref.refs_1_, f32[1024,128]{1,0:T(8,128)} %get-tuple-element.122.cos_ref, f32[1024,128]{1,0:T(8,128)} %get-tuple-element.123.sin_ref, ...), custom_call_target="tpu_custom_call" | custom-call | flops 3758096384 | bytes 12582912 | tf_op jit(solution)/shard_map/attend_forward/pallas_call | solution.py:222
  156.9 20.5 %collective-permute-done.20 = bf16[256,2048]{1,0:T(8,128)(2,1)} collective-permute-done((bf16[256,2048]{1,0:T(8,128)(2,1)S(1)}, bf16[256,2048]{1,0:T(8,128)(2,1)}, u32[]{:S(2)}, u32[]{:S(2)}) %collective-permute-start.20) | collective-permute-done | bytes 1048608 | tf_op jit(solution)/shard_map/ppermute | solution.py:382
  194.8 15.5 %fusion.83 = f32[2048,1024]{1,0:T(8,128)} fusion(bf16[2048,2048]{1,0:T(8,128)(2,1)} %all-gather.3.cloned.1.call-done, bf16[1024,2048]{1,0:T(8,128)(2,1)} %param.22), kind=kOutput, calls=%fused_computation.203 | convolution fusion | flops 8589934592 | bytes 20971520 | tf_op jit(solution)/shard_map/dot_general | solution.py:94
  220.2 48.3 %all-gather.5.cloned.1.call-done = bf16[2048,2048]{1,0:T(8,128)(2,1)} async-done(((bf16[256,2048]{1,0:T(8,128)(2,1)}), bf16[2048,2048]{1,0:T(8,128)(2,1)}) %all-gather.5.cloned.1.call-update) | async-done | bytes 8388624 | tf_op jit(solution)/shard_map/all_gather | solution.py:505
  268.6 18.3 %multiply_reduce_fusion = (f32[2048]{0:T(1024)S(1)}, bf16[2048,1024]{1,0:T(8,128)(2,1)}, bf16[2048,1024]{1,0:T(8,128)(2,1)S(1)}) fusion(f32[2048,1024]{1,0:T(8,128)} %fusion.83, s32[2048]{0:T(1024)S(1)} %bitcast.247, s32[1024]{0:T(1024)S(1)} %add_multiply_fusion.1, f32[2048]{0:T(1024)S(1)} %bitcast.245, bf16[2048,2048]{1,0:T(8,128)(2,1)} %all-gather.5.cloned.1.call-done, ...), kind=kOutput, calls=%fused_computation.8 | convolution fusion | flops 8617195520 | bytes 29388800 | tf_op jit(solution)/shard_map/dot_general | solution.py:94
  288.9 10.9 %convolution_convert_fusion.1 = bf16[2048,2048]{1,0:T(8,128)(2,1)} fusion(bf16[2048,1024]{1,0:T(8,128)(2,1)S(1)} %get-tuple-element.163, bf16[2048,1024]{1,0:T(8,128)(2,1)S(1)} %copy-done.60), kind=kOutput, calls=%fused_computation.11 | convolution fusion | flops 8594128896 | bytes 16777216 | tf_op jit(solution)/shard_map/dot_general | solution.py:94
  299.9 12.9 %convolution_convert_fusion.2 = bf16[2048,1024]{1,0:T(8,128)(2,1)S(1)} fusion(bf16[2048,2048]{1,0:T(8,128)(2,1)} %all-gather.5.cloned.1.call-done, bf16[2048,1024]{1,0:T(8,128)(2,1)} %copy-done.63), kind=kOutput, calls=%fused_computation.17 | convolution fusion | flops 8592031744 | bytes 16777216 | tf_op jit(solution)/shard_map/dot_general | solution.py:94
  317.4 12.3 %fusion.6 = bf16[1024,2048]{1,0:T(8,128)(2,1)S(1)} fusion(bf16[2048,1024]{1,0:T(8,128)(2,1)S(1)} %copy-done.62, bf16[2048,2048]{1,0:T(8,128)(2,1)} %all-gather.3.cloned.1.call-done, f32[2048]{0:T(1024)S(1)} %bitcast.246), kind=kOutput, calls=%fused_computation.16 | convolution fusion | flops 8604614656 | bytes 16785408 | tf_op jit(solution)/shard_map/dot_general | solution.py:94
  334.8 11.3 %convolution_convert_fusion = bf16[2048,2048]{1,0:T(8,128)(2,1)} fusion(bf16[2048,1024]{1,0:T(8,128)(2,1)S(1)} %copy-done.62, bf16[1024,2048]{1,0:T(8,128)(2,1)S(1)} %copy-done.61), kind=kOutput, calls=%fused_computation.10 | convolution fusion | flops 8594128896 | bytes 16777216 | tf_op jit(solution)/shard_map/dot_general | solution.py:94
  349.4 14.6 %collective-permute-done.29 = bf16[2,512,1024]{2,1,0:T(8,128)(2,1)} collective-permute-done((bf16[2,512,1024]{2,1,0:T(8,128)(2,1)}, bf16[2,512,1024]{2,1,0:T(8,128)(2,1)}, u32[]{:S(2)}, u32[]{:S(2)}) %collective-permute-start.29) | collective-permute-done | bytes 2097184 | tf_op jit(solution)/shard_map/ppermute | solution.py:382
  369.2 12.1 %collective-permute-done.28 = bf16[2,256,2048]{2,1,0:T(8,128)(2,1)} collective-permute-done((bf16[2,256,2048]{2,1,0:T(8,128)(2,1)}, bf16[2,256,2048]{2,1,0:T(8,128)(2,1)}, u32[]{:S(2)}, u32[]{:S(2)}) %collective-permute-start.28) | collective-permute-done | bytes 2097184 | tf_op jit(solution)/shard_map/ppermute | solution.py:382
  401.8 19.4 %collective-permute-done.33 = bf16[256,2048]{1,0:T(8,128)(2,1)S(1)} collective-permute-done((bf16[256,2048]{1,0:T(8,128)(2,1)S(1)}, bf16[256,2048]{1,0:T(8,128)(2,1)S(1)}, u32[]{:S(2)}, u32[]{:S(2)}) %collective-permute-start.33) | collective-permute-done | bytes 1048608 | tf_op jit(solution)/shard_map/ppermute | solution.py:362
  430.9 13.5 %attend_backward.2.q_ref.refs_0_ = bf16[1024,768]{1,0:T(8,128)(2,1)} custom-call(bf16[1024,2048]{1,0:T(8,128)(2,1)} %bitcast.57.g_ref, bf16[2048,256]{1,0:T(8,128)(2,1)} %place_blocks.6.refs_3_.w_ref, bf16[1024,768]{1,0:T(8,128)(2,1)} %get-tuple-element.170.qkv_ref, f32[1024,2]{1,0:T(8,128)} %get-tuple-element.171.log_ref, ...), custom_call_target="tpu_custom_call" | custom-call | flops 2415919104 | bytes 12582912 | tf_op jit(solution)/shard_map/attend_backward/pallas_call | solution.py:244
  444.4 8.9 %weight_grads.2 = (bf16[4,256,1024]{2,1,0:T(8,128)(2,1)}, bf16[4,256,1024]{2,1,0:T(8,128)(2,1)}) custom-call(bf16[1024,2048]{1,0:T(8,128)(2,1)} %bitcast.204, bf16[1024,768]{1,0:T(8,128)(2,1)} %attend_backward.2.q_ref.refs_0_, bf16[1024,2048]{1,0:T(8,128)(2,1)} %bitcast.57.g_ref, bf16[1024,256]{1,0:T(8,128)(2,1)} %get-tuple-element.154.refs_2_.h_ref), custom_call_target="tpu_custom_call" | custom-call | flops 4294967296 | bytes 14680064 | tf_op jit(solution)/shard_map/weight_grads/pallas_call | solution.py:290
  457.8 13.2 %attend_backward.3.q_ref.refs_2_ = bf16[1024,768]{1,0:T(8,128)(2,1)} custom-call(bf16[1024,2048]{1,0:T(8,128)(2,1)} %bitcast.57.g_ref, bf16[2048,256]{1,0:T(8,128)(2,1)} %bitcast.201, bf16[1024,768]{1,0:T(8,128)(2,1)} %get-tuple-element.131.qkv_ref, f32[1024,2]{1,0:T(8,128)} %get-tuple-element.175.log_ref, f32[1024,128]{1,0:T(8,128)} %get-tuple-element.122.cos_ref, ...), custom_call_target="tpu_custom_call" | custom-call | flops 2415919104 | bytes 12582912 | tf_op jit(solution)/shard_map/attend_backward/pallas_call | solution.py:244
  487.0 9.2 %collective-permute-done.43 = bf16[256,1024]{1,0:T(8,128)(2,1)S(1)} collective-permute-done((bf16[256,1024]{1,0:T(8,128)(2,1)S(1)}, bf16[256,1024]{1,0:T(8,128)(2,1)S(1)}, u32[]{:S(2)}, u32[]{:S(2)}) %collective-permute-start.43) | collective-permute-done | bytes 524320 | tf_op jit(solution)/shard_map/ppermute | solution.py:382
  497.4 8.9 %weight_grads.3 = (bf16[4,256,1024]{2,1,0:T(8,128)(2,1)}, bf16[4,256,1024]{2,1,0:T(8,128)(2,1)}) custom-call(bf16[1024,2048]{1,0:T(8,128)(2,1)} %bitcast.205, bf16[1024,768]{1,0:T(8,128)(2,1)} %attend_backward.3.q_ref.refs_2_, bf16[1024,2048]{1,0:T(8,128)(2,1)} %bitcast.57.g_ref, bf16[1024,256]{1,0:T(8,128)(2,1)} %get-tuple-element.152.refs_0_.h_ref), custom_call_target="tpu_custom_call" | custom-call | flops 4294967296 | bytes 14680064 | tf_op jit(solution)/shard_map/weight_grads/pallas_call | solution.py:290
  507.3 29.9 %collective-permute-done.42 = bf16[256,1024]{1,0:T(8,128)(2,1)} collective-permute-done((bf16[256,1024]{1,0:T(8,128)(2,1)}, bf16[256,1024]{1,0:T(8,128)(2,1)}, u32[]{:S(2)}, u32[]{:S(2)}) %collective-permute-start.42) | collective-permute-done | bytes 524320 | tf_op jit(solution)/shard_map/ppermute | solution.py:382
  583.4 12.5 %collective-permute-done.51 = bf16[256,1024]{1,0:T(8,128)(2,1)S(1)} collective-permute-done((bf16[256,1024]{1,0:T(8,128)(2,1)}, bf16[256,1024]{1,0:T(8,128)(2,1)S(1)}, u32[]{:S(2)}, u32[]{:S(2)}) %collective-permute-start.51) | collective-permute-done | bytes 524320 | tf_op jit(solution)/shard_map/ppermute | solution.py:557
  595.9 11.3 %collective-permute-done.52 = bf16[256,1024]{1,0:T(8,128)(2,1)} collective-permute-done((bf16[256,1024]{1,0:T(8,128)(2,1)}, bf16[256,1024]{1,0:T(8,128)(2,1)}, u32[]{:S(2)}, u32[]{:S(2)}) %collective-permute-start.52) | collective-permute-done | bytes 524320 | tf_op jit(solution)/shard_map/ppermute | solution.py:557
  656.6 11.9 %collective-permute-done.57 = f32[160,128]{1,0:T(8,128)S(1)} collective-permute-done((f32[160,128]{1,0:T(8,128)S(1)}, f32[160,128]{1,0:T(8,128)S(1)}, u32[]{:S(2)}, u32[]{:S(2)}) %collective-permute-start.57) | collective-permute-done | bytes 81952 | tf_op jit(solution)/shard_map/ppermute | solution.py:413
  (385 shorter events, 304.1 us)
Async XLA Ops:
  7.2 172.5 %all-gather.3.cloned.1.call-start = ((), (), s32[]{:S(2)}) async-start(), calls=%async_computation.2 | async-start | bytes 9437184 | tf_op jit(solution)/shard_map/all_gather | solution.py:482
  12.9 43.1 %collective-permute-start = (bf16[256,2048]{1,0:T(8,128)(2,1)S(1)}, bf16[256,2048]{1,0:T(8,128)(2,1)}, u32[]{:S(2)}, u32[]{:S(2)}) collective-permute-start(bf16[256,2048]{1,0:T(8,128)(2,1)S(1)} %fusion.15), channel_id=1, source_target_pairs={{0,2},{1,3},{2,0},{3,1},{4,6},{5,7},{6,4},{7,5},{8,10},{9,11},{10,... | collective-permute-start | bytes 3145736 | tf_op jit(solution)/shard_map/ppermute | solution.py:362
  15.9 32.1 %collective-permute-start.1 = (bf16[256,768]{1,0:T(8,128)(2,1)}, bf16[256,768]{1,0:T(8,128)(2,1)}, u32[]{:S(2)}, u32[]{:S(2)}) collective-permute-start(bf16[256,768]{1,0:T(8,128)(2,1)} %get-tuple-element.117), channel_id=1, source_target_pairs={{0,4},{1,5},{2,6},{3,7},{4,0},{5,1},{6,2},{7,3},{8,12},{9,13},{10,... | collective-permute-start | bytes 1179656 | tf_op jit(solution)/shard_map/ppermute | solution.py:469
  18.5 36.8 %collective-permute-start.2 = (bf16[256,768]{1,0:T(8,128)(2,1)}, bf16[256,768]{1,0:T(8,128)(2,1)}, u32[]{:S(2)}, u32[]{:S(2)}) collective-permute-start(bf16[256,768]{1,0:T(8,128)(2,1)} %get-tuple-element.118), channel_id=1, source_target_pairs={{0,4},{1,5},{2,6},{3,7},{4,0},{5,1},{6,2},{7,3},{8,12},{9,13},{10,... | collective-permute-start | bytes 1179656 | tf_op jit(solution)/shard_map/ppermute | solution.py:469
  56.0 212.5 %all-gather.5.cloned.1.call-start = ((), (), s32[]{:S(2)}) async-start(), calls=%async_computation.3 | async-start | bytes 9437184 | tf_op jit(solution)/shard_map/all_gather | solution.py:505
  79.7 28.4 %collective-permute-start.10 = (bf16[256,768]{1,0:T(8,128)(2,1)}, bf16[256,768]{1,0:T(8,128)(2,1)S(1)}, u32[]{:S(2)}, u32[]{:S(2)}) collective-permute-start(bf16[256,768]{1,0:T(8,128)(2,1)} %collective-permute-done.5.refs_1_), channel_id=1, source_target_pairs={{0,16},{8,24},{16,0},{24,8},{1,17},{9,25},{17,1},{25,9},{2,18},{10... | collective-permute-start | bytes 1179656 | tf_op jit(solution)/shard_map/ppermute | solution.py:362
  81.6 26.6 %collective-permute-start.11 = (bf16[256,768]{1,0:T(8,128)(2,1)}, bf16[256,768]{1,0:T(8,128)(2,1)S(1)}, u32[]{:S(2)}, u32[]{:S(2)}) collective-permute-start(bf16[256,768]{1,0:T(8,128)(2,1)} %collective-permute-done.2.refs_4_), channel_id=1, source_target_pairs={{0,8},{8,0},{16,24},{24,16},{1,9},{9,1},{17,25},{25,17},{2,10},{10... | collective-permute-start | bytes 1179656 | tf_op jit(solution)/shard_map/ppermute | solution.py:362
  146.5 30.9 %collective-permute-start.20 = (bf16[256,2048]{1,0:T(8,128)(2,1)S(1)}, bf16[256,2048]{1,0:T(8,128)(2,1)}, u32[]{:S(2)}, u32[]{:S(2)}) collective-permute-start(bf16[256,2048]{1,0:T(8,128)(2,1)S(1)} %fusion.32), channel_id=1, source_target_pairs={{0,2},{1,3},{2,0},{3,1},{4,6},{5,7},{6,4},{7,5},{8,10},{9,11},{10,... | collective-permute-start | bytes 3145736 | tf_op jit(solution)/shard_map/ppermute | solution.py:382
  183.1 205.2 %reduce-scatter.3.cloned.1.call-start = ((), (), s32[]{:S(2)}) async-start(), calls=%async_computation.4 | async-start | bytes 9437184 | tf_op jit(solution)/shard_map/reduce_scatter | solution.py:518
  189.6 26.0 %collective-permute-start.24 = (f32[2,128]{1,0:T(2,128)S(1)}, f32[2,128]{1,0:T(2,128)S(1)}, u32[]{:S(2)}, u32[]{:S(2)}) collective-permute-start(f32[2,128]{1,0:T(2,128)S(1)} %fusion.70), channel_id=1, source_target_pairs={{0,4},{1,5},{2,6},{3,7},{4,0},{5,1},{6,2},{7,3},{8,12},{9,13},{10,... | collective-permute-start | bytes 3080 | tf_op jit(solution)/shard_map/ppermute | solution.py:362
  299.8 385.5 %reduce-scatter.5.cloned.1.call-start = ((), (), s32[]{:S(2)}) async-start(), calls=%async_computation.5 | async-start | bytes 9437184 | tf_op jit(solution)/shard_map/reduce_scatter | solution.py:536
  315.9 48.1 %collective-permute-start.29 = (bf16[2,512,1024]{2,1,0:T(8,128)(2,1)}, bf16[2,512,1024]{2,1,0:T(8,128)(2,1)}, u32[]{:S(2)}, u32[]{:S(2)}) collective-permute-start(bf16[2,512,1024]{2,1,0:T(8,128)(2,1)} %dynamic-slice_bitcast_fusion), channel_id=1, source_target_pairs={{0,16},{8,24},{16,0},{24,8},{1,17},{9,25},{17,1},{25,9},{2,18},{10... | collective-permute-start | bytes 6291464 | tf_op jit(solution)/shard_map/ppermute | solution.py:382
  332.8 48.4 %collective-permute-start.28 = (bf16[2,256,2048]{2,1,0:T(8,128)(2,1)}, bf16[2,256,2048]{2,1,0:T(8,128)(2,1)}, u32[]{:S(2)}, u32[]{:S(2)}) collective-permute-start(bf16[2,256,2048]{2,1,0:T(8,128)(2,1)} %dynamic-slice_bitcast_fusion.1), channel_id=1, source_target_pairs={{0,8},{8,0},{16,24},{24,16},{1,9},{9,1},{17,25},{25,17},{2,10},{10... | collective-permute-start | bytes 6291464 | tf_op jit(solution)/shard_map/ppermute | solution.py:382
  482.0 57.1 %collective-permute-start.44 = (bf16[256,2048]{1,0:T(8,128)(2,1)S(1)}, bf16[256,2048]{1,0:T(8,128)(2,1)}, u32[]{:S(2)}, u32[]{:S(2)}) collective-permute-start(bf16[256,2048]{1,0:T(8,128)(2,1)S(1)} %fusion.27.refs_0_), channel_id=1, source_target_pairs={{0,16},{8,24},{16,0},{24,8},{1,17},{9,25},{17,1},{25,9},{2,18},{10... | collective-permute-start | bytes 3145736 | tf_op jit(solution)/shard_map/ppermute | solution.py:362
  483.3 55.9 %collective-permute-start.45 = (bf16[256,2048]{1,0:T(8,128)(2,1)}, bf16[256,2048]{1,0:T(8,128)(2,1)}, u32[]{:S(2)}, u32[]{:S(2)}) collective-permute-start(bf16[256,2048]{1,0:T(8,128)(2,1)} %collective-permute-done.38.refs_1_), channel_id=1, source_target_pairs={{0,16},{8,24},{16,0},{24,8},{1,17},{9,25},{17,1},{25,9},{2,18},{10... | collective-permute-start | bytes 3145736 | tf_op jit(solution)/shard_map/ppermute | solution.py:362
  484.1 55.1 %collective-permute-start.46 = (bf16[512,1024]{1,0:T(8,128)(2,1)}, bf16[512,1024]{1,0:T(8,128)(2,1)}, u32[]{:S(2)}, u32[]{:S(2)}) collective-permute-start(bf16[512,1024]{1,0:T(8,128)(2,1)} %fusion.26.refs_0_), channel_id=1, source_target_pairs={{0,8},{8,0},{16,24},{24,16},{1,9},{9,1},{17,25},{25,17},{2,10},{10... | collective-permute-start | bytes 3145736 | tf_op jit(solution)/shard_map/ppermute | solution.py:362
  485.4 53.8 %collective-permute-start.47 = (bf16[512,1024]{1,0:T(8,128)(2,1)}, bf16[512,1024]{1,0:T(8,128)(2,1)}, u32[]{:S(2)}, u32[]{:S(2)}) collective-permute-start(bf16[512,1024]{1,0:T(8,128)(2,1)} %collective-permute-done.39.refs_2_), channel_id=1, source_target_pairs={{0,8},{8,0},{16,24},{24,16},{1,9},{9,1},{17,25},{25,17},{2,10},{10... | collective-permute-start | bytes 3145736 | tf_op jit(solution)/shard_map/ppermute | solution.py:362
  496.2 41.0 %collective-permute-start.42 = (bf16[256,1024]{1,0:T(8,128)(2,1)}, bf16[256,1024]{1,0:T(8,128)(2,1)}, u32[]{:S(2)}, u32[]{:S(2)}) collective-permute-start(bf16[256,1024]{1,0:T(8,128)(2,1)} %fusion.46), channel_id=1, source_target_pairs={{0,16},{8,24},{16,0},{24,8},{1,17},{9,25},{17,1},{25,9},{2,18},{10... | collective-permute-start | bytes 1572872 | tf_op jit(solution)/shard_map/ppermute | solution.py:382
  547.3 33.0 %collective-permute-start.48 = (bf16[2,256,2048]{2,1,0:T(8,128)(2,1)}, bf16[2,256,2048]{2,1,0:T(8,128)(2,1)}, u32[]{:S(2)}, u32[]{:S(2)}) collective-permute-start(bf16[2,256,2048]{2,1,0:T(8,128)(2,1)} %share_of.6), channel_id=1, source_target_pairs={{0,1},{1,0},{2,3},{3,2},{4,5},{5,4},{6,7},{7,6},{8,9},{9,8},{10,11... | collective-permute-start | bytes 6291464 | tf_op jit(solution)/shard_map/ppermute | solution.py:440
  548.5 25.9 %collective-permute-start.50 = (bf16[2,256,1024]{2,1,0:T(8,128)(2,1)}, bf16[2,256,1024]{2,1,0:T(8,128)(2,1)}, u32[]{:S(2)}, u32[]{:S(2)}) collective-permute-start(bf16[2,256,1024]{2,1,0:T(8,128)(2,1)} %dynamic-slice_bitcast_fusion.2), channel_id=1, source_target_pairs={{0,16},{8,24},{16,0},{24,8},{1,17},{9,25},{17,1},{25,9},{2,18},{10... | collective-permute-start | bytes 3145736 | tf_op jit(solution)/shard_map/ppermute | solution.py:382
  556.7 39.2 %collective-permute-start.51 = (bf16[256,1024]{1,0:T(8,128)(2,1)}, bf16[256,1024]{1,0:T(8,128)(2,1)S(1)}, u32[]{:S(2)}, u32[]{:S(2)}) collective-permute-start(bf16[256,1024]{1,0:T(8,128)(2,1)} %fusion.37), channel_id=1, source_target_pairs={{0,4},{1,5},{2,6},{3,7},{4,0},{5,1},{6,2},{7,3},{8,12},{9,13},{10,... | collective-permute-start | bytes 1572872 | tf_op jit(solution)/shard_map/ppermute | solution.py:557
  561.7 45.5 %collective-permute-start.52 = (bf16[256,1024]{1,0:T(8,128)(2,1)}, bf16[256,1024]{1,0:T(8,128)(2,1)}, u32[]{:S(2)}, u32[]{:S(2)}) collective-permute-start(bf16[256,1024]{1,0:T(8,128)(2,1)} %fusion.36), channel_id=1, source_target_pairs={{0,4},{1,5},{2,6},{3,7},{4,0},{5,1},{6,2},{7,3},{8,12},{9,13},{10,... | collective-permute-start | bytes 1572872 | tf_op jit(solution)/shard_map/ppermute | solution.py:557
  646.8 28.9 %collective-permute-start.64 = (bf16[256,1024]{1,0:T(8,128)(2,1)}, bf16[256,1024]{1,0:T(8,128)(2,1)}, u32[]{:S(2)}, u32[]{:S(2)}) collective-permute-start(bf16[256,1024]{1,0:T(8,128)(2,1)} %add_convert_fusion.1.refs_4_), channel_id=1, source_target_pairs={{0,8},{8,0},{16,24},{24,16},{1,9},{9,1},{17,25},{25,17},{2,10},{10... | collective-permute-start | bytes 1572872 | tf_op jit(solution)/shard_map/ppermute | solution.py:362
  647.8 27.9 %collective-permute-start.62 = (bf16[256,1024]{1,0:T(8,128)(2,1)}, bf16[256,1024]{1,0:T(8,128)(2,1)}, u32[]{:S(2)}, u32[]{:S(2)}) collective-permute-start(bf16[256,1024]{1,0:T(8,128)(2,1)} %add_convert_fusion.2.refs_0_), channel_id=1, source_target_pairs={{0,16},{8,24},{16,0},{24,8},{1,17},{9,25},{17,1},{25,9},{2,18},{10... | collective-permute-start | bytes 1572872 | tf_op jit(solution)/shard_map/ppermute | solution.py:362
  (111 other events, 1893.2 us)
Sparse Core Ops, SparseCore 0:
  56.2 85.8 all-gather.2
  183.2 85.2 all-gather.4
  299.9 88.3 reduce-scatter.2
  428.9 88.8 reduce-scatter.4

commit v8 on v7

--- a/solution.py
+++ b/solution.py
@@ -209,6 +209,15 @@
                             out_ref[here, :] = value
 
 
+def widen_kernel(both_ref, down_ref, up_ref):
+    rows, width = down_ref.shape[0], up_ref.shape[1]
+    down_ref[...] = both_ref[0, :rows].astype(down_ref.dtype)
+    low = both_ref.shape[1] - rows
+    for group in range(up_ref.shape[0] // low):
+        value = both_ref[0, rows:, group * width : (group + 1) * width]
+        up_ref[group * low : (group + 1) * low] = value.astype(up_ref.dtype)
+
+
 VMEM_LIMIT = 56 * 1024 * 1024
 
 
@@ -280,6 +289,27 @@
         ),
         name="share_of",
     )(side.astype(jnp.int32).reshape(1), *[x for pair in pairs for x in pair])
+
+
+def widen(both, down_rows, up_width):
+    count, rows, dim = both.shape
+    up_rows = (rows - down_rows) * dim // up_width
+    return pl.pallas_call(
+        widen_kernel,
+        grid=(count,),
+        out_shape=[
+            jax.ShapeDtypeStruct((count * down_rows, dim), jnp.float32),
+            jax.ShapeDtypeStruct((count * up_rows, up_width), jnp.float32),
+        ],
+        in_specs=[pl.BlockSpec((1, rows, dim), lambda i: (i, 0, 0))],
+        out_specs=[
+            pl.BlockSpec((down_rows, dim), lambda i: (i, 0)),
+            pl.BlockSpec((up_rows, up_width), lambda i: (i, 0)),
+        ],
+        compiler_params=pltpu.CompilerParams(vmem_limit_bytes=VMEM_LIMIT),
+        cost_estimate=pl.CostEstimate(flops=0, bytes_accessed=24 << 20, transcendentals=0),
+        name="widen",
+    )(both)
 
 
 def weight_grads(x, qkv_grad, g, heads_out, count):
@@ -531,10 +561,12 @@
         grads_one = place_sequence(
             xor_gather(narrow(gate_one[:, None] * middle_grad), "mp", ranks, pair_bits + [1])
         )
-        helds = column_gather(lanes, columns, cut=1)
         grads_one, hidden_share, lanes = lax.optimization_barrier((grads_one, hidden_share, lanes))
-        hidden_branch = wide(lax.psum_scatter(hidden_share, "mp", scatter_dimension=0, tiled=True))
-        layer_output = narrow(middle + gate_two[:, None] * hidden_branch)
+        down_piece, up_piece = lanes
+        groups = dim // cols_local
+        up_wide = jnp.concatenate(jnp.split(up_piece, groups, axis=0), axis=1)
+        both = lax.all_gather(jnp.concatenate([down_piece, up_wide], axis=0), "dp", axis=0)
+        down_sum, up_sum = widen(both, down_piece.shape[0], cols_local)
 
         gate_grad_one = jnp.sum(middle_grad * mixer_branch, axis=1)
         pairs, sent = [], []
@@ -547,27 +579,24 @@
             pairs.append((qkv_grad, weights_in[k]))
             part = weight_grads(inputs_one, qkv_grad, grads_one, heads_out, columns)
             if k:
-                grads_now, part, helds = lax.optimization_barrier((grads_now, part, helds))
+                grads_now, part = lax.optimization_barrier((grads_now, part))
+                hidden_share = after(hidden_share, *part)
                 sent.append(column_scatter(part, columns, column, cut=1))
-        helds, sent = lax.optimization_barrier((helds, sent))
         sent = [[narrow(x) for x in column_scatter(lanes, columns, column, start=1)] for lanes in sent]
-        helds = column_gather(helds, columns, start=1)
-        pairs, sent, helds, _ = lax.optimization_barrier((pairs, sent, helds, part))
+        pairs, sent, part = lax.optimization_barrier((pairs, sent, part))
         there = [
             [lax.ppermute(x, "mp", shift_pairs(ranks, -k * group)) for x in lanes]
             for k, lanes in zip(range(1, sequences)[::-1], sent)
         ]
-        pieces = column_scatter(part, columns, column, cut=1)
-        blocks = core_sum(pairs)
-        blocks, pieces, there = lax.optimization_barrier((blocks, pieces, there))
-        normed_grad_one = chip_sum(blocks)
-        pieces = column_scatter(pieces, columns, column, start=1)
-        down_sum, = place_blocks(helds[:1], column, [(1, dim, jnp.float32, False)])
-        up_sum, = place_blocks(helds[1:], column, [(1, cols_local, jnp.float32, False)])
-        pieces, down_sum, up_sum = lax.optimization_barrier((pieces, down_sum, up_sum))
+        normed_grad_one = chip_sum(core_sum(pairs))
+        pieces = column_scatter(part, columns, column)
         for lanes in there:
             pieces = [p + wide(t) for p, t in zip(pieces, lanes)]
-        spread = column_gather([narrow(p) for p in pieces], columns)
+        spread = column_gather([narrow(p) for p in pieces], columns, cut=1)
+        spread, down_sum, up_sum = lax.optimization_barrier((spread, down_sum, up_sum))
+        spread = column_gather(spread, columns, start=1)
+        hidden_branch = wide(lax.psum_scatter(hidden_share, "mp", scatter_dimension=0, tiled=True))
+        layer_output = narrow(middle + gate_two[:, None] * hidden_branch)
         attention_sum, output_sum = place_blocks(
             spread,
             column,

time: 701 us -> 722 us (1.030)
  waiting for transfers between devices: 286 us -> 318 us
    ppermute x14, waiting for transfers between devices: 107 us -> 153 us  [xor_scatter(): lax.ppermute(narrow(pick(blocks, 1 - side, at)), axis_name, swap_pairs(si...]
    ppermute x2, waiting for transfers between devices: 23.8 us -> 0.01 us  [local(): lax.ppermute(x, 'mp', shift_pairs(ranks, -k * group))]
    ppermute x37 -> x31, waiting for transfers between devices: 52.5 us -> 66.7 us  [xor_gather(): held[far ^ bit] = lax.ppermute(held[far], axis, swap_pairs(size, bit))]
    pallas_call x5 -> x3, Pallas kernels: 24.5 us -> 13.3 us  [place_blocks(): pl.pallas_call(functools.partial(place_kernel, count, [o[1] for o in outs...]
    pallas_call x0 -> x1, Pallas kernels: none -> 9.63 us  [widen(): pl.pallas_call(widen_kernel, grid=(count,), out_shape=[jax.ShapeDtypeStru...]
    ppermute x37 -> x31, starting transfers between devices: 40.1 us -> 33.9 us  [xor_gather(): held[far ^ bit] = lax.ppermute(held[far], axis, swap_pairs(size, bit))]
    add x9 -> x7, other arithmetic: 21.4 us -> 16.4 us  [xor_scatter(): blocks = wide(pick(blocks, side, at)) + wide(got)]
    unnamed x129 -> x123, local copies, waits for them, and re-layouts: 14.1 us -> 16 us
  transfers between devices with their start and end apart: 71 -> 66, of which waited for: 30 -> 30; matrix products, arithmetic and copies ran while one was open for 19% -> 18% of each run, Pallas kernels for 17% -> 16%
where the time goes in v8:
time: 722 us; the launch traced here: 717 us
  waiting for transfers between devices  318 us (44%)
  Pallas kernels  117 us (16%)
  matrix products  95.3 us (13%)
  starting transfers between devices  70.8 us (10%)
  other arithmetic  60.3 us (8%)
  local copies, waits for them, and re-layouts  41.2 us (6%)
  between operations  15.2 us (2%)
    ppermute x14, waiting for transfers between devices, xor_scatter(): lax.ppermute(narrow(pick(blocks, 1 - side, at)), axis_name, swap_pairs(si...  153 us
    dot_general x6, matrix products, product(): lax.dot_general(a, b, ((dims[:1], dims[1:]), ((), ())), preferred_element...  81.1 us
    ppermute x31, waiting for transfers between devices, xor_gather(): held[far ^ bit] = lax.ppermute(held[far], axis, swap_pairs(size, bit))  66.7 us
    all_gather x1, waiting for transfers between devices, local(): inputs_two = lax.all_gather(narrow(normed_two), 'mp', axis=0, tiled=True)  48.6 us
    ppermute x31, starting transfers between devices, xor_gather(): held[far ^ bit] = lax.ppermute(held[far], axis, swap_pairs(size, bit))  33.9 us
    ppermute x4, waiting for transfers between devices, local(): lax.ppermute(x, 'mp', shift_pairs(ranks, k * group))  26.9 us
    pallas_call x2, Pallas kernels, attend_backward(): pl.pallas_call(backward_kernel, out_shape=jax.ShapeDtypeStruct((tokens, 3...  26.1 us
    pallas_call x2, Pallas kernels, attend_forward(): pl.pallas_call(forward_kernel, out_shape=[jax.ShapeDtypeStruct((tokens, 3...  25.3 us
  transfers between devices with their start and end apart: 66, of which 30 were waited for; matrix products, arithmetic and copies ran while one was open for 18% of the time, Pallas kernels for 16%

profile of v8, /device:TPU:0, one launch (start us, length us, event | category | flops | bytes accessed | tf_op | source)
XLA Modules:
  0.0 717.5 jit_solution(16512836698896467738)
XLA Ops:
  28.5 19.5 %collective-permute-done.1.refs_0_ = bf16[256,768]{1,0:T(8,128)(2,1)} collective-permute-done((bf16[256,768]{1,0:T(8,128)(2,1)}, bf16[256,768]{1,0:T(8,128)(2,1)}, u32[]{:S(2)}, u32[]{:S(2)}) %collective-permute-start.1) | collective-permute-done | bytes 393248 | tf_op jit(solution)/shard_map/ppermute | solution.py:499
  67.0 12.8 %attend_forward.2 = (bf16[1024,768]{1,0:T(8,128)(2,1)}, bf16[1024,256]{1,0:T(8,128)(2,1)}, f32[1024,2]{1,0:T(8,128)}) custom-call(bf16[1024,2048]{1,0:T(8,128)(2,1)} %bitcast.212, bf16[2048,768]{1,0:T(8,128)(2,1)} %pad_maximum_fusion.w_ref.refs_3_, f32[1024,128]{1,0:T(8,128)} %get-tuple-element.108.cos_ref, f32[1024,128]{1,0:T(8,128)} %get-tuple-element.109.sin_ref, ...), custom_call_target="tpu_custom_call" | custom-call | flops 3758096384 | bytes 12582912 | tf_op jit(solution)/shard_map/attend_forward/pallas_call | solution.py:231
  85.9 17.4 %collective-permute-done.13.refs_1_ = bf16[256,256]{1,0:T(8,128)(2,1)S(1)} collective-permute-done((bf16[256,256]{1,0:T(8,128)(2,1)S(1)}, bf16[256,256]{1,0:T(8,128)(2,1)S(1)}, u32[]{:S(2)}, u32[]{:S(2)}) %collective-permute-start.13) | collective-permute-done | bytes 131104 | tf_op jit(solution)/shard_map/ppermute | solution.py:392
  117.1 12.5 %attend_forward.3 = (bf16[1024,768]{1,0:T(8,128)(2,1)}, bf16[1024,256]{1,0:T(8,128)(2,1)}, f32[1024,2]{1,0:T(8,128)}) custom-call(bf16[1024,2048]{1,0:T(8,128)(2,1)} %bitcast.213, bf16[2048,768]{1,0:T(8,128)(2,1)} %place_blocks.3.w_ref.refs_1_, f32[1024,128]{1,0:T(8,128)} %get-tuple-element.108.cos_ref, f32[1024,128]{1,0:T(8,128)} %get-tuple-element.109.sin_ref, ...), custom_call_target="tpu_custom_call" | custom-call | flops 3758096384 | bytes 12582912 | tf_op jit(solution)/shard_map/attend_forward/pallas_call | solution.py:231
  158.1 20.5 %collective-permute-done.20 = bf16[256,2048]{1,0:T(8,128)(2,1)} collective-permute-done((bf16[256,2048]{1,0:T(8,128)(2,1)S(1)}, bf16[256,2048]{1,0:T(8,128)(2,1)}, u32[]{:S(2)}, u32[]{:S(2)}) %collective-permute-start.20) | collective-permute-done | bytes 1048608 | tf_op jit(solution)/shard_map/ppermute | solution.py:412
  195.7 15.3 %fusion.88 = f32[2048,1024]{1,0:T(8,128)} fusion(bf16[2048,2048]{1,0:T(8,128)(2,1)} %all-gather.5.cloned.1.call-done, bf16[1024,2048]{1,0:T(8,128)(2,1)} %param.22), kind=kOutput, calls=%fused_computation.207 | convolution fusion | flops 8589934592 | bytes 20971520 | tf_op jit(solution)/shard_map/dot_general | solution.py:94
  220.8 48.6 %all-gather.7.cloned.1.call-done = bf16[2048,2048]{1,0:T(8,128)(2,1)} async-done(((bf16[256,2048]{1,0:T(8,128)(2,1)}), bf16[2048,2048]{1,0:T(8,128)(2,1)}) %all-gather.7.cloned.1.call-update) | async-done | bytes 8388624 | tf_op jit(solution)/shard_map/all_gather | solution.py:535
  269.3 18.4 %multiply_reduce_fusion = (f32[2048]{0:T(1024)S(1)}, bf16[2048,1024]{1,0:T(8,128)(2,1)}, bf16[2048,1024]{1,0:T(8,128)(2,1)S(1)}) fusion(f32[2048,1024]{1,0:T(8,128)} %fusion.88, s32[2048]{0:T(1024)S(1)} %bitcast.257, s32[1024]{0:T(1024)S(1)} %add_multiply_fusion.1, f32[2048]{0:T(1024)S(1)} %bitcast.255, bf16[2048,2048]{1,0:T(8,128)(2,1)} %all-gather.7.cloned.1.call-done, ...), kind=kOutput, calls=%fused_computation.8 | convolution fusion | flops 8617195520 | bytes 29388800 | tf_op jit(solution)/shard_map/dot_general | solution.py:94
  289.7 10.9 %convolution_convert_fusion.1 = bf16[2048,2048]{1,0:T(8,128)(2,1)} fusion(bf16[2048,1024]{1,0:T(8,128)(2,1)S(1)} %get-tuple-element.149, bf16[2048,1024]{1,0:T(8,128)(2,1)S(1)} %copy-done.57), kind=kOutput, calls=%fused_computation.11 | convolution fusion | flops 8594128896 | bytes 16777216 | tf_op jit(solution)/shard_map/dot_general | solution.py:94
  300.7 13.1 %convolution_convert_fusion.2 = bf16[2048,1024]{1,0:T(8,128)(2,1)S(1)} fusion(bf16[2048,2048]{1,0:T(8,128)(2,1)} %all-gather.7.cloned.1.call-done, bf16[2048,1024]{1,0:T(8,128)(2,1)} %copy-done.60), kind=kOutput, calls=%fused_computation.17 | convolution fusion | flops 8592031744 | bytes 16777216 | tf_op jit(solution)/shard_map/dot_general | solution.py:94
  318.5 12.2 %fusion.6 = bf16[1024,2048]{1,0:T(8,128)(2,1)S(1)} fusion(bf16[2048,1024]{1,0:T(8,128)(2,1)S(1)} %copy-done.59, bf16[2048,2048]{1,0:T(8,128)(2,1)} %all-gather.5.cloned.1.call-done, f32[2048]{0:T(1024)S(1)} %bitcast.256), kind=kOutput, calls=%fused_computation.16 | convolution fusion | flops 8604614656 | bytes 16785408 | tf_op jit(solution)/shard_map/dot_general | solution.py:94
  335.9 11.1 %convolution_convert_fusion = bf16[2048,2048]{1,0:T(8,128)(2,1)} fusion(bf16[2048,1024]{1,0:T(8,128)(2,1)S(1)} %copy-done.59, bf16[1024,2048]{1,0:T(8,128)(2,1)S(1)} %copy-done.58), kind=kOutput, calls=%fused_computation.10 | convolution fusion | flops 8594128896 | bytes 16777216 | tf_op jit(solution)/shard_map/dot_general | solution.py:94
  350.3 14.8 %collective-permute-done.29 = bf16[2,512,1024]{2,1,0:T(8,128)(2,1)} collective-permute-done((bf16[2,512,1024]{2,1,0:T(8,128)(2,1)}, bf16[2,512,1024]{2,1,0:T(8,128)(2,1)}, u32[]{:S(2)}, u32[]{:S(2)}) %collective-permute-start.29) | collective-permute-done | bytes 2097184 | tf_op jit(solution)/shard_map/ppermute | solution.py:412
  370.3 12.0 %collective-permute-done.28 = bf16[2,256,2048]{2,1,0:T(8,128)(2,1)} collective-permute-done((bf16[2,256,2048]{2,1,0:T(8,128)(2,1)}, bf16[2,256,2048]{2,1,0:T(8,128)(2,1)}, u32[]{:S(2)}, u32[]{:S(2)}) %collective-permute-start.28) | collective-permute-done | bytes 2097184 | tf_op jit(solution)/shard_map/ppermute | solution.py:412
  402.7 19.3 %collective-permute-done.33 = bf16[256,2048]{1,0:T(8,128)(2,1)S(1)} collective-permute-done((bf16[256,2048]{1,0:T(8,128)(2,1)S(1)}, bf16[256,2048]{1,0:T(8,128)(2,1)S(1)}, u32[]{:S(2)}, u32[]{:S(2)}) %collective-permute-start.33) | collective-permute-done | bytes 1048608 | tf_op jit(solution)/shard_map/ppermute | solution.py:392
  430.3 13.0 %attend_backward.2.q_ref.refs_0_ = bf16[1024,768]{1,0:T(8,128)(2,1)} custom-call(bf16[1024,2048]{1,0:T(8,128)(2,1)} %bitcast.57.g_ref, bf16[2048,256]{1,0:T(8,128)(2,1)} %place_blocks.4.refs_3_.w_ref, bf16[1024,768]{1,0:T(8,128)(2,1)} %get-tuple-element.156.qkv_ref, f32[1024,2]{1,0:T(8,128)} %get-tuple-element.157.log_ref, ...), custom_call_target="tpu_custom_call" | custom-call | flops 2415919104 | bytes 12582912 | tf_op jit(solution)/shard_map/attend_backward/pallas_call | solution.py:253
  443.3 9.2 %weight_grads.2 = (bf16[4,256,1024]{2,1,0:T(8,128)(2,1)}, bf16[4,256,1024]{2,1,0:T(8,128)(2,1)}) custom-call(bf16[1024,2048]{1,0:T(8,128)(2,1)} %bitcast.214, bf16[1024,768]{1,0:T(8,128)(2,1)} %attend_backward.2.q_ref.refs_0_, bf16[1024,2048]{1,0:T(8,128)(2,1)} %bitcast.57.g_ref, bf16[1024,256]{1,0:T(8,128)(2,1)} %get-tuple-element.140.refs_2_.h_ref), custom_call_target="tpu_custom_call" | custom-call | flops 4294967296 | bytes 14680064 | tf_op jit(solution)/shard_map/weight_grads/pallas_call | solution.py:320
  457.1 13.1 %attend_backward.3.q_ref.refs_2_ = bf16[1024,768]{1,0:T(8,128)(2,1)} custom-call(bf16[1024,2048]{1,0:T(8,128)(2,1)} %bitcast.57.g_ref, bf16[2048,256]{1,0:T(8,128)(2,1)} %bitcast.210, bf16[1024,768]{1,0:T(8,128)(2,1)} %get-tuple-element.117.qkv_ref, f32[1024,2]{1,0:T(8,128)} %get-tuple-element.164.log_ref, f32[1024,128]{1,0:T(8,128)} %get-tuple-element.108.cos_ref, ...), custom_call_target="tpu_custom_call" | custom-call | flops 2415919104 | bytes 12582912 | tf_op jit(solution)/shard_map/attend_backward/pallas_call | solution.py:253
  470.2 23.3 %collective-permute-done.39 = bf16[2,256,1024]{2,1,0:T(8,128)(2,1)} collective-permute-done((bf16[2,256,1024]{2,1,0:T(8,128)(2,1)S(1)}, bf16[2,256,1024]{2,1,0:T(8,128)(2,1)}, u32[]{:S(2)}, u32[]{:S(2)}) %collective-permute-start.39) | collective-permute-done | bytes 1048608 | tf_op jit(solution)/shard_map/ppermute | solution.py:412
  507.1 14.2 %collective-permute-done.41 = bf16[256,1024]{1,0:T(8,128)(2,1)S(1)} collective-permute-done((bf16[256,1024]{1,0:T(8,128)(2,1)}, bf16[256,1024]{1,0:T(8,128)(2,1)S(1)}, u32[]{:S(2)}, u32[]{:S(2)}) %collective-permute-start.41) | collective-permute-done | bytes 524320 | tf_op jit(solution)/shard_map/ppermute | solution.py:412
  551.2 14.3 %collective-permute-done.53 = bf16[2,256,1024]{2,1,0:T(8,128)(2,1)S(1)} collective-permute-done((bf16[2,256,1024]{2,1,0:T(8,128)(2,1)}, bf16[2,256,1024]{2,1,0:T(8,128)(2,1)S(1)}, u32[]{:S(2)}, u32[]{:S(2)}) %collective-permute-start.53) | collective-permute-done | bytes 1048608 | tf_op jit(solution)/shard_map/ppermute | solution.py:412
  591.5 44.8 %collective-permute-done.43 = bf16[256,2048]{1,0:T(8,128)(2,1)} collective-permute-done((bf16[256,2048]{1,0:T(8,128)(2,1)}, bf16[256,2048]{1,0:T(8,128)(2,1)}, u32[]{:S(2)}, u32[]{:S(2)}) %collective-permute-start.43) | collective-permute-done | bytes 1048608 | tf_op jit(solution)/shard_map/ppermute | solution.py:412
  665.0 9.6 %widen.1 = (f32[1024,2048]{1,0:T(8,128)}, f32[2048,1024]{1,0:T(8,128)}) custom-call(bf16[4,512,2048]{2,1,0:T(8,128)(2,1)} %bitcast.211), custom_call_target="tpu_custom_call" | custom-call | bytes 25165824 | tf_op jit(solution)/shard_map/widen/pallas_call | solution.py:297
  680.7 9.2 %collective-permute-done.57.refs_2_ = bf16[256,1024]{1,0:T(8,128)(2,1)} collective-permute-done((bf16[256,1024]{1,0:T(8,128)(2,1)}, bf16[256,1024]{1,0:T(8,128)(2,1)}, u32[]{:S(2)}, u32[]{:S(2)}) %collective-permute-start.57) | collective-permute-done | bytes 524320 | tf_op jit(solution)/shard_map/ppermute | solution.py:392
  (369 shorter events, 293.2 us)
Async XLA Ops:
  7.2 173.7 %all-gather.5.cloned.1.call-start = ((), (), s32[]{:S(2)}) async-start(), calls=%async_computation.2 | async-start | bytes 9437184 | tf_op jit(solution)/shard_map/all_gather | solution.py:512
  12.9 43.1 %collective-permute-start = (bf16[256,2048]{1,0:T(8,128)(2,1)S(1)}, bf16[256,2048]{1,0:T(8,128)(2,1)}, u32[]{:S(2)}, u32[]{:S(2)}) collective-permute-start(bf16[256,2048]{1,0:T(8,128)(2,1)S(1)} %fusion.15), channel_id=1, source_target_pairs={{0,2},{1,3},{2,0},{3,1},{4,6},{5,7},{6,4},{7,5},{8,10},{9,11},{10,... | collective-permute-start | bytes 3145736 | tf_op jit(solution)/shard_map/ppermute | solution.py:392
  15.9 32.1 %collective-permute-start.1 = (bf16[256,768]{1,0:T(8,128)(2,1)}, bf16[256,768]{1,0:T(8,128)(2,1)}, u32[]{:S(2)}, u32[]{:S(2)}) collective-permute-start(bf16[256,768]{1,0:T(8,128)(2,1)} %get-tuple-element.103), channel_id=1, source_target_pairs={{0,4},{1,5},{2,6},{3,7},{4,0},{5,1},{6,2},{7,3},{8,12},{9,13},{10,... | collective-permute-start | bytes 1179656 | tf_op jit(solution)/shard_map/ppermute | solution.py:499
  18.5 36.8 %collective-permute-start.2 = (bf16[256,768]{1,0:T(8,128)(2,1)}, bf16[256,768]{1,0:T(8,128)(2,1)}, u32[]{:S(2)}, u32[]{:S(2)}) collective-permute-start(bf16[256,768]{1,0:T(8,128)(2,1)} %get-tuple-element.104), channel_id=1, source_target_pairs={{0,4},{1,5},{2,6},{3,7},{4,0},{5,1},{6,2},{7,3},{8,12},{9,13},{10,... | collective-permute-start | bytes 1179656 | tf_op jit(solution)/shard_map/ppermute | solution.py:499
  56.1 213.3 %all-gather.7.cloned.1.call-start = ((), (), s32[]{:S(2)}) async-start(), calls=%async_computation.3 | async-start | bytes 9437184 | tf_op jit(solution)/shard_map/all_gather | solution.py:535
  80.0 28.4 %collective-permute-start.10 = (bf16[256,768]{1,0:T(8,128)(2,1)}, bf16[256,768]{1,0:T(8,128)(2,1)S(1)}, u32[]{:S(2)}, u32[]{:S(2)}) collective-permute-start(bf16[256,768]{1,0:T(8,128)(2,1)} %collective-permute-done.5.refs_1_), channel_id=1, source_target_pairs={{0,16},{8,24},{16,0},{24,8},{1,17},{9,25},{17,1},{25,9},{2,18},{10... | collective-permute-start | bytes 1179656 | tf_op jit(solution)/shard_map/ppermute | solution.py:392
  81.9 26.4 %collective-permute-start.11 = (bf16[256,768]{1,0:T(8,128)(2,1)}, bf16[256,768]{1,0:T(8,128)(2,1)S(1)}, u32[]{:S(2)}, u32[]{:S(2)}) collective-permute-start(bf16[256,768]{1,0:T(8,128)(2,1)} %collective-permute-done.2.refs_4_), channel_id=1, source_target_pairs={{0,8},{8,0},{16,24},{24,16},{1,9},{9,1},{17,25},{25,17},{2,10},{10... | collective-permute-start | bytes 1179656 | tf_op jit(solution)/shard_map/ppermute | solution.py:392
  147.0 31.6 %collective-permute-start.20 = (bf16[256,2048]{1,0:T(8,128)(2,1)S(1)}, bf16[256,2048]{1,0:T(8,128)(2,1)}, u32[]{:S(2)}, u32[]{:S(2)}) collective-permute-start(bf16[256,2048]{1,0:T(8,128)(2,1)S(1)} %fusion.32), channel_id=1, source_target_pairs={{0,2},{1,3},{2,0},{3,1},{4,6},{5,7},{6,4},{7,5},{8,10},{9,11},{10,... | collective-permute-start | bytes 3145736 | tf_op jit(solution)/shard_map/ppermute | solution.py:412
  184.3 204.9 %reduce-scatter.3.cloned.1.call-start = ((), (), s32[]{:S(2)}) async-start(), calls=%async_computation.4 | async-start | bytes 9437184 | tf_op jit(solution)/shard_map/reduce_scatter | solution.py:548
  300.6 364.4 %all-gather.9.cloned.1.call-start = ((), (), s32[]{:S(2)}) async-start(), calls=%async_computation.6 | async-start | bytes 10485760 | tf_op jit(solution)/shard_map/all_gather | solution.py:568
  317.0 48.1 %collective-permute-start.29 = (bf16[2,512,1024]{2,1,0:T(8,128)(2,1)}, bf16[2,512,1024]{2,1,0:T(8,128)(2,1)}, u32[]{:S(2)}, u32[]{:S(2)}) collective-permute-start(bf16[2,512,1024]{2,1,0:T(8,128)(2,1)} %dynamic-slice_bitcast_fusion), channel_id=1, source_target_pairs={{0,16},{8,24},{16,0},{24,8},{1,17},{9,25},{17,1},{25,9},{2,18},{10... | collective-permute-start | bytes 6291464 | tf_op jit(solution)/shard_map/ppermute | solution.py:412
  333.9 48.4 %collective-permute-start.28 = (bf16[2,256,2048]{2,1,0:T(8,128)(2,1)}, bf16[2,256,2048]{2,1,0:T(8,128)(2,1)}, u32[]{:S(2)}, u32[]{:S(2)}) collective-permute-start(bf16[2,256,2048]{2,1,0:T(8,128)(2,1)} %dynamic-slice_bitcast_fusion.1), channel_id=1, source_target_pairs={{0,8},{8,0},{16,24},{24,16},{1,9},{9,1},{17,25},{25,17},{2,10},{10... | collective-permute-start | bytes 6291464 | tf_op jit(solution)/shard_map/ppermute | solution.py:412
  430.2 275.6 %reduce-scatter.5.cloned.1.call-start = ((), (), s32[]{:S(2)}) async-start(), calls=%async_computation.5 | async-start | bytes 9437184 | tf_op jit(solution)/shard_map/reduce_scatter | solution.py:598
  454.0 39.5 %collective-permute-start.39 = (bf16[2,256,1024]{2,1,0:T(8,128)(2,1)S(1)}, bf16[2,256,1024]{2,1,0:T(8,128)(2,1)}, u32[]{:S(2)}, u32[]{:S(2)}) collective-permute-start(bf16[2,256,1024]{2,1,0:T(8,128)(2,1)S(1)} %dynamic-slice_bitcast_fusion.4), channel_id=1, source_target_pairs={{0,16},{8,24},{16,0},{24,8},{1,17},{9,25},{17,1},{25,9},{2,18},{10... | collective-permute-start | bytes 3145736 | tf_op jit(solution)/shard_map/ppermute | solution.py:412
  455.6 39.5 %collective-permute-start.38 = (bf16[2,256,1024]{2,1,0:T(8,128)(2,1)}, bf16[2,256,1024]{2,1,0:T(8,128)(2,1)S(1)}, u32[]{:S(2)}, u32[]{:S(2)}) collective-permute-start(bf16[2,256,1024]{2,1,0:T(8,128)(2,1)} %dynamic-slice_bitcast_fusion.5), channel_id=1, source_target_pairs={{0,8},{8,0},{16,24},{24,16},{1,9},{9,1},{17,25},{25,17},{2,10},{10... | collective-permute-start | bytes 3145736 | tf_op jit(solution)/shard_map/ppermute | solution.py:412
  531.6 34.3 %collective-permute-start.42 = (bf16[2,256,2048]{2,1,0:T(8,128)(2,1)}, bf16[2,256,2048]{2,1,0:T(8,128)(2,1)}, u32[]{:S(2)}, u32[]{:S(2)}) collective-permute-start(bf16[2,256,2048]{2,1,0:T(8,128)(2,1)} %share_of.6), channel_id=1, source_target_pairs={{0,1},{1,0},{2,3},{3,2},{4,5},{5,4},{6,7},{7,6},{8,9},{9,8},{10,11... | collective-permute-start | bytes 6291464 | tf_op jit(solution)/shard_map/ppermute | solution.py:470
  532.7 32.7 %collective-permute-start.53 = (bf16[2,256,1024]{2,1,0:T(8,128)(2,1)}, bf16[2,256,1024]{2,1,0:T(8,128)(2,1)S(1)}, u32[]{:S(2)}, u32[]{:S(2)}) collective-permute-start(bf16[2,256,1024]{2,1,0:T(8,128)(2,1)} %dynamic-slice_bitcast_fusion.2), channel_id=1, source_target_pairs={{0,16},{8,24},{16,0},{24,8},{1,17},{9,25},{17,1},{25,9},{2,18},{10... | collective-permute-start | bytes 3145736 | tf_op jit(solution)/shard_map/ppermute | solution.py:412
  538.8 43.9 %collective-permute-start.55 = (bf16[256,1024]{1,0:T(8,128)(2,1)}, bf16[256,1024]{1,0:T(8,128)(2,1)}, u32[]{:S(2)}, u32[]{:S(2)}) collective-permute-start(bf16[256,1024]{1,0:T(8,128)(2,1)} %fusion.40), channel_id=1, source_target_pairs={{0,4},{1,5},{2,6},{3,7},{4,0},{5,1},{6,2},{7,3},{8,12},{9,13},{10,... | collective-permute-start | bytes 1572872 | tf_op jit(solution)/shard_map/ppermute | solution.py:588
  542.3 37.6 %collective-permute-start.49 = (bf16[2,256,1024]{2,1,0:T(8,128)(2,1)}, bf16[2,256,1024]{2,1,0:T(8,128)(2,1)}, u32[]{:S(2)}, u32[]{:S(2)}) collective-permute-start(bf16[2,256,1024]{2,1,0:T(8,128)(2,1)} %dynamic-slice_bitcast_fusion.3), channel_id=1, source_target_pairs={{0,8},{8,0},{16,24},{24,16},{1,9},{9,1},{17,25},{25,17},{2,10},{10... | collective-permute-start | bytes 3145736 | tf_op jit(solution)/shard_map/ppermute | solution.py:412
  572.1 64.2 %collective-permute-start.43 = (bf16[256,2048]{1,0:T(8,128)(2,1)}, bf16[256,2048]{1,0:T(8,128)(2,1)}, u32[]{:S(2)}, u32[]{:S(2)}) collective-permute-start(bf16[256,2048]{1,0:T(8,128)(2,1)} %fusion.35), channel_id=1, source_target_pairs={{0,2},{1,3},{2,0},{3,1},{4,6},{5,7},{6,4},{7,5},{8,10},{9,11},{10,... | collective-permute-start | bytes 3145736 | tf_op jit(solution)/shard_map/ppermute | solution.py:412
  577.4 62.4 %collective-permute-start.51 = (bf16[256,1024]{1,0:T(8,128)(2,1)}, bf16[256,1024]{1,0:T(8,128)(2,1)S(1)}, u32[]{:S(2)}, u32[]{:S(2)}) collective-permute-start(bf16[256,1024]{1,0:T(8,128)(2,1)} %fusion.41), channel_id=1, source_target_pairs={{0,4},{1,5},{2,6},{3,7},{4,0},{5,1},{6,2},{7,3},{8,12},{9,13},{10,... | collective-permute-start | bytes 1572872 | tf_op jit(solution)/shard_map/ppermute | solution.py:588
  582.1 57.7 %collective-permute-start.50 = (bf16[256,1024]{1,0:T(8,128)(2,1)S(1)}, bf16[256,1024]{1,0:T(8,128)(2,1)S(1)}, u32[]{:S(2)}, u32[]{:S(2)}) collective-permute-start(bf16[256,1024]{1,0:T(8,128)(2,1)S(1)} %fusion.52), channel_id=1, source_target_pairs={{0,16},{8,24},{16,0},{24,8},{1,17},{9,25},{17,1},{25,9},{2,18},{10... | collective-permute-start | bytes 1572872 | tf_op jit(solution)/shard_map/ppermute | solution.py:412
  591.0 83.6 %collective-permute-start.56 = (bf16[256,1024]{1,0:T(8,128)(2,1)}, bf16[256,1024]{1,0:T(8,128)(2,1)}, u32[]{:S(2)}, u32[]{:S(2)}) collective-permute-start(bf16[256,1024]{1,0:T(8,128)(2,1)} %fusion.37.refs_4_), channel_id=1, source_target_pairs={{0,16},{8,24},{16,0},{24,8},{1,17},{9,25},{17,1},{25,9},{2,18},{10... | collective-permute-start | bytes 1572872 | tf_op jit(solution)/shard_map/ppermute | solution.py:392
  640.8 33.8 %collective-permute-start.52 = (bf16[256,1024]{1,0:T(8,128)(2,1)}, bf16[256,1024]{1,0:T(8,128)(2,1)}, u32[]{:S(2)}, u32[]{:S(2)}) collective-permute-start(bf16[256,1024]{1,0:T(8,128)(2,1)} %fusion.39.refs_0_), channel_id=1, source_target_pairs={{0,8},{8,0},{16,24},{24,16},{1,9},{9,1},{17,25},{25,17},{2,10},{10... | collective-permute-start | bytes 1572872 | tf_op jit(solution)/shard_map/ppermute | solution.py:392
  (103 other events, 1780.2 us)
Sparse Core Ops, SparseCore 0:
  56.2 86.3 all-gather.4
  184.4 84.8 all-gather.6
  300.7 88.3 reduce-scatter.2
  430.4 119.7 all-gather.8
  552.3 126.3 reduce-scatter.4

commit v9 on v7

--- a/solution.py
+++ b/solution.py
@@ -407,6 +407,25 @@
     ]
 
 
+def first_scatter(x, size, column):
+    count = len(bits_of(size))
+    view = x.reshape((2,) * count + x.shape[1:])
+    out = []
+    for lane, bits in enumerate(lane_bits(size)):
+        at = count - 1 - bits_of(size).index(bits[0])
+        sizes = tuple(1 if d in (at, count) else n for d, n in enumerate(view.shape))
+        side = (column // bits[0]) % 2
+
+        def half(which):
+            starts = [0] * view.ndim
+            starts[at], starts[count] = which, lane
+            return lax.dynamic_slice(view, starts, sizes).reshape((-1,) + x.shape[2:])
+
+        got = lax.ppermute(half(1 - side), "dp", swap_pairs(size, bits[0]))
+        out.append(wide(half(side)) + wide(got))
+    return out
+
+
 def all_sum(x, sizes):
     for axis, size in sizes.items():
         for bit in bits_of(size):
@@ -518,21 +537,28 @@
         normed_grad_two = wide(lax.psum_scatter(share, "mp", scatter_dimension=0, tiled=True))
         gate_grad_two = lax.dynamic_slice_in_dim(all_sum(dots, {"mp": ranks}).reshape(-1), rank * rows, rows, 0)
         gated = narrow(gates[:, None] * wide(grads_all))
-        lanes = [narrow(product(hidden, gated, (0, 0))), narrow(product(inputs_two, pre_grad, (0, 0)))]
-        lanes = [x.reshape(columns, -1, x.shape[1]) for x in lanes]
-        lanes = column_scatter(lanes, columns, column, cut=1)
+        up_lanes, down_lanes = [
+            first_scatter(narrow(product(a, b, (0, 0))).reshape(columns, 2, -1, b.shape[1]), columns, column)
+            for a, b in ((inputs_two, pre_grad), (hidden, gated))
+        ]
         hidden_share = narrow(product(hidden, down_weight, (1, 0)))
-        normed_grad_two, hidden_share, *lanes = lax.optimization_barrier((normed_grad_two, hidden_share, *lanes))
-        lanes = [narrow(x) for x in column_scatter(lanes, columns, column, start=1)]
+        up_lanes, hidden_share = lax.optimization_barrier((up_lanes, hidden_share))
+        up_lanes = [narrow(x) for x in column_scatter(up_lanes, columns, column, start=1)]
+        normed_grad_two, hidden_share, up_lanes, down_lanes = lax.optimization_barrier(
+            (normed_grad_two, hidden_share, up_lanes, down_lanes)
+        )
+        down_lanes = [narrow(x) for x in column_scatter(down_lanes, columns, column, start=1)]
+        up_held = column_gather(up_lanes, columns, cut=1)
 
         router_part, router_two = gate_backward(normed_two, hidden_router, state_two, gate_grad_two)
         middle_part, gain_two = norm_backward(normed_grad_two + router_part, scaled_two, inverse_two, hidden_gain)
         middle_grad = wide(out_grad) + middle_part
-        grads_one = place_sequence(
-            xor_gather(narrow(gate_one[:, None] * middle_grad), "mp", ranks, pair_bits + [1])
-        )
-        helds = column_gather(lanes, columns, cut=1)
-        grads_one, hidden_share, lanes = lax.optimization_barrier((grads_one, hidden_share, lanes))
+        held = xor_gather(narrow(gate_one[:, None] * middle_grad), "mp", ranks, pair_bits)
+        held, down_lanes, up_held = lax.optimization_barrier((held, down_lanes, up_held))
+        down_held = column_gather(down_lanes, columns, cut=1)
+        up_held = column_gather(up_held, columns, start=1)
+        grads_one = place_sequence(xor_gather(held, "mp", ranks, [1]))
+        grads_one, hidden_share = lax.optimization_barrier((grads_one, hidden_share))
         hidden_branch = wide(lax.psum_scatter(hidden_share, "mp", scatter_dimension=0, tiled=True))
         layer_output = narrow(middle + gate_two[:, None] * hidden_branch)
 
@@ -542,31 +568,22 @@
         for k in range(sequences)[::-1]:
             qkv, heads_out, log_total, mask = kept[k]
             qkv_grad = attend_backward(grads_now, weights_out[k], qkv, log_total, cos, sin, mask)
-            if sent:
-                qkv_grad, sent[-1] = lax.optimization_barrier((qkv_grad, sent[-1]))
             pairs.append((qkv_grad, weights_in[k]))
+            if k == 0:
+                down_held = column_gather(down_held, columns, start=1)
+                sent, qkv_grad = lax.optimization_barrier((sent, qkv_grad))
             part = weight_grads(inputs_one, qkv_grad, grads_one, heads_out, columns)
             if k:
-                grads_now, part, helds = lax.optimization_barrier((grads_now, part, helds))
+                grads_now, part, up_held, down_held = lax.optimization_barrier((grads_now, part, up_held, down_held))
                 sent.append(column_scatter(part, columns, column, cut=1))
-        helds, sent = lax.optimization_barrier((helds, sent))
+        pairs, part = lax.optimization_barrier((pairs, part))
+        blocks, down_held = lax.optimization_barrier((core_sum(pairs), down_held))
+        normed_grad_one = chip_sum(blocks)
+        pieces = column_scatter(part, columns, column)
         sent = [[narrow(x) for x in column_scatter(lanes, columns, column, start=1)] for lanes in sent]
-        helds = column_gather(helds, columns, start=1)
-        pairs, sent, helds, _ = lax.optimization_barrier((pairs, sent, helds, part))
-        there = [
-            [lax.ppermute(x, "mp", shift_pairs(ranks, -k * group)) for x in lanes]
-            for k, lanes in zip(range(1, sequences)[::-1], sent)
-        ]
-        pieces = column_scatter(part, columns, column, cut=1)
-        blocks = core_sum(pairs)
-        blocks, pieces, there = lax.optimization_barrier((blocks, pieces, there))
-        normed_grad_one = chip_sum(blocks)
-        pieces = column_scatter(pieces, columns, column, start=1)
-        down_sum, = place_blocks(helds[:1], column, [(1, dim, jnp.float32, False)])
-        up_sum, = place_blocks(helds[1:], column, [(1, cols_local, jnp.float32, False)])
-        pieces, down_sum, up_sum = lax.optimization_barrier((pieces, down_sum, up_sum))
-        for lanes in there:
-            pieces = [p + wide(t) for p, t in zip(pieces, lanes)]
+        for k, lanes in zip(range(1, sequences)[::-1], sent):
+            back = shift_pairs(ranks, -k * group)
+            pieces = [p + wide(lax.ppermute(x, "mp", back)) for p, x in zip(pieces, lanes)]
         spread = column_gather([narrow(p) for p in pieces], columns)
         attention_sum, output_sum = place_blocks(
             spread,
@@ -582,7 +599,14 @@
         sizes = {"mp": ranks, "dp": columns}
 
         smalls = [gain_two, gain_one, router_two.T, router_one.T]
-        small_sum = all_sum(jnp.concatenate([x.reshape(-1, 128) for x in smalls], axis=0), sizes)
+        small = jnp.concatenate([x.reshape(-1, 128) for x in smalls], axis=0)
+        *steps, last = [(axis, size, bit) for axis, size in sizes.items() for bit in bits_of(size)]
+        for axis, size, bit in steps:
+            small = small + lax.ppermute(small, axis, swap_pairs(size, bit))
+        small, down_held, up_held = lax.optimization_barrier((small, down_held, up_held))
+        small_sum = small + lax.ppermute(small, last[0], swap_pairs(*last[1:]))
+        down_sum, = place_blocks(down_held, column, [(1, dim, jnp.float32, False)])
+        up_sum, = place_blocks(up_held, column, [(1, cols_local, jnp.float32, False)])
         cuts = [dim // 128, 2 * dim // 128, (2 * dim + router_two.size) // 128]
         hidden_gain_sum, mixer_gain_sum, hidden_router_sum, mixer_router_sum = (
             x.reshape(-1, dim) for x in jnp.split(small_sum, cuts)

time: 701 us -> 708 us (level)
  other arithmetic: 64.8 us -> 53.8 us
  waiting for transfers between devices: 286 us -> 296 us
    ppermute x2 -> x11, waiting for transfers between devices: 23.8 us -> 64.8 us  [the longest x4 31.4 us: first_scatter(): got = lax.ppermute(half(1 - side), 'dp', swap_pairs(size, bits[0]))]
    ppermute x14, waiting for transfers between devices: 107 us -> 67.8 us  [xor_scatter(): lax.ppermute(narrow(pick(blocks, 1 - side, at)), axis_name, swap_pairs(si...]
    ppermute x37 -> x43, waiting for transfers between devices: 52.5 us -> 79.9 us  [xor_gather(): held[far ^ bit] = lax.ppermute(held[far], axis, swap_pairs(size, bit))]
    ppermute x8 -> x3, waiting for transfers between devices: 24.2 us -> 6.85 us  [all_sum(): x = x + lax.ppermute(x, axis, swap_pairs(size, bit))]
    add x9 -> x5, other arithmetic: 21.4 us -> 6.13 us  [xor_scatter(): blocks = wide(pick(blocks, side, at)) + wide(got)]
    ppermute x37 -> x43, starting transfers between devices: 40.1 us -> 47 us  [xor_gather(): held[far ^ bit] = lax.ppermute(held[far], axis, swap_pairs(size, bit))]
    unnamed x129 -> x151, local copies, waits for them, and re-layouts: 14.1 us -> 16.2 us
    convert_element_type x9 -> x12, other arithmetic: 15 us -> 14.3 us  [narrow(): return x.astype(jnp.bfloat16)]
  transfers between devices with their start and end apart: 71 -> 81, of which waited for: 30 -> 34; matrix products, arithmetic and copies ran while one was open for 19% -> 18% of each run, Pallas kernels for 17% -> 17%
where the time goes in v9:
time: 708 us; the launch traced here: 704 us
  waiting for transfers between devices  296 us (42%)
  Pallas kernels  118 us (17%)
  matrix products  95.4 us (13%)
  starting transfers between devices  80.6 us (11%)
  other arithmetic  53.8 us (8%)
  local copies, waits for them, and re-layouts  43.7 us (6%)
  between operations  15.4 us (2%)
    dot_general x6, matrix products, product(): lax.dot_general(a, b, ((dims[:1], dims[1:]), ((), ())), preferred_element...  82.5 us
    ppermute x43, waiting for transfers between devices, xor_gather(): held[far ^ bit] = lax.ppermute(held[far], axis, swap_pairs(size, bit))  79.9 us
    ppermute x14, waiting for transfers between devices, xor_scatter(): lax.ppermute(narrow(pick(blocks, 1 - side, at)), axis_name, swap_pairs(si...  67.8 us
    all_gather x1, waiting for transfers between devices, local(): inputs_two = lax.all_gather(narrow(normed_two), 'mp', axis=0, tiled=True)  49.7 us
    ppermute x43, starting transfers between devices, xor_gather(): held[far ^ bit] = lax.ppermute(held[far], axis, swap_pairs(size, bit))  47 us
    ppermute x4, waiting for transfers between devices, first_scatter(): got = lax.ppermute(half(1 - side), 'dp', swap_pairs(size, bits[0]))  31.4 us
    ppermute x4, waiting for transfers between devices, local(): lax.ppermute(x, 'mp', shift_pairs(ranks, k * group))  27.2 us
    pallas_call x2, Pallas kernels, attend_backward(): pl.pallas_call(backward_kernel, out_shape=jax.ShapeDtypeStruct((tokens, 3...  26.4 us
  transfers between devices with their start and end apart: 81, of which 34 were waited for; matrix products, arithmetic and copies ran while one was open for 18% of the time, Pallas kernels for 17%

profile of v9, /device:TPU:0, one launch (start us, length us, event | category | flops | bytes accessed | tf_op | source)
XLA Modules:
  0.0 703.6 jit_solution(15776848601082734721)
XLA Ops:
  29.7 19.9 %collective-permute-done.1.refs_0_ = bf16[256,768]{1,0:T(8,128)(2,1)} collective-permute-done((bf16[256,768]{1,0:T(8,128)(2,1)}, bf16[256,768]{1,0:T(8,128)(2,1)}, u32[]{:S(2)}, u32[]{:S(2)}) %collective-permute-start.1) | collective-permute-done | bytes 393248 | tf_op jit(solution)/shard_map/ppermute | solution.py:488
  68.4 12.8 %attend_forward.2 = (bf16[1024,768]{1,0:T(8,128)(2,1)}, bf16[1024,256]{1,0:T(8,128)(2,1)}, f32[1024,2]{1,0:T(8,128)}) custom-call(bf16[1024,2048]{1,0:T(8,128)(2,1)} %bitcast.244, bf16[2048,768]{1,0:T(8,128)(2,1)} %pad_maximum_fusion.w_ref.refs_3_, f32[1024,128]{1,0:T(8,128)} %get-tuple-element.146.cos_ref, f32[1024,128]{1,0:T(8,128)} %get-tuple-element.147.sin_ref, ...), custom_call_target="tpu_custom_call" | custom-call | flops 3758096384 | bytes 12582912 | tf_op jit(solution)/shard_map/attend_forward/pallas_call | solution.py:222
  87.1 18.3 %collective-permute-done.13.refs_1_ = bf16[256,256]{1,0:T(8,128)(2,1)S(1)} collective-permute-done((bf16[256,256]{1,0:T(8,128)(2,1)S(1)}, bf16[256,256]{1,0:T(8,128)(2,1)S(1)}, u32[]{:S(2)}, u32[]{:S(2)}) %collective-permute-start.13) | collective-permute-done | bytes 131104 | tf_op jit(solution)/shard_map/ppermute | solution.py:362
  118.9 12.5 %attend_forward.3 = (bf16[1024,768]{1,0:T(8,128)(2,1)}, bf16[1024,256]{1,0:T(8,128)(2,1)}, f32[1024,2]{1,0:T(8,128)}) custom-call(bf16[1024,2048]{1,0:T(8,128)(2,1)} %bitcast.245, bf16[2048,768]{1,0:T(8,128)(2,1)} %place_blocks.5.w_ref.refs_1_, f32[1024,128]{1,0:T(8,128)} %get-tuple-element.146.cos_ref, f32[1024,128]{1,0:T(8,128)} %get-tuple-element.147.sin_ref, ...), custom_call_target="tpu_custom_call" | custom-call | flops 3758096384 | bytes 12582912 | tf_op jit(solution)/shard_map/attend_forward/pallas_call | solution.py:222
  159.0 20.5 %collective-permute-done.20 = bf16[256,2048]{1,0:T(8,128)(2,1)} collective-permute-done((bf16[256,2048]{1,0:T(8,128)(2,1)S(1)}, bf16[256,2048]{1,0:T(8,128)(2,1)}, u32[]{:S(2)}, u32[]{:S(2)}) %collective-permute-start.20) | collective-permute-done | bytes 1048608 | tf_op jit(solution)/shard_map/ppermute | solution.py:382
  196.8 15.7 %fusion.91 = f32[2048,1024]{1,0:T(8,128)} fusion(bf16[2048,2048]{1,0:T(8,128)(2,1)} %all-gather.3.cloned.1.call-done, bf16[1024,2048]{1,0:T(8,128)(2,1)} %param.22), kind=kOutput, calls=%fused_computation.217 | convolution fusion | flops 8589934592 | bytes 20971520 | tf_op jit(solution)/shard_map/dot_general | solution.py:94
  221.5 49.7 %all-gather.5.cloned.1.call-done = bf16[2048,2048]{1,0:T(8,128)(2,1)} async-done(((bf16[256,2048]{1,0:T(8,128)(2,1)}), bf16[2048,2048]{1,0:T(8,128)(2,1)}) %all-gather.5.cloned.1.call-update) | async-done | bytes 8388624 | tf_op jit(solution)/shard_map/all_gather | solution.py:524
  271.2 18.2 %multiply_reduce_fusion = (f32[2048]{0:T(1024)S(1)}, bf16[2048,1024]{1,0:T(8,128)(2,1)}, bf16[2048,1024]{1,0:T(8,128)(2,1)S(1)}) fusion(f32[2048,1024]{1,0:T(8,128)} %fusion.91, s32[2048]{0:T(1024)S(1)} %bitcast.285, s32[1024]{0:T(1024)S(1)} %add_multiply_fusion.1, f32[2048]{0:T(1024)S(1)} %bitcast.283, bf16[2048,2048]{1,0:T(8,128)(2,1)} %all-gather.5.cloned.1.call-done, ...), kind=kOutput, calls=%fused_computation.8 | convolution fusion | flops 8617195520 | bytes 29388800 | tf_op jit(solution)/shard_map/dot_general | solution.py:94
  291.5 10.9 %convolution_convert_fusion.1 = bf16[2048,2048]{1,0:T(8,128)(2,1)} fusion(bf16[2048,1024]{1,0:T(8,128)(2,1)S(1)} %get-tuple-element.186, bf16[2048,1024]{1,0:T(8,128)(2,1)S(1)} %copy-done.71), kind=kOutput, calls=%fused_computation.11 | convolution fusion | flops 8594128896 | bytes 16777216 | tf_op jit(solution)/shard_map/dot_general | solution.py:94
  302.5 13.0 %convolution_convert_fusion.2 = bf16[2048,1024]{1,0:T(8,128)(2,1)S(1)} fusion(bf16[2048,2048]{1,0:T(8,128)(2,1)} %all-gather.5.cloned.1.call-done, bf16[2048,1024]{1,0:T(8,128)(2,1)} %copy-done.74), kind=kOutput, calls=%fused_computation.15 | convolution fusion | flops 8592031744 | bytes 16777216 | tf_op jit(solution)/shard_map/dot_general | solution.py:94
  320.1 11.0 %convolution_convert_fusion = bf16[2048,2048]{1,0:T(8,128)(2,1)} fusion(bf16[2048,1024]{1,0:T(8,128)(2,1)S(1)} %copy-done.73, bf16[1024,2048]{1,0:T(8,128)(2,1)S(1)} %copy-done.72), kind=kOutput, calls=%fused_computation.10 | convolution fusion | flops 8594128896 | bytes 16777216 | tf_op jit(solution)/shard_map/dot_general | solution.py:94
  331.1 13.7 %fusion.6 = bf16[1024,2048]{1,0:T(8,128)(2,1)S(1)} fusion(bf16[2048,1024]{1,0:T(8,128)(2,1)} %get-tuple-element.187, bf16[2048,2048]{1,0:T(8,128)(2,1)} %all-gather.3.cloned.1.call-done, f32[2048]{0:T(1024)S(1)} %bitcast.284), kind=kOutput, calls=%fused_computation.14 | convolution fusion | flops 8604614656 | bytes 16785408 | tf_op jit(solution)/shard_map/dot_general | solution.py:94
  358.7 12.2 %collective-permute-done.28 = bf16[2,256,1024]{2,1,0:T(8,128)(2,1)S(1)} collective-permute-done((bf16[2,256,1024]{2,1,0:T(8,128)(2,1)S(1)}, bf16[2,256,1024]{2,1,0:T(8,128)(2,1)S(1)}, u32[]{:S(2)}, u32[]{:S(2)}) %collective-permute-start.28) | collective-permute-done | bytes 1048608 | tf_op jit(solution)/shard_map/ppermute | solution.py:424
  377.3 16.1 %collective-permute-done.32 = bf16[2,128,2048]{2,1,0:T(8,128)(2,1)S(1)} collective-permute-done((bf16[2,128,2048]{2,1,0:T(8,128)(2,1)S(1)}, bf16[2,128,2048]{2,1,0:T(8,128)(2,1)S(1)}, u32[]{:S(2)}, u32[]{:S(2)}) %collective-permute-start.32) | collective-permute-done | bytes 1048608 | tf_op jit(solution)/shard_map/ppermute | solution.py:424
  451.4 9.2 %collective-permute-done.44.refs_2_ = bf16[256,1024]{1,0:T(8,128)(2,1)S(1)} collective-permute-done((bf16[256,1024]{1,0:T(8,128)(2,1)S(1)}, bf16[256,1024]{1,0:T(8,128)(2,1)S(1)}, u32[]{:S(2)}, u32[]{:S(2)}) %collective-permute-start.44) | collective-permute-done | bytes 524320 | tf_op jit(solution)/shard_map/ppermute | solution.py:362
  462.9 13.2 %attend_backward.2.q_ref.refs_0_ = bf16[1024,768]{1,0:T(8,128)(2,1)} custom-call(bf16[1024,2048]{1,0:T(8,128)(2,1)} %bitcast.69.g_ref, bf16[2048,256]{1,0:T(8,128)(2,1)} %place_blocks.6.refs_3_.w_ref, bf16[1024,768]{1,0:T(8,128)(2,1)} %get-tuple-element.201.qkv_ref, f32[1024,2]{1,0:T(8,128)} %get-tuple-element.202.log_ref, ...), custom_call_target="tpu_custom_call" | custom-call | flops 2415919104 | bytes 12582912 | tf_op jit(solution)/shard_map/attend_backward/pallas_call | solution.py:244
  476.1 8.9 %weight_grads.2 = (bf16[4,256,1024]{2,1,0:T(8,128)(2,1)}, bf16[4,256,1024]{2,1,0:T(8,128)(2,1)}) custom-call(bf16[1024,2048]{1,0:T(8,128)(2,1)} %bitcast.246, bf16[1024,768]{1,0:T(8,128)(2,1)} %attend_backward.2.q_ref.refs_0_, bf16[1024,2048]{1,0:T(8,128)(2,1)} %bitcast.69.g_ref, bf16[1024,256]{1,0:T(8,128)(2,1)} %get-tuple-element.178.refs_2_.h_ref), custom_call_target="tpu_custom_call" | custom-call | flops 4294967296 | bytes 14680064 | tf_op jit(solution)/shard_map/weight_grads/pallas_call | solution.py:290
  493.4 13.2 %attend_backward.3.q_ref.refs_2_ = bf16[1024,768]{1,0:T(8,128)(2,1)} custom-call(bf16[1024,2048]{1,0:T(8,128)(2,1)} %bitcast.69.g_ref, bf16[2048,256]{1,0:T(8,128)(2,1)} %bitcast.237, bf16[1024,768]{1,0:T(8,128)(2,1)} %get-tuple-element.155.qkv_ref, f32[1024,2]{1,0:T(8,128)} %get-tuple-element.212.log_ref, f32[1024,128]{1,0:T(8,128)} %get-tuple-element.146.cos_ref, ...), custom_call_target="tpu_custom_call" | custom-call | flops 2415919104 | bytes 12582912 | tf_op jit(solution)/shard_map/attend_backward/pallas_call | solution.py:244
  514.8 8.9 %weight_grads.3 = (bf16[4,256,1024]{2,1,0:T(8,128)(2,1)}, bf16[4,256,1024]{2,1,0:T(8,128)(2,1)}) custom-call(bf16[1024,2048]{1,0:T(8,128)(2,1)} %bitcast.247, bf16[1024,768]{1,0:T(8,128)(2,1)} %attend_backward.3.q_ref.refs_2_, bf16[1024,2048]{1,0:T(8,128)(2,1)} %bitcast.69.g_ref, bf16[1024,256]{1,0:T(8,128)(2,1)} %get-tuple-element.176.refs_0_.h_ref), custom_call_target="tpu_custom_call" | custom-call | flops 4294967296 | bytes 14680064 | tf_op jit(solution)/shard_map/weight_grads/pallas_call | solution.py:290
  550.7 21.7 %collective-permute-done.72 = bf16[256,1024]{1,0:T(8,128)(2,1)} collective-permute-done((bf16[256,1024]{1,0:T(8,128)(2,1)}, bf16[256,1024]{1,0:T(8,128)(2,1)}, u32[]{:S(2)}, u32[]{:S(2)}) %collective-permute-start.72) | collective-permute-done | bytes 524320 | tf_op jit(solution)/shard_map/ppermute | solution.py:382
  582.1 10.0 %collective-permute-done.54.refs_3_ = bf16[128,2048]{1,0:T(8,128)(2,1)S(1)} collective-permute-done((bf16[128,2048]{1,0:T(8,128)(2,1)}, bf16[128,2048]{1,0:T(8,128)(2,1)S(1)}, u32[]{:S(2)}, u32[]{:S(2)}) %collective-permute-start.54) | collective-permute-done | bytes 524320 | tf_op jit(solution)/shard_map/ppermute | solution.py:362
  602.5 14.8 %collective-permute-done.66 = bf16[256,1024]{1,0:T(8,128)(2,1)S(1)} collective-permute-done((bf16[256,1024]{1,0:T(8,128)(2,1)S(1)}, bf16[256,1024]{1,0:T(8,128)(2,1)S(1)}, u32[]{:S(2)}, u32[]{:S(2)}) %collective-permute-start.66) | collective-permute-done | bytes 524320 | tf_op jit(solution)/shard_map/ppermute | solution.py:586
  619.1 9.3 %collective-permute-done.73 = bf16[256,1024]{1,0:T(8,128)(2,1)S(1)} collective-permute-done((bf16[256,1024]{1,0:T(8,128)(2,1)S(1)}, bf16[256,1024]{1,0:T(8,128)(2,1)S(1)}, u32[]{:S(2)}, u32[]{:S(2)}) %collective-permute-start.73) | collective-permute-done | bytes 524320 | tf_op jit(solution)/shard_map/ppermute | solution.py:586
  656.5 9.4 %collective-permute-done.69.refs_3_ = bf16[256,1024]{1,0:T(8,128)(2,1)S(1)} collective-permute-done((bf16[256,1024]{1,0:T(8,128)(2,1)}, bf16[256,1024]{1,0:T(8,128)(2,1)S(1)}, u32[]{:S(2)}, u32[]{:S(2)}) %collective-permute-start.69) | collective-permute-done | bytes 524320 | tf_op jit(solution)/shard_map/ppermute | solution.py:362
  (432 shorter events, 325.1 us)
Async XLA Ops:
  7.2 174.6 %all-gather.3.cloned.1.call-start = ((), (), s32[]{:S(2)}) async-start(), calls=%async_computation.2 | async-start | bytes 9437184 | tf_op jit(solution)/shard_map/all_gather | solution.py:501
  14.5 43.1 %collective-permute-start = (bf16[256,2048]{1,0:T(8,128)(2,1)S(1)}, bf16[256,2048]{1,0:T(8,128)(2,1)}, u32[]{:S(2)}, u32[]{:S(2)}) collective-permute-start(bf16[256,2048]{1,0:T(8,128)(2,1)S(1)} %fusion.15), channel_id=1, source_target_pairs={{0,2},{1,3},{2,0},{3,1},{4,6},{5,7},{6,4},{7,5},{8,10},{9,11},{10,... | collective-permute-start | bytes 3145736 | tf_op jit(solution)/shard_map/ppermute | solution.py:362
  17.5 32.1 %collective-permute-start.1 = (bf16[256,768]{1,0:T(8,128)(2,1)}, bf16[256,768]{1,0:T(8,128)(2,1)}, u32[]{:S(2)}, u32[]{:S(2)}) collective-permute-start(bf16[256,768]{1,0:T(8,128)(2,1)} %get-tuple-element.141), channel_id=1, source_target_pairs={{0,4},{1,5},{2,6},{3,7},{4,0},{5,1},{6,2},{7,3},{8,12},{9,13},{10,... | collective-permute-start | bytes 1179656 | tf_op jit(solution)/shard_map/ppermute | solution.py:488
  20.1 36.8 %collective-permute-start.2 = (bf16[256,768]{1,0:T(8,128)(2,1)}, bf16[256,768]{1,0:T(8,128)(2,1)}, u32[]{:S(2)}, u32[]{:S(2)}) collective-permute-start(bf16[256,768]{1,0:T(8,128)(2,1)} %get-tuple-element.142), channel_id=1, source_target_pairs={{0,4},{1,5},{2,6},{3,7},{4,0},{5,1},{6,2},{7,3},{8,12},{9,13},{10,... | collective-permute-start | bytes 1179656 | tf_op jit(solution)/shard_map/ppermute | solution.py:488
  57.6 213.6 %all-gather.5.cloned.1.call-start = ((), (), s32[]{:S(2)}) async-start(), calls=%async_computation.3 | async-start | bytes 9437184 | tf_op jit(solution)/shard_map/all_gather | solution.py:524
  148.8 30.8 %collective-permute-start.20 = (bf16[256,2048]{1,0:T(8,128)(2,1)S(1)}, bf16[256,2048]{1,0:T(8,128)(2,1)}, u32[]{:S(2)}, u32[]{:S(2)}) collective-permute-start(bf16[256,2048]{1,0:T(8,128)(2,1)S(1)} %fusion.30), channel_id=1, source_target_pairs={{0,2},{1,3},{2,0},{3,1},{4,6},{5,7},{6,4},{7,5},{8,10},{9,11},{10,... | collective-permute-start | bytes 3145736 | tf_op jit(solution)/shard_map/ppermute | solution.py:382
  185.1 219.3 %reduce-scatter.3.cloned.1.call-start = ((), (), s32[]{:S(2)}) async-start(), calls=%async_computation.4 | async-start | bytes 9437184 | tf_op jit(solution)/shard_map/reduce_scatter | solution.py:537
  302.4 389.5 %reduce-scatter.5.cloned.1.call-start = ((), (), s32[]{:S(2)}) async-start(), calls=%async_computation.5 | async-start | bytes 9437184 | tf_op jit(solution)/shard_map/reduce_scatter | solution.py:562
  318.6 40.1 %collective-permute-start.29 = (bf16[2,256,1024]{2,1,0:T(8,128)(2,1)}, bf16[2,256,1024]{2,1,0:T(8,128)(2,1)S(1)}, u32[]{:S(2)}, u32[]{:S(2)}) collective-permute-start(bf16[2,256,1024]{2,1,0:T(8,128)(2,1)} %dynamic-slice_bitcast_fusion.6), channel_id=1, source_target_pairs={{0,16},{8,24},{16,0},{24,8},{1,17},{9,25},{17,1},{25,9},{2,18},{10... | collective-permute-start | bytes 3145736 | tf_op jit(solution)/shard_map/ppermute | solution.py:424
  352.0 41.4 %collective-permute-start.32 = (bf16[2,128,2048]{2,1,0:T(8,128)(2,1)S(1)}, bf16[2,128,2048]{2,1,0:T(8,128)(2,1)S(1)}, u32[]{:S(2)}, u32[]{:S(2)}) collective-permute-start(bf16[2,128,2048]{2,1,0:T(8,128)(2,1)S(1)} %dynamic-slice_bitcast_fusion.5), channel_id=1, source_target_pairs={{0,8},{8,0},{16,24},{24,16},{1,9},{9,1},{17,25},{25,17},{2,10},{10... | collective-permute-start | bytes 3145736 | tf_op jit(solution)/shard_map/ppermute | solution.py:424
  372.6 31.6 %collective-permute-start.31 = (bf16[256,1024]{1,0:T(8,128)(2,1)S(1)}, bf16[256,1024]{1,0:T(8,128)(2,1)S(1)}, u32[]{:S(2)}, u32[]{:S(2)}) collective-permute-start(bf16[256,1024]{1,0:T(8,128)(2,1)S(1)} %fusion.51), channel_id=1, source_target_pairs={{0,8},{8,0},{16,24},{24,16},{1,9},{9,1},{17,25},{25,17},{2,10},{10... | collective-permute-start | bytes 1572872 | tf_op jit(solution)/shard_map/ppermute | solution.py:382
  447.4 37.7 %collective-permute-start.45 = (bf16[256,1024]{1,0:T(8,128)(2,1)}, bf16[256,1024]{1,0:T(8,128)(2,1)S(1)}, u32[]{:S(2)}, u32[]{:S(2)}) collective-permute-start(bf16[256,1024]{1,0:T(8,128)(2,1)} %copy-done.28), channel_id=1, source_target_pairs={{0,16},{8,24},{16,0},{24,8},{1,17},{9,25},{17,1},{25,9},{2,18},{10... | collective-permute-start | bytes 1572872 | tf_op jit(solution)/shard_map/ppermute | solution.py:362
  447.8 37.2 %collective-permute-start.46 = (bf16[256,1024]{1,0:T(8,128)(2,1)S(1)}, bf16[256,1024]{1,0:T(8,128)(2,1)S(1)}, u32[]{:S(2)}, u32[]{:S(2)}) collective-permute-start(bf16[256,1024]{1,0:T(8,128)(2,1)S(1)} %fusion.40.refs_4_), channel_id=1, source_target_pairs={{0,8},{8,0},{16,24},{24,16},{1,9},{9,1},{17,25},{25,17},{2,10},{10... | collective-permute-start | bytes 1572872 | tf_op jit(solution)/shard_map/ppermute | solution.py:362
  449.3 35.8 %collective-permute-start.47 = (bf16[256,1024]{1,0:T(8,128)(2,1)}, bf16[256,1024]{1,0:T(8,128)(2,1)S(1)}, u32[]{:S(2)}, u32[]{:S(2)}) collective-permute-start(bf16[256,1024]{1,0:T(8,128)(2,1)} %copy-done.29), channel_id=1, source_target_pairs={{0,8},{8,0},{16,24},{24,16},{1,9},{9,1},{17,25},{25,17},{2,10},{10... | collective-permute-start | bytes 1572872 | tf_op jit(solution)/shard_map/ppermute | solution.py:362
  449.9 35.3 %collective-permute-start.48 = (bf16[128,2048]{1,0:T(8,128)(2,1)}, bf16[128,2048]{1,0:T(8,128)(2,1)S(1)}, u32[]{:S(2)}, u32[]{:S(2)}) collective-permute-start(bf16[128,2048]{1,0:T(8,128)(2,1)} %fusion.39.refs_0_), channel_id=1, source_target_pairs={{0,8},{8,0},{16,24},{24,16},{1,9},{9,1},{17,25},{25,17},{2,10},{10... | collective-permute-start | bytes 1572872 | tf_op jit(solution)/shard_map/ppermute | solution.py:362
  531.7 61.9 %collective-permute-start.52 = (bf16[2,256,2048]{2,1,0:T(8,128)(2,1)}, bf16[2,256,2048]{2,1,0:T(8,128)(2,1)}, u32[]{:S(2)}, u32[]{:S(2)}) collective-permute-start(bf16[2,256,2048]{2,1,0:T(8,128)(2,1)} %share_of.6), channel_id=1, source_target_pairs={{0,1},{1,0},{2,3},{3,2},{4,5},{5,4},{6,7},{7,6},{8,9},{9,8},{10,11... | collective-permute-start | bytes 6291464 | tf_op jit(solution)/shard_map/ppermute | solution.py:459
  535.7 39.3 %collective-permute-start.63 = (bf16[2,256,1024]{2,1,0:T(8,128)(2,1)}, bf16[2,256,1024]{2,1,0:T(8,128)(2,1)}, u32[]{:S(2)}, u32[]{:S(2)}) collective-permute-start(bf16[2,256,1024]{2,1,0:T(8,128)(2,1)} %dynamic-slice_bitcast_fusion.1), channel_id=1, source_target_pairs={{0,8},{8,0},{16,24},{24,16},{1,9},{9,1},{17,25},{25,17},{2,10},{10... | collective-permute-start | bytes 3145736 | tf_op jit(solution)/shard_map/ppermute | solution.py:382
  537.4 35.0 %collective-permute-start.72 = (bf16[256,1024]{1,0:T(8,128)(2,1)}, bf16[256,1024]{1,0:T(8,128)(2,1)}, u32[]{:S(2)}, u32[]{:S(2)}) collective-permute-start(bf16[256,1024]{1,0:T(8,128)(2,1)} %fusion.57), channel_id=1, source_target_pairs={{0,8},{8,0},{16,24},{24,16},{1,9},{9,1},{17,25},{25,17},{2,10},{10... | collective-permute-start | bytes 1572872 | tf_op jit(solution)/shard_map/ppermute | solution.py:382
  539.7 38.0 %collective-permute-start.70 = (bf16[2,256,1024]{2,1,0:T(8,128)(2,1)}, bf16[2,256,1024]{2,1,0:T(8,128)(2,1)S(1)}, u32[]{:S(2)}, u32[]{:S(2)}) collective-permute-start(bf16[2,256,1024]{2,1,0:T(8,128)(2,1)} %dynamic-slice_bitcast_fusion), channel_id=1, source_target_pairs={{0,16},{8,24},{16,0},{24,8},{1,17},{9,25},{17,1},{25,9},{2,18},{10... | collective-permute-start | bytes 3145736 | tf_op jit(solution)/shard_map/ppermute | solution.py:382
  548.8 32.6 %collective-permute-start.53 = (bf16[128,2048]{1,0:T(8,128)(2,1)S(1)}, bf16[128,2048]{1,0:T(8,128)(2,1)S(1)}, u32[]{:S(2)}, u32[]{:S(2)}) collective-permute-start(bf16[128,2048]{1,0:T(8,128)(2,1)S(1)} %copy-done.23), channel_id=1, source_target_pairs={{0,16},{8,24},{16,0},{24,8},{1,17},{9,25},{17,1},{25,9},{2,18},{10... | collective-permute-start | bytes 1572872 | tf_op jit(solution)/shard_map/ppermute | solution.py:362
  581.3 35.9 %collective-permute-start.66 = (bf16[256,1024]{1,0:T(8,128)(2,1)S(1)}, bf16[256,1024]{1,0:T(8,128)(2,1)S(1)}, u32[]{:S(2)}, u32[]{:S(2)}) collective-permute-start(bf16[256,1024]{1,0:T(8,128)(2,1)S(1)} %fusion.35), channel_id=1, source_target_pairs={{0,4},{1,5},{2,6},{3,7},{4,0},{5,1},{6,2},{7,3},{8,12},{9,13},{10,... | collective-permute-start | bytes 1572872 | tf_op jit(solution)/shard_map/ppermute | solution.py:586
  592.2 36.2 %collective-permute-start.73 = (bf16[256,1024]{1,0:T(8,128)(2,1)S(1)}, bf16[256,1024]{1,0:T(8,128)(2,1)S(1)}, u32[]{:S(2)}, u32[]{:S(2)}) collective-permute-start(bf16[256,1024]{1,0:T(8,128)(2,1)S(1)} %fusion.32), channel_id=1, source_target_pairs={{0,4},{1,5},{2,6},{3,7},{4,0},{5,1},{6,2},{7,3},{8,12},{9,13},{10,... | collective-permute-start | bytes 1572872 | tf_op jit(solution)/shard_map/ppermute | solution.py:586
  593.6 34.7 %collective-permute-start.71 = (bf16[256,1024]{1,0:T(8,128)(2,1)S(1)}, bf16[256,1024]{1,0:T(8,128)(2,1)S(1)}, u32[]{:S(2)}, u32[]{:S(2)}) collective-permute-start(bf16[256,1024]{1,0:T(8,128)(2,1)S(1)} %fusion.56), channel_id=1, source_target_pairs={{0,8},{8,0},{16,24},{24,16},{1,9},{9,1},{17,25},{25,17},{2,10},{10... | collective-permute-start | bytes 1572872 | tf_op jit(solution)/shard_map/ppermute | solution.py:382
  602.4 44.0 %collective-permute-start.57 = (bf16[256,2048]{1,0:T(8,128)(2,1)}, bf16[256,2048]{1,0:T(8,128)(2,1)}, u32[]{:S(2)}, u32[]{:S(2)}) collective-permute-start(bf16[256,2048]{1,0:T(8,128)(2,1)} %fusion.31), channel_id=1, source_target_pairs={{0,2},{1,3},{2,0},{3,1},{4,6},{5,7},{6,4},{7,5},{8,10},{9,11},{10,... | collective-permute-start | bytes 3145736 | tf_op jit(solution)/shard_map/ppermute | solution.py:382
  (132 other events, 2311.6 us)
Sparse Core Ops, SparseCore 0:
  57.7 86.5 all-gather.2
  185.3 85.8 all-gather.4
  302.5 88.3 reduce-scatter.2
  445.8 88.0 reduce-scatter.4

commit v10 on v7

--- a/solution.py
+++ b/solution.py
@@ -542,32 +542,25 @@
         for k in range(sequences)[::-1]:
             qkv, heads_out, log_total, mask = kept[k]
             qkv_grad = attend_backward(grads_now, weights_out[k], qkv, log_total, cos, sin, mask)
-            if sent:
-                qkv_grad, sent[-1] = lax.optimization_barrier((qkv_grad, sent[-1]))
             pairs.append((qkv_grad, weights_in[k]))
+            if k == 0:
+                helds = column_gather(helds, columns, start=1)
+                qkv_grad, helds = lax.optimization_barrier((qkv_grad, helds))
             part = weight_grads(inputs_one, qkv_grad, grads_one, heads_out, columns)
             if k:
                 grads_now, part, helds = lax.optimization_barrier((grads_now, part, helds))
-                sent.append(column_scatter(part, columns, column, cut=1))
-        helds, sent = lax.optimization_barrier((helds, sent))
-        sent = [[narrow(x) for x in column_scatter(lanes, columns, column, start=1)] for lanes in sent]
-        helds = column_gather(helds, columns, start=1)
-        pairs, sent, helds, _ = lax.optimization_barrier((pairs, sent, helds, part))
-        there = [
-            [lax.ppermute(x, "mp", shift_pairs(ranks, -k * group)) for x in lanes]
-            for k, lanes in zip(range(1, sequences)[::-1], sent)
-        ]
-        pieces = column_scatter(part, columns, column, cut=1)
-        blocks = core_sum(pairs)
-        blocks, pieces, there = lax.optimization_barrier((blocks, pieces, there))
-        normed_grad_one = chip_sum(blocks)
-        pieces = column_scatter(pieces, columns, column, start=1)
+                sent.append((k, part))
+        normed_grad_one = chip_sum(core_sum(pairs))
+        pieces = column_scatter(part, columns, column)
+        for k, lanes in sent:
+            lanes = [narrow(x) for x in column_scatter(lanes, columns, column)]
+            back = shift_pairs(ranks, -k * group)
+            pieces = [p + wide(lax.ppermute(x, "mp", back)) for p, x in zip(pieces, lanes)]
+        spread = column_gather([narrow(p) for p in pieces], columns, cut=1)
+        spread, helds = lax.optimization_barrier((spread, helds))
+        spread = column_gather(spread, columns, start=1)
         down_sum, = place_blocks(helds[:1], column, [(1, dim, jnp.float32, False)])
         up_sum, = place_blocks(helds[1:], column, [(1, cols_local, jnp.float32, False)])
-        pieces, down_sum, up_sum = lax.optimization_barrier((pieces, down_sum, up_sum))
-        for lanes in there:
-            pieces = [p + wide(t) for p, t in zip(pieces, lanes)]
-        spread = column_gather([narrow(p) for p in pieces], columns)
         attention_sum, output_sum = place_blocks(
             spread,
             column,

time: 701 us -> 676 us (0.964)
  waiting for transfers between devices: 286 us -> 272 us
  other arithmetic: 64.8 us -> 55.3 us
    ppermute x14, waiting for transfers between devices: 107 us -> 84.1 us  [xor_scatter(): lax.ppermute(narrow(pick(blocks, 1 - side, at)), axis_name, swap_pairs(si...]
    ppermute x37, waiting for transfers between devices: 52.5 us -> 67.3 us  [xor_gather(): held[far ^ bit] = lax.ppermute(held[far], axis, swap_pairs(size, bit))]
    ppermute x2, waiting for transfers between devices: 23.8 us -> 12.1 us  [local(): lax.ppermute(x, 'mp', back)]
    add x9 -> x7, other arithmetic: 21.4 us -> 15.8 us  [xor_scatter(): blocks = wide(pick(blocks, side, at)) + wide(got)]
    unnamed x129 -> x91, local copies, waits for them, and re-layouts: 14.1 us -> 14 us
  transfers between devices with their start and end apart: 71 -> 71, of which waited for: 30 -> 29; matrix products, arithmetic and copies ran while one was open for 19% -> 18% of each run, Pallas kernels for 17% -> 18%
where the time goes in v10:
time: 676 us; the launch traced here: 671 us
  waiting for transfers between devices  272 us (40%)
  Pallas kernels  119 us (18%)
  matrix products  93.8 us (14%)
  starting transfers between devices  77.2 us (11%)
  other arithmetic  55.3 us (8%)
  local copies, waits for them, and re-layouts  39 us (6%)
  between operations  15.1 us (2%)
    ppermute x14, waiting for transfers between devices, xor_scatter(): lax.ppermute(narrow(pick(blocks, 1 - side, at)), axis_name, swap_pairs(si...  84.1 us
    dot_general x6, matrix products, product(): lax.dot_general(a, b, ((dims[:1], dims[1:]), ((), ())), preferred_element...  80.9 us
    ppermute x37, waiting for transfers between devices, xor_gather(): held[far ^ bit] = lax.ppermute(held[far], axis, swap_pairs(size, bit))  67.3 us
    all_gather x1, waiting for transfers between devices, local(): inputs_two = lax.all_gather(narrow(normed_two), 'mp', axis=0, tiled=True)  49.6 us
    ppermute x37, starting transfers between devices, xor_gather(): held[far ^ bit] = lax.ppermute(held[far], axis, swap_pairs(size, bit))  41.7 us
    ppermute x8, waiting for transfers between devices, all_sum(): x = x + lax.ppermute(x, axis, swap_pairs(size, bit))  29.5 us
    ppermute x4, waiting for transfers between devices, local(): lax.ppermute(x, 'mp', shift_pairs(ranks, k * group))  26.9 us
    pallas_call x2, Pallas kernels, attend_backward(): pl.pallas_call(backward_kernel, out_shape=jax.ShapeDtypeStruct((tokens, 3...  26.8 us
  transfers between devices with their start and end apart: 71, of which 29 were waited for; matrix products, arithmetic and copies ran while one was open for 18% of the time, Pallas kernels for 18%

profile of v10, /device:TPU:0, one launch (start us, length us, event | category | flops | bytes accessed | tf_op | source)
XLA Modules:
  0.0 671.5 jit_solution(6588192559951860342)
XLA Ops:
  28.4 19.6 %collective-permute-done.1.refs_0_ = bf16[256,768]{1,0:T(8,128)(2,1)} collective-permute-done((bf16[256,768]{1,0:T(8,128)(2,1)}, bf16[256,768]{1,0:T(8,128)(2,1)}, u32[]{:S(2)}, u32[]{:S(2)}) %collective-permute-start.1) | collective-permute-done | bytes 393248 | tf_op jit(solution)/shard_map/ppermute | solution.py:469
  66.8 12.8 %attend_forward.2 = (bf16[1024,768]{1,0:T(8,128)(2,1)}, bf16[1024,256]{1,0:T(8,128)(2,1)}, f32[1024,2]{1,0:T(8,128)}) custom-call(bf16[1024,2048]{1,0:T(8,128)(2,1)} %bitcast.210, bf16[2048,768]{1,0:T(8,128)(2,1)} %pad_maximum_fusion.w_ref.refs_3_, f32[1024,128]{1,0:T(8,128)} %get-tuple-element.111.cos_ref, f32[1024,128]{1,0:T(8,128)} %get-tuple-element.112.sin_ref, ...), custom_call_target="tpu_custom_call" | custom-call | flops 3758096384 | bytes 12582912 | tf_op jit(solution)/shard_map/attend_forward/pallas_call | solution.py:222
  85.6 17.6 %collective-permute-done.13.refs_1_ = bf16[256,256]{1,0:T(8,128)(2,1)S(1)} collective-permute-done((bf16[256,256]{1,0:T(8,128)(2,1)S(1)}, bf16[256,256]{1,0:T(8,128)(2,1)S(1)}, u32[]{:S(2)}, u32[]{:S(2)}) %collective-permute-start.13) | collective-permute-done | bytes 131104 | tf_op jit(solution)/shard_map/ppermute | solution.py:362
  116.6 12.5 %attend_forward.3 = (bf16[1024,768]{1,0:T(8,128)(2,1)}, bf16[1024,256]{1,0:T(8,128)(2,1)}, f32[1024,2]{1,0:T(8,128)}) custom-call(bf16[1024,2048]{1,0:T(8,128)(2,1)} %bitcast.211, bf16[2048,768]{1,0:T(8,128)(2,1)} %place_blocks.5.w_ref.refs_1_, f32[1024,128]{1,0:T(8,128)} %get-tuple-element.111.cos_ref, f32[1024,128]{1,0:T(8,128)} %get-tuple-element.112.sin_ref, ...), custom_call_target="tpu_custom_call" | custom-call | flops 3758096384 | bytes 12582912 | tf_op jit(solution)/shard_map/attend_forward/pallas_call | solution.py:222
  156.3 21.1 %collective-permute-done.20 = bf16[256,2048]{1,0:T(8,128)(2,1)} collective-permute-done((bf16[256,2048]{1,0:T(8,128)(2,1)S(1)}, bf16[256,2048]{1,0:T(8,128)(2,1)}, u32[]{:S(2)}, u32[]{:S(2)}) %collective-permute-start.20) | collective-permute-done | bytes 1048608 | tf_op jit(solution)/shard_map/ppermute | solution.py:382
  194.9 15.4 %fusion.87 = f32[2048,1024]{1,0:T(8,128)} fusion(bf16[2048,2048]{1,0:T(8,128)(2,1)} %all-gather.3.cloned.1.call-done, bf16[1024,2048]{1,0:T(8,128)(2,1)} %param.22), kind=kOutput, calls=%fused_computation.205 | convolution fusion | flops 8589934592 | bytes 20971520 | tf_op jit(solution)/shard_map/dot_general | solution.py:94
  218.9 49.6 %all-gather.5.cloned.1.call-done = bf16[2048,2048]{1,0:T(8,128)(2,1)} async-done(((bf16[256,2048]{1,0:T(8,128)(2,1)}), bf16[2048,2048]{1,0:T(8,128)(2,1)}) %all-gather.5.cloned.1.call-update) | async-done | bytes 8388624 | tf_op jit(solution)/shard_map/all_gather | solution.py:505
  268.5 18.2 %multiply_reduce_fusion = (f32[2048]{0:T(1024)S(1)}, bf16[2048,1024]{1,0:T(8,128)(2,1)}, bf16[2048,1024]{1,0:T(8,128)(2,1)S(1)}) fusion(f32[2048,1024]{1,0:T(8,128)} %fusion.87, s32[2048]{0:T(1024)S(1)} %bitcast.255, s32[1024]{0:T(1024)S(1)} %add_multiply_fusion.1, f32[2048]{0:T(1024)S(1)} %bitcast.253, bf16[2048,2048]{1,0:T(8,128)(2,1)} %all-gather.5.cloned.1.call-done, ...), kind=kOutput, calls=%fused_computation.8 | convolution fusion | flops 8617195520 | bytes 29388800 | tf_op jit(solution)/shard_map/dot_general | solution.py:94
  288.7 10.9 %convolution_convert_fusion.1 = bf16[2048,2048]{1,0:T(8,128)(2,1)} fusion(bf16[2048,1024]{1,0:T(8,128)(2,1)S(1)} %get-tuple-element.152, bf16[2048,1024]{1,0:T(8,128)(2,1)S(1)} %copy-done.41), kind=kOutput, calls=%fused_computation.11 | convolution fusion | flops 8594128896 | bytes 16777216 | tf_op jit(solution)/shard_map/dot_general | solution.py:94
  299.8 12.9 %convolution_convert_fusion.2 = bf16[2048,1024]{1,0:T(8,128)(2,1)S(1)} fusion(bf16[2048,2048]{1,0:T(8,128)(2,1)} %all-gather.5.cloned.1.call-done, bf16[2048,1024]{1,0:T(8,128)(2,1)} %copy-done.44), kind=kOutput, calls=%fused_computation.17 | convolution fusion | flops 8592031744 | bytes 16777216 | tf_op jit(solution)/shard_map/dot_general | solution.py:94
  317.3 12.3 %fusion.6 = bf16[1024,2048]{1,0:T(8,128)(2,1)S(1)} fusion(bf16[2048,1024]{1,0:T(8,128)(2,1)S(1)} %copy-done.43, bf16[2048,2048]{1,0:T(8,128)(2,1)} %all-gather.3.cloned.1.call-done, f32[2048]{0:T(1024)S(1)} %bitcast.254), kind=kOutput, calls=%fused_computation.16 | convolution fusion | flops 8604614656 | bytes 16785408 | tf_op jit(solution)/shard_map/dot_general | solution.py:94
  334.7 11.3 %convolution_convert_fusion = bf16[2048,2048]{1,0:T(8,128)(2,1)} fusion(bf16[2048,1024]{1,0:T(8,128)(2,1)S(1)} %copy-done.43, bf16[1024,2048]{1,0:T(8,128)(2,1)S(1)} %copy-done.42), kind=kOutput, calls=%fused_computation.10 | convolution fusion | flops 8594128896 | bytes 16777216 | tf_op jit(solution)/shard_map/dot_general | solution.py:94
  349.2 14.6 %collective-permute-done.29 = bf16[2,512,1024]{2,1,0:T(8,128)(2,1)} collective-permute-done((bf16[2,512,1024]{2,1,0:T(8,128)(2,1)}, bf16[2,512,1024]{2,1,0:T(8,128)(2,1)}, u32[]{:S(2)}, u32[]{:S(2)}) %collective-permute-start.29) | collective-permute-done | bytes 2097184 | tf_op jit(solution)/shard_map/ppermute | solution.py:382
  369.0 12.1 %collective-permute-done.28 = bf16[2,256,2048]{2,1,0:T(8,128)(2,1)} collective-permute-done((bf16[2,256,2048]{2,1,0:T(8,128)(2,1)}, bf16[2,256,2048]{2,1,0:T(8,128)(2,1)}, u32[]{:S(2)}, u32[]{:S(2)}) %collective-permute-start.28) | collective-permute-done | bytes 2097184 | tf_op jit(solution)/shard_map/ppermute | solution.py:382
  401.8 19.4 %collective-permute-done.33 = bf16[256,2048]{1,0:T(8,128)(2,1)S(1)} collective-permute-done((bf16[256,2048]{1,0:T(8,128)(2,1)S(1)}, bf16[256,2048]{1,0:T(8,128)(2,1)S(1)}, u32[]{:S(2)}, u32[]{:S(2)}) %collective-permute-start.33) | collective-permute-done | bytes 1048608 | tf_op jit(solution)/shard_map/ppermute | solution.py:362
  431.6 13.8 %attend_backward.2.q_ref.refs_0_ = bf16[1024,768]{1,0:T(8,128)(2,1)} custom-call(bf16[1024,2048]{1,0:T(8,128)(2,1)} %bitcast.57.g_ref, bf16[2048,256]{1,0:T(8,128)(2,1)} %place_blocks.6.refs_3_.w_ref, bf16[1024,768]{1,0:T(8,128)(2,1)} %get-tuple-element.159.qkv_ref, f32[1024,2]{1,0:T(8,128)} %get-tuple-element.160.log_ref, ...), custom_call_target="tpu_custom_call" | custom-call | flops 2415919104 | bytes 12582912 | tf_op jit(solution)/shard_map/attend_backward/pallas_call | solution.py:244
  445.3 9.0 %weight_grads.2 = (bf16[4,256,1024]{2,1,0:T(8,128)(2,1)}, bf16[4,256,1024]{2,1,0:T(8,128)(2,1)}) custom-call(bf16[1024,2048]{1,0:T(8,128)(2,1)} %bitcast.212, bf16[1024,768]{1,0:T(8,128)(2,1)} %attend_backward.2.q_ref.refs_0_, bf16[1024,2048]{1,0:T(8,128)(2,1)} %bitcast.57.g_ref, bf16[1024,256]{1,0:T(8,128)(2,1)} %get-tuple-element.143.refs_2_.h_ref), custom_call_target="tpu_custom_call" | custom-call | flops 4294967296 | bytes 14680064 | tf_op jit(solution)/shard_map/weight_grads/pallas_call | solution.py:290
  463.8 13.1 %attend_backward.3.refs_2_.q_ref = bf16[1024,768]{1,0:T(8,128)(2,1)} custom-call(bf16[1024,2048]{1,0:T(8,128)(2,1)} %bitcast.57.g_ref, bf16[2048,256]{1,0:T(8,128)(2,1)} %bitcast.209, bf16[1024,768]{1,0:T(8,128)(2,1)} %get-tuple-element.120.qkv_ref, f32[1024,2]{1,0:T(8,128)} %get-tuple-element.164.log_ref, f32[1024,128]{1,0:T(8,128)} %get-tuple-element.111.cos_ref, ...), custom_call_target="tpu_custom_call" | custom-call | flops 2415919104 | bytes 12582912 | tf_op jit(solution)/shard_map/attend_backward/pallas_call | solution.py:244
  489.7 13.6 %collective-permute-done.48.refs_3_ = bf16[256,2048]{1,0:T(8,128)(2,1)} collective-permute-done((bf16[256,2048]{1,0:T(8,128)(2,1)}, bf16[256,2048]{1,0:T(8,128)(2,1)}, u32[]{:S(2)}, u32[]{:S(2)}) %collective-permute-start.48) | collective-permute-done | bytes 1048608 | tf_op jit(solution)/shard_map/ppermute | solution.py:362
  507.2 9.1 %weight_grads.3 = (bf16[4,256,1024]{2,1,0:T(8,128)(2,1)}, bf16[4,256,1024]{2,1,0:T(8,128)(2,1)}) custom-call(bf16[1024,2048]{1,0:T(8,128)(2,1)} %bitcast.213, bf16[1024,768]{1,0:T(8,128)(2,1)} %attend_backward.3.refs_2_.q_ref, bf16[1024,2048]{1,0:T(8,128)(2,1)} %bitcast.57.g_ref, bf16[1024,256]{1,0:T(8,128)(2,1)} %get-tuple-element.141.refs_0_.h_ref), custom_call_target="tpu_custom_call" | custom-call | flops 4294967296 | bytes 14680064 | tf_op jit(solution)/shard_map/weight_grads/pallas_call | solution.py:290
  544.1 11.9 %collective-permute-done.54 = bf16[256,1024]{1,0:T(8,128)(2,1)} collective-permute-done((bf16[256,1024]{1,0:T(8,128)(2,1)}, bf16[256,1024]{1,0:T(8,128)(2,1)}, u32[]{:S(2)}, u32[]{:S(2)}) %collective-permute-start.54) | collective-permute-done | bytes 524320 | tf_op jit(solution)/shard_map/ppermute | solution.py:382
  577.4 7.9 %collective-permute-done.55 = bf16[256,1024]{1,0:T(8,128)(2,1)S(1)} collective-permute-done((bf16[256,1024]{1,0:T(8,128)(2,1)S(1)}, bf16[256,1024]{1,0:T(8,128)(2,1)S(1)}, u32[]{:S(2)}, u32[]{:S(2)}) %collective-permute-start.55) | collective-permute-done | bytes 524320 | tf_op jit(solution)/shard_map/ppermute | solution.py:558
  586.9 15.6 %collective-permute-done.41 = bf16[256,2048]{1,0:T(8,128)(2,1)S(1)} collective-permute-done((bf16[256,2048]{1,0:T(8,128)(2,1)S(1)}, bf16[256,2048]{1,0:T(8,128)(2,1)S(1)}, u32[]{:S(2)}, u32[]{:S(2)}) %collective-permute-start.41) | collective-permute-done | bytes 1048608 | tf_op jit(solution)/shard_map/ppermute | solution.py:382
  617.1 22.0 %collective-permute-done.45 = f32[160,128]{1,0:T(8,128)S(1)} collective-permute-done((f32[160,128]{1,0:T(8,128)S(1)}, f32[160,128]{1,0:T(8,128)S(1)}, u32[]{:S(2)}, u32[]{:S(2)}) %collective-permute-start.45) | collective-permute-done | bytes 81952 | tf_op jit(solution)/shard_map/ppermute | solution.py:413
  (345 shorter events, 280.3 us)
Async XLA Ops:
  7.2 172.5 %all-gather.3.cloned.1.call-start = ((), (), s32[]{:S(2)}) async-start(), calls=%async_computation.2 | async-start | bytes 9437184 | tf_op jit(solution)/shard_map/all_gather | solution.py:482
  12.9 43.1 %collective-permute-start = (bf16[256,2048]{1,0:T(8,128)(2,1)S(1)}, bf16[256,2048]{1,0:T(8,128)(2,1)}, u32[]{:S(2)}, u32[]{:S(2)}) collective-permute-start(bf16[256,2048]{1,0:T(8,128)(2,1)S(1)} %fusion.15), channel_id=1, source_target_pairs={{0,2},{1,3},{2,0},{3,1},{4,6},{5,7},{6,4},{7,5},{8,10},{9,11},{10,... | collective-permute-start | bytes 3145736 | tf_op jit(solution)/shard_map/ppermute | solution.py:362
  15.9 32.1 %collective-permute-start.1 = (bf16[256,768]{1,0:T(8,128)(2,1)}, bf16[256,768]{1,0:T(8,128)(2,1)}, u32[]{:S(2)}, u32[]{:S(2)}) collective-permute-start(bf16[256,768]{1,0:T(8,128)(2,1)} %get-tuple-element.106), channel_id=1, source_target_pairs={{0,4},{1,5},{2,6},{3,7},{4,0},{5,1},{6,2},{7,3},{8,12},{9,13},{10,... | collective-permute-start | bytes 1179656 | tf_op jit(solution)/shard_map/ppermute | solution.py:469
  18.5 36.8 %collective-permute-start.2 = (bf16[256,768]{1,0:T(8,128)(2,1)}, bf16[256,768]{1,0:T(8,128)(2,1)}, u32[]{:S(2)}, u32[]{:S(2)}) collective-permute-start(bf16[256,768]{1,0:T(8,128)(2,1)} %get-tuple-element.107), channel_id=1, source_target_pairs={{0,4},{1,5},{2,6},{3,7},{4,0},{5,1},{6,2},{7,3},{8,12},{9,13},{10,... | collective-permute-start | bytes 1179656 | tf_op jit(solution)/shard_map/ppermute | solution.py:469
  56.0 212.5 %all-gather.5.cloned.1.call-start = ((), (), s32[]{:S(2)}) async-start(), calls=%async_computation.3 | async-start | bytes 9437184 | tf_op jit(solution)/shard_map/all_gather | solution.py:505
  146.5 30.9 %collective-permute-start.20 = (bf16[256,2048]{1,0:T(8,128)(2,1)S(1)}, bf16[256,2048]{1,0:T(8,128)(2,1)}, u32[]{:S(2)}, u32[]{:S(2)}) collective-permute-start(bf16[256,2048]{1,0:T(8,128)(2,1)S(1)} %fusion.32), channel_id=1, source_target_pairs={{0,2},{1,3},{2,0},{3,1},{4,6},{5,7},{6,4},{7,5},{8,10},{9,11},{10,... | collective-permute-start | bytes 3145736 | tf_op jit(solution)/shard_map/ppermute | solution.py:382
  183.1 205.2 %reduce-scatter.3.cloned.1.call-start = ((), (), s32[]{:S(2)}) async-start(), calls=%async_computation.4 | async-start | bytes 9437184 | tf_op jit(solution)/shard_map/reduce_scatter | solution.py:518
  299.7 360.1 %reduce-scatter.5.cloned.1.call-start = ((), (), s32[]{:S(2)}) async-start(), calls=%async_computation.5 | async-start | bytes 9437184 | tf_op jit(solution)/shard_map/reduce_scatter | solution.py:536
  315.8 48.1 %collective-permute-start.29 = (bf16[2,512,1024]{2,1,0:T(8,128)(2,1)}, bf16[2,512,1024]{2,1,0:T(8,128)(2,1)}, u32[]{:S(2)}, u32[]{:S(2)}) collective-permute-start(bf16[2,512,1024]{2,1,0:T(8,128)(2,1)} %dynamic-slice_bitcast_fusion), channel_id=1, source_target_pairs={{0,16},{8,24},{16,0},{24,8},{1,17},{9,25},{17,1},{25,9},{2,18},{10... | collective-permute-start | bytes 6291464 | tf_op jit(solution)/shard_map/ppermute | solution.py:382
  332.7 48.4 %collective-permute-start.28 = (bf16[2,256,2048]{2,1,0:T(8,128)(2,1)}, bf16[2,256,2048]{2,1,0:T(8,128)(2,1)}, u32[]{:S(2)}, u32[]{:S(2)}) collective-permute-start(bf16[2,256,2048]{2,1,0:T(8,128)(2,1)} %dynamic-slice_bitcast_fusion.1), channel_id=1, source_target_pairs={{0,8},{8,0},{16,24},{24,16},{1,9},{9,1},{17,25},{25,17},{2,10},{10... | collective-permute-start | bytes 6291464 | tf_op jit(solution)/shard_map/ppermute | solution.py:382
  456.5 46.8 %collective-permute-start.48 = (bf16[256,2048]{1,0:T(8,128)(2,1)}, bf16[256,2048]{1,0:T(8,128)(2,1)}, u32[]{:S(2)}, u32[]{:S(2)}) collective-permute-start(bf16[256,2048]{1,0:T(8,128)(2,1)} %collective-permute-done.38.refs_1_), channel_id=1, source_target_pairs={{0,16},{8,24},{16,0},{24,8},{1,17},{9,25},{17,1},{25,9},{2,18},{10... | collective-permute-start | bytes 3145736 | tf_op jit(solution)/shard_map/ppermute | solution.py:362
  458.3 45.0 %collective-permute-start.49 = (bf16[512,1024]{1,0:T(8,128)(2,1)}, bf16[512,1024]{1,0:T(8,128)(2,1)}, u32[]{:S(2)}, u32[]{:S(2)}) collective-permute-start(bf16[512,1024]{1,0:T(8,128)(2,1)} %fusion.26.refs_0_), channel_id=1, source_target_pairs={{0,8},{8,0},{16,24},{24,16},{1,9},{9,1},{17,25},{25,17},{2,10},{10... | collective-permute-start | bytes 3145736 | tf_op jit(solution)/shard_map/ppermute | solution.py:362
  459.4 47.8 %collective-permute-start.50 = (bf16[512,1024]{1,0:T(8,128)(2,1)}, bf16[512,1024]{1,0:T(8,128)(2,1)}, u32[]{:S(2)}, u32[]{:S(2)}) collective-permute-start(bf16[512,1024]{1,0:T(8,128)(2,1)} %collective-permute-done.39.refs_2_), channel_id=1, source_target_pairs={{0,8},{8,0},{16,24},{24,16},{1,9},{9,1},{17,25},{25,17},{2,10},{10... | collective-permute-start | bytes 3145736 | tf_op jit(solution)/shard_map/ppermute | solution.py:362
  463.3 62.4 %collective-permute-start.59 = (bf16[2,256,1024]{2,1,0:T(8,128)(2,1)S(1)}, bf16[2,256,1024]{2,1,0:T(8,128)(2,1)S(1)}, u32[]{:S(2)}, u32[]{:S(2)}) collective-permute-start(bf16[2,256,1024]{2,1,0:T(8,128)(2,1)S(1)} %dynamic-slice_bitcast_fusion.2), channel_id=1, source_target_pairs={{0,16},{8,24},{16,0},{24,8},{1,17},{9,25},{17,1},{25,9},{2,18},{10... | collective-permute-start | bytes 3145736 | tf_op jit(solution)/shard_map/ppermute | solution.py:382
  480.8 47.3 %collective-permute-start.53 = (bf16[2,256,1024]{2,1,0:T(8,128)(2,1)S(1)}, bf16[2,256,1024]{2,1,0:T(8,128)(2,1)}, u32[]{:S(2)}, u32[]{:S(2)}) collective-permute-start(bf16[2,256,1024]{2,1,0:T(8,128)(2,1)S(1)} %dynamic-slice_bitcast_fusion.4), channel_id=1, source_target_pairs={{0,8},{8,0},{16,24},{24,16},{1,9},{9,1},{17,25},{25,17},{2,10},{10... | collective-permute-start | bytes 3145736 | tf_op jit(solution)/shard_map/ppermute | solution.py:382
  503.3 60.4 %collective-permute-start.40 = (bf16[2,256,2048]{2,1,0:T(8,128)(2,1)}, bf16[2,256,2048]{2,1,0:T(8,128)(2,1)}, u32[]{:S(2)}, u32[]{:S(2)}) collective-permute-start(bf16[2,256,2048]{2,1,0:T(8,128)(2,1)} %share_of.6), channel_id=1, source_target_pairs={{0,1},{1,0},{2,3},{3,2},{4,5},{5,4},{6,7},{7,6},{8,9},{9,8},{10,11... | collective-permute-start | bytes 6291464 | tf_op jit(solution)/shard_map/ppermute | solution.py:440
  518.7 41.8 %collective-permute-start.57 = (bf16[2,256,1024]{2,1,0:T(8,128)(2,1)}, bf16[2,256,1024]{2,1,0:T(8,128)(2,1)}, u32[]{:S(2)}, u32[]{:S(2)}) collective-permute-start(bf16[2,256,1024]{2,1,0:T(8,128)(2,1)} %dynamic-slice_bitcast_fusion.3), channel_id=1, source_target_pairs={{0,16},{8,24},{16,0},{24,8},{1,17},{9,25},{17,1},{25,9},{2,18},{10... | collective-permute-start | bytes 3145736 | tf_op jit(solution)/shard_map/ppermute | solution.py:382
  541.6 33.4 %collective-permute-start.61 = (bf16[256,1024]{1,0:T(8,128)(2,1)S(1)}, bf16[256,1024]{1,0:T(8,128)(2,1)S(1)}, u32[]{:S(2)}, u32[]{:S(2)}) collective-permute-start(bf16[256,1024]{1,0:T(8,128)(2,1)S(1)} %fusion.36), channel_id=1, source_target_pairs={{0,4},{1,5},{2,6},{3,7},{4,0},{5,1},{6,2},{7,3},{8,12},{9,13},{10,... | collective-permute-start | bytes 1572872 | tf_op jit(solution)/shard_map/ppermute | solution.py:558
  566.3 36.2 %collective-permute-start.41 = (bf16[256,2048]{1,0:T(8,128)(2,1)S(1)}, bf16[256,2048]{1,0:T(8,128)(2,1)S(1)}, u32[]{:S(2)}, u32[]{:S(2)}) collective-permute-start(bf16[256,2048]{1,0:T(8,128)(2,1)S(1)} %fusion.35), channel_id=1, source_target_pairs={{0,2},{1,3},{2,0},{3,1},{4,6},{5,7},{6,4},{7,5},{8,10},{9,11},{10,... | collective-permute-start | bytes 3145736 | tf_op jit(solution)/shard_map/ppermute | solution.py:382
  576.0 35.3 %collective-permute-start.62 = (bf16[256,1024]{1,0:T(8,128)(2,1)}, bf16[256,1024]{1,0:T(8,128)(2,1)}, u32[]{:S(2)}, u32[]{:S(2)}) collective-permute-start(bf16[256,1024]{1,0:T(8,128)(2,1)} %fusion.38.refs_4_), channel_id=1, source_target_pairs={{0,16},{8,24},{16,0},{24,8},{1,17},{9,25},{17,1},{25,9},{2,18},{10... | collective-permute-start | bytes 1572872 | tf_op jit(solution)/shard_map/ppermute | solution.py:362
  611.2 42.7 %collective-permute-start.63 = (bf16[256,1024]{1,0:T(8,128)(2,1)}, bf16[256,1024]{1,0:T(8,128)(2,1)}, u32[]{:S(2)}, u32[]{:S(2)}) collective-permute-start(bf16[256,1024]{1,0:T(8,128)(2,1)} %fusion.41.refs_0_), channel_id=1, source_target_pairs={{0,16},{8,24},{16,0},{24,8},{1,17},{9,25},{17,1},{25,9},{2,18},{10... | collective-permute-start | bytes 1572872 | tf_op jit(solution)/shard_map/ppermute | solution.py:362
  612.5 41.4 %collective-permute-start.64 = (bf16[256,1024]{1,0:T(8,128)(2,1)}, bf16[256,1024]{1,0:T(8,128)(2,1)}, u32[]{:S(2)}, u32[]{:S(2)}) collective-permute-start(bf16[256,1024]{1,0:T(8,128)(2,1)} %collective-permute-done.56.refs_1_), channel_id=1, source_target_pairs={{0,16},{8,24},{16,0},{24,8},{1,17},{9,25},{17,1},{25,9},{2,18},{10... | collective-permute-start | bytes 1572872 | tf_op jit(solution)/shard_map/ppermute | solution.py:362
  613.3 40.7 %collective-permute-start.65 = (bf16[256,1024]{1,0:T(8,128)(2,1)}, bf16[256,1024]{1,0:T(8,128)(2,1)}, u32[]{:S(2)}, u32[]{:S(2)}) collective-permute-start(bf16[256,1024]{1,0:T(8,128)(2,1)} %fusion.38.refs_4_), channel_id=1, source_target_pairs={{0,8},{8,0},{16,24},{24,16},{1,9},{9,1},{17,25},{25,17},{2,10},{10... | collective-permute-start | bytes 1572872 | tf_op jit(solution)/shard_map/ppermute | solution.py:362
  613.3 40.7 %collective-permute-start.66 = (bf16[256,1024]{1,0:T(8,128)(2,1)}, bf16[256,1024]{1,0:T(8,128)(2,1)}, u32[]{:S(2)}, u32[]{:S(2)}) collective-permute-start(bf16[256,1024]{1,0:T(8,128)(2,1)} %collective-permute-done.62.refs_6_), channel_id=1, source_target_pairs={{0,8},{8,0},{16,24},{24,16},{1,9},{9,1},{17,25},{25,17},{2,10},{10... | collective-permute-start | bytes 1572872 | tf_op jit(solution)/shard_map/ppermute | solution.py:362
  (92 other events, 1349.9 us)
Sparse Core Ops, SparseCore 0:
  56.2 85.7 all-gather.2
  183.2 85.2 all-gather.4
  299.8 88.4 reduce-scatter.2
  428.8 89.2 reduce-scatter.4

commit v11 on v10

--- a/solution.py
+++ b/solution.py
@@ -550,10 +550,14 @@
             if k:
                 grads_now, part, helds = lax.optimization_barrier((grads_now, part, helds))
                 sent.append((k, part))
-        normed_grad_one = chip_sum(core_sum(pairs))
+        blocks = core_sum(pairs)
+        sent = [(k, column_scatter(lanes, columns, column, cut=1)) for k, lanes in sent]
+        blocks, gated = lax.optimization_barrier((blocks, [lanes for _, lanes in sent]))
+        sent = [(k, lanes) for (k, _), lanes in zip(sent, gated)]
+        normed_grad_one = chip_sum(blocks)
         pieces = column_scatter(part, columns, column)
         for k, lanes in sent:
-            lanes = [narrow(x) for x in column_scatter(lanes, columns, column)]
+            lanes = [narrow(x) for x in column_scatter(lanes, columns, column, start=1)]
             back = shift_pairs(ranks, -k * group)
             pieces = [p + wide(lax.ppermute(x, "mp", back)) for p, x in zip(pieces, lanes)]
         spread = column_gather([narrow(p) for p in pieces], columns, cut=1)

time: 676 us -> 672 us (level)
    ppermute x8, waiting for transfers between devices: 29.5 us -> 11.5 us  [all_sum(): x = x + lax.ppermute(x, axis, swap_pairs(size, bit))]
    ppermute x2, waiting for transfers between devices: 12.1 us -> 28.2 us  [local(): lax.ppermute(x, 'mp', back)]
    unnamed x91 -> x85, local copies, waits for them, and re-layouts: 14 us -> 13.6 us
  transfers between devices with their start and end apart: 71 -> 71, of which waited for: 29 -> 28; matrix products, arithmetic and copies ran while one was open for 18% -> 18% of each run, Pallas kernels for 18% -> 18%
where the time goes in v11:
time: 672 us; the launch traced here: 669 us
  waiting for transfers between devices  274 us (41%)
  Pallas kernels  119 us (18%)
  matrix products  97.5 us (15%)
  starting transfers between devices  77.3 us (12%)
  other arithmetic  50 us (7%)
  local copies, waits for them, and re-layouts  36.7 us (5%)
  between operations  15.1 us (2%)
    ppermute x14, waiting for transfers between devices, xor_scatter(): lax.ppermute(narrow(pick(blocks, 1 - side, at)), axis_name, swap_pairs(si...  84.1 us
    dot_general x6, matrix products, product(): lax.dot_general(a, b, ((dims[:1], dims[1:]), ((), ())), preferred_element...  81 us
    ppermute x37, waiting for transfers between devices, xor_gather(): held[far ^ bit] = lax.ppermute(held[far], axis, swap_pairs(size, bit))  70.6 us
    all_gather x1, waiting for transfers between devices, local(): inputs_two = lax.all_gather(narrow(normed_two), 'mp', axis=0, tiled=True)  49.6 us
    ppermute x37, starting transfers between devices, xor_gather(): held[far ^ bit] = lax.ppermute(held[far], axis, swap_pairs(size, bit))  41.1 us
    ppermute x2, waiting for transfers between devices, local(): lax.ppermute(x, 'mp', back)  28.2 us
    ppermute x4, waiting for transfers between devices, local(): lax.ppermute(x, 'mp', shift_pairs(ranks, k * group))  26.8 us
    pallas_call x2, Pallas kernels, attend_backward(): pl.pallas_call(backward_kernel, out_shape=jax.ShapeDtypeStruct((tokens, 3...  26.4 us
  transfers between devices with their start and end apart: 71, of which 28 were waited for; matrix products, arithmetic and copies ran while one was open for 18% of the time, Pallas kernels for 18%

profile of v11, /device:TPU:0, one launch (start us, length us, event | category | flops | bytes accessed | tf_op | source)
XLA Modules:
  0.0 668.6 jit_solution(9562533040247596275)
XLA Ops:
  28.5 19.5 %collective-permute-done.1.refs_0_ = bf16[256,768]{1,0:T(8,128)(2,1)} collective-permute-done((bf16[256,768]{1,0:T(8,128)(2,1)}, bf16[256,768]{1,0:T(8,128)(2,1)}, u32[]{:S(2)}, u32[]{:S(2)}) %collective-permute-start.1) | collective-permute-done | bytes 393248 | tf_op jit(solution)/shard_map/ppermute | solution.py:469
  66.8 12.8 %attend_forward.2 = (bf16[1024,768]{1,0:T(8,128)(2,1)}, bf16[1024,256]{1,0:T(8,128)(2,1)}, f32[1024,2]{1,0:T(8,128)}) custom-call(bf16[1024,2048]{1,0:T(8,128)(2,1)} %bitcast.209, bf16[2048,768]{1,0:T(8,128)(2,1)} %pad_maximum_fusion.w_ref.refs_3_, f32[1024,128]{1,0:T(8,128)} %get-tuple-element.114.cos_ref, f32[1024,128]{1,0:T(8,128)} %get-tuple-element.115.sin_ref, ...), custom_call_target="tpu_custom_call" | custom-call | flops 3758096384 | bytes 12582912 | tf_op jit(solution)/shard_map/attend_forward/pallas_call | solution.py:222
  85.6 17.6 %collective-permute-done.13.refs_1_ = bf16[256,256]{1,0:T(8,128)(2,1)S(1)} collective-permute-done((bf16[256,256]{1,0:T(8,128)(2,1)S(1)}, bf16[256,256]{1,0:T(8,128)(2,1)S(1)}, u32[]{:S(2)}, u32[]{:S(2)}) %collective-permute-start.13) | collective-permute-done | bytes 131104 | tf_op jit(solution)/shard_map/ppermute | solution.py:362
  116.7 12.5 %attend_forward.3 = (bf16[1024,768]{1,0:T(8,128)(2,1)}, bf16[1024,256]{1,0:T(8,128)(2,1)}, f32[1024,2]{1,0:T(8,128)}) custom-call(bf16[1024,2048]{1,0:T(8,128)(2,1)} %bitcast.210, bf16[2048,768]{1,0:T(8,128)(2,1)} %place_blocks.5.w_ref.refs_1_, f32[1024,128]{1,0:T(8,128)} %get-tuple-element.114.cos_ref, f32[1024,128]{1,0:T(8,128)} %get-tuple-element.115.sin_ref, ...), custom_call_target="tpu_custom_call" | custom-call | flops 3758096384 | bytes 12582912 | tf_op jit(solution)/shard_map/attend_forward/pallas_call | solution.py:222
  156.4 21.1 %collective-permute-done.20 = bf16[256,2048]{1,0:T(8,128)(2,1)} collective-permute-done((bf16[256,2048]{1,0:T(8,128)(2,1)S(1)}, bf16[256,2048]{1,0:T(8,128)(2,1)}, u32[]{:S(2)}, u32[]{:S(2)}) %collective-permute-start.20) | collective-permute-done | bytes 1048608 | tf_op jit(solution)/shard_map/ppermute | solution.py:382
  194.9 15.4 %fusion.86 = f32[2048,1024]{1,0:T(8,128)} fusion(bf16[2048,2048]{1,0:T(8,128)(2,1)} %all-gather.3.cloned.1.call-done, bf16[1024,2048]{1,0:T(8,128)(2,1)} %param.22), kind=kOutput, calls=%fused_computation.205 | convolution fusion | flops 8589934592 | bytes 20971520 | tf_op jit(solution)/shard_map/dot_general | solution.py:94
  218.9 49.6 %all-gather.5.cloned.1.call-done = bf16[2048,2048]{1,0:T(8,128)(2,1)} async-done(((bf16[256,2048]{1,0:T(8,128)(2,1)}), bf16[2048,2048]{1,0:T(8,128)(2,1)}) %all-gather.5.cloned.1.call-update) | async-done | bytes 8388624 | tf_op jit(solution)/shard_map/all_gather | solution.py:505
  268.5 18.3 %multiply_reduce_fusion = (f32[2048]{0:T(1024)S(1)}, bf16[2048,1024]{1,0:T(8,128)(2,1)}, bf16[2048,1024]{1,0:T(8,128)(2,1)S(1)}) fusion(f32[2048,1024]{1,0:T(8,128)} %fusion.86, s32[2048]{0:T(1024)S(1)} %bitcast.251, s32[1024]{0:T(1024)S(1)} %add_multiply_fusion.1, f32[2048]{0:T(1024)S(1)} %bitcast.249, bf16[2048,2048]{1,0:T(8,128)(2,1)} %all-gather.5.cloned.1.call-done, ...), kind=kOutput, calls=%fused_computation.8 | convolution fusion | flops 8617195520 | bytes 29388800 | tf_op jit(solution)/shard_map/dot_general | solution.py:94
  288.8 10.9 %convolution_convert_fusion.1 = bf16[2048,2048]{1,0:T(8,128)(2,1)} fusion(bf16[2048,1024]{1,0:T(8,128)(2,1)S(1)} %get-tuple-element.155, bf16[2048,1024]{1,0:T(8,128)(2,1)S(1)} %copy-done.38), kind=kOutput, calls=%fused_computation.11 | convolution fusion | flops 8594128896 | bytes 16777216 | tf_op jit(solution)/shard_map/dot_general | solution.py:94
  299.9 12.9 %convolution_convert_fusion.2 = bf16[2048,1024]{1,0:T(8,128)(2,1)S(1)} fusion(bf16[2048,2048]{1,0:T(8,128)(2,1)} %all-gather.5.cloned.1.call-done, bf16[2048,1024]{1,0:T(8,128)(2,1)} %copy-done.41), kind=kOutput, calls=%fused_computation.17 | convolution fusion | flops 8592031744 | bytes 16777216 | tf_op jit(solution)/shard_map/dot_general | solution.py:94
  317.5 12.3 %fusion.6 = bf16[1024,2048]{1,0:T(8,128)(2,1)S(1)} fusion(bf16[2048,1024]{1,0:T(8,128)(2,1)S(1)} %copy-done.40, bf16[2048,2048]{1,0:T(8,128)(2,1)} %all-gather.3.cloned.1.call-done, f32[2048]{0:T(1024)S(1)} %bitcast.250), kind=kOutput, calls=%fused_computation.16 | convolution fusion | flops 8604614656 | bytes 16785408 | tf_op jit(solution)/shard_map/dot_general | solution.py:94
  334.8 11.3 %convolution_convert_fusion = bf16[2048,2048]{1,0:T(8,128)(2,1)} fusion(bf16[2048,1024]{1,0:T(8,128)(2,1)S(1)} %copy-done.40, bf16[1024,2048]{1,0:T(8,128)(2,1)S(1)} %copy-done.39), kind=kOutput, calls=%fused_computation.10 | convolution fusion | flops 8594128896 | bytes 16777216 | tf_op jit(solution)/shard_map/dot_general | solution.py:94
  349.4 14.6 %collective-permute-done.29 = bf16[2,512,1024]{2,1,0:T(8,128)(2,1)} collective-permute-done((bf16[2,512,1024]{2,1,0:T(8,128)(2,1)}, bf16[2,512,1024]{2,1,0:T(8,128)(2,1)}, u32[]{:S(2)}, u32[]{:S(2)}) %collective-permute-start.29) | collective-permute-done | bytes 2097184 | tf_op jit(solution)/shard_map/ppermute | solution.py:382
  369.1 12.1 %collective-permute-done.28 = bf16[2,256,2048]{2,1,0:T(8,128)(2,1)} collective-permute-done((bf16[2,256,2048]{2,1,0:T(8,128)(2,1)}, bf16[2,256,2048]{2,1,0:T(8,128)(2,1)}, u32[]{:S(2)}, u32[]{:S(2)}) %collective-permute-start.28) | collective-permute-done | bytes 2097184 | tf_op jit(solution)/shard_map/ppermute | solution.py:382
  401.9 19.4 %collective-permute-done.33 = bf16[256,2048]{1,0:T(8,128)(2,1)S(1)} collective-permute-done((bf16[256,2048]{1,0:T(8,128)(2,1)S(1)}, bf16[256,2048]{1,0:T(8,128)(2,1)S(1)}, u32[]{:S(2)}, u32[]{:S(2)}) %collective-permute-start.33) | collective-permute-done | bytes 1048608 | tf_op jit(solution)/shard_map/ppermute | solution.py:362
  434.5 13.4 %attend_backward.2.q_ref.refs_0_ = bf16[1024,768]{1,0:T(8,128)(2,1)} custom-call(bf16[1024,2048]{1,0:T(8,128)(2,1)} %bitcast.57.g_ref, bf16[2048,256]{1,0:T(8,128)(2,1)} %place_blocks.6.refs_3_.w_ref, bf16[1024,768]{1,0:T(8,128)(2,1)} %get-tuple-element.162.qkv_ref, f32[1024,2]{1,0:T(8,128)} %get-tuple-element.163.log_ref, ...), custom_call_target="tpu_custom_call" | custom-call | flops 2415919104 | bytes 12582912 | tf_op jit(solution)/shard_map/attend_backward/pallas_call | solution.py:244
  448.0 8.9 %weight_grads.2 = (bf16[4,256,1024]{2,1,0:T(8,128)(2,1)}, bf16[4,256,1024]{2,1,0:T(8,128)(2,1)}) custom-call(bf16[1024,2048]{1,0:T(8,128)(2,1)} %bitcast.211, bf16[1024,768]{1,0:T(8,128)(2,1)} %attend_backward.2.q_ref.refs_0_, bf16[1024,2048]{1,0:T(8,128)(2,1)} %bitcast.57.g_ref, bf16[1024,256]{1,0:T(8,128)(2,1)} %get-tuple-element.146.refs_2_.h_ref), custom_call_target="tpu_custom_call" | custom-call | flops 4294967296 | bytes 14680064 | tf_op jit(solution)/shard_map/weight_grads/pallas_call | solution.py:290
  461.6 13.0 %attend_backward.3.refs_2_.q_ref = bf16[1024,768]{1,0:T(8,128)(2,1)} custom-call(bf16[1024,2048]{1,0:T(8,128)(2,1)} %bitcast.57.g_ref, bf16[2048,256]{1,0:T(8,128)(2,1)} %bitcast.208, bf16[1024,768]{1,0:T(8,128)(2,1)} %get-tuple-element.123.qkv_ref, f32[1024,2]{1,0:T(8,128)} %get-tuple-element.167.log_ref, f32[1024,128]{1,0:T(8,128)} %get-tuple-element.114.cos_ref, ...), custom_call_target="tpu_custom_call" | custom-call | flops 2415919104 | bytes 12582912 | tf_op jit(solution)/shard_map/attend_backward/pallas_call | solution.py:244
  474.7 7.8 %share_of.6 = bf16[2,256,2048]{2,1,0:T(8,128)(2,1)} custom-call(s32[1]{0:T(128)} %bitcast.23.side_ref, bf16[1024,768]{1,0:T(8,128)(2,1)} %attend_backward.2.q_ref.refs_0_, bf16[2048,768]{1,0:T(8,128)(2,1)} %place_blocks.5.w_ref.refs_1_, bf16[1024,768]{1,0:T(8,128)(2,1)} %attend_backward.3.refs_2_.q_ref, bf16[2048,768]{1,0:T(8,128)(2,1)} %pad_maximum_fusion.w_ref.refs_3_), custom_call_target="tpu_custom_call" | custom-call | flops 3221225472 | bytes 12582912 | tf_op jit(solution)/shard_map/share_of/pallas_call | solution.py:268
  488.7 17.1 %collective-permute-done.50.refs_3_ = bf16[256,2048]{1,0:T(8,128)(2,1)} collective-permute-done((bf16[256,2048]{1,0:T(8,128)(2,1)}, bf16[256,2048]{1,0:T(8,128)(2,1)}, u32[]{:S(2)}, u32[]{:S(2)}) %collective-permute-start.50) | collective-permute-done | bytes 1048608 | tf_op jit(solution)/shard_map/ppermute | solution.py:362
  514.6 9.1 %weight_grads.3 = (bf16[4,256,1024]{2,1,0:T(8,128)(2,1)}, bf16[4,256,1024]{2,1,0:T(8,128)(2,1)}) custom-call(bf16[1024,2048]{1,0:T(8,128)(2,1)} %bitcast.212, bf16[1024,768]{1,0:T(8,128)(2,1)} %attend_backward.3.refs_2_.q_ref, bf16[1024,2048]{1,0:T(8,128)(2,1)} %bitcast.57.g_ref, bf16[1024,256]{1,0:T(8,128)(2,1)} %get-tuple-element.144.refs_0_.h_ref), custom_call_target="tpu_custom_call" | custom-call | flops 4294967296 | bytes 14680064 | tf_op jit(solution)/shard_map/weight_grads/pallas_call | solution.py:290
  535.2 13.2 %collective-permute-done.58 = bf16[2,256,1024]{2,1,0:T(8,128)(2,1)S(1)} collective-permute-done((bf16[2,256,1024]{2,1,0:T(8,128)(2,1)S(1)}, bf16[2,256,1024]{2,1,0:T(8,128)(2,1)S(1)}, u32[]{:S(2)}, u32[]{:S(2)}) %collective-permute-start.58) | collective-permute-done | bytes 1048608 | tf_op jit(solution)/shard_map/ppermute | solution.py:382
  551.6 14.2 %collective-permute-done.60 = bf16[256,1024]{1,0:T(8,128)(2,1)S(1)} collective-permute-done((bf16[256,1024]{1,0:T(8,128)(2,1)S(1)}, bf16[256,1024]{1,0:T(8,128)(2,1)S(1)}, u32[]{:S(2)}, u32[]{:S(2)}) %collective-permute-start.60) | collective-permute-done | bytes 524320 | tf_op jit(solution)/shard_map/ppermute | solution.py:382
  573.0 28.2 %collective-permute-done.61 = bf16[256,1024]{1,0:T(8,128)(2,1)S(1)} collective-permute-done((bf16[256,1024]{1,0:T(8,128)(2,1)S(1)}, bf16[256,1024]{1,0:T(8,128)(2,1)S(1)}, u32[]{:S(2)}, u32[]{:S(2)}) %collective-permute-start.61) | collective-permute-done | bytes 524320 | tf_op jit(solution)/shard_map/ppermute | solution.py:562
  (338 shorter events, 268.5 us)
Async XLA Ops:
  7.2 172.6 %all-gather.3.cloned.1.call-start = ((), (), s32[]{:S(2)}) async-start(), calls=%async_computation.2 | async-start | bytes 9437184 | tf_op jit(solution)/shard_map/all_gather | solution.py:482
  12.9 43.1 %collective-permute-start = (bf16[256,2048]{1,0:T(8,128)(2,1)S(1)}, bf16[256,2048]{1,0:T(8,128)(2,1)}, u32[]{:S(2)}, u32[]{:S(2)}) collective-permute-start(bf16[256,2048]{1,0:T(8,128)(2,1)S(1)} %fusion.15), channel_id=1, source_target_pairs={{0,2},{1,3},{2,0},{3,1},{4,6},{5,7},{6,4},{7,5},{8,10},{9,11},{10,... | collective-permute-start | bytes 3145736 | tf_op jit(solution)/shard_map/ppermute | solution.py:362
  15.9 32.1 %collective-permute-start.1 = (bf16[256,768]{1,0:T(8,128)(2,1)}, bf16[256,768]{1,0:T(8,128)(2,1)}, u32[]{:S(2)}, u32[]{:S(2)}) collective-permute-start(bf16[256,768]{1,0:T(8,128)(2,1)} %get-tuple-element.109), channel_id=1, source_target_pairs={{0,4},{1,5},{2,6},{3,7},{4,0},{5,1},{6,2},{7,3},{8,12},{9,13},{10,... | collective-permute-start | bytes 1179656 | tf_op jit(solution)/shard_map/ppermute | solution.py:469
  18.5 36.8 %collective-permute-start.2 = (bf16[256,768]{1,0:T(8,128)(2,1)}, bf16[256,768]{1,0:T(8,128)(2,1)}, u32[]{:S(2)}, u32[]{:S(2)}) collective-permute-start(bf16[256,768]{1,0:T(8,128)(2,1)} %get-tuple-element.110), channel_id=1, source_target_pairs={{0,4},{1,5},{2,6},{3,7},{4,0},{5,1},{6,2},{7,3},{8,12},{9,13},{10,... | collective-permute-start | bytes 1179656 | tf_op jit(solution)/shard_map/ppermute | solution.py:469
  56.0 212.5 %all-gather.5.cloned.1.call-start = ((), (), s32[]{:S(2)}) async-start(), calls=%async_computation.3 | async-start | bytes 9437184 | tf_op jit(solution)/shard_map/all_gather | solution.py:505
  79.8 28.4 %collective-permute-start.10 = (bf16[256,768]{1,0:T(8,128)(2,1)}, bf16[256,768]{1,0:T(8,128)(2,1)S(1)}, u32[]{:S(2)}, u32[]{:S(2)}) collective-permute-start(bf16[256,768]{1,0:T(8,128)(2,1)} %collective-permute-done.5.refs_1_), channel_id=1, source_target_pairs={{0,16},{8,24},{16,0},{24,8},{1,17},{9,25},{17,1},{25,9},{2,18},{10... | collective-permute-start | bytes 1179656 | tf_op jit(solution)/shard_map/ppermute | solution.py:362
  146.6 30.9 %collective-permute-start.20 = (bf16[256,2048]{1,0:T(8,128)(2,1)S(1)}, bf16[256,2048]{1,0:T(8,128)(2,1)}, u32[]{:S(2)}, u32[]{:S(2)}) collective-permute-start(bf16[256,2048]{1,0:T(8,128)(2,1)S(1)} %fusion.32), channel_id=1, source_target_pairs={{0,2},{1,3},{2,0},{3,1},{4,6},{5,7},{6,4},{7,5},{8,10},{9,11},{10,... | collective-permute-start | bytes 3145736 | tf_op jit(solution)/shard_map/ppermute | solution.py:382
  183.2 205.2 %reduce-scatter.3.cloned.1.call-start = ((), (), s32[]{:S(2)}) async-start(), calls=%async_computation.4 | async-start | bytes 9437184 | tf_op jit(solution)/shard_map/reduce_scatter | solution.py:518
  299.8 357.2 %reduce-scatter.5.cloned.1.call-start = ((), (), s32[]{:S(2)}) async-start(), calls=%async_computation.5 | async-start | bytes 9437184 | tf_op jit(solution)/shard_map/reduce_scatter | solution.py:536
  315.9 48.1 %collective-permute-start.29 = (bf16[2,512,1024]{2,1,0:T(8,128)(2,1)}, bf16[2,512,1024]{2,1,0:T(8,128)(2,1)}, u32[]{:S(2)}, u32[]{:S(2)}) collective-permute-start(bf16[2,512,1024]{2,1,0:T(8,128)(2,1)} %dynamic-slice_bitcast_fusion), channel_id=1, source_target_pairs={{0,16},{8,24},{16,0},{24,8},{1,17},{9,25},{17,1},{25,9},{2,18},{10... | collective-permute-start | bytes 6291464 | tf_op jit(solution)/shard_map/ppermute | solution.py:382
  332.8 48.4 %collective-permute-start.28 = (bf16[2,256,2048]{2,1,0:T(8,128)(2,1)}, bf16[2,256,2048]{2,1,0:T(8,128)(2,1)}, u32[]{:S(2)}, u32[]{:S(2)}) collective-permute-start(bf16[2,256,2048]{2,1,0:T(8,128)(2,1)} %dynamic-slice_bitcast_fusion.1), channel_id=1, source_target_pairs={{0,8},{8,0},{16,24},{24,16},{1,9},{9,1},{17,25},{25,17},{2,10},{10... | collective-permute-start | bytes 6291464 | tf_op jit(solution)/shard_map/ppermute | solution.py:382
  428.9 27.9 %collective-permute-start.39 = (bf16[512,1024]{1,0:T(8,128)(2,1)}, bf16[512,1024]{1,0:T(8,128)(2,1)}, u32[]{:S(2)}, u32[]{:S(2)}) collective-permute-start(bf16[512,1024]{1,0:T(8,128)(2,1)} %fusion.26.refs_0_), channel_id=1, source_target_pairs={{0,16},{8,24},{16,0},{24,8},{1,17},{9,25},{17,1},{25,9},{2,18},{10... | collective-permute-start | bytes 3145736 | tf_op jit(solution)/shard_map/ppermute | solution.py:362
  456.8 29.6 %collective-permute-start.49 = (bf16[256,2048]{1,0:T(8,128)(2,1)}, bf16[256,2048]{1,0:T(8,128)(2,1)}, u32[]{:S(2)}, u32[]{:S(2)}) collective-permute-start(bf16[256,2048]{1,0:T(8,128)(2,1)} %fusion.27.refs_0_), channel_id=1, source_target_pairs={{0,16},{8,24},{16,0},{24,8},{1,17},{9,25},{17,1},{25,9},{2,18},{10... | collective-permute-start | bytes 3145736 | tf_op jit(solution)/shard_map/ppermute | solution.py:362
  458.8 47.0 %collective-permute-start.50 = (bf16[256,2048]{1,0:T(8,128)(2,1)}, bf16[256,2048]{1,0:T(8,128)(2,1)}, u32[]{:S(2)}, u32[]{:S(2)}) collective-permute-start(bf16[256,2048]{1,0:T(8,128)(2,1)} %collective-permute-done.38.refs_1_), channel_id=1, source_target_pairs={{0,16},{8,24},{16,0},{24,8},{1,17},{9,25},{17,1},{25,9},{2,18},{10... | collective-permute-start | bytes 3145736 | tf_op jit(solution)/shard_map/ppermute | solution.py:362
  459.6 55.0 %collective-permute-start.51 = (bf16[512,1024]{1,0:T(8,128)(2,1)}, bf16[512,1024]{1,0:T(8,128)(2,1)}, u32[]{:S(2)}, u32[]{:S(2)}) collective-permute-start(bf16[512,1024]{1,0:T(8,128)(2,1)} %fusion.26.refs_0_), channel_id=1, source_target_pairs={{0,8},{8,0},{16,24},{24,16},{1,9},{9,1},{17,25},{25,17},{2,10},{10... | collective-permute-start | bytes 3145736 | tf_op jit(solution)/shard_map/ppermute | solution.py:362
  460.7 53.9 %collective-permute-start.52 = (bf16[512,1024]{1,0:T(8,128)(2,1)}, bf16[512,1024]{1,0:T(8,128)(2,1)}, u32[]{:S(2)}, u32[]{:S(2)}) collective-permute-start(bf16[512,1024]{1,0:T(8,128)(2,1)} %collective-permute-done.39.refs_2_), channel_id=1, source_target_pairs={{0,8},{8,0},{16,24},{24,16},{1,9},{9,1},{17,25},{25,17},{2,10},{10... | collective-permute-start | bytes 3145736 | tf_op jit(solution)/shard_map/ppermute | solution.py:362
  482.5 50.0 %collective-permute-start.40 = (bf16[2,256,2048]{2,1,0:T(8,128)(2,1)}, bf16[2,256,2048]{2,1,0:T(8,128)(2,1)}, u32[]{:S(2)}, u32[]{:S(2)}) collective-permute-start(bf16[2,256,2048]{2,1,0:T(8,128)(2,1)} %share_of.6), channel_id=1, source_target_pairs={{0,1},{1,0},{2,3},{3,2},{4,5},{5,4},{6,7},{7,6},{8,9},{9,8},{10,11... | collective-permute-start | bytes 6291464 | tf_op jit(solution)/shard_map/ppermute | solution.py:440
  486.4 41.7 %collective-permute-start.42 = (bf16[2,256,1024]{2,1,0:T(8,128)(2,1)}, bf16[2,256,1024]{2,1,0:T(8,128)(2,1)S(1)}, u32[]{:S(2)}, u32[]{:S(2)}) collective-permute-start(bf16[2,256,1024]{2,1,0:T(8,128)(2,1)} %dynamic-slice_bitcast_fusion.4), channel_id=1, source_target_pairs={{0,16},{8,24},{16,0},{24,8},{1,17},{9,25},{17,1},{25,9},{2,18},{10... | collective-permute-start | bytes 3145736 | tf_op jit(solution)/shard_map/ppermute | solution.py:382
  526.2 42.2 %collective-permute-start.53 = (bf16[2,256,1024]{2,1,0:T(8,128)(2,1)S(1)}, bf16[2,256,1024]{2,1,0:T(8,128)(2,1)S(1)}, u32[]{:S(2)}, u32[]{:S(2)}) collective-permute-start(bf16[2,256,1024]{2,1,0:T(8,128)(2,1)S(1)} %dynamic-slice_bitcast_fusion.3), channel_id=1, source_target_pairs={{0,8},{8,0},{16,24},{24,16},{1,9},{9,1},{17,25},{25,17},{2,10},{10... | collective-permute-start | bytes 3145736 | tf_op jit(solution)/shard_map/ppermute | solution.py:382
  535.1 30.7 %collective-permute-start.60 = (bf16[256,1024]{1,0:T(8,128)(2,1)S(1)}, bf16[256,1024]{1,0:T(8,128)(2,1)S(1)}, u32[]{:S(2)}, u32[]{:S(2)}) collective-permute-start(bf16[256,1024]{1,0:T(8,128)(2,1)S(1)} %fusion.53), channel_id=1, source_target_pairs={{0,8},{8,0},{16,24},{24,16},{1,9},{9,1},{17,25},{25,17},{2,10},{10... | collective-permute-start | bytes 1572872 | tf_op jit(solution)/shard_map/ppermute | solution.py:382
  549.6 53.2 %collective-permute-start.43 = (bf16[256,2048]{1,0:T(8,128)(2,1)S(1)}, bf16[256,2048]{1,0:T(8,128)(2,1)S(1)}, u32[]{:S(2)}, u32[]{:S(2)}) collective-permute-start(bf16[256,2048]{1,0:T(8,128)(2,1)S(1)} %fusion.35), channel_id=1, source_target_pairs={{0,2},{1,3},{2,0},{3,1},{4,6},{5,7},{6,4},{7,5},{8,10},{9,11},{10,... | collective-permute-start | bytes 3145736 | tf_op jit(solution)/shard_map/ppermute | solution.py:382
  565.9 35.2 %collective-permute-start.61 = (bf16[256,1024]{1,0:T(8,128)(2,1)S(1)}, bf16[256,1024]{1,0:T(8,128)(2,1)S(1)}, u32[]{:S(2)}, u32[]{:S(2)}) collective-permute-start(bf16[256,1024]{1,0:T(8,128)(2,1)S(1)} %fusion.36), channel_id=1, source_target_pairs={{0,4},{1,5},{2,6},{3,7},{4,0},{5,1},{6,2},{7,3},{8,12},{9,13},{10,... | collective-permute-start | bytes 1572872 | tf_op jit(solution)/shard_map/ppermute | solution.py:562
  568.9 37.8 %collective-permute-start.54 = (bf16[256,1024]{1,0:T(8,128)(2,1)S(1)}, bf16[256,1024]{1,0:T(8,128)(2,1)S(1)}, u32[]{:S(2)}, u32[]{:S(2)}) collective-permute-start(bf16[256,1024]{1,0:T(8,128)(2,1)S(1)} %fusion.50), channel_id=1, source_target_pairs={{0,16},{8,24},{16,0},{24,8},{1,17},{9,25},{17,1},{25,9},{2,18},{10... | collective-permute-start | bytes 1572872 | tf_op jit(solution)/shard_map/ppermute | solution.py:382
  569.1 37.6 %collective-permute-start.56 = (bf16[256,1024]{1,0:T(8,128)(2,1)S(1)}, bf16[256,1024]{1,0:T(8,128)(2,1)S(1)}, u32[]{:S(2)}, u32[]{:S(2)}) collective-permute-start(bf16[256,1024]{1,0:T(8,128)(2,1)S(1)} %fusion.39), channel_id=1, source_target_pairs={{0,4},{1,5},{2,6},{3,7},{4,0},{5,1},{6,2},{7,3},{8,12},{9,13},{10,... | collective-permute-start | bytes 1572872 | tf_op jit(solution)/shard_map/ppermute | solution.py:562
  (89 other events, 1263.0 us)
Sparse Core Ops, SparseCore 0:
  56.2 85.8 all-gather.2
  183.3 85.2 all-gather.4
  299.9 88.4 reduce-scatter.2
  429.0 89.3 reduce-scatter.4

commit v12 on v11

--- a/solution.py
+++ b/solution.py
@@ -185,6 +185,21 @@
         out_ref[0, :, 3 * width :] = narrow(product(g_ref[:, here], h_ref[...], (0, 0)))
 
 
+def hidden_kernel(offset_ref, x_ref, up_ref, top_ref, gate_ref, width_ref, share_ref, hidden_ref, grad_ref, dots_ref):
+    pre = product(x_ref[...], up_ref[...], (1, 0))
+    column = lax.broadcasted_iota(jnp.int32, pre.shape, 1) + offset_ref[0]
+    live = column * 4 < (width_ref[...] + 1) * FF
+    relu_act = jnp.where(live, jnp.maximum(pre, 0.0), 0.0)
+    hidden = narrow(relu_act * relu_act)
+    top = top_ref[...]
+    grad = narrow(top * gate_ref[...] * 2.0 * relu_act)
+    hidden_ref[...] = hidden
+    grad_ref[...] = grad
+    dots = jnp.sum(wide(hidden) * top, axis=1, keepdims=True)
+    dots_ref[...] = jnp.broadcast_to(dots, (dots.shape[0], 128)).T[:1]
+    share_ref[...] = narrow(product(grad, up_ref[...], (1, 1)))
+
+
 def place_kernel(count, widths, turned, at_ref, *refs):
     lanes = (len(refs) - len(widths)) // count
     blocks, outs = refs[: lanes * count], refs[lanes * count :]
@@ -280,6 +295,31 @@
         ),
         name="share_of",
     )(side.astype(jnp.int32).reshape(1), *[x for pair in pairs for x in pair])
+
+
+def hidden_pass(x, up, top_down, gates, widths, offset):
+    tokens, dim = x.shape
+    cols = up.shape[1]
+    block = 256
+    rows_of = lambda n: pl.BlockSpec((block, n), lambda i, at: (i, 0))
+    return pl.pallas_call(
+        hidden_kernel,
+        grid_spec=pltpu.PrefetchScalarGridSpec(
+            num_scalar_prefetch=1,
+            grid=(tokens // block,),
+            in_specs=[rows_of(dim), pl.BlockSpec((dim, cols), lambda i, at: (0, 0)), rows_of(cols), rows_of(1), rows_of(1)],
+            out_specs=[rows_of(dim), rows_of(cols), rows_of(cols), pl.BlockSpec((1, block), lambda i, at: (0, i))],
+        ),
+        out_shape=[
+            jax.ShapeDtypeStruct((tokens, dim), jnp.bfloat16),
+            jax.ShapeDtypeStruct((tokens, cols), jnp.bfloat16),
+            jax.ShapeDtypeStruct((tokens, cols), jnp.bfloat16),
+            jax.ShapeDtypeStruct((1, tokens), jnp.float32),
+        ],
+        compiler_params=pltpu.CompilerParams(vmem_limit_bytes=VMEM_LIMIT),
+        cost_estimate=pl.CostEstimate(flops=4 * tokens * dim * cols, bytes_accessed=40 << 20, transcendentals=0),
+        name="hidden_pass",
+    )(offset.astype(jnp.int32).reshape(1), x, up, top_down, gates[:, None], widths)
 
 
 def weight_grads(x, qkv_grad, g, heads_out, count):
@@ -363,9 +403,10 @@
     return held
 
 
-def by_index(held, index, axis=0):
+def by_index(held, index, axis=0, out=None):
     shape = held[0].shape
-    out = jnp.zeros(shape[:axis] + (len(held),) + shape[axis:], held[0].dtype)
+    if out is None:
+        out = jnp.zeros(shape[:axis] + (len(held),) + shape[axis:], held[0].dtype)
     for far, block in held.items():
         out = lax.dynamic_update_index_in_dim(out, block, index ^ far, axis)
     return out
@@ -432,8 +473,8 @@
         routed_own = lax.dynamic_slice_in_dim(routed_flag, rank * rows, rows, 0)
         cos, sin = rope_tables(SEQ_LEN, HD)
 
-        def place_sequence(held):
-            return by_index(held, place).reshape(SEQ_LEN, -1)
+        def place_sequence(held, out=None):
+            return by_index(held, place, 0, out).reshape(SEQ_LEN, -1)
 
         def core_sum(pairs):
             theirs = share_of(pairs, rows, 1 - core)
@@ -505,15 +546,11 @@
         inputs_two = lax.all_gather(narrow(normed_two), "mp", axis=0, tiled=True)
         gates = by_index(xor_gather(gate_two.reshape(-1, 128), "mp", ranks, bits_of(ranks)), rank).reshape(-1)
 
-        col_ids = rank * cols_local + jnp.arange(cols_local, dtype=jnp.int32)
-        col_mask = (col_ids[None, :] * 4 < (width_choice[:, 1:2] + 1) * FF).astype(jnp.float32)
         inputs_two, top_down = lax.optimization_barrier((inputs_two, top_down))
-        pre = product(inputs_two, up_weight, (1, 0))
-        relu_act = jax.nn.relu(pre)
-        hidden = narrow(relu_act * relu_act * col_mask)
-        pre_grad = narrow(top_down * gates[:, None] * col_mask * 2.0 * relu_act)
-        dots = jnp.sum(wide(hidden) * top_down, axis=1).reshape(-1, 128)
-        share = narrow(product(pre_grad, up_weight, (1, 1)))
+        share, hidden, pre_grad, dots = hidden_pass(
+            inputs_two, up_weight, top_down, gates, width_choice[:, 1:2], rank * cols_local
+        )
+        dots = dots.reshape(-1, 128)
         share, hidden, pre_grad = lax.optimization_barrier((share, hidden, pre_grad))
         normed_grad_two = wide(lax.psum_scatter(share, "mp", scatter_dimension=0, tiled=True))
         gate_grad_two = lax.dynamic_slice_in_dim(all_sum(dots, {"mp": ranks}).reshape(-1), rank * rows, rows, 0)
@@ -522,21 +559,23 @@
         lanes = [x.reshape(columns, -1, x.shape[1]) for x in lanes]
         lanes = column_scatter(lanes, columns, column, cut=1)
         hidden_share = narrow(product(hidden, down_weight, (1, 0)))
-        normed_grad_two, hidden_share, *lanes = lax.optimization_barrier((normed_grad_two, hidden_share, *lanes))
+        blank = jnp.zeros((group, rows, dim), jnp.bfloat16)
+        normed_grad_two, hidden_share, blank, *lanes = lax.optimization_barrier(
+            (normed_grad_two, hidden_share, blank, *lanes)
+        )
         lanes = [narrow(x) for x in column_scatter(lanes, columns, column, start=1)]
 
-        router_part, router_two = gate_backward(normed_two, hidden_router, state_two, gate_grad_two)
+        router_part, _ = gate_backward(normed_two, hidden_router, state_two, gate_grad_two)
         middle_part, gain_two = norm_backward(normed_grad_two + router_part, scaled_two, inverse_two, hidden_gain)
         middle_grad = wide(out_grad) + middle_part
         grads_one = place_sequence(
-            xor_gather(narrow(gate_one[:, None] * middle_grad), "mp", ranks, pair_bits + [1])
+            xor_gather(narrow(gate_one[:, None] * middle_grad), "mp", ranks, pair_bits + [1]), blank
         )
         helds = column_gather(lanes, columns, cut=1)
         grads_one, hidden_share, lanes = lax.optimization_barrier((grads_one, hidden_share, lanes))
         hidden_branch = wide(lax.psum_scatter(hidden_share, "mp", scatter_dimension=0, tiled=True))
         layer_output = narrow(middle + gate_two[:, None] * hidden_branch)
 
-        gate_grad_one = jnp.sum(middle_grad * mixer_branch, axis=1)
         pairs, sent = [], []
         grads_now = grads_one
         for k in range(sequences)[::-1]:
@@ -550,6 +589,11 @@
             if k:
                 grads_now, part, helds = lax.optimization_barrier((grads_now, part, helds))
                 sent.append((k, part))
+                normed_late, state_late, dots_late, middle_late, _ = lax.optimization_barrier(
+                    (normed_two, state_two, gate_grad_two, middle_grad, part)
+                )
+                router_two = gate_backward(normed_late, hidden_router, state_late, dots_late)[1]
+                gate_grad_one = jnp.sum(middle_late * mixer_branch, axis=1)
         blocks = core_sum(pairs)
         sent = [(k, column_scatter(lanes, columns, column, cut=1)) for k, lanes in sent]
         blocks, gated = lax.optimization_barrier((blocks, [lanes for _, lanes in sent]))

time: 672 us -> 670 us (level)
  matrix products: 97.5 us -> 64.8 us
  Pallas kernels: 119 us -> 145 us
    dot_general x6 -> x4, matrix products: 81 us -> 51.1 us  [product(): lax.dot_general(a, b, ((dims[:1], dims[1:]), ((), ())), preferred_element...]
    pallas_call x0 -> x1, Pallas kernels: none -> 25.4 us  [hidden_pass(): pl.pallas_call(hidden_kernel, grid_spec=pltpu.PrefetchScalarGridSpec(num_...]
    unnamed x85 -> x92, local copies, waits for them, and re-layouts: 13.6 us -> 12.2 us
  transfers between devices with their start and end apart: 71 -> 71, of which waited for: 28 -> 28; matrix products, arithmetic and copies ran while one was open for 18% -> 19% of each run, Pallas kernels for 18% -> 18%
where the time goes in v12:
time: 670 us; the launch traced here: 666 us
  waiting for transfers between devices  271 us (40%)
  Pallas kernels  145 us (22%)
  starting transfers between devices  78.2 us (12%)
  matrix products  64.8 us (10%)
  other arithmetic  54.4 us (8%)
  local copies, waits for them, and re-layouts  37.4 us (6%)
  between operations  15.1 us (2%)
    ppermute x14, waiting for transfers between devices, xor_scatter(): lax.ppermute(narrow(pick(blocks, 1 - side, at)), axis_name, swap_pairs(si...  83.8 us
    ppermute x37, waiting for transfers between devices, xor_gather(): held[far ^ bit] = lax.ppermute(held[far], axis, swap_pairs(size, bit))  69.7 us
    dot_general x4, matrix products, product(): lax.dot_general(a, b, ((dims[:1], dims[1:]), ((), ())), preferred_element...  51.1 us
    all_gather x1, waiting for transfers between devices, local(): inputs_two = lax.all_gather(narrow(normed_two), 'mp', axis=0, tiled=True)  46.6 us
    ppermute x37, starting transfers between devices, xor_gather(): held[far ^ bit] = lax.ppermute(held[far], axis, swap_pairs(size, bit))  41.8 us
    ppermute x2, waiting for transfers between devices, local(): lax.ppermute(x, 'mp', back)  31.4 us
    pallas_call x2, Pallas kernels, attend_backward(): pl.pallas_call(backward_kernel, out_shape=jax.ShapeDtypeStruct((tokens, 3...  26.9 us
    ppermute x4, waiting for transfers between devices, local(): lax.ppermute(x, 'mp', shift_pairs(ranks, k * group))  26.9 us
  transfers between devices with their start and end apart: 71, of which 28 were waited for; matrix products, arithmetic and copies ran while one was open for 19% of the time, Pallas kernels for 18%

profile of v12, /device:TPU:0, one launch (start us, length us, event | category | flops | bytes accessed | tf_op | source)
XLA Modules:
  0.0 665.8 jit_solution(11456686007300480657)
XLA Ops:
  28.4 19.6 %collective-permute-done.1.refs_0_ = bf16[256,768]{1,0:T(8,128)(2,1)} collective-permute-done((bf16[256,768]{1,0:T(8,128)(2,1)}, bf16[256,768]{1,0:T(8,128)(2,1)}, u32[]{:S(2)}, u32[]{:S(2)}) %collective-permute-start.1) | collective-permute-done | bytes 393248 | tf_op jit(solution)/shard_map/ppermute | solution.py:510
  66.8 12.8 %attend_forward.2 = (bf16[1024,768]{1,0:T(8,128)(2,1)}, bf16[1024,256]{1,0:T(8,128)(2,1)}, f32[1024,2]{1,0:T(8,128)}) custom-call(bf16[1024,2048]{1,0:T(8,128)(2,1)} %bitcast.205, bf16[2048,768]{1,0:T(8,128)(2,1)} %pad_maximum_fusion.w_ref.refs_3_, f32[1024,128]{1,0:T(8,128)} %get-tuple-element.126.cos_ref, f32[1024,128]{1,0:T(8,128)} %get-tuple-element.127.sin_ref, ...), custom_call_target="tpu_custom_call" | custom-call | flops 3758096384 | bytes 12582912 | tf_op jit(solution)/shard_map/attend_forward/pallas_call | solution.py:237
  85.6 17.6 %collective-permute-done.13.refs_1_ = bf16[256,256]{1,0:T(8,128)(2,1)S(1)} collective-permute-done((bf16[256,256]{1,0:T(8,128)(2,1)S(1)}, bf16[256,256]{1,0:T(8,128)(2,1)S(1)}, u32[]{:S(2)}, u32[]{:S(2)}) %collective-permute-start.13) | collective-permute-done | bytes 131104 | tf_op jit(solution)/shard_map/ppermute | solution.py:402
  116.7 12.5 %attend_forward.3 = (bf16[1024,768]{1,0:T(8,128)(2,1)}, bf16[1024,256]{1,0:T(8,128)(2,1)}, f32[1024,2]{1,0:T(8,128)}) custom-call(bf16[1024,2048]{1,0:T(8,128)(2,1)} %bitcast.206, bf16[2048,768]{1,0:T(8,128)(2,1)} %place_blocks.5.w_ref.refs_1_, f32[1024,128]{1,0:T(8,128)} %get-tuple-element.126.cos_ref, f32[1024,128]{1,0:T(8,128)} %get-tuple-element.127.sin_ref, ...), custom_call_target="tpu_custom_call" | custom-call | flops 3758096384 | bytes 12582912 | tf_op jit(solution)/shard_map/attend_forward/pallas_call | solution.py:237
  156.4 21.0 %collective-permute-done.20 = bf16[256,2048]{1,0:T(8,128)(2,1)S(1)} collective-permute-done((bf16[256,2048]{1,0:T(8,128)(2,1)S(1)}, bf16[256,2048]{1,0:T(8,128)(2,1)S(1)}, u32[]{:S(2)}, u32[]{:S(2)}) %collective-permute-start.20) | collective-permute-done | bytes 1048608 | tf_op jit(solution)/shard_map/ppermute | solution.py:423
  198.9 14.6 %fusion.84.top_ref = f32[2048,1024]{1,0:T(8,128)} fusion(bf16[2048,2048]{1,0:T(8,128)(2,1)} %all-gather.3.cloned.1.call-done, bf16[1024,2048]{1,0:T(8,128)(2,1)} %param.22), kind=kOutput, calls=%fused_computation.194 | convolution fusion | flops 8589934592 | bytes 20971520 | tf_op jit(solution)/shard_map/dot_general | solution.py:94
  224.5 46.6 %all-gather.5.cloned.1.call-done.x_ref = bf16[2048,2048]{1,0:T(8,128)(2,1)} async-done(((bf16[256,2048]{1,0:T(8,128)(2,1)}), bf16[2048,2048]{1,0:T(8,128)(2,1)}) %all-gather.5.cloned.1.call-update) | async-done | bytes 8388624 | tf_op jit(solution)/shard_map/all_gather | solution.py:546
  271.1 25.4 %hidden_pass.1 = (bf16[2048,2048]{1,0:T(8,128)(2,1)}, bf16[2048,1024]{1,0:T(8,128)(2,1)}, bf16[2048,1024]{1,0:T(8,128)(2,1)}, f32[1,2048]{1,0:T(1,128)}) custom-call(s32[1]{0:T(128)} %bitcast.29.offset_ref, bf16[2048,2048]{1,0:T(8,128)(2,1)} %all-gather.5.cloned.1.call-done.x_ref, bf16[2048,1024]{1,0:T(8,128)(2,1)} %up_ref.1, f32[2048,1024]{1,0:T(8,128)} %fusion.84.top_ref, ...), custom_call_target="tpu_custom_call" | custom-call | flops 17179869184 | bytes 41943040 | tf_op jit(solution)/shard_map/hidden_pass/pallas_call | solution.py:305
  296.6 13.0 %convolution_convert_fusion.1 = bf16[2048,1024]{1,0:T(8,128)(2,1)S(1)} fusion(bf16[2048,2048]{1,0:T(8,128)(2,1)} %all-gather.5.cloned.1.call-done.x_ref, bf16[2048,1024]{1,0:T(8,128)(2,1)} %get-tuple-element.170), kind=kOutput, calls=%fused_computation.9 | convolution fusion | flops 8592031744 | bytes 16777216 | tf_op jit(solution)/shard_map/dot_general | solution.py:94
  313.8 12.3 %fusion.2 = bf16[1024,2048]{1,0:T(8,128)(2,1)S(1)} fusion(bf16[2048,1024]{1,0:T(8,128)(2,1)S(1)} %copy-done.44, bf16[2048,2048]{1,0:T(8,128)(2,1)} %all-gather.3.cloned.1.call-done, f32[2048]{0:T(1024)S(1)} %bitcast.225), kind=kOutput, calls=%fused_computation.8 | convolution fusion | flops 8604614656 | bytes 16785408 | tf_op jit(solution)/shard_map/dot_general | solution.py:94
  331.2 11.3 %convolution_convert_fusion = bf16[2048,2048]{1,0:T(8,128)(2,1)} fusion(bf16[2048,1024]{1,0:T(8,128)(2,1)S(1)} %copy-done.44, bf16[1024,2048]{1,0:T(8,128)(2,1)S(1)} %copy-done.43), kind=kOutput, calls=%fused_computation.3 | convolution fusion | flops 8594128896 | bytes 16777216 | tf_op jit(solution)/shard_map/dot_general | solution.py:94
  345.7 14.7 %collective-permute-done.29 = bf16[2,512,1024]{2,1,0:T(8,128)(2,1)} collective-permute-done((bf16[2,512,1024]{2,1,0:T(8,128)(2,1)}, bf16[2,512,1024]{2,1,0:T(8,128)(2,1)}, u32[]{:S(2)}, u32[]{:S(2)}) %collective-permute-start.29) | collective-permute-done | bytes 2097184 | tf_op jit(solution)/shard_map/ppermute | solution.py:423
  365.5 12.1 %collective-permute-done.28 = bf16[2,256,2048]{2,1,0:T(8,128)(2,1)} collective-permute-done((bf16[2,256,2048]{2,1,0:T(8,128)(2,1)}, bf16[2,256,2048]{2,1,0:T(8,128)(2,1)}, u32[]{:S(2)}, u32[]{:S(2)}) %collective-permute-start.28) | collective-permute-done | bytes 2097184 | tf_op jit(solution)/shard_map/ppermute | solution.py:423
  396.8 19.4 %collective-permute-done.33 = bf16[256,2048]{1,0:T(8,128)(2,1)S(1)} collective-permute-done((bf16[256,2048]{1,0:T(8,128)(2,1)S(1)}, bf16[256,2048]{1,0:T(8,128)(2,1)S(1)}, u32[]{:S(2)}, u32[]{:S(2)}) %collective-permute-start.33) | collective-permute-done | bytes 1048608 | tf_op jit(solution)/shard_map/ppermute | solution.py:402
  426.8 13.8 %attend_backward.2.q_ref.refs_0_ = bf16[1024,768]{1,0:T(8,128)(2,1)} custom-call(bf16[1024,2048]{1,0:T(8,128)(2,1)} %bitcast.58.g_ref, bf16[2048,256]{1,0:T(8,128)(2,1)} %place_blocks.6.refs_3_.w_ref, bf16[1024,768]{1,0:T(8,128)(2,1)} %get-tuple-element.179.qkv_ref, f32[1024,2]{1,0:T(8,128)} %get-tuple-element.180.log_ref, ...), custom_call_target="tpu_custom_call" | custom-call | flops 2415919104 | bytes 12582912 | tf_op jit(solution)/shard_map/attend_backward/pallas_call | solution.py:259
  440.6 8.9 %weight_grads.2 = (bf16[4,256,1024]{2,1,0:T(8,128)(2,1)}, bf16[4,256,1024]{2,1,0:T(8,128)(2,1)}) custom-call(bf16[1024,2048]{1,0:T(8,128)(2,1)} %bitcast.207, bf16[1024,768]{1,0:T(8,128)(2,1)} %attend_backward.2.q_ref.refs_0_, bf16[1024,2048]{1,0:T(8,128)(2,1)} %bitcast.58.g_ref, bf16[1024,256]{1,0:T(8,128)(2,1)} %get-tuple-element.158.refs_2_.h_ref), custom_call_target="tpu_custom_call" | custom-call | flops 4294967296 | bytes 14680064 | tf_op jit(solution)/shard_map/weight_grads/pallas_call | solution.py:330
  456.1 13.2 %attend_backward.3.refs_2_.q_ref = bf16[1024,768]{1,0:T(8,128)(2,1)} custom-call(bf16[1024,2048]{1,0:T(8,128)(2,1)} %bitcast.58.g_ref, bf16[2048,256]{1,0:T(8,128)(2,1)} %bitcast.204, bf16[1024,768]{1,0:T(8,128)(2,1)} %get-tuple-element.135.qkv_ref, f32[1024,2]{1,0:T(8,128)} %get-tuple-element.184.log_ref, f32[1024,128]{1,0:T(8,128)} %get-tuple-element.126.cos_ref, ...), custom_call_target="tpu_custom_call" | custom-call | flops 2415919104 | bytes 12582912 | tf_op jit(solution)/shard_map/attend_backward/pallas_call | solution.py:259
  472.9 8.0 %share_of.6 = bf16[2,256,2048]{2,1,0:T(8,128)(2,1)} custom-call(s32[1]{0:T(128)} %bitcast.23.side_ref, bf16[1024,768]{1,0:T(8,128)(2,1)} %attend_backward.2.q_ref.refs_0_, bf16[2048,768]{1,0:T(8,128)(2,1)} %place_blocks.5.w_ref.refs_1_, bf16[1024,768]{1,0:T(8,128)(2,1)} %attend_backward.3.refs_2_.q_ref, bf16[2048,768]{1,0:T(8,128)(2,1)} %pad_maximum_fusion.w_ref.refs_3_), custom_call_target="tpu_custom_call" | custom-call | flops 3221225472 | bytes 12582912 | tf_op jit(solution)/shard_map/share_of/pallas_call | solution.py:283
  482.0 16.4 %collective-permute-done.50.refs_3_ = bf16[256,2048]{1,0:T(8,128)(2,1)} collective-permute-done((bf16[256,2048]{1,0:T(8,128)(2,1)}, bf16[256,2048]{1,0:T(8,128)(2,1)}, u32[]{:S(2)}, u32[]{:S(2)}) %collective-permute-start.50) | collective-permute-done | bytes 1048608 | tf_op jit(solution)/shard_map/ppermute | solution.py:402
  499.6 9.1 %weight_grads.3 = (bf16[4,256,1024]{2,1,0:T(8,128)(2,1)}, bf16[4,256,1024]{2,1,0:T(8,128)(2,1)}) custom-call(bf16[1024,2048]{1,0:T(8,128)(2,1)} %bitcast.208, bf16[1024,768]{1,0:T(8,128)(2,1)} %attend_backward.3.refs_2_.q_ref, bf16[1024,2048]{1,0:T(8,128)(2,1)} %bitcast.58.g_ref, bf16[1024,256]{1,0:T(8,128)(2,1)} %get-tuple-element.156.refs_0_.h_ref), custom_call_target="tpu_custom_call" | custom-call | flops 4294967296 | bytes 14680064 | tf_op jit(solution)/shard_map/weight_grads/pallas_call | solution.py:330
  511.6 8.0 %share_of.7 = bf16[2,256,2048]{2,1,0:T(8,128)(2,1)} custom-call(s32[1]{0:T(128)} %bitcast.3.side_ref, bf16[1024,768]{1,0:T(8,128)(2,1)} %attend_backward.2.q_ref.refs_0_, bf16[2048,768]{1,0:T(8,128)(2,1)} %place_blocks.5.w_ref.refs_1_, bf16[1024,768]{1,0:T(8,128)(2,1)} %attend_backward.3.refs_2_.q_ref, bf16[2048,768]{1,0:T(8,128)(2,1)} %pad_maximum_fusion.w_ref.refs_3_), custom_call_target="tpu_custom_call" | custom-call | flops 3221225472 | bytes 12582912 | tf_op jit(solution)/shard_map/share_of/pallas_call | solution.py:283
  524.6 15.3 %collective-permute-done.58 = bf16[2,256,1024]{2,1,0:T(8,128)(2,1)} collective-permute-done((bf16[2,256,1024]{2,1,0:T(8,128)(2,1)}, bf16[2,256,1024]{2,1,0:T(8,128)(2,1)}, u32[]{:S(2)}, u32[]{:S(2)}) %collective-permute-start.58) | collective-permute-done | bytes 1048608 | tf_op jit(solution)/shard_map/ppermute | solution.py:423
  551.4 12.3 %collective-permute-done.60 = bf16[256,1024]{1,0:T(8,128)(2,1)S(1)} collective-permute-done((bf16[256,1024]{1,0:T(8,128)(2,1)S(1)}, bf16[256,1024]{1,0:T(8,128)(2,1)S(1)}, u32[]{:S(2)}, u32[]{:S(2)}) %collective-permute-start.60) | collective-permute-done | bytes 524320 | tf_op jit(solution)/shard_map/ppermute | solution.py:423
  577.1 25.2 %collective-permute-done.61 = bf16[256,1024]{1,0:T(8,128)(2,1)S(1)} collective-permute-done((bf16[256,1024]{1,0:T(8,128)(2,1)S(1)}, bf16[256,1024]{1,0:T(8,128)(2,1)S(1)}, u32[]{:S(2)}, u32[]{:S(2)}) %collective-permute-start.61) | collective-permute-done | bytes 524320 | tf_op jit(solution)/shard_map/ppermute | solution.py:606
  (348 shorter events, 268.0 us)
Async XLA Ops:
  7.2 173.5 %all-gather.3.cloned.1.call-start = ((), (), s32[]{:S(2)}) async-start(), calls=%async_computation.2 | async-start | bytes 9437184 | tf_op jit(solution)/shard_map/all_gather | solution.py:523
  12.9 43.1 %collective-permute-start = (bf16[256,2048]{1,0:T(8,128)(2,1)S(1)}, bf16[256,2048]{1,0:T(8,128)(2,1)}, u32[]{:S(2)}, u32[]{:S(2)}) collective-permute-start(bf16[256,2048]{1,0:T(8,128)(2,1)S(1)} %fusion.11), channel_id=1, source_target_pairs={{0,2},{1,3},{2,0},{3,1},{4,6},{5,7},{6,4},{7,5},{8,10},{9,11},{10,... | collective-permute-start | bytes 3145736 | tf_op jit(solution)/shard_map/ppermute | solution.py:402
  15.9 32.1 %collective-permute-start.1 = (bf16[256,768]{1,0:T(8,128)(2,1)}, bf16[256,768]{1,0:T(8,128)(2,1)}, u32[]{:S(2)}, u32[]{:S(2)}) collective-permute-start(bf16[256,768]{1,0:T(8,128)(2,1)} %get-tuple-element.121), channel_id=1, source_target_pairs={{0,4},{1,5},{2,6},{3,7},{4,0},{5,1},{6,2},{7,3},{8,12},{9,13},{10,... | collective-permute-start | bytes 1179656 | tf_op jit(solution)/shard_map/ppermute | solution.py:510
  18.5 36.8 %collective-permute-start.2 = (bf16[256,768]{1,0:T(8,128)(2,1)}, bf16[256,768]{1,0:T(8,128)(2,1)}, u32[]{:S(2)}, u32[]{:S(2)}) collective-permute-start(bf16[256,768]{1,0:T(8,128)(2,1)} %get-tuple-element.122), channel_id=1, source_target_pairs={{0,4},{1,5},{2,6},{3,7},{4,0},{5,1},{6,2},{7,3},{8,12},{9,13},{10,... | collective-permute-start | bytes 1179656 | tf_op jit(solution)/shard_map/ppermute | solution.py:510
  56.0 215.1 %all-gather.5.cloned.1.call-start = ((), (), s32[]{:S(2)}) async-start(), calls=%async_computation.3 | async-start | bytes 9437184 | tf_op jit(solution)/shard_map/all_gather | solution.py:546
  79.7 28.5 %collective-permute-start.10 = (bf16[256,768]{1,0:T(8,128)(2,1)}, bf16[256,768]{1,0:T(8,128)(2,1)S(1)}, u32[]{:S(2)}, u32[]{:S(2)}) collective-permute-start(bf16[256,768]{1,0:T(8,128)(2,1)} %collective-permute-done.5.refs_1_), channel_id=1, source_target_pairs={{0,16},{8,24},{16,0},{24,8},{1,17},{9,25},{17,1},{25,9},{2,18},{10... | collective-permute-start | bytes 1179656 | tf_op jit(solution)/shard_map/ppermute | solution.py:402
  146.8 30.7 %collective-permute-start.20 = (bf16[256,2048]{1,0:T(8,128)(2,1)S(1)}, bf16[256,2048]{1,0:T(8,128)(2,1)S(1)}, u32[]{:S(2)}, u32[]{:S(2)}) collective-permute-start(bf16[256,2048]{1,0:T(8,128)(2,1)S(1)} %fusion.25), channel_id=1, source_target_pairs={{0,2},{1,3},{2,0},{3,1},{4,6},{5,7},{6,4},{7,5},{8,10},{9,11},{10,... | collective-permute-start | bytes 3145736 | tf_op jit(solution)/shard_map/ppermute | solution.py:423
  185.5 199.6 %reduce-scatter.3.cloned.1.call-start = ((), (), s32[]{:S(2)}) async-start(), calls=%async_computation.4 | async-start | bytes 9437184 | tf_op jit(solution)/shard_map/reduce_scatter | solution.py:555
  296.5 360.0 %reduce-scatter.5.cloned.1.call-start = ((), (), s32[]{:S(2)}) async-start(), calls=%async_computation.5 | async-start | bytes 9437184 | tf_op jit(solution)/shard_map/reduce_scatter | solution.py:576
  312.3 48.1 %collective-permute-start.29 = (bf16[2,512,1024]{2,1,0:T(8,128)(2,1)}, bf16[2,512,1024]{2,1,0:T(8,128)(2,1)}, u32[]{:S(2)}, u32[]{:S(2)}) collective-permute-start(bf16[2,512,1024]{2,1,0:T(8,128)(2,1)} %dynamic-slice_bitcast_fusion), channel_id=1, source_target_pairs={{0,16},{8,24},{16,0},{24,8},{1,17},{9,25},{17,1},{25,9},{2,18},{10... | collective-permute-start | bytes 6291464 | tf_op jit(solution)/shard_map/ppermute | solution.py:423
  329.2 48.3 %collective-permute-start.28 = (bf16[2,256,2048]{2,1,0:T(8,128)(2,1)}, bf16[2,256,2048]{2,1,0:T(8,128)(2,1)}, u32[]{:S(2)}, u32[]{:S(2)}) collective-permute-start(bf16[2,256,2048]{2,1,0:T(8,128)(2,1)} %dynamic-slice_bitcast_fusion.1), channel_id=1, source_target_pairs={{0,8},{8,0},{16,24},{24,16},{1,9},{9,1},{17,25},{25,17},{2,10},{10... | collective-permute-start | bytes 6291464 | tf_op jit(solution)/shard_map/ppermute | solution.py:423
  449.4 31.5 %collective-permute-start.49 = (bf16[256,2048]{1,0:T(8,128)(2,1)}, bf16[256,2048]{1,0:T(8,128)(2,1)}, u32[]{:S(2)}, u32[]{:S(2)}) collective-permute-start(bf16[256,2048]{1,0:T(8,128)(2,1)} %fusion.23.refs_0_), channel_id=1, source_target_pairs={{0,16},{8,24},{16,0},{24,8},{1,17},{9,25},{17,1},{25,9},{2,18},{10... | collective-permute-start | bytes 3145736 | tf_op jit(solution)/shard_map/ppermute | solution.py:402
  449.8 48.6 %collective-permute-start.50 = (bf16[256,2048]{1,0:T(8,128)(2,1)}, bf16[256,2048]{1,0:T(8,128)(2,1)}, u32[]{:S(2)}, u32[]{:S(2)}) collective-permute-start(bf16[256,2048]{1,0:T(8,128)(2,1)} %collective-permute-done.38.refs_1_), channel_id=1, source_target_pairs={{0,16},{8,24},{16,0},{24,8},{1,17},{9,25},{17,1},{25,9},{2,18},{10... | collective-permute-start | bytes 3145736 | tf_op jit(solution)/shard_map/ppermute | solution.py:402
  451.5 48.1 %collective-permute-start.51 = (bf16[512,1024]{1,0:T(8,128)(2,1)}, bf16[512,1024]{1,0:T(8,128)(2,1)}, u32[]{:S(2)}, u32[]{:S(2)}) collective-permute-start(bf16[512,1024]{1,0:T(8,128)(2,1)} %fusion.22.refs_0_), channel_id=1, source_target_pairs={{0,8},{8,0},{16,24},{24,16},{1,9},{9,1},{17,25},{25,17},{2,10},{10... | collective-permute-start | bytes 3145736 | tf_op jit(solution)/shard_map/ppermute | solution.py:402
  452.8 46.9 %collective-permute-start.52 = (bf16[512,1024]{1,0:T(8,128)(2,1)}, bf16[512,1024]{1,0:T(8,128)(2,1)}, u32[]{:S(2)}, u32[]{:S(2)}) collective-permute-start(bf16[512,1024]{1,0:T(8,128)(2,1)} %collective-permute-done.39.refs_2_), channel_id=1, source_target_pairs={{0,8},{8,0},{16,24},{24,16},{1,9},{9,1},{17,25},{25,17},{2,10},{10... | collective-permute-start | bytes 3145736 | tf_op jit(solution)/shard_map/ppermute | solution.py:402
  455.8 65.0 %collective-permute-start.42 = (bf16[2,256,1024]{2,1,0:T(8,128)(2,1)}, bf16[2,256,1024]{2,1,0:T(8,128)(2,1)}, u32[]{:S(2)}, u32[]{:S(2)}) collective-permute-start(bf16[2,256,1024]{2,1,0:T(8,128)(2,1)} %dynamic-slice_bitcast_fusion.4), channel_id=1, source_target_pairs={{0,16},{8,24},{16,0},{24,8},{1,17},{9,25},{17,1},{25,9},{2,18},{10... | collective-permute-start | bytes 3145736 | tf_op jit(solution)/shard_map/ppermute | solution.py:423
  480.9 62.0 %collective-permute-start.40 = (bf16[2,256,2048]{2,1,0:T(8,128)(2,1)}, bf16[2,256,2048]{2,1,0:T(8,128)(2,1)}, u32[]{:S(2)}, u32[]{:S(2)}) collective-permute-start(bf16[2,256,2048]{2,1,0:T(8,128)(2,1)} %share_of.6), channel_id=1, source_target_pairs={{0,1},{1,0},{2,3},{3,2},{4,5},{5,4},{6,7},{7,6},{8,9},{9,8},{10,11... | collective-permute-start | bytes 6291464 | tf_op jit(solution)/shard_map/ppermute | solution.py:481
  511.0 28.9 %collective-permute-start.58 = (bf16[2,256,1024]{2,1,0:T(8,128)(2,1)}, bf16[2,256,1024]{2,1,0:T(8,128)(2,1)}, u32[]{:S(2)}, u32[]{:S(2)}) collective-permute-start(bf16[2,256,1024]{2,1,0:T(8,128)(2,1)} %dynamic-slice_bitcast_fusion.2), channel_id=1, source_target_pairs={{0,16},{8,24},{16,0},{24,8},{1,17},{9,25},{17,1},{25,9},{2,18},{10... | collective-permute-start | bytes 3145736 | tf_op jit(solution)/shard_map/ppermute | solution.py:423
  519.7 29.8 %collective-permute-start.53 = (bf16[2,256,1024]{2,1,0:T(8,128)(2,1)S(1)}, bf16[2,256,1024]{2,1,0:T(8,128)(2,1)S(1)}, u32[]{:S(2)}, u32[]{:S(2)}) collective-permute-start(bf16[2,256,1024]{2,1,0:T(8,128)(2,1)S(1)} %dynamic-slice_bitcast_fusion.3), channel_id=1, source_target_pairs={{0,8},{8,0},{16,24},{24,16},{1,9},{9,1},{17,25},{25,17},{2,10},{10... | collective-permute-start | bytes 3145736 | tf_op jit(solution)/shard_map/ppermute | solution.py:423
  541.6 35.5 %collective-permute-start.59 = (bf16[256,1024]{1,0:T(8,128)(2,1)S(1)}, bf16[256,1024]{1,0:T(8,128)(2,1)S(1)}, u32[]{:S(2)}, u32[]{:S(2)}) collective-permute-start(bf16[256,1024]{1,0:T(8,128)(2,1)S(1)} %fusion.43), channel_id=1, source_target_pairs={{0,8},{8,0},{16,24},{24,16},{1,9},{9,1},{17,25},{25,17},{2,10},{10... | collective-permute-start | bytes 1572872 | tf_op jit(solution)/shard_map/ppermute | solution.py:423
  546.3 28.0 %collective-permute-start.43 = (bf16[256,2048]{1,0:T(8,128)(2,1)S(1)}, bf16[256,2048]{1,0:T(8,128)(2,1)S(1)}, u32[]{:S(2)}, u32[]{:S(2)}) collective-permute-start(bf16[256,2048]{1,0:T(8,128)(2,1)S(1)} %fusion.28), channel_id=1, source_target_pairs={{0,2},{1,3},{2,0},{3,1},{4,6},{5,7},{6,4},{7,5},{8,10},{9,11},{10,... | collective-permute-start | bytes 3145736 | tf_op jit(solution)/shard_map/ppermute | solution.py:423
  549.9 54.3 %collective-permute-start.54 = (bf16[256,1024]{1,0:T(8,128)(2,1)S(1)}, bf16[256,1024]{1,0:T(8,128)(2,1)S(1)}, u32[]{:S(2)}, u32[]{:S(2)}) collective-permute-start(bf16[256,1024]{1,0:T(8,128)(2,1)S(1)} %fusion.41), channel_id=1, source_target_pairs={{0,16},{8,24},{16,0},{24,8},{1,17},{9,25},{17,1},{25,9},{2,18},{10... | collective-permute-start | bytes 1572872 | tf_op jit(solution)/shard_map/ppermute | solution.py:423
  563.9 38.4 %collective-permute-start.61 = (bf16[256,1024]{1,0:T(8,128)(2,1)S(1)}, bf16[256,1024]{1,0:T(8,128)(2,1)S(1)}, u32[]{:S(2)}, u32[]{:S(2)}) collective-permute-start(bf16[256,1024]{1,0:T(8,128)(2,1)S(1)} %fusion.29), channel_id=1, source_target_pairs={{0,4},{1,5},{2,6},{3,7},{4,0},{5,1},{6,2},{7,3},{8,12},{9,13},{10,... | collective-permute-start | bytes 1572872 | tf_op jit(solution)/shard_map/ppermute | solution.py:606
  568.0 42.5 %collective-permute-start.56 = (bf16[256,1024]{1,0:T(8,128)(2,1)S(1)}, bf16[256,1024]{1,0:T(8,128)(2,1)S(1)}, u32[]{:S(2)}, u32[]{:S(2)}) collective-permute-start(bf16[256,1024]{1,0:T(8,128)(2,1)S(1)} %fusion.32), channel_id=1, source_target_pairs={{0,4},{1,5},{2,6},{3,7},{4,0},{5,1},{6,2},{7,3},{8,12},{9,13},{10,... | collective-permute-start | bytes 1572872 | tf_op jit(solution)/shard_map/ppermute | solution.py:606
  (92 other events, 1335.8 us)
Sparse Core Ops, SparseCore 0:
  56.1 85.9 all-gather.2
  185.6 85.4 all-gather.4
  296.7 88.4 reduce-scatter.2
  424.0 89.3 reduce-scatter.4

commit v13 on v12

--- a/solution.py
+++ b/solution.py
@@ -582,28 +582,32 @@
             qkv, heads_out, log_total, mask = kept[k]
             qkv_grad = attend_backward(grads_now, weights_out[k], qkv, log_total, cos, sin, mask)
             pairs.append((qkv_grad, weights_in[k]))
-            if k == 0:
-                helds = column_gather(helds, columns, start=1)
-                qkv_grad, helds = lax.optimization_barrier((qkv_grad, helds))
+            if sent:
+                qkv_grad, sent = lax.optimization_barrier((qkv_grad, sent))
             part = weight_grads(inputs_one, qkv_grad, grads_one, heads_out, columns)
             if k:
                 grads_now, part, helds = lax.optimization_barrier((grads_now, part, helds))
-                sent.append((k, part))
+                sent.append(column_scatter(part, columns, column, cut=1))
                 normed_late, state_late, dots_late, middle_late, _ = lax.optimization_barrier(
                     (normed_two, state_two, gate_grad_two, middle_grad, part)
                 )
                 router_two = gate_backward(normed_late, hidden_router, state_late, dots_late)[1]
                 gate_grad_one = jnp.sum(middle_late * mixer_branch, axis=1)
+        helds, sent = lax.optimization_barrier((helds, sent))
+        sent = [[narrow(x) for x in column_scatter(lanes, columns, column, start=1)] for lanes in sent]
+        there = [
+            [lax.ppermute(x, "mp", shift_pairs(ranks, -k * group)) for x in lanes]
+            for k, lanes in zip(range(1, sequences)[::-1], sent)
+        ]
+        pairs, part = lax.optimization_barrier((pairs, part))
         blocks = core_sum(pairs)
-        sent = [(k, column_scatter(lanes, columns, column, cut=1)) for k, lanes in sent]
-        blocks, gated = lax.optimization_barrier((blocks, [lanes for _, lanes in sent]))
-        sent = [(k, lanes) for (k, _), lanes in zip(sent, gated)]
+        blocks, there = lax.optimization_barrier((blocks, there))
         normed_grad_one = chip_sum(blocks)
+        helds = column_gather(helds, columns, start=1)
         pieces = column_scatter(part, columns, column)
-        for k, lanes in sent:
-            lanes = [narrow(x) for x in column_scatter(lanes, columns, column, start=1)]
-            back = shift_pairs(ranks, -k * group)
-            pieces = [p + wide(lax.ppermute(x, "mp", back)) for p, x in zip(pieces, lanes)]
+        pieces, helds = lax.optimization_barrier((pieces, helds))
+        for lanes in there:
+            pieces = [p + wide(t) for p, t in zip(pieces, lanes)]
         spread = column_gather([narrow(p) for p in pieces], columns, cut=1)
         spread, helds = lax.optimization_barrier((spread, helds))
         spread = column_gather(spread, columns, start=1)

time: 670 us -> 675 us (level)
  waiting for transfers between devices: 271 us -> 256 us
  other arithmetic: 54.4 us -> 62.7 us
    ppermute x2, waiting for transfers between devices: 31.4 us -> 12.6 us  [local(): lax.ppermute(x, 'mp', shift_pairs(ranks, -k * group))]
    ppermute x14, waiting for transfers between devices: 83.8 us -> 102 us  [xor_scatter(): lax.ppermute(narrow(pick(blocks, 1 - side, at)), axis_name, swap_pairs(si...]
    ppermute x37, waiting for transfers between devices: 69.7 us -> 55 us  [xor_gather(): held[far ^ bit] = lax.ppermute(held[far], axis, swap_pairs(size, bit))]
    add x7 -> x9, other arithmetic: 18.1 us -> 21.2 us  [xor_scatter(): blocks = wide(pick(blocks, side, at)) + wide(got)]
  transfers between devices with their start and end apart: 71 -> 71, of which waited for: 28 -> 29; matrix products, arithmetic and copies ran while one was open for 19% -> 21% of each run, Pallas kernels for 18% -> 18%
where the time goes in v13:
time: 675 us; the launch traced here: 671 us
  waiting for transfers between devices  256 us (38%)
  Pallas kernels  145 us (21%)
  starting transfers between devices  81.5 us (12%)
  matrix products  65.4 us (10%)
  other arithmetic  62.7 us (9%)
  local copies, waits for them, and re-layouts  44.1 us (7%)
  between operations  15.2 us (2%)
    ppermute x14, waiting for transfers between devices, xor_scatter(): lax.ppermute(narrow(pick(blocks, 1 - side, at)), axis_name, swap_pairs(si...  102 us
    ppermute x37, waiting for transfers between devices, xor_gather(): held[far ^ bit] = lax.ppermute(held[far], axis, swap_pairs(size, bit))  55 us
    dot_general x4, matrix products, product(): lax.dot_general(a, b, ((dims[:1], dims[1:]), ((), ())), preferred_element...  51.2 us
    all_gather x1, waiting for transfers between devices, local(): inputs_two = lax.all_gather(narrow(normed_two), 'mp', axis=0, tiled=True)  46.6 us
    ppermute x37, starting transfers between devices, xor_gather(): held[far ^ bit] = lax.ppermute(held[far], axis, swap_pairs(size, bit))  41.4 us
    pallas_call x2, Pallas kernels, attend_backward(): pl.pallas_call(backward_kernel, out_shape=jax.ShapeDtypeStruct((tokens, 3...  26.9 us
    ppermute x4, waiting for transfers between devices, local(): lax.ppermute(x, 'mp', shift_pairs(ranks, k * group))  26.8 us
    pallas_call x1, Pallas kernels, hidden_pass(): pl.pallas_call(hidden_kernel, grid_spec=pltpu.PrefetchScalarGridSpec(num_...  25.4 us
  transfers between devices with their start and end apart: 71, of which 29 were waited for; matrix products, arithmetic and copies ran while one was open for 21% of the time, Pallas kernels for 18%

profile of v13, /device:TPU:0, one launch (start us, length us, event | category | flops | bytes accessed | tf_op | source)
XLA Modules:
  0.0 670.6 jit_solution(18263725634356049466)
XLA Ops:
  28.5 19.5 %collective-permute-done.1.refs_0_ = bf16[256,768]{1,0:T(8,128)(2,1)} collective-permute-done((bf16[256,768]{1,0:T(8,128)(2,1)}, bf16[256,768]{1,0:T(8,128)(2,1)}, u32[]{:S(2)}, u32[]{:S(2)}) %collective-permute-start.1) | collective-permute-done | bytes 393248 | tf_op jit(solution)/shard_map/ppermute | solution.py:510
  48.0 7.3 %collective-permute-done.2.refs_4_ = bf16[256,768]{1,0:T(8,128)(2,1)} collective-permute-done((bf16[256,768]{1,0:T(8,128)(2,1)}, bf16[256,768]{1,0:T(8,128)(2,1)}, u32[]{:S(2)}, u32[]{:S(2)}) %collective-permute-start.2) | collective-permute-done | bytes 393248 | tf_op jit(solution)/shard_map/ppermute | solution.py:510
  66.8 12.8 %attend_forward.2 = (bf16[1024,768]{1,0:T(8,128)(2,1)}, bf16[1024,256]{1,0:T(8,128)(2,1)}, f32[1024,2]{1,0:T(8,128)}) custom-call(bf16[1024,2048]{1,0:T(8,128)(2,1)} %bitcast.198, bf16[2048,768]{1,0:T(8,128)(2,1)} %pad_maximum_fusion.w_ref.refs_3_, f32[1024,128]{1,0:T(8,128)} %get-tuple-element.142.cos_ref, f32[1024,128]{1,0:T(8,128)} %get-tuple-element.143.sin_ref, ...), custom_call_target="tpu_custom_call" | custom-call | flops 3758096384 | bytes 12582912 | tf_op jit(solution)/shard_map/attend_forward/pallas_call | solution.py:237
  85.5 17.6 %collective-permute-done.13.refs_1_ = bf16[256,256]{1,0:T(8,128)(2,1)S(1)} collective-permute-done((bf16[256,256]{1,0:T(8,128)(2,1)S(1)}, bf16[256,256]{1,0:T(8,128)(2,1)S(1)}, u32[]{:S(2)}, u32[]{:S(2)}) %collective-permute-start.13) | collective-permute-done | bytes 131104 | tf_op jit(solution)/shard_map/ppermute | solution.py:402
  116.5 12.4 %attend_forward.3 = (bf16[1024,768]{1,0:T(8,128)(2,1)}, bf16[1024,256]{1,0:T(8,128)(2,1)}, f32[1024,2]{1,0:T(8,128)}) custom-call(bf16[1024,2048]{1,0:T(8,128)(2,1)} %bitcast.199, bf16[2048,768]{1,0:T(8,128)(2,1)} %place_blocks.5.w_ref.refs_1_, f32[1024,128]{1,0:T(8,128)} %get-tuple-element.142.cos_ref, f32[1024,128]{1,0:T(8,128)} %get-tuple-element.143.sin_ref, ...), custom_call_target="tpu_custom_call" | custom-call | flops 3758096384 | bytes 12582912 | tf_op jit(solution)/shard_map/attend_forward/pallas_call | solution.py:237
  156.4 21.0 %collective-permute-done.20 = bf16[256,2048]{1,0:T(8,128)(2,1)S(1)} collective-permute-done((bf16[256,2048]{1,0:T(8,128)(2,1)S(1)}, bf16[256,2048]{1,0:T(8,128)(2,1)S(1)}, u32[]{:S(2)}, u32[]{:S(2)}) %collective-permute-start.20) | collective-permute-done | bytes 1048608 | tf_op jit(solution)/shard_map/ppermute | solution.py:423
  198.7 14.6 %fusion.81.top_ref = f32[2048,1024]{1,0:T(8,128)} fusion(bf16[2048,2048]{1,0:T(8,128)(2,1)} %all-gather.3.cloned.1.call-done, bf16[1024,2048]{1,0:T(8,128)(2,1)} %param.22), kind=kOutput, calls=%fused_computation.192 | convolution fusion | flops 8589934592 | bytes 20971520 | tf_op jit(solution)/shard_map/dot_general | solution.py:94
  224.3 46.6 %all-gather.5.cloned.1.call-done.x_ref = bf16[2048,2048]{1,0:T(8,128)(2,1)} async-done(((bf16[256,2048]{1,0:T(8,128)(2,1)}), bf16[2048,2048]{1,0:T(8,128)(2,1)}) %all-gather.5.cloned.1.call-update) | async-done | bytes 8388624 | tf_op jit(solution)/shard_map/all_gather | solution.py:546
  270.9 25.4 %hidden_pass.1 = (bf16[2048,2048]{1,0:T(8,128)(2,1)}, bf16[2048,1024]{1,0:T(8,128)(2,1)}, bf16[2048,1024]{1,0:T(8,128)(2,1)}, f32[1,2048]{1,0:T(1,128)}) custom-call(s32[1]{0:T(128)} %bitcast.29.offset_ref, bf16[2048,2048]{1,0:T(8,128)(2,1)} %all-gather.5.cloned.1.call-done.x_ref, bf16[2048,1024]{1,0:T(8,128)(2,1)} %up_ref.1, f32[2048,1024]{1,0:T(8,128)} %fusion.81.top_ref, ...), custom_call_target="tpu_custom_call" | custom-call | flops 17179869184 | bytes 41943040 | tf_op jit(solution)/shard_map/hidden_pass/pallas_call | solution.py:305
  296.4 13.0 %convolution_convert_fusion.1 = bf16[2048,1024]{1,0:T(8,128)(2,1)S(1)} fusion(bf16[2048,2048]{1,0:T(8,128)(2,1)} %all-gather.5.cloned.1.call-done.x_ref, bf16[2048,1024]{1,0:T(8,128)(2,1)} %get-tuple-element.186), kind=kOutput, calls=%fused_computation.9 | convolution fusion | flops 8592031744 | bytes 16777216 | tf_op jit(solution)/shard_map/dot_general | solution.py:94
  313.6 12.3 %fusion.2 = bf16[1024,2048]{1,0:T(8,128)(2,1)S(1)} fusion(bf16[2048,1024]{1,0:T(8,128)(2,1)S(1)} %copy-done.58, bf16[2048,2048]{1,0:T(8,128)(2,1)} %all-gather.3.cloned.1.call-done, f32[2048]{0:T(1024)S(1)} %bitcast.220), kind=kOutput, calls=%fused_computation.8 | convolution fusion | flops 8604614656 | bytes 16785408 | tf_op jit(solution)/shard_map/dot_general | solution.py:94
  331.0 11.3 %convolution_convert_fusion = bf16[2048,2048]{1,0:T(8,128)(2,1)} fusion(bf16[2048,1024]{1,0:T(8,128)(2,1)S(1)} %copy-done.58, bf16[1024,2048]{1,0:T(8,128)(2,1)S(1)} %copy-done.57), kind=kOutput, calls=%fused_computation.3 | convolution fusion | flops 8594128896 | bytes 16777216 | tf_op jit(solution)/shard_map/dot_general | solution.py:94
  345.6 14.5 %collective-permute-done.29 = bf16[2,512,1024]{2,1,0:T(8,128)(2,1)} collective-permute-done((bf16[2,512,1024]{2,1,0:T(8,128)(2,1)}, bf16[2,512,1024]{2,1,0:T(8,128)(2,1)}, u32[]{:S(2)}, u32[]{:S(2)}) %collective-permute-start.29) | collective-permute-done | bytes 2097184 | tf_op jit(solution)/shard_map/ppermute | solution.py:423
  365.4 12.0 %collective-permute-done.28 = bf16[2,256,2048]{2,1,0:T(8,128)(2,1)} collective-permute-done((bf16[2,256,2048]{2,1,0:T(8,128)(2,1)}, bf16[2,256,2048]{2,1,0:T(8,128)(2,1)}, u32[]{:S(2)}, u32[]{:S(2)}) %collective-permute-start.28) | collective-permute-done | bytes 2097184 | tf_op jit(solution)/shard_map/ppermute | solution.py:423
  396.6 19.4 %collective-permute-done.33 = bf16[256,2048]{1,0:T(8,128)(2,1)S(1)} collective-permute-done((bf16[256,2048]{1,0:T(8,128)(2,1)S(1)}, bf16[256,2048]{1,0:T(8,128)(2,1)S(1)}, u32[]{:S(2)}, u32[]{:S(2)}) %collective-permute-start.33) | collective-permute-done | bytes 1048608 | tf_op jit(solution)/shard_map/ppermute | solution.py:402
  426.5 13.9 %attend_backward.2.q_ref.refs_0_ = bf16[1024,768]{1,0:T(8,128)(2,1)} custom-call(bf16[1024,2048]{1,0:T(8,128)(2,1)} %bitcast.58.g_ref, bf16[2048,256]{1,0:T(8,128)(2,1)} %place_blocks.6.refs_3_.w_ref, bf16[1024,768]{1,0:T(8,128)(2,1)} %get-tuple-element.195.qkv_ref, f32[1024,2]{1,0:T(8,128)} %get-tuple-element.196.log_ref, ...), custom_call_target="tpu_custom_call" | custom-call | flops 2415919104 | bytes 12582912 | tf_op jit(solution)/shard_map/attend_backward/pallas_call | solution.py:259
  440.4 8.9 %weight_grads.2 = (bf16[4,256,1024]{2,1,0:T(8,128)(2,1)}, bf16[4,256,1024]{2,1,0:T(8,128)(2,1)}) custom-call(bf16[1024,2048]{1,0:T(8,128)(2,1)} %bitcast.200, bf16[1024,768]{1,0:T(8,128)(2,1)} %attend_backward.2.q_ref.refs_0_, bf16[1024,2048]{1,0:T(8,128)(2,1)} %bitcast.58.g_ref, bf16[1024,256]{1,0:T(8,128)(2,1)} %get-tuple-element.174.refs_2_.h_ref), custom_call_target="tpu_custom_call" | custom-call | flops 4294967296 | bytes 14680064 | tf_op jit(solution)/shard_map/weight_grads/pallas_call | solution.py:330
  458.2 13.0 %attend_backward.3.q_ref.refs_2_ = bf16[1024,768]{1,0:T(8,128)(2,1)} custom-call(bf16[1024,2048]{1,0:T(8,128)(2,1)} %bitcast.58.g_ref, bf16[2048,256]{1,0:T(8,128)(2,1)} %bitcast.197, bf16[1024,768]{1,0:T(8,128)(2,1)} %get-tuple-element.151.qkv_ref, f32[1024,2]{1,0:T(8,128)} %get-tuple-element.200.log_ref, f32[1024,128]{1,0:T(8,128)} %get-tuple-element.142.cos_ref, ...), custom_call_target="tpu_custom_call" | custom-call | flops 2415919104 | bytes 12582912 | tf_op jit(solution)/shard_map/attend_backward/pallas_call | solution.py:259
  479.7 9.7 %weight_grads.3 = (bf16[4,256,1024]{2,1,0:T(8,128)(2,1)}, bf16[4,256,1024]{2,1,0:T(8,128)(2,1)}) custom-call(bf16[1024,2048]{1,0:T(8,128)(2,1)} %bitcast.201, bf16[1024,768]{1,0:T(8,128)(2,1)} %attend_backward.3.q_ref.refs_2_, bf16[1024,2048]{1,0:T(8,128)(2,1)} %bitcast.58.g_ref, bf16[1024,256]{1,0:T(8,128)(2,1)} %get-tuple-element.172.refs_0_.h_ref), custom_call_target="tpu_custom_call" | custom-call | flops 4294967296 | bytes 14680064 | tf_op jit(solution)/shard_map/weight_grads/pallas_call | solution.py:330
  494.8 7.8 %share_of.6 = bf16[2,256,2048]{2,1,0:T(8,128)(2,1)} custom-call(s32[1]{0:T(128)} %bitcast.23.side_ref, bf16[1024,768]{1,0:T(8,128)(2,1)} %attend_backward.2.q_ref.refs_0_, bf16[2048,768]{1,0:T(8,128)(2,1)} %place_blocks.5.w_ref.refs_1_, bf16[1024,768]{1,0:T(8,128)(2,1)} %attend_backward.3.q_ref.refs_2_, bf16[2048,768]{1,0:T(8,128)(2,1)} %pad_maximum_fusion.w_ref.refs_3_), custom_call_target="tpu_custom_call" | custom-call | flops 3221225472 | bytes 12582912 | tf_op jit(solution)/shard_map/share_of/pallas_call | solution.py:283
  513.8 11.4 %collective-permute-done.43 = bf16[256,1024]{1,0:T(8,128)(2,1)} collective-permute-done((bf16[256,1024]{1,0:T(8,128)(2,1)}, bf16[256,1024]{1,0:T(8,128)(2,1)}, u32[]{:S(2)}, u32[]{:S(2)}) %collective-permute-start.43) | collective-permute-done | bytes 524320 | tf_op jit(solution)/shard_map/ppermute | solution.py:423
  535.2 7.8 %share_of.7 = bf16[2,256,2048]{2,1,0:T(8,128)(2,1)} custom-call(s32[1]{0:T(128)} %bitcast.3.side_ref, bf16[1024,768]{1,0:T(8,128)(2,1)} %attend_backward.2.q_ref.refs_0_, bf16[2048,768]{1,0:T(8,128)(2,1)} %place_blocks.5.w_ref.refs_1_, bf16[1024,768]{1,0:T(8,128)(2,1)} %attend_backward.3.q_ref.refs_2_, bf16[2048,768]{1,0:T(8,128)(2,1)} %pad_maximum_fusion.w_ref.refs_3_), custom_call_target="tpu_custom_call" | custom-call | flops 3221225472 | bytes 12582912 | tf_op jit(solution)/shard_map/share_of/pallas_call | solution.py:283
  550.2 9.5 %collective-permute-done.44 = bf16[256,1024]{1,0:T(8,128)(2,1)} collective-permute-done((bf16[256,1024]{1,0:T(8,128)(2,1)}, bf16[256,1024]{1,0:T(8,128)(2,1)}, u32[]{:S(2)}, u32[]{:S(2)}) %collective-permute-start.44) | collective-permute-done | bytes 524320 | tf_op jit(solution)/shard_map/ppermute | solution.py:599
  565.2 32.9 %collective-permute-done.54 = bf16[256,1024]{1,0:T(8,128)(2,1)S(1)} collective-permute-done((bf16[256,1024]{1,0:T(8,128)(2,1)S(1)}, bf16[256,1024]{1,0:T(8,128)(2,1)S(1)}, u32[]{:S(2)}, u32[]{:S(2)}) %collective-permute-start.54) | collective-permute-done | bytes 524320 | tf_op jit(solution)/shard_map/ppermute | solution.py:423
  (379 shorter events, 280.9 us)
Async XLA Ops:
  7.2 173.5 %all-gather.3.cloned.1.call-start = ((), (), s32[]{:S(2)}) async-start(), calls=%async_computation.2 | async-start | bytes 9437184 | tf_op jit(solution)/shard_map/all_gather | solution.py:523
  12.9 43.1 %collective-permute-start = (bf16[256,2048]{1,0:T(8,128)(2,1)S(1)}, bf16[256,2048]{1,0:T(8,128)(2,1)}, u32[]{:S(2)}, u32[]{:S(2)}) collective-permute-start(bf16[256,2048]{1,0:T(8,128)(2,1)S(1)} %fusion.11), channel_id=1, source_target_pairs={{0,2},{1,3},{2,0},{3,1},{4,6},{5,7},{6,4},{7,5},{8,10},{9,11},{10,... | collective-permute-start | bytes 3145736 | tf_op jit(solution)/shard_map/ppermute | solution.py:402
  15.9 32.1 %collective-permute-start.1 = (bf16[256,768]{1,0:T(8,128)(2,1)}, bf16[256,768]{1,0:T(8,128)(2,1)}, u32[]{:S(2)}, u32[]{:S(2)}) collective-permute-start(bf16[256,768]{1,0:T(8,128)(2,1)} %get-tuple-element.137), channel_id=1, source_target_pairs={{0,4},{1,5},{2,6},{3,7},{4,0},{5,1},{6,2},{7,3},{8,12},{9,13},{10,... | collective-permute-start | bytes 1179656 | tf_op jit(solution)/shard_map/ppermute | solution.py:510
  18.5 36.8 %collective-permute-start.2 = (bf16[256,768]{1,0:T(8,128)(2,1)}, bf16[256,768]{1,0:T(8,128)(2,1)}, u32[]{:S(2)}, u32[]{:S(2)}) collective-permute-start(bf16[256,768]{1,0:T(8,128)(2,1)} %get-tuple-element.138), channel_id=1, source_target_pairs={{0,4},{1,5},{2,6},{3,7},{4,0},{5,1},{6,2},{7,3},{8,12},{9,13},{10,... | collective-permute-start | bytes 1179656 | tf_op jit(solution)/shard_map/ppermute | solution.py:510
  56.0 214.9 %all-gather.5.cloned.1.call-start = ((), (), s32[]{:S(2)}) async-start(), calls=%async_computation.3 | async-start | bytes 9437184 | tf_op jit(solution)/shard_map/all_gather | solution.py:546
  79.7 28.4 %collective-permute-start.10 = (bf16[256,768]{1,0:T(8,128)(2,1)}, bf16[256,768]{1,0:T(8,128)(2,1)S(1)}, u32[]{:S(2)}, u32[]{:S(2)}) collective-permute-start(bf16[256,768]{1,0:T(8,128)(2,1)} %collective-permute-done.5.refs_1_), channel_id=1, source_target_pairs={{0,16},{8,24},{16,0},{24,8},{1,17},{9,25},{17,1},{25,9},{2,18},{10... | collective-permute-start | bytes 1179656 | tf_op jit(solution)/shard_map/ppermute | solution.py:402
  146.6 30.8 %collective-permute-start.20 = (bf16[256,2048]{1,0:T(8,128)(2,1)S(1)}, bf16[256,2048]{1,0:T(8,128)(2,1)S(1)}, u32[]{:S(2)}, u32[]{:S(2)}) collective-permute-start(bf16[256,2048]{1,0:T(8,128)(2,1)S(1)} %fusion.25), channel_id=1, source_target_pairs={{0,2},{1,3},{2,0},{3,1},{4,6},{5,7},{6,4},{7,5},{8,10},{9,11},{10,... | collective-permute-start | bytes 3145736 | tf_op jit(solution)/shard_map/ppermute | solution.py:423
  185.5 199.4 %reduce-scatter.3.cloned.1.call-start = ((), (), s32[]{:S(2)}) async-start(), calls=%async_computation.4 | async-start | bytes 9437184 | tf_op jit(solution)/shard_map/reduce_scatter | solution.py:555
  296.3 364.9 %reduce-scatter.5.cloned.1.call-start = ((), (), s32[]{:S(2)}) async-start(), calls=%async_computation.5 | async-start | bytes 9437184 | tf_op jit(solution)/shard_map/reduce_scatter | solution.py:576
  312.1 48.1 %collective-permute-start.29 = (bf16[2,512,1024]{2,1,0:T(8,128)(2,1)}, bf16[2,512,1024]{2,1,0:T(8,128)(2,1)}, u32[]{:S(2)}, u32[]{:S(2)}) collective-permute-start(bf16[2,512,1024]{2,1,0:T(8,128)(2,1)} %dynamic-slice_bitcast_fusion), channel_id=1, source_target_pairs={{0,16},{8,24},{16,0},{24,8},{1,17},{9,25},{17,1},{25,9},{2,18},{10... | collective-permute-start | bytes 6291464 | tf_op jit(solution)/shard_map/ppermute | solution.py:423
  329.0 48.4 %collective-permute-start.28 = (bf16[2,256,2048]{2,1,0:T(8,128)(2,1)}, bf16[2,256,2048]{2,1,0:T(8,128)(2,1)}, u32[]{:S(2)}, u32[]{:S(2)}) collective-permute-start(bf16[2,256,2048]{2,1,0:T(8,128)(2,1)} %dynamic-slice_bitcast_fusion.1), channel_id=1, source_target_pairs={{0,8},{8,0},{16,24},{24,16},{1,9},{9,1},{17,25},{25,17},{2,10},{10... | collective-permute-start | bytes 6291464 | tf_op jit(solution)/shard_map/ppermute | solution.py:423
  491.7 39.5 %collective-permute-start.55 = (bf16[2,256,1024]{2,1,0:T(8,128)(2,1)}, bf16[2,256,1024]{2,1,0:T(8,128)(2,1)}, u32[]{:S(2)}, u32[]{:S(2)}) collective-permute-start(bf16[2,256,1024]{2,1,0:T(8,128)(2,1)} %dynamic-slice_bitcast_fusion.2), channel_id=1, source_target_pairs={{0,16},{8,24},{16,0},{24,8},{1,17},{9,25},{17,1},{25,9},{2,18},{10... | collective-permute-start | bytes 3145736 | tf_op jit(solution)/shard_map/ppermute | solution.py:423
  502.6 59.1 %collective-permute-start.42 = (bf16[2,256,2048]{2,1,0:T(8,128)(2,1)}, bf16[2,256,2048]{2,1,0:T(8,128)(2,1)}, u32[]{:S(2)}, u32[]{:S(2)}) collective-permute-start(bf16[2,256,2048]{2,1,0:T(8,128)(2,1)} %share_of.6), channel_id=1, source_target_pairs={{0,1},{1,0},{2,3},{3,2},{4,5},{5,4},{6,7},{7,6},{8,9},{9,8},{10,11... | collective-permute-start | bytes 6291464 | tf_op jit(solution)/shard_map/ppermute | solution.py:481
  508.3 34.7 %collective-permute-start.53 = (bf16[2,256,1024]{2,1,0:T(8,128)(2,1)}, bf16[2,256,1024]{2,1,0:T(8,128)(2,1)}, u32[]{:S(2)}, u32[]{:S(2)}) collective-permute-start(bf16[2,256,1024]{2,1,0:T(8,128)(2,1)} %dynamic-slice_bitcast_fusion.3), channel_id=1, source_target_pairs={{0,8},{8,0},{16,24},{24,16},{1,9},{9,1},{17,25},{25,17},{2,10},{10... | collective-permute-start | bytes 3145736 | tf_op jit(solution)/shard_map/ppermute | solution.py:423
  510.4 38.7 %collective-permute-start.46 = (bf16[256,1024]{1,0:T(8,128)(2,1)S(1)}, bf16[256,1024]{1,0:T(8,128)(2,1)}, u32[]{:S(2)}, u32[]{:S(2)}) collective-permute-start(bf16[256,1024]{1,0:T(8,128)(2,1)S(1)} %fusion.29), channel_id=1, source_target_pairs={{0,4},{1,5},{2,6},{3,7},{4,0},{5,1},{6,2},{7,3},{8,12},{9,13},{10,... | collective-permute-start | bytes 1572872 | tf_op jit(solution)/shard_map/ppermute | solution.py:599
  527.2 32.5 %collective-permute-start.44 = (bf16[256,1024]{1,0:T(8,128)(2,1)}, bf16[256,1024]{1,0:T(8,128)(2,1)}, u32[]{:S(2)}, u32[]{:S(2)}) collective-permute-start(bf16[256,1024]{1,0:T(8,128)(2,1)} %fusion.30), channel_id=1, source_target_pairs={{0,4},{1,5},{2,6},{3,7},{4,0},{5,1},{6,2},{7,3},{8,12},{9,13},{10,... | collective-permute-start | bytes 1572872 | tf_op jit(solution)/shard_map/ppermute | solution.py:599
  543.0 57.5 %collective-permute-start.57 = (bf16[256,2048]{1,0:T(8,128)(2,1)S(1)}, bf16[256,2048]{1,0:T(8,128)(2,1)S(1)}, u32[]{:S(2)}, u32[]{:S(2)}) collective-permute-start(bf16[256,2048]{1,0:T(8,128)(2,1)S(1)} %copy-done.16), channel_id=1, source_target_pairs={{0,16},{8,24},{16,0},{24,8},{1,17},{9,25},{17,1},{25,9},{2,18},{10... | collective-permute-start | bytes 3145736 | tf_op jit(solution)/shard_map/ppermute | solution.py:402
  549.1 51.3 %collective-permute-start.58 = (bf16[256,2048]{1,0:T(8,128)(2,1)S(1)}, bf16[256,2048]{1,0:T(8,128)(2,1)S(1)}, u32[]{:S(2)}, u32[]{:S(2)}) collective-permute-start(bf16[256,2048]{1,0:T(8,128)(2,1)S(1)} %copy-done.34), channel_id=1, source_target_pairs={{0,16},{8,24},{16,0},{24,8},{1,17},{9,25},{17,1},{25,9},{2,18},{10... | collective-permute-start | bytes 3145736 | tf_op jit(solution)/shard_map/ppermute | solution.py:402
  559.7 40.8 %collective-permute-start.59 = (bf16[512,1024]{1,0:T(8,128)(2,1)S(1)}, bf16[512,1024]{1,0:T(8,128)(2,1)S(1)}, u32[]{:S(2)}, u32[]{:S(2)}) collective-permute-start(bf16[512,1024]{1,0:T(8,128)(2,1)S(1)} %copy-done.17), channel_id=1, source_target_pairs={{0,8},{8,0},{16,24},{24,16},{1,9},{9,1},{17,25},{25,17},{2,10},{10... | collective-permute-start | bytes 3145736 | tf_op jit(solution)/shard_map/ppermute | solution.py:402
  561.0 45.7 %collective-permute-start.60 = (bf16[512,1024]{1,0:T(8,128)(2,1)S(1)}, bf16[512,1024]{1,0:T(8,128)(2,1)S(1)}, u32[]{:S(2)}, u32[]{:S(2)}) collective-permute-start(bf16[512,1024]{1,0:T(8,128)(2,1)S(1)} %copy-done.32), channel_id=1, source_target_pairs={{0,8},{8,0},{16,24},{24,16},{1,9},{9,1},{17,25},{25,17},{2,10},{10... | collective-permute-start | bytes 3145736 | tf_op jit(solution)/shard_map/ppermute | solution.py:402
  561.7 36.4 %collective-permute-start.54 = (bf16[256,1024]{1,0:T(8,128)(2,1)S(1)}, bf16[256,1024]{1,0:T(8,128)(2,1)S(1)}, u32[]{:S(2)}, u32[]{:S(2)}) collective-permute-start(bf16[256,1024]{1,0:T(8,128)(2,1)S(1)} %fusion.39), channel_id=1, source_target_pairs={{0,16},{8,24},{16,0},{24,8},{1,17},{9,25},{17,1},{25,9},{2,18},{10... | collective-permute-start | bytes 1572872 | tf_op jit(solution)/shard_map/ppermute | solution.py:423
  623.5 30.0 %collective-permute-start.63 = (bf16[256,1024]{1,0:T(8,128)(2,1)}, bf16[256,1024]{1,0:T(8,128)(2,1)}, u32[]{:S(2)}, u32[]{:S(2)}) collective-permute-start(bf16[256,1024]{1,0:T(8,128)(2,1)} %add_convert_fusion.2.refs_0_), channel_id=1, source_target_pairs={{0,16},{8,24},{16,0},{24,8},{1,17},{9,25},{17,1},{25,9},{2,18},{10... | collective-permute-start | bytes 1572872 | tf_op jit(solution)/shard_map/ppermute | solution.py:402
  624.8 28.7 %collective-permute-start.64 = (bf16[256,1024]{1,0:T(8,128)(2,1)}, bf16[256,1024]{1,0:T(8,128)(2,1)}, u32[]{:S(2)}, u32[]{:S(2)}) collective-permute-start(bf16[256,1024]{1,0:T(8,128)(2,1)} %collective-permute-done.61.refs_1_), channel_id=1, source_target_pairs={{0,16},{8,24},{16,0},{24,8},{1,17},{9,25},{17,1},{25,9},{2,18},{10... | collective-permute-start | bytes 1572872 | tf_op jit(solution)/shard_map/ppermute | solution.py:402
  625.5 28.0 %collective-permute-start.65 = (bf16[256,1024]{1,0:T(8,128)(2,1)S(1)}, bf16[256,1024]{1,0:T(8,128)(2,1)}, u32[]{:S(2)}, u32[]{:S(2)}) collective-permute-start(bf16[256,1024]{1,0:T(8,128)(2,1)S(1)} %add_convert_fusion.1.refs_4_), channel_id=1, source_target_pairs={{0,8},{8,0},{16,24},{24,16},{1,9},{9,1},{17,25},{25,17},{2,10},{10... | collective-permute-start | bytes 1572872 | tf_op jit(solution)/shard_map/ppermute | solution.py:402
  (106 other events, 1538.2 us)
Sparse Core Ops, SparseCore 0:
  56.1 85.7 all-gather.2
  185.6 85.2 all-gather.4
  296.5 88.3 reduce-scatter.2
  423.7 89.3 reduce-scatter.4

commit v14 on v13

--- a/solution.py
+++ b/solution.py
@@ -441,6 +441,25 @@
     return [{far: next(flat) for far in held} for held in lanes]
 
 
+def xor_span(bits):
+    span = [0]
+    for bit in bits:
+        span += [far ^ bit for far in span]
+    return span
+
+
+def gather_part(lanes, size, part):
+    out = []
+    for held, bits in zip(lanes, lane_bits(size)):
+        held = dict(held)
+        sends = [(bits[i], far) for i in range(1, len(bits)) for far in xor_span(bits[:i])]
+        half = len(sends) // 2
+        for bit, far in sends[half:] if part else sends[:half]:
+            held[far ^ bit] = lax.ppermute(held[far], "dp", swap_pairs(size, bit))
+        out.append(held)
+    return out
+
+
 def column_scatter(lanes, size, column, cut=None, start=None):
     return [
         xor_scatter(x, "dp", size, bits[start:cut], bits[start:cut], column, 0, bits)
@@ -476,11 +495,11 @@
         def place_sequence(held, out=None):
             return by_index(held, place, 0, out).reshape(SEQ_LEN, -1)
 
-        def core_sum(pairs):
+        def core_sum(pairs, before=()):
             theirs = share_of(pairs, rows, 1 - core)
             got = lax.ppermute(theirs, "mp", swap_pairs(ranks, 1))
-            pairs, theirs = lax.optimization_barrier((pairs, theirs))
-            return wide(share_of(pairs, rows, core)) + wide(got)
+            pairs, theirs, before = lax.optimization_barrier((pairs, theirs, before))
+            return wide(share_of(pairs, rows, core)) + wide(got), before
 
         def chip_sum(blocks):
             bits = pair_bits[::-1]
@@ -536,7 +555,7 @@
                 weights_in += place_blocks(held, column, [(1, 3 * width, jnp.bfloat16, False)])
                 weights_out += place_blocks(held_out, column, [(1, width, jnp.bfloat16, False)])
             kept.append((*attend_forward(inputs_one, weights_in[k], cos, sin, mask), mask))
-        mixer_branch = chip_sum(core_sum([(x[1], w) for x, w in zip(kept, weights_out)]))
+        mixer_branch = chip_sum(core_sum([(x[1], w) for x, w in zip(kept, weights_out)])[0])
         mixer_branch, grads_all = lax.optimization_barrier((mixer_branch, grads_all))
         top_down = product(grads_all, down_weight, (1, 1))
 
@@ -600,10 +619,10 @@
             for k, lanes in zip(range(1, sequences)[::-1], sent)
         ]
         pairs, part = lax.optimization_barrier((pairs, part))
-        blocks = core_sum(pairs)
+        blocks, helds = core_sum(pairs, gather_part(helds, columns, 0))
         blocks, there = lax.optimization_barrier((blocks, there))
         normed_grad_one = chip_sum(blocks)
-        helds = column_gather(helds, columns, start=1)
+        helds = gather_part(helds, columns, 1)
         pieces = column_scatter(part, columns, column)
         pieces, helds = lax.optimization_barrier((pieces, helds))
         for lanes in there:

time: 675 us -> 654 us (0.969)
  waiting for transfers between devices: 256 us -> 245 us
    ppermute x0 -> x4, waiting for transfers between devices: none -> 26.7 us  [gather_part(): held[far ^ bit] = lax.ppermute(held[far], 'dp', swap_pairs(size, bit))]
    ppermute x14, waiting for transfers between devices: 102 us -> 77.5 us  [xor_scatter(): lax.ppermute(narrow(pick(blocks, 1 - side, at)), axis_name, swap_pairs(si...]
    ppermute x2, waiting for transfers between devices: 12.6 us -> 3.49 us  [local(): lax.ppermute(x, 'mp', shift_pairs(ranks, -k * group))]
    ppermute x37 -> x33, waiting for transfers between devices: 55 us -> 50.4 us  [xor_gather(): held[far ^ bit] = lax.ppermute(held[far], axis, swap_pairs(size, bit))]
    ppermute x37 -> x33, starting transfers between devices: 41.4 us -> 37.4 us  [xor_gather(): held[far ^ bit] = lax.ppermute(held[far], axis, swap_pairs(size, bit))]
where the time goes in v14:
time: 654 us; the launch traced here: 650 us
  waiting for transfers between devices  245 us (37%)
  Pallas kernels  145 us (22%)
  starting transfers between devices  76.7 us (12%)
  matrix products  64.1 us (10%)
  other arithmetic  60.6 us (9%)
  local copies, waits for them, and re-layouts  43.2 us (7%)
  between operations  15.2 us (2%)
    ppermute x14, waiting for transfers between devices, xor_scatter(): lax.ppermute(narrow(pick(blocks, 1 - side, at)), axis_name, swap_pairs(si...  77.5 us
    dot_general x4, matrix products, product(): lax.dot_general(a, b, ((dims[:1], dims[1:]), ((), ())), preferred_element...  51.2 us
    ppermute x33, waiting for transfers between devices, xor_gather(): held[far ^ bit] = lax.ppermute(held[far], axis, swap_pairs(size, bit))  50.4 us
    all_gather x1, waiting for transfers between devices, local(): inputs_two = lax.all_gather(narrow(normed_two), 'mp', axis=0, tiled=True)  46.6 us
    ppermute x33, starting transfers between devices, xor_gather(): held[far ^ bit] = lax.ppermute(held[far], axis, swap_pairs(size, bit))  37.4 us
    pallas_call x2, Pallas kernels, attend_backward(): pl.pallas_call(backward_kernel, out_shape=jax.ShapeDtypeStruct((tokens, 3...  26.9 us
    ppermute x4, waiting for transfers between devices, local(): lax.ppermute(x, 'mp', shift_pairs(ranks, k * group))  26.8 us
    ppermute x4, waiting for transfers between devices, gather_part(): held[far ^ bit] = lax.ppermute(held[far], 'dp', swap_pairs(size, bit))  26.7 us
  transfers between devices with their start and end apart: 71, of which 29 were waited for; matrix products, arithmetic and copies ran while one was open for 21% of the time, Pallas kernels for 18%

profile of v14, /device:TPU:0, one launch (start us, length us, event | category | flops | bytes accessed | tf_op | source)
XLA Modules:
  0.0 649.9 jit_solution(3417945846328851942)
XLA Ops:
  28.5 19.5 %collective-permute-done.1.refs_0_ = bf16[256,768]{1,0:T(8,128)(2,1)} collective-permute-done((bf16[256,768]{1,0:T(8,128)(2,1)}, bf16[256,768]{1,0:T(8,128)(2,1)}, u32[]{:S(2)}, u32[]{:S(2)}) %collective-permute-start.1) | collective-permute-done | bytes 393248 | tf_op jit(solution)/shard_map/ppermute | solution.py:529
  48.0 7.3 %collective-permute-done.2.refs_4_ = bf16[256,768]{1,0:T(8,128)(2,1)} collective-permute-done((bf16[256,768]{1,0:T(8,128)(2,1)}, bf16[256,768]{1,0:T(8,128)(2,1)}, u32[]{:S(2)}, u32[]{:S(2)}) %collective-permute-start.2) | collective-permute-done | bytes 393248 | tf_op jit(solution)/shard_map/ppermute | solution.py:529
  66.8 12.8 %attend_forward.2 = (bf16[1024,768]{1,0:T(8,128)(2,1)}, bf16[1024,256]{1,0:T(8,128)(2,1)}, f32[1024,2]{1,0:T(8,128)}) custom-call(bf16[1024,2048]{1,0:T(8,128)(2,1)} %bitcast.198, bf16[2048,768]{1,0:T(8,128)(2,1)} %pad_maximum_fusion.w_ref.refs_3_, f32[1024,128]{1,0:T(8,128)} %get-tuple-element.148.cos_ref, f32[1024,128]{1,0:T(8,128)} %get-tuple-element.149.sin_ref, ...), custom_call_target="tpu_custom_call" | custom-call | flops 3758096384 | bytes 12582912 | tf_op jit(solution)/shard_map/attend_forward/pallas_call | solution.py:237
  85.6 17.6 %collective-permute-done.13.refs_1_ = bf16[256,256]{1,0:T(8,128)(2,1)S(1)} collective-permute-done((bf16[256,256]{1,0:T(8,128)(2,1)S(1)}, bf16[256,256]{1,0:T(8,128)(2,1)S(1)}, u32[]{:S(2)}, u32[]{:S(2)}) %collective-permute-start.13) | collective-permute-done | bytes 131104 | tf_op jit(solution)/shard_map/ppermute | solution.py:402
  116.6 12.4 %attend_forward.3 = (bf16[1024,768]{1,0:T(8,128)(2,1)}, bf16[1024,256]{1,0:T(8,128)(2,1)}, f32[1024,2]{1,0:T(8,128)}) custom-call(bf16[1024,2048]{1,0:T(8,128)(2,1)} %bitcast.199, bf16[2048,768]{1,0:T(8,128)(2,1)} %place_blocks.5.w_ref.refs_1_, f32[1024,128]{1,0:T(8,128)} %get-tuple-element.148.cos_ref, f32[1024,128]{1,0:T(8,128)} %get-tuple-element.149.sin_ref, ...), custom_call_target="tpu_custom_call" | custom-call | flops 3758096384 | bytes 12582912 | tf_op jit(solution)/shard_map/attend_forward/pallas_call | solution.py:237
  156.4 21.0 %collective-permute-done.20 = bf16[256,2048]{1,0:T(8,128)(2,1)S(1)} collective-permute-done((bf16[256,2048]{1,0:T(8,128)(2,1)S(1)}, bf16[256,2048]{1,0:T(8,128)(2,1)S(1)}, u32[]{:S(2)}, u32[]{:S(2)}) %collective-permute-start.20) | collective-permute-done | bytes 1048608 | tf_op jit(solution)/shard_map/ppermute | solution.py:423
  198.7 14.6 %fusion.81.top_ref = f32[2048,1024]{1,0:T(8,128)} fusion(bf16[2048,2048]{1,0:T(8,128)(2,1)} %all-gather.3.cloned.1.call-done, bf16[1024,2048]{1,0:T(8,128)(2,1)} %param.22), kind=kOutput, calls=%fused_computation.192 | convolution fusion | flops 8589934592 | bytes 20971520 | tf_op jit(solution)/shard_map/dot_general | solution.py:94
  224.4 46.6 %all-gather.5.cloned.1.call-done.x_ref = bf16[2048,2048]{1,0:T(8,128)(2,1)} async-done(((bf16[256,2048]{1,0:T(8,128)(2,1)}), bf16[2048,2048]{1,0:T(8,128)(2,1)}) %all-gather.5.cloned.1.call-update) | async-done | bytes 8388624 | tf_op jit(solution)/shard_map/all_gather | solution.py:565
  271.0 25.4 %hidden_pass.1 = (bf16[2048,2048]{1,0:T(8,128)(2,1)}, bf16[2048,1024]{1,0:T(8,128)(2,1)}, bf16[2048,1024]{1,0:T(8,128)(2,1)}, f32[1,2048]{1,0:T(1,128)}) custom-call(s32[1]{0:T(128)} %bitcast.29.offset_ref, bf16[2048,2048]{1,0:T(8,128)(2,1)} %all-gather.5.cloned.1.call-done.x_ref, bf16[2048,1024]{1,0:T(8,128)(2,1)} %up_ref.1, f32[2048,1024]{1,0:T(8,128)} %fusion.81.top_ref, ...), custom_call_target="tpu_custom_call" | custom-call | flops 17179869184 | bytes 41943040 | tf_op jit(solution)/shard_map/hidden_pass/pallas_call | solution.py:305
  296.5 13.0 %convolution_convert_fusion.1 = bf16[2048,1024]{1,0:T(8,128)(2,1)S(1)} fusion(bf16[2048,2048]{1,0:T(8,128)(2,1)} %all-gather.5.cloned.1.call-done.x_ref, bf16[2048,1024]{1,0:T(8,128)(2,1)} %get-tuple-element.192), kind=kOutput, calls=%fused_computation.9 | convolution fusion | flops 8592031744 | bytes 16777216 | tf_op jit(solution)/shard_map/dot_general | solution.py:94
  313.6 12.3 %fusion.2 = bf16[1024,2048]{1,0:T(8,128)(2,1)S(1)} fusion(bf16[2048,1024]{1,0:T(8,128)(2,1)S(1)} %copy-done.56, bf16[2048,2048]{1,0:T(8,128)(2,1)} %all-gather.3.cloned.1.call-done, f32[2048]{0:T(1024)S(1)} %bitcast.220), kind=kOutput, calls=%fused_computation.8 | convolution fusion | flops 8604614656 | bytes 16785408 | tf_op jit(solution)/shard_map/dot_general | solution.py:94
  331.0 11.3 %convolution_convert_fusion = bf16[2048,2048]{1,0:T(8,128)(2,1)} fusion(bf16[2048,1024]{1,0:T(8,128)(2,1)S(1)} %copy-done.56, bf16[1024,2048]{1,0:T(8,128)(2,1)S(1)} %copy-done.55), kind=kOutput, calls=%fused_computation.3 | convolution fusion | flops 8594128896 | bytes 16777216 | tf_op jit(solution)/shard_map/dot_general | solution.py:94
  345.7 14.6 %collective-permute-done.29 = bf16[2,512,1024]{2,1,0:T(8,128)(2,1)} collective-permute-done((bf16[2,512,1024]{2,1,0:T(8,128)(2,1)}, bf16[2,512,1024]{2,1,0:T(8,128)(2,1)}, u32[]{:S(2)}, u32[]{:S(2)}) %collective-permute-start.29) | collective-permute-done | bytes 2097184 | tf_op jit(solution)/shard_map/ppermute | solution.py:423
  365.4 12.0 %collective-permute-done.28 = bf16[2,256,2048]{2,1,0:T(8,128)(2,1)} collective-permute-done((bf16[2,256,2048]{2,1,0:T(8,128)(2,1)}, bf16[2,256,2048]{2,1,0:T(8,128)(2,1)}, u32[]{:S(2)}, u32[]{:S(2)}) %collective-permute-start.28) | collective-permute-done | bytes 2097184 | tf_op jit(solution)/shard_map/ppermute | solution.py:423
  396.6 19.4 %collective-permute-done.33 = bf16[256,2048]{1,0:T(8,128)(2,1)S(1)} collective-permute-done((bf16[256,2048]{1,0:T(8,128)(2,1)S(1)}, bf16[256,2048]{1,0:T(8,128)(2,1)S(1)}, u32[]{:S(2)}, u32[]{:S(2)}) %collective-permute-start.33) | collective-permute-done | bytes 1048608 | tf_op jit(solution)/shard_map/ppermute | solution.py:402
  426.6 13.8 %attend_backward.2.q_ref.refs_0_ = bf16[1024,768]{1,0:T(8,128)(2,1)} custom-call(bf16[1024,2048]{1,0:T(8,128)(2,1)} %bitcast.58.g_ref, bf16[2048,256]{1,0:T(8,128)(2,1)} %place_blocks.6.refs_3_.w_ref, bf16[1024,768]{1,0:T(8,128)(2,1)} %get-tuple-element.201.qkv_ref, f32[1024,2]{1,0:T(8,128)} %get-tuple-element.202.log_ref, ...), custom_call_target="tpu_custom_call" | custom-call | flops 2415919104 | bytes 12582912 | tf_op jit(solution)/shard_map/attend_backward/pallas_call | solution.py:259
  440.4 8.9 %weight_grads.2 = (bf16[4,256,1024]{2,1,0:T(8,128)(2,1)}, bf16[4,256,1024]{2,1,0:T(8,128)(2,1)}) custom-call(bf16[1024,2048]{1,0:T(8,128)(2,1)} %bitcast.200, bf16[1024,768]{1,0:T(8,128)(2,1)} %attend_backward.2.q_ref.refs_0_, bf16[1024,2048]{1,0:T(8,128)(2,1)} %bitcast.58.g_ref, bf16[1024,256]{1,0:T(8,128)(2,1)} %get-tuple-element.180.refs_2_.h_ref), custom_call_target="tpu_custom_call" | custom-call | flops 4294967296 | bytes 14680064 | tf_op jit(solution)/shard_map/weight_grads/pallas_call | solution.py:330
  459.8 13.2 %attend_backward.3.q_ref.refs_2_ = bf16[1024,768]{1,0:T(8,128)(2,1)} custom-call(bf16[1024,2048]{1,0:T(8,128)(2,1)} %bitcast.58.g_ref, bf16[2048,256]{1,0:T(8,128)(2,1)} %bitcast.197, bf16[1024,768]{1,0:T(8,128)(2,1)} %get-tuple-element.157.qkv_ref, f32[1024,2]{1,0:T(8,128)} %get-tuple-element.206.log_ref, f32[1024,128]{1,0:T(8,128)} %get-tuple-element.148.cos_ref, ...), custom_call_target="tpu_custom_call" | custom-call | flops 2415919104 | bytes 12582912 | tf_op jit(solution)/shard_map/attend_backward/pallas_call | solution.py:259
  479.8 9.0 %weight_grads.3 = (bf16[4,256,1024]{2,1,0:T(8,128)(2,1)}, bf16[4,256,1024]{2,1,0:T(8,128)(2,1)}) custom-call(bf16[1024,2048]{1,0:T(8,128)(2,1)} %bitcast.201, bf16[1024,768]{1,0:T(8,128)(2,1)} %attend_backward.3.q_ref.refs_2_, bf16[1024,2048]{1,0:T(8,128)(2,1)} %bitcast.58.g_ref, bf16[1024,256]{1,0:T(8,128)(2,1)} %get-tuple-element.178.refs_0_.h_ref), custom_call_target="tpu_custom_call" | custom-call | flops 4294967296 | bytes 14680064 | tf_op jit(solution)/shard_map/weight_grads/pallas_call | solution.py:330
  494.3 7.8 %share_of.6 = bf16[2,256,2048]{2,1,0:T(8,128)(2,1)} custom-call(s32[1]{0:T(128)} %bitcast.23.side_ref, bf16[1024,768]{1,0:T(8,128)(2,1)} %attend_backward.2.q_ref.refs_0_, bf16[2048,768]{1,0:T(8,128)(2,1)} %place_blocks.5.w_ref.refs_1_, bf16[1024,768]{1,0:T(8,128)(2,1)} %attend_backward.3.q_ref.refs_2_, bf16[2048,768]{1,0:T(8,128)(2,1)} %pad_maximum_fusion.w_ref.refs_3_), custom_call_target="tpu_custom_call" | custom-call | flops 3221225472 | bytes 12582912 | tf_op jit(solution)/shard_map/share_of/pallas_call | solution.py:283
  508.5 20.2 %collective-permute-done.45 = bf16[256,1024]{1,0:T(8,128)(2,1)S(1)} collective-permute-done((bf16[256,1024]{1,0:T(8,128)(2,1)S(1)}, bf16[256,1024]{1,0:T(8,128)(2,1)S(1)}, u32[]{:S(2)}, u32[]{:S(2)}) %collective-permute-start.45) | collective-permute-done | bytes 524320 | tf_op jit(solution)/shard_map/ppermute | solution.py:423
  538.3 8.9 %collective-permute-done.42.refs_2_ = bf16[256,2048]{1,0:T(8,128)(2,1)S(1)} collective-permute-done((bf16[256,2048]{1,0:T(8,128)(2,1)S(1)}, bf16[256,2048]{1,0:T(8,128)(2,1)S(1)}, u32[]{:S(2)}, u32[]{:S(2)}) %collective-permute-start.42) | collective-permute-done | bytes 1048608 | tf_op jit(solution)/shard_map/ppermute | solution.py:458
  557.0 7.8 %share_of.7 = bf16[2,256,2048]{2,1,0:T(8,128)(2,1)} custom-call(s32[1]{0:T(128)} %bitcast.3.side_ref, bf16[1024,768]{1,0:T(8,128)(2,1)} %attend_backward.2.q_ref.refs_0_, bf16[2048,768]{1,0:T(8,128)(2,1)} %place_blocks.5.w_ref.refs_1_, bf16[1024,768]{1,0:T(8,128)(2,1)} %attend_backward.3.q_ref.refs_2_, bf16[2048,768]{1,0:T(8,128)(2,1)} %pad_maximum_fusion.w_ref.refs_3_), custom_call_target="tpu_custom_call" | custom-call | flops 3221225472 | bytes 12582912 | tf_op jit(solution)/shard_map/share_of/pallas_call | solution.py:283
  575.9 11.5 %collective-permute-done.59.refs_3_ = bf16[256,2048]{1,0:T(8,128)(2,1)S(1)} collective-permute-done((bf16[256,2048]{1,0:T(8,128)(2,1)}, bf16[256,2048]{1,0:T(8,128)(2,1)S(1)}, u32[]{:S(2)}, u32[]{:S(2)}) %collective-permute-start.59) | collective-permute-done | bytes 1048608 | tf_op jit(solution)/shard_map/ppermute | solution.py:458
  (375 shorter events, 273.9 us)
Async XLA Ops:
  7.2 173.5 %all-gather.3.cloned.1.call-start = ((), (), s32[]{:S(2)}) async-start(), calls=%async_computation.2 | async-start | bytes 9437184 | tf_op jit(solution)/shard_map/all_gather | solution.py:542
  12.9 43.1 %collective-permute-start = (bf16[256,2048]{1,0:T(8,128)(2,1)S(1)}, bf16[256,2048]{1,0:T(8,128)(2,1)}, u32[]{:S(2)}, u32[]{:S(2)}) collective-permute-start(bf16[256,2048]{1,0:T(8,128)(2,1)S(1)} %fusion.11), channel_id=1, source_target_pairs={{0,2},{1,3},{2,0},{3,1},{4,6},{5,7},{6,4},{7,5},{8,10},{9,11},{10,... | collective-permute-start | bytes 3145736 | tf_op jit(solution)/shard_map/ppermute | solution.py:402
  15.9 32.1 %collective-permute-start.1 = (bf16[256,768]{1,0:T(8,128)(2,1)}, bf16[256,768]{1,0:T(8,128)(2,1)}, u32[]{:S(2)}, u32[]{:S(2)}) collective-permute-start(bf16[256,768]{1,0:T(8,128)(2,1)} %get-tuple-element.143), channel_id=1, source_target_pairs={{0,4},{1,5},{2,6},{3,7},{4,0},{5,1},{6,2},{7,3},{8,12},{9,13},{10,... | collective-permute-start | bytes 1179656 | tf_op jit(solution)/shard_map/ppermute | solution.py:529
  18.5 36.8 %collective-permute-start.2 = (bf16[256,768]{1,0:T(8,128)(2,1)}, bf16[256,768]{1,0:T(8,128)(2,1)}, u32[]{:S(2)}, u32[]{:S(2)}) collective-permute-start(bf16[256,768]{1,0:T(8,128)(2,1)} %get-tuple-element.144), channel_id=1, source_target_pairs={{0,4},{1,5},{2,6},{3,7},{4,0},{5,1},{6,2},{7,3},{8,12},{9,13},{10,... | collective-permute-start | bytes 1179656 | tf_op jit(solution)/shard_map/ppermute | solution.py:529
  56.0 214.9 %all-gather.5.cloned.1.call-start = ((), (), s32[]{:S(2)}) async-start(), calls=%async_computation.3 | async-start | bytes 9437184 | tf_op jit(solution)/shard_map/all_gather | solution.py:565
  79.7 28.4 %collective-permute-start.10 = (bf16[256,768]{1,0:T(8,128)(2,1)}, bf16[256,768]{1,0:T(8,128)(2,1)S(1)}, u32[]{:S(2)}, u32[]{:S(2)}) collective-permute-start(bf16[256,768]{1,0:T(8,128)(2,1)} %collective-permute-done.5.refs_1_), channel_id=1, source_target_pairs={{0,16},{8,24},{16,0},{24,8},{1,17},{9,25},{17,1},{25,9},{2,18},{10... | collective-permute-start | bytes 1179656 | tf_op jit(solution)/shard_map/ppermute | solution.py:402
  81.5 26.6 %collective-permute-start.11 = (bf16[256,768]{1,0:T(8,128)(2,1)}, bf16[256,768]{1,0:T(8,128)(2,1)S(1)}, u32[]{:S(2)}, u32[]{:S(2)}) collective-permute-start(bf16[256,768]{1,0:T(8,128)(2,1)} %collective-permute-done.2.refs_4_), channel_id=1, source_target_pairs={{0,8},{8,0},{16,24},{24,16},{1,9},{9,1},{17,25},{25,17},{2,10},{10... | collective-permute-start | bytes 1179656 | tf_op jit(solution)/shard_map/ppermute | solution.py:402
  146.7 30.8 %collective-permute-start.20 = (bf16[256,2048]{1,0:T(8,128)(2,1)S(1)}, bf16[256,2048]{1,0:T(8,128)(2,1)S(1)}, u32[]{:S(2)}, u32[]{:S(2)}) collective-permute-start(bf16[256,2048]{1,0:T(8,128)(2,1)S(1)} %fusion.25), channel_id=1, source_target_pairs={{0,2},{1,3},{2,0},{3,1},{4,6},{5,7},{6,4},{7,5},{8,10},{9,11},{10,... | collective-permute-start | bytes 3145736 | tf_op jit(solution)/shard_map/ppermute | solution.py:423
  185.5 199.4 %reduce-scatter.3.cloned.1.call-start = ((), (), s32[]{:S(2)}) async-start(), calls=%async_computation.4 | async-start | bytes 9437184 | tf_op jit(solution)/shard_map/reduce_scatter | solution.py:574
  296.4 344.2 %reduce-scatter.5.cloned.1.call-start = ((), (), s32[]{:S(2)}) async-start(), calls=%async_computation.5 | async-start | bytes 9437184 | tf_op jit(solution)/shard_map/reduce_scatter | solution.py:595
  312.1 48.1 %collective-permute-start.29 = (bf16[2,512,1024]{2,1,0:T(8,128)(2,1)}, bf16[2,512,1024]{2,1,0:T(8,128)(2,1)}, u32[]{:S(2)}, u32[]{:S(2)}) collective-permute-start(bf16[2,512,1024]{2,1,0:T(8,128)(2,1)} %dynamic-slice_bitcast_fusion), channel_id=1, source_target_pairs={{0,16},{8,24},{16,0},{24,8},{1,17},{9,25},{17,1},{25,9},{2,18},{10... | collective-permute-start | bytes 6291464 | tf_op jit(solution)/shard_map/ppermute | solution.py:423
  329.1 48.4 %collective-permute-start.28 = (bf16[2,256,2048]{2,1,0:T(8,128)(2,1)}, bf16[2,256,2048]{2,1,0:T(8,128)(2,1)}, u32[]{:S(2)}, u32[]{:S(2)}) collective-permute-start(bf16[2,256,2048]{2,1,0:T(8,128)(2,1)} %dynamic-slice_bitcast_fusion.1), channel_id=1, source_target_pairs={{0,8},{8,0},{16,24},{24,16},{1,9},{9,1},{17,25},{25,17},{2,10},{10... | collective-permute-start | bytes 6291464 | tf_op jit(solution)/shard_map/ppermute | solution.py:423
  491.1 38.9 %collective-permute-start.57 = (bf16[2,256,1024]{2,1,0:T(8,128)(2,1)}, bf16[2,256,1024]{2,1,0:T(8,128)(2,1)}, u32[]{:S(2)}, u32[]{:S(2)}) collective-permute-start(bf16[2,256,1024]{2,1,0:T(8,128)(2,1)} %dynamic-slice_bitcast_fusion.2), channel_id=1, source_target_pairs={{0,16},{8,24},{16,0},{24,8},{1,17},{9,25},{17,1},{25,9},{2,18},{10... | collective-permute-start | bytes 3145736 | tf_op jit(solution)/shard_map/ppermute | solution.py:423
  502.2 63.1 %collective-permute-start.44 = (bf16[2,256,2048]{2,1,0:T(8,128)(2,1)}, bf16[2,256,2048]{2,1,0:T(8,128)(2,1)}, u32[]{:S(2)}, u32[]{:S(2)}) collective-permute-start(bf16[2,256,2048]{2,1,0:T(8,128)(2,1)} %share_of.6), channel_id=1, source_target_pairs={{0,1},{1,0},{2,3},{3,2},{4,5},{5,4},{6,7},{7,6},{8,9},{9,8},{10,11... | collective-permute-start | bytes 6291464 | tf_op jit(solution)/shard_map/ppermute | solution.py:500
  502.3 33.0 %collective-permute-start.55 = (bf16[2,256,1024]{2,1,0:T(8,128)(2,1)S(1)}, bf16[2,256,1024]{2,1,0:T(8,128)(2,1)S(1)}, u32[]{:S(2)}, u32[]{:S(2)}) collective-permute-start(bf16[2,256,1024]{2,1,0:T(8,128)(2,1)S(1)} %dynamic-slice_bitcast_fusion.3), channel_id=1, source_target_pairs={{0,8},{8,0},{16,24},{24,16},{1,9},{9,1},{17,25},{25,17},{2,10},{10... | collective-permute-start | bytes 3145736 | tf_op jit(solution)/shard_map/ppermute | solution.py:423
  506.0 41.1 %collective-permute-start.42 = (bf16[256,2048]{1,0:T(8,128)(2,1)S(1)}, bf16[256,2048]{1,0:T(8,128)(2,1)S(1)}, u32[]{:S(2)}, u32[]{:S(2)}) collective-permute-start(bf16[256,2048]{1,0:T(8,128)(2,1)S(1)} %copy-done.15), channel_id=1, source_target_pairs={{0,16},{8,24},{16,0},{24,8},{1,17},{9,25},{17,1},{25,9},{2,18},{10... | collective-permute-start | bytes 3145736 | tf_op jit(solution)/shard_map/ppermute | solution.py:458
  528.6 25.9 %collective-permute-start.43 = (bf16[512,1024]{1,0:T(8,128)(2,1)S(1)}, bf16[512,1024]{1,0:T(8,128)(2,1)S(1)}, u32[]{:S(2)}, u32[]{:S(2)}) collective-permute-start(bf16[512,1024]{1,0:T(8,128)(2,1)S(1)} %copy-done.16), channel_id=1, source_target_pairs={{0,8},{8,0},{16,24},{24,16},{1,9},{9,1},{17,25},{25,17},{2,10},{10... | collective-permute-start | bytes 3145736 | tf_op jit(solution)/shard_map/ppermute | solution.py:458
  530.0 34.7 %collective-permute-start.48 = (bf16[256,1024]{1,0:T(8,128)(2,1)}, bf16[256,1024]{1,0:T(8,128)(2,1)}, u32[]{:S(2)}, u32[]{:S(2)}) collective-permute-start(bf16[256,1024]{1,0:T(8,128)(2,1)} %fusion.29), channel_id=1, source_target_pairs={{0,4},{1,5},{2,6},{3,7},{4,0},{5,1},{6,2},{7,3},{8,12},{9,13},{10,... | collective-permute-start | bytes 1572872 | tf_op jit(solution)/shard_map/ppermute | solution.py:618
  535.3 37.7 %collective-permute-start.46 = (bf16[256,1024]{1,0:T(8,128)(2,1)S(1)}, bf16[256,1024]{1,0:T(8,128)(2,1)}, u32[]{:S(2)}, u32[]{:S(2)}) collective-permute-start(bf16[256,1024]{1,0:T(8,128)(2,1)S(1)} %fusion.30), channel_id=1, source_target_pairs={{0,4},{1,5},{2,6},{3,7},{4,0},{5,1},{6,2},{7,3},{8,12},{9,13},{10,... | collective-permute-start | bytes 1572872 | tf_op jit(solution)/shard_map/ppermute | solution.py:618
  547.2 26.2 %collective-permute-start.58 = (bf16[256,1024]{1,0:T(8,128)(2,1)}, bf16[256,1024]{1,0:T(8,128)(2,1)}, u32[]{:S(2)}, u32[]{:S(2)}) collective-permute-start(bf16[256,1024]{1,0:T(8,128)(2,1)} %fusion.40), channel_id=1, source_target_pairs={{0,8},{8,0},{16,24},{24,16},{1,9},{9,1},{17,25},{25,17},{2,10},{10... | collective-permute-start | bytes 1572872 | tf_op jit(solution)/shard_map/ppermute | solution.py:423
  603.7 29.1 %collective-permute-start.63 = (bf16[256,1024]{1,0:T(8,128)(2,1)}, bf16[256,1024]{1,0:T(8,128)(2,1)}, u32[]{:S(2)}, u32[]{:S(2)}) collective-permute-start(bf16[256,1024]{1,0:T(8,128)(2,1)} %add_convert_fusion.2.refs_0_), channel_id=1, source_target_pairs={{0,16},{8,24},{16,0},{24,8},{1,17},{9,25},{17,1},{25,9},{2,18},{10... | collective-permute-start | bytes 1572872 | tf_op jit(solution)/shard_map/ppermute | solution.py:402
  604.1 28.7 %collective-permute-start.64 = (bf16[256,1024]{1,0:T(8,128)(2,1)}, bf16[256,1024]{1,0:T(8,128)(2,1)}, u32[]{:S(2)}, u32[]{:S(2)}) collective-permute-start(bf16[256,1024]{1,0:T(8,128)(2,1)} %collective-permute-done.61.refs_1_), channel_id=1, source_target_pairs={{0,16},{8,24},{16,0},{24,8},{1,17},{9,25},{17,1},{25,9},{2,18},{10... | collective-permute-start | bytes 1572872 | tf_op jit(solution)/shard_map/ppermute | solution.py:402
  605.7 27.1 %collective-permute-start.65 = (bf16[256,1024]{1,0:T(8,128)(2,1)S(1)}, bf16[256,1024]{1,0:T(8,128)(2,1)}, u32[]{:S(2)}, u32[]{:S(2)}) collective-permute-start(bf16[256,1024]{1,0:T(8,128)(2,1)S(1)} %add_convert_fusion.1.refs_4_), channel_id=1, source_target_pairs={{0,8},{8,0},{16,24},{24,16},{1,9},{9,1},{17,25},{25,17},{2,10},{10... | collective-permute-start | bytes 1572872 | tf_op jit(solution)/shard_map/ppermute | solution.py:402
  606.0 26.8 %collective-permute-start.66 = (bf16[256,1024]{1,0:T(8,128)(2,1)}, bf16[256,1024]{1,0:T(8,128)(2,1)}, u32[]{:S(2)}, u32[]{:S(2)}) collective-permute-start(bf16[256,1024]{1,0:T(8,128)(2,1)} %collective-permute-done.62.refs_6_), channel_id=1, source_target_pairs={{0,8},{8,0},{16,24},{24,16},{1,9},{9,1},{17,25},{25,17},{2,10},{10... | collective-permute-start | bytes 1572872 | tf_op jit(solution)/shard_map/ppermute | solution.py:402
  (104 other events, 1443.5 us)
Sparse Core Ops, SparseCore 0:
  56.1 85.7 all-gather.2
  185.6 85.2 all-gather.4
  296.5 88.3 reduce-scatter.2
  423.9 89.3 reduce-scatter.4

commit v15 on v14

--- a/solution.py
+++ b/solution.py
@@ -516,14 +516,11 @@
             in_slice(lax.dynamic_slice_in_dim(attention_weight, column * chunk_rows + at, half_rows, 0))
             for at in (0, half_rows)
         ]
-        lanes_out = [
-            lax.dynamic_slice_in_dim(output_weight, column * chunk_rows + at, half_rows, 1).T
-            for at in (0, half_rows)
-        ]
+        lanes_out = [lax.dynamic_slice_in_dim(output_weight, column * chunk_rows, chunk_rows, 1).T]
         input_wide = wide(layer_input)
         normed_one, scaled_one, inverse_one = norm_forward(input_wide, mixer_gain)
         low_one = narrow(normed_one)
-        low_one, lanes_in, lanes_out = lax.optimization_barrier((low_one, lanes_in, lanes_out))
+        low_one, lanes_in = lax.optimization_barrier((low_one, lanes_in))
         held = xor_gather(low_one, "mp", ranks, pair_bits)
         fetched_in, fetched_out = [
             [[lax.ppermute(x, "mp", shift_pairs(ranks, k * group)) for x in lanes] for k in range(1, sequences)]
@@ -571,7 +568,7 @@
         )
         dots = dots.reshape(-1, 128)
         share, hidden, pre_grad = lax.optimization_barrier((share, hidden, pre_grad))
-        normed_grad_two = wide(lax.psum_scatter(share, "mp", scatter_dimension=0, tiled=True))
+        normed_grad_two = lax.psum_scatter(share, "mp", scatter_dimension=0, tiled=True)
         gate_grad_two = lax.dynamic_slice_in_dim(all_sum(dots, {"mp": ranks}).reshape(-1), rank * rows, rows, 0)
         gated = narrow(gates[:, None] * wide(grads_all))
         lanes = [narrow(product(hidden, gated, (0, 0))), narrow(product(inputs_two, pre_grad, (0, 0)))]
@@ -582,6 +579,7 @@
         normed_grad_two, hidden_share, blank, *lanes = lax.optimization_barrier(
             (normed_grad_two, hidden_share, blank, *lanes)
         )
+        normed_grad_two = wide(normed_grad_two)
         lanes = [narrow(x) for x in column_scatter(lanes, columns, column, start=1)]
 
         router_part, _ = gate_backward(normed_two, hidden_router, state_two, gate_grad_two)

time: 654 us -> 652 us (level)
    ppermute x33 -> x30, starting transfers between devices: 37.4 us -> 32.4 us  [xor_gather(): held[far ^ bit] = lax.ppermute(held[far], axis, swap_pairs(size, bit))]
    ppermute x4 -> x3, waiting for transfers between devices: 26.8 us -> 25 us  [local(): lax.ppermute(x, 'mp', shift_pairs(ranks, k * group))]
    ppermute x33 -> x30, waiting for transfers between devices: 50.4 us -> 49.5 us  [xor_gather(): held[far ^ bit] = lax.ppermute(held[far], axis, swap_pairs(size, bit))]
    unnamed x116 -> x108, local copies, waits for them, and re-layouts: 13.4 us -> 12.9 us
  transfers between devices with their start and end apart: 71 -> 67, of which waited for: 29 -> 26; matrix products, arithmetic and copies ran while one was open for 21% -> 21% of each run, Pallas kernels for 18% -> 18%
where the time goes in v15:
time: 652 us; the launch traced here: 648 us
  waiting for transfers between devices  244 us (37%)
  Pallas kernels  144 us (22%)
  starting transfers between devices  74 us (11%)
  matrix products  64.9 us (10%)
  other arithmetic  60.6 us (9%)
  local copies, waits for them, and re-layouts  44.7 us (7%)
  between operations  15.2 us (2%)
    ppermute x14, waiting for transfers between devices, xor_scatter(): lax.ppermute(narrow(pick(blocks, 1 - side, at)), axis_name, swap_pairs(si...  80.1 us
    dot_general x4, matrix products, product(): lax.dot_general(a, b, ((dims[:1], dims[1:]), ((), ())), preferred_element...  51.4 us
    ppermute x30, waiting for transfers between devices, xor_gather(): held[far ^ bit] = lax.ppermute(held[far], axis, swap_pairs(size, bit))  49.5 us
    all_gather x1, waiting for transfers between devices, local(): inputs_two = lax.all_gather(narrow(normed_two), 'mp', axis=0, tiled=True)  46.6 us
    ppermute x30, starting transfers between devices, xor_gather(): held[far ^ bit] = lax.ppermute(held[far], axis, swap_pairs(size, bit))  32.4 us
    pallas_call x2, Pallas kernels, attend_backward(): pl.pallas_call(backward_kernel, out_shape=jax.ShapeDtypeStruct((tokens, 3...  26.9 us
    ppermute x4, waiting for transfers between devices, gather_part(): held[far ^ bit] = lax.ppermute(held[far], 'dp', swap_pairs(size, bit))  26.8 us
    pallas_call x1, Pallas kernels, hidden_pass(): pl.pallas_call(hidden_kernel, grid_spec=pltpu.PrefetchScalarGridSpec(num_...  25.4 us
  transfers between devices with their start and end apart: 67, of which 26 were waited for; matrix products, arithmetic and copies ran while one was open for 21% of the time, Pallas kernels for 18%

profile of v15, /device:TPU:0, one launch (start us, length us, event | category | flops | bytes accessed | tf_op | source)
XLA Modules:
  0.0 647.6 jit_solution(7063552535113771439)
XLA Ops:
  30.5 17.7 %collective-permute-done.1.refs_0_ = bf16[256,768]{1,0:T(8,128)(2,1)} collective-permute-done((bf16[256,768]{1,0:T(8,128)(2,1)}, bf16[256,768]{1,0:T(8,128)(2,1)}, u32[]{:S(2)}, u32[]{:S(2)}) %collective-permute-start.1) | collective-permute-done | bytes 393248 | tf_op jit(solution)/shard_map/ppermute | solution.py:526
  68.7 12.4 %attend_forward.2 = (bf16[1024,768]{1,0:T(8,128)(2,1)}, bf16[1024,256]{1,0:T(8,128)(2,1)}, f32[1024,2]{1,0:T(8,128)}) custom-call(bf16[1024,2048]{1,0:T(8,128)(2,1)} %bitcast.196, bf16[2048,768]{1,0:T(8,128)(2,1)} %pad_maximum_fusion.w_ref.refs_3_, f32[1024,128]{1,0:T(8,128)} %get-tuple-element.143.cos_ref, f32[1024,128]{1,0:T(8,128)} %get-tuple-element.144.sin_ref, ...), custom_call_target="tpu_custom_call" | custom-call | flops 3758096384 | bytes 12582912 | tf_op jit(solution)/shard_map/attend_forward/pallas_call | solution.py:237
  87.1 19.9 %collective-permute-done.12.refs_1_ = bf16[512,256]{1,0:T(8,128)(2,1)S(1)} collective-permute-done((bf16[512,256]{1,0:T(8,128)(2,1)S(1)}, bf16[512,256]{1,0:T(8,128)(2,1)S(1)}, u32[]{:S(2)}, u32[]{:S(2)}) %collective-permute-start.12) | collective-permute-done | bytes 262176 | tf_op jit(solution)/shard_map/ppermute | solution.py:402
  113.6 12.6 %attend_forward.3 = (bf16[1024,768]{1,0:T(8,128)(2,1)}, bf16[1024,256]{1,0:T(8,128)(2,1)}, f32[1024,2]{1,0:T(8,128)}) custom-call(bf16[1024,2048]{1,0:T(8,128)(2,1)} %bitcast.197, bf16[2048,768]{1,0:T(8,128)(2,1)} %place_blocks.5.w_ref.refs_1_, f32[1024,128]{1,0:T(8,128)} %get-tuple-element.143.cos_ref, f32[1024,128]{1,0:T(8,128)} %get-tuple-element.144.sin_ref, ...), custom_call_target="tpu_custom_call" | custom-call | flops 3758096384 | bytes 12582912 | tf_op jit(solution)/shard_map/attend_forward/pallas_call | solution.py:237
  143.7 8.5 %collective-permute-start.16 = (bf16[256,2048]{1,0:T(8,128)(2,1)S(1)}, bf16[256,2048]{1,0:T(8,128)(2,1)S(1)}, u32[]{:S(2)}, u32[]{:S(2)}) collective-permute-start(bf16[256,2048]{1,0:T(8,128)(2,1)S(1)} %fusion.25), channel_id=1, source_target_pairs={{0,2},{1,3},{2,0},{3,1},{4,6},{5,7},{6,4},{7,5},{8,10},{9,11},{10,... | collective-permute-start | bytes 3145736 | tf_op jit(solution)/shard_map/ppermute | solution.py:423
  154.9 21.0 %collective-permute-done.16 = bf16[256,2048]{1,0:T(8,128)(2,1)S(1)} collective-permute-done((bf16[256,2048]{1,0:T(8,128)(2,1)S(1)}, bf16[256,2048]{1,0:T(8,128)(2,1)S(1)}, u32[]{:S(2)}, u32[]{:S(2)}) %collective-permute-start.16) | collective-permute-done | bytes 1048608 | tf_op jit(solution)/shard_map/ppermute | solution.py:423
  195.6 14.7 %fusion.81.top_ref = f32[2048,1024]{1,0:T(8,128)} fusion(bf16[2048,2048]{1,0:T(8,128)(2,1)} %all-gather.3.cloned.1.call-done, bf16[1024,2048]{1,0:T(8,128)(2,1)} %param.22), kind=kOutput, calls=%fused_computation.192 | convolution fusion | flops 8589934592 | bytes 20971520 | tf_op jit(solution)/shard_map/dot_general | solution.py:94
  221.9 46.6 %all-gather.5.cloned.1.call-done.x_ref = bf16[2048,2048]{1,0:T(8,128)(2,1)} async-done(((bf16[256,2048]{1,0:T(8,128)(2,1)}), bf16[2048,2048]{1,0:T(8,128)(2,1)}) %all-gather.5.cloned.1.call-update) | async-done | bytes 8388624 | tf_op jit(solution)/shard_map/all_gather | solution.py:562
  268.5 25.4 %hidden_pass.1 = (bf16[2048,2048]{1,0:T(8,128)(2,1)}, bf16[2048,1024]{1,0:T(8,128)(2,1)}, bf16[2048,1024]{1,0:T(8,128)(2,1)}, f32[1,2048]{1,0:T(1,128)}) custom-call(s32[1]{0:T(128)} %bitcast.28.offset_ref, bf16[2048,2048]{1,0:T(8,128)(2,1)} %all-gather.5.cloned.1.call-done.x_ref, bf16[2048,1024]{1,0:T(8,128)(2,1)} %up_ref.1, f32[2048,1024]{1,0:T(8,128)} %fusion.81.top_ref, ...), custom_call_target="tpu_custom_call" | custom-call | flops 17179869184 | bytes 41943040 | tf_op jit(solution)/shard_map/hidden_pass/pallas_call | solution.py:305
  294.0 13.0 %convolution_convert_fusion.1 = bf16[2048,1024]{1,0:T(8,128)(2,1)S(1)} fusion(bf16[2048,2048]{1,0:T(8,128)(2,1)} %all-gather.5.cloned.1.call-done.x_ref, bf16[2048,1024]{1,0:T(8,128)(2,1)} %get-tuple-element.182), kind=kOutput, calls=%fused_computation.9 | convolution fusion | flops 8592031744 | bytes 16777216 | tf_op jit(solution)/shard_map/dot_general | solution.py:94
  311.1 12.3 %fusion.2 = bf16[1024,2048]{1,0:T(8,128)(2,1)S(1)} fusion(bf16[2048,1024]{1,0:T(8,128)(2,1)S(1)} %copy-done.52, bf16[2048,2048]{1,0:T(8,128)(2,1)} %all-gather.3.cloned.1.call-done, f32[2048]{0:T(1024)S(1)} %bitcast.218), kind=kOutput, calls=%fused_computation.8 | convolution fusion | flops 8604614656 | bytes 16785408 | tf_op jit(solution)/shard_map/dot_general | solution.py:94
  328.5 11.3 %convolution_convert_fusion = bf16[2048,2048]{1,0:T(8,128)(2,1)} fusion(bf16[2048,1024]{1,0:T(8,128)(2,1)S(1)} %copy-done.52, bf16[1024,2048]{1,0:T(8,128)(2,1)S(1)} %copy-done.51), kind=kOutput, calls=%fused_computation.3 | convolution fusion | flops 8594128896 | bytes 16777216 | tf_op jit(solution)/shard_map/dot_general | solution.py:94
  340.0 17.8 %collective-permute-done.25 = bf16[2,512,1024]{2,1,0:T(8,128)(2,1)} collective-permute-done((bf16[2,512,1024]{2,1,0:T(8,128)(2,1)}, bf16[2,512,1024]{2,1,0:T(8,128)(2,1)}, u32[]{:S(2)}, u32[]{:S(2)}) %collective-permute-start.25) | collective-permute-done | bytes 2097184 | tf_op jit(solution)/shard_map/ppermute | solution.py:423
  363.0 11.9 %collective-permute-done.24 = bf16[2,256,2048]{2,1,0:T(8,128)(2,1)} collective-permute-done((bf16[2,256,2048]{2,1,0:T(8,128)(2,1)}, bf16[2,256,2048]{2,1,0:T(8,128)(2,1)}, u32[]{:S(2)}, u32[]{:S(2)}) %collective-permute-start.24) | collective-permute-done | bytes 2097184 | tf_op jit(solution)/shard_map/ppermute | solution.py:423
  395.2 19.5 %collective-permute-done.29 = bf16[256,2048]{1,0:T(8,128)(2,1)S(1)} collective-permute-done((bf16[256,2048]{1,0:T(8,128)(2,1)S(1)}, bf16[256,2048]{1,0:T(8,128)(2,1)S(1)}, u32[]{:S(2)}, u32[]{:S(2)}) %collective-permute-start.29) | collective-permute-done | bytes 1048608 | tf_op jit(solution)/shard_map/ppermute | solution.py:402
  425.4 13.7 %attend_backward.2.q_ref.refs_0_ = bf16[1024,768]{1,0:T(8,128)(2,1)} custom-call(bf16[1024,2048]{1,0:T(8,128)(2,1)} %bitcast.57.g_ref, bf16[2048,256]{1,0:T(8,128)(2,1)} %place_blocks.6.refs_3_.w_ref, bf16[1024,768]{1,0:T(8,128)(2,1)} %get-tuple-element.191.qkv_ref, f32[1024,2]{1,0:T(8,128)} %get-tuple-element.192.log_ref, ...), custom_call_target="tpu_custom_call" | custom-call | flops 2415919104 | bytes 12582912 | tf_op jit(solution)/shard_map/attend_backward/pallas_call | solution.py:259
  439.1 8.9 %weight_grads.2 = (bf16[4,256,1024]{2,1,0:T(8,128)(2,1)}, bf16[4,256,1024]{2,1,0:T(8,128)(2,1)}) custom-call(bf16[1024,2048]{1,0:T(8,128)(2,1)} %bitcast.198, bf16[1024,768]{1,0:T(8,128)(2,1)} %attend_backward.2.q_ref.refs_0_, bf16[1024,2048]{1,0:T(8,128)(2,1)} %bitcast.57.g_ref, bf16[1024,256]{1,0:T(8,128)(2,1)} %get-tuple-element.170.refs_2_.h_ref), custom_call_target="tpu_custom_call" | custom-call | flops 4294967296 | bytes 14680064 | tf_op jit(solution)/shard_map/weight_grads/pallas_call | solution.py:330
  458.6 13.2 %attend_backward.3.q_ref.refs_2_ = bf16[1024,768]{1,0:T(8,128)(2,1)} custom-call(bf16[1024,2048]{1,0:T(8,128)(2,1)} %bitcast.57.g_ref, bf16[2048,256]{1,0:T(8,128)(2,1)} %bitcast.195, bf16[1024,768]{1,0:T(8,128)(2,1)} %get-tuple-element.150.qkv_ref, f32[1024,2]{1,0:T(8,128)} %get-tuple-element.196.log_ref, f32[1024,128]{1,0:T(8,128)} %get-tuple-element.143.cos_ref, ...), custom_call_target="tpu_custom_call" | custom-call | flops 2415919104 | bytes 12582912 | tf_op jit(solution)/shard_map/attend_backward/pallas_call | solution.py:259
  478.5 9.0 %weight_grads.3 = (bf16[4,256,1024]{2,1,0:T(8,128)(2,1)}, bf16[4,256,1024]{2,1,0:T(8,128)(2,1)}) custom-call(bf16[1024,2048]{1,0:T(8,128)(2,1)} %bitcast.199, bf16[1024,768]{1,0:T(8,128)(2,1)} %attend_backward.3.q_ref.refs_2_, bf16[1024,2048]{1,0:T(8,128)(2,1)} %bitcast.57.g_ref, bf16[1024,256]{1,0:T(8,128)(2,1)} %get-tuple-element.168.refs_0_.h_ref), custom_call_target="tpu_custom_call" | custom-call | flops 4294967296 | bytes 14680064 | tf_op jit(solution)/shard_map/weight_grads/pallas_call | solution.py:330
  493.0 7.8 %share_of.6 = bf16[2,256,2048]{2,1,0:T(8,128)(2,1)} custom-call(s32[1]{0:T(128)} %bitcast.22.side_ref, bf16[1024,768]{1,0:T(8,128)(2,1)} %attend_backward.2.q_ref.refs_0_, bf16[2048,768]{1,0:T(8,128)(2,1)} %place_blocks.5.w_ref.refs_1_, bf16[1024,768]{1,0:T(8,128)(2,1)} %attend_backward.3.q_ref.refs_2_, bf16[2048,768]{1,0:T(8,128)(2,1)} %pad_maximum_fusion.w_ref.refs_3_), custom_call_target="tpu_custom_call" | custom-call | flops 3221225472 | bytes 12582912 | tf_op jit(solution)/shard_map/share_of/pallas_call | solution.py:283
  507.2 20.1 %collective-permute-done.41 = bf16[256,1024]{1,0:T(8,128)(2,1)S(1)} collective-permute-done((bf16[256,1024]{1,0:T(8,128)(2,1)S(1)}, bf16[256,1024]{1,0:T(8,128)(2,1)S(1)}, u32[]{:S(2)}, u32[]{:S(2)}) %collective-permute-start.41) | collective-permute-done | bytes 524320 | tf_op jit(solution)/shard_map/ppermute | solution.py:423
  536.9 8.9 %collective-permute-done.38.refs_2_ = bf16[256,2048]{1,0:T(8,128)(2,1)S(1)} collective-permute-done((bf16[256,2048]{1,0:T(8,128)(2,1)S(1)}, bf16[256,2048]{1,0:T(8,128)(2,1)S(1)}, u32[]{:S(2)}, u32[]{:S(2)}) %collective-permute-start.38) | collective-permute-done | bytes 1048608 | tf_op jit(solution)/shard_map/ppermute | solution.py:458
  555.8 7.8 %share_of.7 = bf16[2,256,2048]{2,1,0:T(8,128)(2,1)} custom-call(s32[1]{0:T(128)} %bitcast.3.side_ref, bf16[1024,768]{1,0:T(8,128)(2,1)} %attend_backward.2.q_ref.refs_0_, bf16[2048,768]{1,0:T(8,128)(2,1)} %place_blocks.5.w_ref.refs_1_, bf16[1024,768]{1,0:T(8,128)(2,1)} %attend_backward.3.q_ref.refs_2_, bf16[2048,768]{1,0:T(8,128)(2,1)} %pad_maximum_fusion.w_ref.refs_3_), custom_call_target="tpu_custom_call" | custom-call | flops 3221225472 | bytes 12582912 | tf_op jit(solution)/shard_map/share_of/pallas_call | solution.py:283
  574.5 11.6 %collective-permute-done.55.refs_3_ = bf16[256,2048]{1,0:T(8,128)(2,1)S(1)} collective-permute-done((bf16[256,2048]{1,0:T(8,128)(2,1)}, bf16[256,2048]{1,0:T(8,128)(2,1)S(1)}, u32[]{:S(2)}, u32[]{:S(2)}) %collective-permute-start.55) | collective-permute-done | bytes 1048608 | tf_op jit(solution)/shard_map/ppermute | solution.py:458
  (357 shorter events, 266.7 us)
Async XLA Ops:
  7.2 172.0 %all-gather.3.cloned.1.call-start = ((), (), s32[]{:S(2)}) async-start(), calls=%async_computation.2 | async-start | bytes 9437184 | tf_op jit(solution)/shard_map/all_gather | solution.py:539
  13.1 43.1 %collective-permute-start = (bf16[256,2048]{1,0:T(8,128)(2,1)S(1)}, bf16[256,2048]{1,0:T(8,128)(2,1)}, u32[]{:S(2)}, u32[]{:S(2)}) collective-permute-start(bf16[256,2048]{1,0:T(8,128)(2,1)S(1)} %fusion.11), channel_id=1, source_target_pairs={{0,2},{1,3},{2,0},{3,1},{4,6},{5,7},{6,4},{7,5},{8,10},{9,11},{10,... | collective-permute-start | bytes 3145736 | tf_op jit(solution)/shard_map/ppermute | solution.py:402
  16.1 32.1 %collective-permute-start.1 = (bf16[256,768]{1,0:T(8,128)(2,1)}, bf16[256,768]{1,0:T(8,128)(2,1)}, u32[]{:S(2)}, u32[]{:S(2)}) collective-permute-start(bf16[256,768]{1,0:T(8,128)(2,1)} %get-tuple-element.138), channel_id=1, source_target_pairs={{0,4},{1,5},{2,6},{3,7},{4,0},{5,1},{6,2},{7,3},{8,12},{9,13},{10,... | collective-permute-start | bytes 1179656 | tf_op jit(solution)/shard_map/ppermute | solution.py:526
  18.7 36.8 %collective-permute-start.2 = (bf16[256,768]{1,0:T(8,128)(2,1)}, bf16[256,768]{1,0:T(8,128)(2,1)}, u32[]{:S(2)}, u32[]{:S(2)}) collective-permute-start(bf16[256,768]{1,0:T(8,128)(2,1)} %get-tuple-element.139), channel_id=1, source_target_pairs={{0,4},{1,5},{2,6},{3,7},{4,0},{5,1},{6,2},{7,3},{8,12},{9,13},{10,... | collective-permute-start | bytes 1179656 | tf_op jit(solution)/shard_map/ppermute | solution.py:526
  56.2 212.2 %all-gather.5.cloned.1.call-start = ((), (), s32[]{:S(2)}) async-start(), calls=%async_computation.3 | async-start | bytes 9437184 | tf_op jit(solution)/shard_map/all_gather | solution.py:562
  81.2 25.8 %collective-permute-start.10 = (bf16[256,768]{1,0:T(8,128)(2,1)}, bf16[256,768]{1,0:T(8,128)(2,1)S(1)}, u32[]{:S(2)}, u32[]{:S(2)}) collective-permute-start(bf16[256,768]{1,0:T(8,128)(2,1)} %collective-permute-done.2.refs_4_), channel_id=1, source_target_pairs={{0,8},{8,0},{16,24},{24,16},{1,9},{9,1},{17,25},{25,17},{2,10},{10... | collective-permute-start | bytes 1179656 | tf_op jit(solution)/shard_map/ppermute | solution.py:402
  143.7 32.3 %collective-permute-start.16 = (bf16[256,2048]{1,0:T(8,128)(2,1)S(1)}, bf16[256,2048]{1,0:T(8,128)(2,1)S(1)}, u32[]{:S(2)}, u32[]{:S(2)}) collective-permute-start(bf16[256,2048]{1,0:T(8,128)(2,1)S(1)} %fusion.25), channel_id=1, source_target_pairs={{0,2},{1,3},{2,0},{3,1},{4,6},{5,7},{6,4},{7,5},{8,10},{9,11},{10,... | collective-permute-start | bytes 3145736 | tf_op jit(solution)/shard_map/ppermute | solution.py:423
  184.0 198.4 %reduce-scatter.3.cloned.1.call-start = ((), (), s32[]{:S(2)}) async-start(), calls=%async_computation.4 | async-start | bytes 9437184 | tf_op jit(solution)/shard_map/reduce_scatter | solution.py:571
  293.9 344.4 %reduce-scatter.5.cloned.1.call-start = ((), (), s32[]{:S(2)}) async-start(), calls=%async_computation.5 | async-start | bytes 9437184 | tf_op jit(solution)/shard_map/reduce_scatter | solution.py:593
  309.6 48.1 %collective-permute-start.25 = (bf16[2,512,1024]{2,1,0:T(8,128)(2,1)}, bf16[2,512,1024]{2,1,0:T(8,128)(2,1)}, u32[]{:S(2)}, u32[]{:S(2)}) collective-permute-start(bf16[2,512,1024]{2,1,0:T(8,128)(2,1)} %dynamic-slice_bitcast_fusion), channel_id=1, source_target_pairs={{0,16},{8,24},{16,0},{24,8},{1,17},{9,25},{17,1},{25,9},{2,18},{10... | collective-permute-start | bytes 6291464 | tf_op jit(solution)/shard_map/ppermute | solution.py:423
  326.6 48.3 %collective-permute-start.24 = (bf16[2,256,2048]{2,1,0:T(8,128)(2,1)}, bf16[2,256,2048]{2,1,0:T(8,128)(2,1)}, u32[]{:S(2)}, u32[]{:S(2)}) collective-permute-start(bf16[2,256,2048]{2,1,0:T(8,128)(2,1)} %dynamic-slice_bitcast_fusion.1), channel_id=1, source_target_pairs={{0,8},{8,0},{16,24},{24,16},{1,9},{9,1},{17,25},{25,17},{2,10},{10... | collective-permute-start | bytes 6291464 | tf_op jit(solution)/shard_map/ppermute | solution.py:423
  422.5 25.5 %collective-permute-start.35 = (bf16[512,1024]{1,0:T(8,128)(2,1)}, bf16[512,1024]{1,0:T(8,128)(2,1)S(1)}, u32[]{:S(2)}, u32[]{:S(2)}) collective-permute-start(bf16[512,1024]{1,0:T(8,128)(2,1)} %fusion.22.refs_0_), channel_id=1, source_target_pairs={{0,16},{8,24},{16,0},{24,8},{1,17},{9,25},{17,1},{25,9},{2,18},{10... | collective-permute-start | bytes 3145736 | tf_op jit(solution)/shard_map/ppermute | solution.py:402
  489.8 39.0 %collective-permute-start.53 = (bf16[2,256,1024]{2,1,0:T(8,128)(2,1)}, bf16[2,256,1024]{2,1,0:T(8,128)(2,1)}, u32[]{:S(2)}, u32[]{:S(2)}) collective-permute-start(bf16[2,256,1024]{2,1,0:T(8,128)(2,1)} %dynamic-slice_bitcast_fusion.2), channel_id=1, source_target_pairs={{0,16},{8,24},{16,0},{24,8},{1,17},{9,25},{17,1},{25,9},{2,18},{10... | collective-permute-start | bytes 3145736 | tf_op jit(solution)/shard_map/ppermute | solution.py:423
  500.9 63.1 %collective-permute-start.40 = (bf16[2,256,2048]{2,1,0:T(8,128)(2,1)}, bf16[2,256,2048]{2,1,0:T(8,128)(2,1)}, u32[]{:S(2)}, u32[]{:S(2)}) collective-permute-start(bf16[2,256,2048]{2,1,0:T(8,128)(2,1)} %share_of.6), channel_id=1, source_target_pairs={{0,1},{1,0},{2,3},{3,2},{4,5},{5,4},{6,7},{7,6},{8,9},{9,8},{10,11... | collective-permute-start | bytes 6291464 | tf_op jit(solution)/shard_map/ppermute | solution.py:500
  501.0 32.9 %collective-permute-start.51 = (bf16[2,256,1024]{2,1,0:T(8,128)(2,1)S(1)}, bf16[2,256,1024]{2,1,0:T(8,128)(2,1)S(1)}, u32[]{:S(2)}, u32[]{:S(2)}) collective-permute-start(bf16[2,256,1024]{2,1,0:T(8,128)(2,1)S(1)} %dynamic-slice_bitcast_fusion.3), channel_id=1, source_target_pairs={{0,8},{8,0},{16,24},{24,16},{1,9},{9,1},{17,25},{25,17},{2,10},{10... | collective-permute-start | bytes 3145736 | tf_op jit(solution)/shard_map/ppermute | solution.py:423
  504.7 41.1 %collective-permute-start.38 = (bf16[256,2048]{1,0:T(8,128)(2,1)S(1)}, bf16[256,2048]{1,0:T(8,128)(2,1)S(1)}, u32[]{:S(2)}, u32[]{:S(2)}) collective-permute-start(bf16[256,2048]{1,0:T(8,128)(2,1)S(1)} %copy-done.14), channel_id=1, source_target_pairs={{0,16},{8,24},{16,0},{24,8},{1,17},{9,25},{17,1},{25,9},{2,18},{10... | collective-permute-start | bytes 3145736 | tf_op jit(solution)/shard_map/ppermute | solution.py:458
  527.3 25.9 %collective-permute-start.39 = (bf16[512,1024]{1,0:T(8,128)(2,1)S(1)}, bf16[512,1024]{1,0:T(8,128)(2,1)S(1)}, u32[]{:S(2)}, u32[]{:S(2)}) collective-permute-start(bf16[512,1024]{1,0:T(8,128)(2,1)S(1)} %copy-done.15), channel_id=1, source_target_pairs={{0,8},{8,0},{16,24},{24,16},{1,9},{9,1},{17,25},{25,17},{2,10},{10... | collective-permute-start | bytes 3145736 | tf_op jit(solution)/shard_map/ppermute | solution.py:458
  528.8 34.8 %collective-permute-start.44 = (bf16[256,1024]{1,0:T(8,128)(2,1)}, bf16[256,1024]{1,0:T(8,128)(2,1)}, u32[]{:S(2)}, u32[]{:S(2)}) collective-permute-start(bf16[256,1024]{1,0:T(8,128)(2,1)} %fusion.29), channel_id=1, source_target_pairs={{0,4},{1,5},{2,6},{3,7},{4,0},{5,1},{6,2},{7,3},{8,12},{9,13},{10,... | collective-permute-start | bytes 1572872 | tf_op jit(solution)/shard_map/ppermute | solution.py:616
  533.9 37.6 %collective-permute-start.42 = (bf16[256,1024]{1,0:T(8,128)(2,1)S(1)}, bf16[256,1024]{1,0:T(8,128)(2,1)}, u32[]{:S(2)}, u32[]{:S(2)}) collective-permute-start(bf16[256,1024]{1,0:T(8,128)(2,1)S(1)} %fusion.30), channel_id=1, source_target_pairs={{0,4},{1,5},{2,6},{3,7},{4,0},{5,1},{6,2},{7,3},{8,12},{9,13},{10,... | collective-permute-start | bytes 1572872 | tf_op jit(solution)/shard_map/ppermute | solution.py:616
  545.9 26.2 %collective-permute-start.54 = (bf16[256,1024]{1,0:T(8,128)(2,1)}, bf16[256,1024]{1,0:T(8,128)(2,1)}, u32[]{:S(2)}, u32[]{:S(2)}) collective-permute-start(bf16[256,1024]{1,0:T(8,128)(2,1)} %fusion.40), channel_id=1, source_target_pairs={{0,8},{8,0},{16,24},{24,16},{1,9},{9,1},{17,25},{25,17},{2,10},{10... | collective-permute-start | bytes 1572872 | tf_op jit(solution)/shard_map/ppermute | solution.py:423
  602.3 28.3 %collective-permute-start.59 = (bf16[256,1024]{1,0:T(8,128)(2,1)}, bf16[256,1024]{1,0:T(8,128)(2,1)}, u32[]{:S(2)}, u32[]{:S(2)}) collective-permute-start(bf16[256,1024]{1,0:T(8,128)(2,1)} %add_convert_fusion.2.refs_0_), channel_id=1, source_target_pairs={{0,16},{8,24},{16,0},{24,8},{1,17},{9,25},{17,1},{25,9},{2,18},{10... | collective-permute-start | bytes 1572872 | tf_op jit(solution)/shard_map/ppermute | solution.py:402
  602.7 27.8 %collective-permute-start.60 = (bf16[256,1024]{1,0:T(8,128)(2,1)}, bf16[256,1024]{1,0:T(8,128)(2,1)}, u32[]{:S(2)}, u32[]{:S(2)}) collective-permute-start(bf16[256,1024]{1,0:T(8,128)(2,1)} %collective-permute-done.57.refs_1_), channel_id=1, source_target_pairs={{0,16},{8,24},{16,0},{24,8},{1,17},{9,25},{17,1},{25,9},{2,18},{10... | collective-permute-start | bytes 1572872 | tf_op jit(solution)/shard_map/ppermute | solution.py:402
  604.3 26.2 %collective-permute-start.61 = (bf16[256,1024]{1,0:T(8,128)(2,1)S(1)}, bf16[256,1024]{1,0:T(8,128)(2,1)}, u32[]{:S(2)}, u32[]{:S(2)}) collective-permute-start(bf16[256,1024]{1,0:T(8,128)(2,1)S(1)} %add_convert_fusion.1.refs_4_), channel_id=1, source_target_pairs={{0,8},{8,0},{16,24},{24,16},{1,9},{9,1},{17,25},{25,17},{2,10},{10... | collective-permute-start | bytes 1572872 | tf_op jit(solution)/shard_map/ppermute | solution.py:402
  604.6 26.0 %collective-permute-start.62 = (bf16[256,1024]{1,0:T(8,128)(2,1)}, bf16[256,1024]{1,0:T(8,128)(2,1)}, u32[]{:S(2)}, u32[]{:S(2)}) collective-permute-start(bf16[256,1024]{1,0:T(8,128)(2,1)} %collective-permute-done.58.refs_6_), channel_id=1, source_target_pairs={{0,8},{8,0},{16,24},{24,16},{1,9},{9,1},{17,25},{25,17},{2,10},{10... | collective-permute-start | bytes 1572872 | tf_op jit(solution)/shard_map/ppermute | solution.py:402
  (96 other events, 1291.6 us)
Sparse Core Ops, SparseCore 0:
  56.4 85.8 all-gather.2
  184.1 84.2 all-gather.4
  294.0 88.3 reduce-scatter.2
  422.6 89.3 reduce-scatter.4

commit v16 on v15

--- a/solution.py
+++ b/solution.py
@@ -641,10 +641,10 @@
         input_part, gain_one = norm_backward(normed_grad_one + router_part_one, scaled_one, inverse_one, mixer_gain)
         input_grad = narrow(middle_grad + input_part)
 
-        sizes = {"mp": ranks, "dp": columns}
-
         smalls = [gain_two, gain_one, router_two.T, router_one.T]
-        small_sum = all_sum(jnp.concatenate([x.reshape(-1, 128) for x in smalls], axis=0), sizes)
+        small = all_sum(jnp.concatenate([x.reshape(-1, 128) for x in smalls], axis=0), {"mp": ranks})
+        small, layer_output = lax.optimization_barrier((small, layer_output))
+        small_sum = all_sum(small, {"dp": columns})
         cuts = [dim // 128, 2 * dim // 128, (2 * dim + router_two.size) // 128]
         hidden_gain_sum, mixer_gain_sum, hidden_router_sum, mixer_router_sum = (
             x.reshape(-1, dim) for x in jnp.split(small_sum, cuts)

time: 652 us -> 653 us (level)
  transfers between devices with their start and end apart: 67 -> 67, of which waited for: 26 -> 26; matrix products, arithmetic and copies ran while one was open for 21% -> 22% of each run, Pallas kernels for 18% -> 18%
where the time goes in v16:
time: 653 us; the launch traced here: 648 us
  waiting for transfers between devices  244 us (37%)
  Pallas kernels  144 us (22%)
  starting transfers between devices  72.8 us (11%)
  matrix products  64.9 us (10%)
  other arithmetic  62.7 us (10%)
  local copies, waits for them, and re-layouts  44.7 us (7%)
  between operations  15.2 us (2%)
    ppermute x14, waiting for transfers between devices, xor_scatter(): lax.ppermute(narrow(pick(blocks, 1 - side, at)), axis_name, swap_pairs(si...  79.3 us
    dot_general x4, matrix products, product(): lax.dot_general(a, b, ((dims[:1], dims[1:]), ((), ())), preferred_element...  51.4 us
    ppermute x30, waiting for transfers between devices, xor_gather(): held[far ^ bit] = lax.ppermute(held[far], axis, swap_pairs(size, bit))  49 us
    all_gather x1, waiting for transfers between devices, local(): inputs_two = lax.all_gather(narrow(normed_two), 'mp', axis=0, tiled=True)  46.6 us
    ppermute x30, starting transfers between devices, xor_gather(): held[far ^ bit] = lax.ppermute(held[far], axis, swap_pairs(size, bit))  32.3 us
    ppermute x4, waiting for transfers between devices, gather_part(): held[far ^ bit] = lax.ppermute(held[far], 'dp', swap_pairs(size, bit))  26.9 us
    pallas_call x2, Pallas kernels, attend_backward(): pl.pallas_call(backward_kernel, out_shape=jax.ShapeDtypeStruct((tokens, 3...  26.9 us
    pallas_call x1, Pallas kernels, hidden_pass(): pl.pallas_call(hidden_kernel, grid_spec=pltpu.PrefetchScalarGridSpec(num_...  25.4 us
  transfers between devices with their start and end apart: 67, of which 26 were waited for; matrix products, arithmetic and copies ran while one was open for 22% of the time, Pallas kernels for 18%

profile of v16, /device:TPU:0, one launch (start us, length us, event | category | flops | bytes accessed | tf_op | source)
XLA Modules:
  0.0 648.2 jit_solution(7901253698467671533)
XLA Ops:
  30.5 17.7 %collective-permute-done.1.refs_0_ = bf16[256,768]{1,0:T(8,128)(2,1)} collective-permute-done((bf16[256,768]{1,0:T(8,128)(2,1)}, bf16[256,768]{1,0:T(8,128)(2,1)}, u32[]{:S(2)}, u32[]{:S(2)}) %collective-permute-start.1) | collective-permute-done | bytes 393248 | tf_op jit(solution)/shard_map/ppermute | solution.py:526
  68.7 12.4 %attend_forward.2 = (bf16[1024,768]{1,0:T(8,128)(2,1)}, bf16[1024,256]{1,0:T(8,128)(2,1)}, f32[1024,2]{1,0:T(8,128)}) custom-call(bf16[1024,2048]{1,0:T(8,128)(2,1)} %bitcast.196, bf16[2048,768]{1,0:T(8,128)(2,1)} %pad_maximum_fusion.w_ref.refs_3_, f32[1024,128]{1,0:T(8,128)} %get-tuple-element.145.cos_ref, f32[1024,128]{1,0:T(8,128)} %get-tuple-element.146.sin_ref, ...), custom_call_target="tpu_custom_call" | custom-call | flops 3758096384 | bytes 12582912 | tf_op jit(solution)/shard_map/attend_forward/pallas_call | solution.py:237
  87.1 19.9 %collective-permute-done.12.refs_1_ = bf16[512,256]{1,0:T(8,128)(2,1)S(1)} collective-permute-done((bf16[512,256]{1,0:T(8,128)(2,1)S(1)}, bf16[512,256]{1,0:T(8,128)(2,1)S(1)}, u32[]{:S(2)}, u32[]{:S(2)}) %collective-permute-start.12) | collective-permute-done | bytes 262176 | tf_op jit(solution)/shard_map/ppermute | solution.py:402
  113.6 12.6 %attend_forward.3 = (bf16[1024,768]{1,0:T(8,128)(2,1)}, bf16[1024,256]{1,0:T(8,128)(2,1)}, f32[1024,2]{1,0:T(8,128)}) custom-call(bf16[1024,2048]{1,0:T(8,128)(2,1)} %bitcast.197, bf16[2048,768]{1,0:T(8,128)(2,1)} %place_blocks.5.w_ref.refs_1_, f32[1024,128]{1,0:T(8,128)} %get-tuple-element.145.cos_ref, f32[1024,128]{1,0:T(8,128)} %get-tuple-element.146.sin_ref, ...), custom_call_target="tpu_custom_call" | custom-call | flops 3758096384 | bytes 12582912 | tf_op jit(solution)/shard_map/attend_forward/pallas_call | solution.py:237
  143.7 8.5 %collective-permute-start.16 = (bf16[256,2048]{1,0:T(8,128)(2,1)S(1)}, bf16[256,2048]{1,0:T(8,128)(2,1)S(1)}, u32[]{:S(2)}, u32[]{:S(2)}) collective-permute-start(bf16[256,2048]{1,0:T(8,128)(2,1)S(1)} %fusion.25), channel_id=1, source_target_pairs={{0,2},{1,3},{2,0},{3,1},{4,6},{5,7},{6,4},{7,5},{8,10},{9,11},{10,... | collective-permute-start | bytes 3145736 | tf_op jit(solution)/shard_map/ppermute | solution.py:423
  154.9 21.0 %collective-permute-done.16 = bf16[256,2048]{1,0:T(8,128)(2,1)S(1)} collective-permute-done((bf16[256,2048]{1,0:T(8,128)(2,1)S(1)}, bf16[256,2048]{1,0:T(8,128)(2,1)S(1)}, u32[]{:S(2)}, u32[]{:S(2)}) %collective-permute-start.16) | collective-permute-done | bytes 1048608 | tf_op jit(solution)/shard_map/ppermute | solution.py:423
  195.6 14.7 %fusion.81.top_ref = f32[2048,1024]{1,0:T(8,128)} fusion(bf16[2048,2048]{1,0:T(8,128)(2,1)} %all-gather.3.cloned.1.call-done, bf16[1024,2048]{1,0:T(8,128)(2,1)} %param.22), kind=kOutput, calls=%fused_computation.192 | convolution fusion | flops 8589934592 | bytes 20971520 | tf_op jit(solution)/shard_map/dot_general | solution.py:94
  221.8 46.6 %all-gather.5.cloned.1.call-done.x_ref = bf16[2048,2048]{1,0:T(8,128)(2,1)} async-done(((bf16[256,2048]{1,0:T(8,128)(2,1)}), bf16[2048,2048]{1,0:T(8,128)(2,1)}) %all-gather.5.cloned.1.call-update) | async-done | bytes 8388624 | tf_op jit(solution)/shard_map/all_gather | solution.py:562
  268.5 25.4 %hidden_pass.1 = (bf16[2048,2048]{1,0:T(8,128)(2,1)}, bf16[2048,1024]{1,0:T(8,128)(2,1)}, bf16[2048,1024]{1,0:T(8,128)(2,1)}, f32[1,2048]{1,0:T(1,128)}) custom-call(s32[1]{0:T(128)} %bitcast.offset_ref, bf16[2048,2048]{1,0:T(8,128)(2,1)} %all-gather.5.cloned.1.call-done.x_ref, bf16[2048,1024]{1,0:T(8,128)(2,1)} %up_ref.1, f32[2048,1024]{1,0:T(8,128)} %fusion.81.top_ref, ...), custom_call_target="tpu_custom_call" | custom-call | flops 17179869184 | bytes 41943040 | tf_op jit(solution)/shard_map/hidden_pass/pallas_call | solution.py:305
  294.0 13.0 %convolution_convert_fusion.1 = bf16[2048,1024]{1,0:T(8,128)(2,1)S(1)} fusion(bf16[2048,2048]{1,0:T(8,128)(2,1)} %all-gather.5.cloned.1.call-done.x_ref, bf16[2048,1024]{1,0:T(8,128)(2,1)} %get-tuple-element.184), kind=kOutput, calls=%fused_computation.9 | convolution fusion | flops 8592031744 | bytes 16777216 | tf_op jit(solution)/shard_map/dot_general | solution.py:94
  311.1 12.3 %fusion.2 = bf16[1024,2048]{1,0:T(8,128)(2,1)S(1)} fusion(bf16[2048,1024]{1,0:T(8,128)(2,1)S(1)} %copy-done.52, bf16[2048,2048]{1,0:T(8,128)(2,1)} %all-gather.3.cloned.1.call-done, f32[2048]{0:T(1024)S(1)} %bitcast.218), kind=kOutput, calls=%fused_computation.8 | convolution fusion | flops 8604614656 | bytes 16785408 | tf_op jit(solution)/shard_map/dot_general | solution.py:94
  328.5 11.3 %convolution_convert_fusion = bf16[2048,2048]{1,0:T(8,128)(2,1)} fusion(bf16[2048,1024]{1,0:T(8,128)(2,1)S(1)} %copy-done.52, bf16[1024,2048]{1,0:T(8,128)(2,1)S(1)} %copy-done.51), kind=kOutput, calls=%fused_computation.3 | convolution fusion | flops 8594128896 | bytes 16777216 | tf_op jit(solution)/shard_map/dot_general | solution.py:94
  340.0 17.8 %collective-permute-done.25 = bf16[2,512,1024]{2,1,0:T(8,128)(2,1)} collective-permute-done((bf16[2,512,1024]{2,1,0:T(8,128)(2,1)}, bf16[2,512,1024]{2,1,0:T(8,128)(2,1)}, u32[]{:S(2)}, u32[]{:S(2)}) %collective-permute-start.25) | collective-permute-done | bytes 2097184 | tf_op jit(solution)/shard_map/ppermute | solution.py:423
  363.0 11.9 %collective-permute-done.24 = bf16[2,256,2048]{2,1,0:T(8,128)(2,1)} collective-permute-done((bf16[2,256,2048]{2,1,0:T(8,128)(2,1)}, bf16[2,256,2048]{2,1,0:T(8,128)(2,1)}, u32[]{:S(2)}, u32[]{:S(2)}) %collective-permute-start.24) | collective-permute-done | bytes 2097184 | tf_op jit(solution)/shard_map/ppermute | solution.py:423
  395.2 19.5 %collective-permute-done.29 = bf16[256,2048]{1,0:T(8,128)(2,1)S(1)} collective-permute-done((bf16[256,2048]{1,0:T(8,128)(2,1)S(1)}, bf16[256,2048]{1,0:T(8,128)(2,1)S(1)}, u32[]{:S(2)}, u32[]{:S(2)}) %collective-permute-start.29) | collective-permute-done | bytes 1048608 | tf_op jit(solution)/shard_map/ppermute | solution.py:402
  425.4 13.7 %attend_backward.2.q_ref.refs_0_ = bf16[1024,768]{1,0:T(8,128)(2,1)} custom-call(bf16[1024,2048]{1,0:T(8,128)(2,1)} %bitcast.56.g_ref, bf16[2048,256]{1,0:T(8,128)(2,1)} %place_blocks.6.refs_3_.w_ref, bf16[1024,768]{1,0:T(8,128)(2,1)} %get-tuple-element.192.qkv_ref, f32[1024,2]{1,0:T(8,128)} %get-tuple-element.193.log_ref, ...), custom_call_target="tpu_custom_call" | custom-call | flops 2415919104 | bytes 12582912 | tf_op jit(solution)/shard_map/attend_backward/pallas_call | solution.py:259
  439.1 8.9 %weight_grads.2 = (bf16[4,256,1024]{2,1,0:T(8,128)(2,1)}, bf16[4,256,1024]{2,1,0:T(8,128)(2,1)}) custom-call(bf16[1024,2048]{1,0:T(8,128)(2,1)} %bitcast.198, bf16[1024,768]{1,0:T(8,128)(2,1)} %attend_backward.2.q_ref.refs_0_, bf16[1024,2048]{1,0:T(8,128)(2,1)} %bitcast.56.g_ref, bf16[1024,256]{1,0:T(8,128)(2,1)} %get-tuple-element.172.refs_2_.h_ref), custom_call_target="tpu_custom_call" | custom-call | flops 4294967296 | bytes 14680064 | tf_op jit(solution)/shard_map/weight_grads/pallas_call | solution.py:330
  458.6 13.2 %attend_backward.3.q_ref.refs_2_ = bf16[1024,768]{1,0:T(8,128)(2,1)} custom-call(bf16[1024,2048]{1,0:T(8,128)(2,1)} %bitcast.56.g_ref, bf16[2048,256]{1,0:T(8,128)(2,1)} %bitcast.195, bf16[1024,768]{1,0:T(8,128)(2,1)} %get-tuple-element.152.qkv_ref, f32[1024,2]{1,0:T(8,128)} %get-tuple-element.197.log_ref, f32[1024,128]{1,0:T(8,128)} %get-tuple-element.145.cos_ref, ...), custom_call_target="tpu_custom_call" | custom-call | flops 2415919104 | bytes 12582912 | tf_op jit(solution)/shard_map/attend_backward/pallas_call | solution.py:259
  478.5 9.0 %weight_grads.3 = (bf16[4,256,1024]{2,1,0:T(8,128)(2,1)}, bf16[4,256,1024]{2,1,0:T(8,128)(2,1)}) custom-call(bf16[1024,2048]{1,0:T(8,128)(2,1)} %bitcast.199, bf16[1024,768]{1,0:T(8,128)(2,1)} %attend_backward.3.q_ref.refs_2_, bf16[1024,2048]{1,0:T(8,128)(2,1)} %bitcast.56.g_ref, bf16[1024,256]{1,0:T(8,128)(2,1)} %get-tuple-element.170.refs_0_.h_ref), custom_call_target="tpu_custom_call" | custom-call | flops 4294967296 | bytes 14680064 | tf_op jit(solution)/shard_map/weight_grads/pallas_call | solution.py:330
  493.0 7.8 %share_of.6 = bf16[2,256,2048]{2,1,0:T(8,128)(2,1)} custom-call(s32[1]{0:T(128)} %bitcast.23.side_ref, bf16[1024,768]{1,0:T(8,128)(2,1)} %attend_backward.2.q_ref.refs_0_, bf16[2048,768]{1,0:T(8,128)(2,1)} %place_blocks.5.w_ref.refs_1_, bf16[1024,768]{1,0:T(8,128)(2,1)} %attend_backward.3.q_ref.refs_2_, bf16[2048,768]{1,0:T(8,128)(2,1)} %pad_maximum_fusion.w_ref.refs_3_), custom_call_target="tpu_custom_call" | custom-call | flops 3221225472 | bytes 12582912 | tf_op jit(solution)/shard_map/share_of/pallas_call | solution.py:283
  507.2 20.1 %collective-permute-done.41 = bf16[256,1024]{1,0:T(8,128)(2,1)S(1)} collective-permute-done((bf16[256,1024]{1,0:T(8,128)(2,1)S(1)}, bf16[256,1024]{1,0:T(8,128)(2,1)S(1)}, u32[]{:S(2)}, u32[]{:S(2)}) %collective-permute-start.41) | collective-permute-done | bytes 524320 | tf_op jit(solution)/shard_map/ppermute | solution.py:423
  536.9 8.9 %collective-permute-done.38.refs_2_ = bf16[256,2048]{1,0:T(8,128)(2,1)S(1)} collective-permute-done((bf16[256,2048]{1,0:T(8,128)(2,1)S(1)}, bf16[256,2048]{1,0:T(8,128)(2,1)S(1)}, u32[]{:S(2)}, u32[]{:S(2)}) %collective-permute-start.38) | collective-permute-done | bytes 1048608 | tf_op jit(solution)/shard_map/ppermute | solution.py:458
  555.8 7.8 %share_of.7 = bf16[2,256,2048]{2,1,0:T(8,128)(2,1)} custom-call(s32[1]{0:T(128)} %bitcast.4.side_ref, bf16[1024,768]{1,0:T(8,128)(2,1)} %attend_backward.2.q_ref.refs_0_, bf16[2048,768]{1,0:T(8,128)(2,1)} %place_blocks.5.w_ref.refs_1_, bf16[1024,768]{1,0:T(8,128)(2,1)} %attend_backward.3.q_ref.refs_2_, bf16[2048,768]{1,0:T(8,128)(2,1)} %pad_maximum_fusion.w_ref.refs_3_), custom_call_target="tpu_custom_call" | custom-call | flops 3221225472 | bytes 12582912 | tf_op jit(solution)/shard_map/share_of/pallas_call | solution.py:283
  574.5 11.7 %collective-permute-done.55.refs_3_ = bf16[256,2048]{1,0:T(8,128)(2,1)S(1)} collective-permute-done((bf16[256,2048]{1,0:T(8,128)(2,1)}, bf16[256,2048]{1,0:T(8,128)(2,1)S(1)}, u32[]{:S(2)}, u32[]{:S(2)}) %collective-permute-start.55) | collective-permute-done | bytes 1048608 | tf_op jit(solution)/shard_map/ppermute | solution.py:458
  (357 shorter events, 267.2 us)
Async XLA Ops:
  7.2 172.0 %all-gather.3.cloned.1.call-start = ((), (), s32[]{:S(2)}) async-start(), calls=%async_computation.2 | async-start | bytes 9437184 | tf_op jit(solution)/shard_map/all_gather | solution.py:539
  13.1 43.1 %collective-permute-start = (bf16[256,2048]{1,0:T(8,128)(2,1)S(1)}, bf16[256,2048]{1,0:T(8,128)(2,1)}, u32[]{:S(2)}, u32[]{:S(2)}) collective-permute-start(bf16[256,2048]{1,0:T(8,128)(2,1)S(1)} %fusion.11), channel_id=1, source_target_pairs={{0,2},{1,3},{2,0},{3,1},{4,6},{5,7},{6,4},{7,5},{8,10},{9,11},{10,... | collective-permute-start | bytes 3145736 | tf_op jit(solution)/shard_map/ppermute | solution.py:402
  16.1 32.1 %collective-permute-start.1 = (bf16[256,768]{1,0:T(8,128)(2,1)}, bf16[256,768]{1,0:T(8,128)(2,1)}, u32[]{:S(2)}, u32[]{:S(2)}) collective-permute-start(bf16[256,768]{1,0:T(8,128)(2,1)} %get-tuple-element.140), channel_id=1, source_target_pairs={{0,4},{1,5},{2,6},{3,7},{4,0},{5,1},{6,2},{7,3},{8,12},{9,13},{10,... | collective-permute-start | bytes 1179656 | tf_op jit(solution)/shard_map/ppermute | solution.py:526
  18.7 36.8 %collective-permute-start.2 = (bf16[256,768]{1,0:T(8,128)(2,1)}, bf16[256,768]{1,0:T(8,128)(2,1)}, u32[]{:S(2)}, u32[]{:S(2)}) collective-permute-start(bf16[256,768]{1,0:T(8,128)(2,1)} %get-tuple-element.141), channel_id=1, source_target_pairs={{0,4},{1,5},{2,6},{3,7},{4,0},{5,1},{6,2},{7,3},{8,12},{9,13},{10,... | collective-permute-start | bytes 1179656 | tf_op jit(solution)/shard_map/ppermute | solution.py:526
  56.2 212.2 %all-gather.5.cloned.1.call-start = ((), (), s32[]{:S(2)}) async-start(), calls=%async_computation.3 | async-start | bytes 9437184 | tf_op jit(solution)/shard_map/all_gather | solution.py:562
  81.2 25.8 %collective-permute-start.10 = (bf16[256,768]{1,0:T(8,128)(2,1)}, bf16[256,768]{1,0:T(8,128)(2,1)S(1)}, u32[]{:S(2)}, u32[]{:S(2)}) collective-permute-start(bf16[256,768]{1,0:T(8,128)(2,1)} %collective-permute-done.2.refs_4_), channel_id=1, source_target_pairs={{0,8},{8,0},{16,24},{24,16},{1,9},{9,1},{17,25},{25,17},{2,10},{10... | collective-permute-start | bytes 1179656 | tf_op jit(solution)/shard_map/ppermute | solution.py:402
  143.7 32.3 %collective-permute-start.16 = (bf16[256,2048]{1,0:T(8,128)(2,1)S(1)}, bf16[256,2048]{1,0:T(8,128)(2,1)S(1)}, u32[]{:S(2)}, u32[]{:S(2)}) collective-permute-start(bf16[256,2048]{1,0:T(8,128)(2,1)S(1)} %fusion.25), channel_id=1, source_target_pairs={{0,2},{1,3},{2,0},{3,1},{4,6},{5,7},{6,4},{7,5},{8,10},{9,11},{10,... | collective-permute-start | bytes 3145736 | tf_op jit(solution)/shard_map/ppermute | solution.py:423
  184.0 198.4 %reduce-scatter.3.cloned.1.call-start = ((), (), s32[]{:S(2)}) async-start(), calls=%async_computation.4 | async-start | bytes 9437184 | tf_op jit(solution)/shard_map/reduce_scatter | solution.py:571
  293.9 330.4 %reduce-scatter.5.cloned.1.call-start = ((), (), s32[]{:S(2)}) async-start(), calls=%async_computation.5 | async-start | bytes 9437184 | tf_op jit(solution)/shard_map/reduce_scatter | solution.py:593
  309.6 48.1 %collective-permute-start.25 = (bf16[2,512,1024]{2,1,0:T(8,128)(2,1)}, bf16[2,512,1024]{2,1,0:T(8,128)(2,1)}, u32[]{:S(2)}, u32[]{:S(2)}) collective-permute-start(bf16[2,512,1024]{2,1,0:T(8,128)(2,1)} %dynamic-slice_bitcast_fusion), channel_id=1, source_target_pairs={{0,16},{8,24},{16,0},{24,8},{1,17},{9,25},{17,1},{25,9},{2,18},{10... | collective-permute-start | bytes 6291464 | tf_op jit(solution)/shard_map/ppermute | solution.py:423
  326.6 48.3 %collective-permute-start.24 = (bf16[2,256,2048]{2,1,0:T(8,128)(2,1)}, bf16[2,256,2048]{2,1,0:T(8,128)(2,1)}, u32[]{:S(2)}, u32[]{:S(2)}) collective-permute-start(bf16[2,256,2048]{2,1,0:T(8,128)(2,1)} %dynamic-slice_bitcast_fusion.1), channel_id=1, source_target_pairs={{0,8},{8,0},{16,24},{24,16},{1,9},{9,1},{17,25},{25,17},{2,10},{10... | collective-permute-start | bytes 6291464 | tf_op jit(solution)/shard_map/ppermute | solution.py:423
  422.5 25.5 %collective-permute-start.35 = (bf16[512,1024]{1,0:T(8,128)(2,1)}, bf16[512,1024]{1,0:T(8,128)(2,1)S(1)}, u32[]{:S(2)}, u32[]{:S(2)}) collective-permute-start(bf16[512,1024]{1,0:T(8,128)(2,1)} %fusion.22.refs_0_), channel_id=1, source_target_pairs={{0,16},{8,24},{16,0},{24,8},{1,17},{9,25},{17,1},{25,9},{2,18},{10... | collective-permute-start | bytes 3145736 | tf_op jit(solution)/shard_map/ppermute | solution.py:402
  489.8 39.0 %collective-permute-start.53 = (bf16[2,256,1024]{2,1,0:T(8,128)(2,1)}, bf16[2,256,1024]{2,1,0:T(8,128)(2,1)}, u32[]{:S(2)}, u32[]{:S(2)}) collective-permute-start(bf16[2,256,1024]{2,1,0:T(8,128)(2,1)} %dynamic-slice_bitcast_fusion.2), channel_id=1, source_target_pairs={{0,16},{8,24},{16,0},{24,8},{1,17},{9,25},{17,1},{25,9},{2,18},{10... | collective-permute-start | bytes 3145736 | tf_op jit(solution)/shard_map/ppermute | solution.py:423
  500.9 63.2 %collective-permute-start.40 = (bf16[2,256,2048]{2,1,0:T(8,128)(2,1)}, bf16[2,256,2048]{2,1,0:T(8,128)(2,1)}, u32[]{:S(2)}, u32[]{:S(2)}) collective-permute-start(bf16[2,256,2048]{2,1,0:T(8,128)(2,1)} %share_of.6), channel_id=1, source_target_pairs={{0,1},{1,0},{2,3},{3,2},{4,5},{5,4},{6,7},{7,6},{8,9},{9,8},{10,11... | collective-permute-start | bytes 6291464 | tf_op jit(solution)/shard_map/ppermute | solution.py:500
  501.0 32.9 %collective-permute-start.51 = (bf16[2,256,1024]{2,1,0:T(8,128)(2,1)S(1)}, bf16[2,256,1024]{2,1,0:T(8,128)(2,1)S(1)}, u32[]{:S(2)}, u32[]{:S(2)}) collective-permute-start(bf16[2,256,1024]{2,1,0:T(8,128)(2,1)S(1)} %dynamic-slice_bitcast_fusion.3), channel_id=1, source_target_pairs={{0,8},{8,0},{16,24},{24,16},{1,9},{9,1},{17,25},{25,17},{2,10},{10... | collective-permute-start | bytes 3145736 | tf_op jit(solution)/shard_map/ppermute | solution.py:423
  504.7 41.1 %collective-permute-start.38 = (bf16[256,2048]{1,0:T(8,128)(2,1)S(1)}, bf16[256,2048]{1,0:T(8,128)(2,1)S(1)}, u32[]{:S(2)}, u32[]{:S(2)}) collective-permute-start(bf16[256,2048]{1,0:T(8,128)(2,1)S(1)} %copy-done.15), channel_id=1, source_target_pairs={{0,16},{8,24},{16,0},{24,8},{1,17},{9,25},{17,1},{25,9},{2,18},{10... | collective-permute-start | bytes 3145736 | tf_op jit(solution)/shard_map/ppermute | solution.py:458
  527.3 26.0 %collective-permute-start.39 = (bf16[512,1024]{1,0:T(8,128)(2,1)S(1)}, bf16[512,1024]{1,0:T(8,128)(2,1)S(1)}, u32[]{:S(2)}, u32[]{:S(2)}) collective-permute-start(bf16[512,1024]{1,0:T(8,128)(2,1)S(1)} %copy-done.16), channel_id=1, source_target_pairs={{0,8},{8,0},{16,24},{24,16},{1,9},{9,1},{17,25},{25,17},{2,10},{10... | collective-permute-start | bytes 3145736 | tf_op jit(solution)/shard_map/ppermute | solution.py:458
  528.8 34.8 %collective-permute-start.44 = (bf16[256,1024]{1,0:T(8,128)(2,1)}, bf16[256,1024]{1,0:T(8,128)(2,1)}, u32[]{:S(2)}, u32[]{:S(2)}) collective-permute-start(bf16[256,1024]{1,0:T(8,128)(2,1)} %fusion.29), channel_id=1, source_target_pairs={{0,4},{1,5},{2,6},{3,7},{4,0},{5,1},{6,2},{7,3},{8,12},{9,13},{10,... | collective-permute-start | bytes 1572872 | tf_op jit(solution)/shard_map/ppermute | solution.py:616
  534.0 37.6 %collective-permute-start.42 = (bf16[256,1024]{1,0:T(8,128)(2,1)S(1)}, bf16[256,1024]{1,0:T(8,128)(2,1)}, u32[]{:S(2)}, u32[]{:S(2)}) collective-permute-start(bf16[256,1024]{1,0:T(8,128)(2,1)S(1)} %fusion.30), channel_id=1, source_target_pairs={{0,4},{1,5},{2,6},{3,7},{4,0},{5,1},{6,2},{7,3},{8,12},{9,13},{10,... | collective-permute-start | bytes 1572872 | tf_op jit(solution)/shard_map/ppermute | solution.py:616
  545.8 26.2 %collective-permute-start.54 = (bf16[256,1024]{1,0:T(8,128)(2,1)}, bf16[256,1024]{1,0:T(8,128)(2,1)}, u32[]{:S(2)}, u32[]{:S(2)}) collective-permute-start(bf16[256,1024]{1,0:T(8,128)(2,1)} %fusion.40), channel_id=1, source_target_pairs={{0,8},{8,0},{16,24},{24,16},{1,9},{9,1},{17,25},{25,17},{2,10},{10... | collective-permute-start | bytes 1572872 | tf_op jit(solution)/shard_map/ppermute | solution.py:423
  602.9 30.7 %collective-permute-start.59 = (bf16[256,1024]{1,0:T(8,128)(2,1)}, bf16[256,1024]{1,0:T(8,128)(2,1)}, u32[]{:S(2)}, u32[]{:S(2)}) collective-permute-start(bf16[256,1024]{1,0:T(8,128)(2,1)} %add_convert_fusion.2.refs_0_), channel_id=1, source_target_pairs={{0,16},{8,24},{16,0},{24,8},{1,17},{9,25},{17,1},{25,9},{2,18},{10... | collective-permute-start | bytes 1572872 | tf_op jit(solution)/shard_map/ppermute | solution.py:402
  603.2 30.4 %collective-permute-start.60 = (bf16[256,1024]{1,0:T(8,128)(2,1)}, bf16[256,1024]{1,0:T(8,128)(2,1)}, u32[]{:S(2)}, u32[]{:S(2)}) collective-permute-start(bf16[256,1024]{1,0:T(8,128)(2,1)} %collective-permute-done.57.refs_1_), channel_id=1, source_target_pairs={{0,16},{8,24},{16,0},{24,8},{1,17},{9,25},{17,1},{25,9},{2,18},{10... | collective-permute-start | bytes 1572872 | tf_op jit(solution)/shard_map/ppermute | solution.py:402
  605.0 28.7 %collective-permute-start.61 = (bf16[256,1024]{1,0:T(8,128)(2,1)}, bf16[256,1024]{1,0:T(8,128)(2,1)}, u32[]{:S(2)}, u32[]{:S(2)}) collective-permute-start(bf16[256,1024]{1,0:T(8,128)(2,1)} %add_convert_fusion.1.refs_4_), channel_id=1, source_target_pairs={{0,8},{8,0},{16,24},{24,16},{1,9},{9,1},{17,25},{25,17},{2,10},{10... | collective-permute-start | bytes 1572872 | tf_op jit(solution)/shard_map/ppermute | solution.py:402
  605.3 28.4 %collective-permute-start.62 = (bf16[256,1024]{1,0:T(8,128)(2,1)}, bf16[256,1024]{1,0:T(8,128)(2,1)}, u32[]{:S(2)}, u32[]{:S(2)}) collective-permute-start(bf16[256,1024]{1,0:T(8,128)(2,1)} %collective-permute-done.58.refs_6_), channel_id=1, source_target_pairs={{0,8},{8,0},{16,24},{24,16},{1,9},{9,1},{17,25},{25,17},{2,10},{10... | collective-permute-start | bytes 1572872 | tf_op jit(solution)/shard_map/ppermute | solution.py:402
  (96 other events, 1277.9 us)
Sparse Core Ops, SparseCore 0:
  56.4 85.8 all-gather.2
  184.1 84.2 all-gather.4
  294.0 88.3 reduce-scatter.2
  422.6 89.3 reduce-scatter.4

commit v17 on v15

--- a/solution.py
+++ b/solution.py
@@ -575,19 +575,15 @@
         lanes = [x.reshape(columns, -1, x.shape[1]) for x in lanes]
         lanes = column_scatter(lanes, columns, column, cut=1)
         hidden_share = narrow(product(hidden, down_weight, (1, 0)))
-        blank = jnp.zeros((group, rows, dim), jnp.bfloat16)
-        normed_grad_two, hidden_share, blank, *lanes = lax.optimization_barrier(
-            (normed_grad_two, hidden_share, blank, *lanes)
-        )
+        normed_grad_two, hidden_share, *lanes = lax.optimization_barrier((normed_grad_two, hidden_share, *lanes))
         normed_grad_two = wide(normed_grad_two)
         lanes = [narrow(x) for x in column_scatter(lanes, columns, column, start=1)]
 
         router_part, _ = gate_backward(normed_two, hidden_router, state_two, gate_grad_two)
         middle_part, gain_two = norm_backward(normed_grad_two + router_part, scaled_two, inverse_two, hidden_gain)
         middle_grad = wide(out_grad) + middle_part
-        grads_one = place_sequence(
-            xor_gather(narrow(gate_one[:, None] * middle_grad), "mp", ranks, pair_bits + [1]), blank
-        )
+        held = xor_gather(narrow(gate_one[:, None] * middle_grad), "mp", ranks, pair_bits + [1])
+        grads_one, = place_blocks([held], place, [(1, dim, jnp.bfloat16, False)])
         helds = column_gather(lanes, columns, cut=1)
         grads_one, hidden_share, lanes = lax.optimization_barrier((grads_one, hidden_share, lanes))
         hidden_branch = wide(lax.psum_scatter(hidden_share, "mp", scatter_dimension=0, tiled=True))

time: 652 us -> 654 us (level)
    pallas_call x5 -> x6, Pallas kernels: 25 us -> 30 us  [place_blocks(): pl.pallas_call(functools.partial(place_kernel, count, [o[1] for o in outs...]
    convert_element_type x10 -> x11, other arithmetic: 14.1 us -> 16.4 us  [narrow(): return x.astype(jnp.bfloat16)]
    unnamed x108 -> x116, local copies, waits for them, and re-layouts: 12.9 us -> 14.7 us
  transfers between devices with their start and end apart: 67 -> 67, of which waited for: 26 -> 25; matrix products, arithmetic and copies ran while one was open for 21% -> 21% of each run, Pallas kernels for 18% -> 18%
where the time goes in v17:
time: 654 us; the launch traced here: 649 us
  waiting for transfers between devices  245 us (37%)
  Pallas kernels  149 us (23%)
  starting transfers between devices  73.6 us (11%)
  matrix products  64.8 us (10%)
  other arithmetic  60.2 us (9%)
  local copies, waits for them, and re-layouts  40.7 us (6%)
  between operations  15.2 us (2%)
    ppermute x14, waiting for transfers between devices, xor_scatter(): lax.ppermute(narrow(pick(blocks, 1 - side, at)), axis_name, swap_pairs(si...  81.9 us
    dot_general x4, matrix products, product(): lax.dot_general(a, b, ((dims[:1], dims[1:]), ((), ())), preferred_element...  51.1 us
    ppermute x30, waiting for transfers between devices, xor_gather(): held[far ^ bit] = lax.ppermute(held[far], axis, swap_pairs(size, bit))  48.1 us
    all_gather x1, waiting for transfers between devices, local(): inputs_two = lax.all_gather(narrow(normed_two), 'mp', axis=0, tiled=True)  46.6 us
    ppermute x30, starting transfers between devices, xor_gather(): held[far ^ bit] = lax.ppermute(held[far], axis, swap_pairs(size, bit))  32.7 us
    pallas_call x6, Pallas kernels, place_blocks(): pl.pallas_call(functools.partial(place_kernel, count, [o[1] for o in outs...  30 us
    pallas_call x2, Pallas kernels, attend_backward(): pl.pallas_call(backward_kernel, out_shape=jax.ShapeDtypeStruct((tokens, 3...  26.7 us
    ppermute x4, waiting for transfers between devices, gather_part(): held[far ^ bit] = lax.ppermute(held[far], 'dp', swap_pairs(size, bit))  26 us
  transfers between devices with their start and end apart: 67, of which 25 were waited for; matrix products, arithmetic and copies ran while one was open for 21% of the time, Pallas kernels for 18%

profile of v17, /device:TPU:0, one launch (start us, length us, event | category | flops | bytes accessed | tf_op | source)
XLA Modules:
  0.0 649.3 jit_solution(16151446438526361449)
XLA Ops:
  30.5 17.7 %collective-permute-done.1.refs_0_ = bf16[256,768]{1,0:T(8,128)(2,1)} collective-permute-done((bf16[256,768]{1,0:T(8,128)(2,1)}, bf16[256,768]{1,0:T(8,128)(2,1)}, u32[]{:S(2)}, u32[]{:S(2)}) %collective-permute-start.1) | collective-permute-done | bytes 393248 | tf_op jit(solution)/shard_map/ppermute | solution.py:526
  68.7 12.4 %attend_forward.2 = (bf16[1024,768]{1,0:T(8,128)(2,1)}, bf16[1024,256]{1,0:T(8,128)(2,1)}, f32[1024,2]{1,0:T(8,128)}) custom-call(bf16[1024,2048]{1,0:T(8,128)(2,1)} %bitcast.188, bf16[2048,768]{1,0:T(8,128)(2,1)} %pad_maximum_fusion.w_ref.refs_3_, f32[1024,128]{1,0:T(8,128)} %get-tuple-element.142.cos_ref, f32[1024,128]{1,0:T(8,128)} %get-tuple-element.143.sin_ref, ...), custom_call_target="tpu_custom_call" | custom-call | flops 3758096384 | bytes 12582912 | tf_op jit(solution)/shard_map/attend_forward/pallas_call | solution.py:237
  87.1 19.9 %collective-permute-done.12.refs_1_ = bf16[512,256]{1,0:T(8,128)(2,1)S(1)} collective-permute-done((bf16[512,256]{1,0:T(8,128)(2,1)S(1)}, bf16[512,256]{1,0:T(8,128)(2,1)S(1)}, u32[]{:S(2)}, u32[]{:S(2)}) %collective-permute-start.12) | collective-permute-done | bytes 262176 | tf_op jit(solution)/shard_map/ppermute | solution.py:402
  113.6 12.6 %attend_forward.3 = (bf16[1024,768]{1,0:T(8,128)(2,1)}, bf16[1024,256]{1,0:T(8,128)(2,1)}, f32[1024,2]{1,0:T(8,128)}) custom-call(bf16[1024,2048]{1,0:T(8,128)(2,1)} %bitcast.189, bf16[2048,768]{1,0:T(8,128)(2,1)} %place_blocks.6.w_ref.refs_1_, f32[1024,128]{1,0:T(8,128)} %get-tuple-element.142.cos_ref, f32[1024,128]{1,0:T(8,128)} %get-tuple-element.143.sin_ref, ...), custom_call_target="tpu_custom_call" | custom-call | flops 3758096384 | bytes 12582912 | tf_op jit(solution)/shard_map/attend_forward/pallas_call | solution.py:237
  143.7 8.5 %collective-permute-start.16 = (bf16[256,2048]{1,0:T(8,128)(2,1)S(1)}, bf16[256,2048]{1,0:T(8,128)(2,1)S(1)}, u32[]{:S(2)}, u32[]{:S(2)}) collective-permute-start(bf16[256,2048]{1,0:T(8,128)(2,1)S(1)} %fusion.25), channel_id=1, source_target_pairs={{0,2},{1,3},{2,0},{3,1},{4,6},{5,7},{6,4},{7,5},{8,10},{9,11},{10,... | collective-permute-start | bytes 3145736 | tf_op jit(solution)/shard_map/ppermute | solution.py:423
  155.0 21.0 %collective-permute-done.16 = bf16[256,2048]{1,0:T(8,128)(2,1)S(1)} collective-permute-done((bf16[256,2048]{1,0:T(8,128)(2,1)S(1)}, bf16[256,2048]{1,0:T(8,128)(2,1)S(1)}, u32[]{:S(2)}, u32[]{:S(2)}) %collective-permute-start.16) | collective-permute-done | bytes 1048608 | tf_op jit(solution)/shard_map/ppermute | solution.py:423
  195.6 14.7 %fusion.81.top_ref = f32[2048,1024]{1,0:T(8,128)} fusion(bf16[2048,2048]{1,0:T(8,128)(2,1)} %all-gather.3.cloned.1.call-done, bf16[1024,2048]{1,0:T(8,128)(2,1)} %param.22), kind=kOutput, calls=%fused_computation.188 | convolution fusion | flops 8589934592 | bytes 20971520 | tf_op jit(solution)/shard_map/dot_general | solution.py:94
  221.9 46.6 %all-gather.5.cloned.1.call-done.x_ref = bf16[2048,2048]{1,0:T(8,128)(2,1)} async-done(((bf16[256,2048]{1,0:T(8,128)(2,1)}), bf16[2048,2048]{1,0:T(8,128)(2,1)}) %all-gather.5.cloned.1.call-update) | async-done | bytes 8388624 | tf_op jit(solution)/shard_map/all_gather | solution.py:562
  268.5 25.4 %hidden_pass.1 = (bf16[2048,2048]{1,0:T(8,128)(2,1)}, bf16[2048,1024]{1,0:T(8,128)(2,1)}, bf16[2048,1024]{1,0:T(8,128)(2,1)}, f32[1,2048]{1,0:T(1,128)}) custom-call(s32[1]{0:T(128)} %bitcast.29.offset_ref, bf16[2048,2048]{1,0:T(8,128)(2,1)} %all-gather.5.cloned.1.call-done.x_ref, bf16[2048,1024]{1,0:T(8,128)(2,1)} %up_ref.1, f32[2048,1024]{1,0:T(8,128)} %fusion.81.top_ref, ...), custom_call_target="tpu_custom_call" | custom-call | flops 17179869184 | bytes 41943040 | tf_op jit(solution)/shard_map/hidden_pass/pallas_call | solution.py:305
  294.0 13.0 %convolution_convert_fusion.1 = bf16[2048,1024]{1,0:T(8,128)(2,1)S(1)} fusion(bf16[2048,2048]{1,0:T(8,128)(2,1)} %all-gather.5.cloned.1.call-done.x_ref, bf16[2048,1024]{1,0:T(8,128)(2,1)} %get-tuple-element.181), kind=kOutput, calls=%fused_computation.9 | convolution fusion | flops 8592031744 | bytes 16777216 | tf_op jit(solution)/shard_map/dot_general | solution.py:94
  311.1 12.3 %fusion.2 = bf16[1024,2048]{1,0:T(8,128)(2,1)S(1)} fusion(bf16[2048,1024]{1,0:T(8,128)(2,1)S(1)} %copy-done.56, bf16[2048,2048]{1,0:T(8,128)(2,1)} %all-gather.3.cloned.1.call-done, f32[2048]{0:T(1024)S(1)} %bitcast.210), kind=kOutput, calls=%fused_computation.8 | convolution fusion | flops 8604614656 | bytes 16785408 | tf_op jit(solution)/shard_map/dot_general | solution.py:94
  328.6 11.1 %convolution_convert_fusion = bf16[2048,2048]{1,0:T(8,128)(2,1)} fusion(bf16[2048,1024]{1,0:T(8,128)(2,1)S(1)} %copy-done.56, bf16[1024,2048]{1,0:T(8,128)(2,1)S(1)} %copy-done.55), kind=kOutput, calls=%fused_computation.3 | convolution fusion | flops 8594128896 | bytes 16777216 | tf_op jit(solution)/shard_map/dot_general | solution.py:94
  339.8 18.0 %collective-permute-done.25 = bf16[2,512,1024]{2,1,0:T(8,128)(2,1)} collective-permute-done((bf16[2,512,1024]{2,1,0:T(8,128)(2,1)}, bf16[2,512,1024]{2,1,0:T(8,128)(2,1)}, u32[]{:S(2)}, u32[]{:S(2)}) %collective-permute-start.25) | collective-permute-done | bytes 2097184 | tf_op jit(solution)/shard_map/ppermute | solution.py:423
  362.8 12.1 %collective-permute-done.24 = bf16[2,256,2048]{2,1,0:T(8,128)(2,1)} collective-permute-done((bf16[2,256,2048]{2,1,0:T(8,128)(2,1)}, bf16[2,256,2048]{2,1,0:T(8,128)(2,1)}, u32[]{:S(2)}, u32[]{:S(2)}) %collective-permute-start.24) | collective-permute-done | bytes 2097184 | tf_op jit(solution)/shard_map/ppermute | solution.py:423
  392.9 19.2 %collective-permute-done.30.refs_2_ = bf16[256,2048]{1,0:T(8,128)(2,1)S(1)} collective-permute-done((bf16[256,2048]{1,0:T(8,128)(2,1)S(1)}, bf16[256,2048]{1,0:T(8,128)(2,1)S(1)}, u32[]{:S(2)}, u32[]{:S(2)}) %collective-permute-start.30) | collective-permute-done | bytes 1048608 | tf_op jit(solution)/shard_map/ppermute | solution.py:402
  425.9 13.6 %attend_backward.2.q_ref.refs_0_ = bf16[1024,768]{1,0:T(8,128)(2,1)} custom-call(bf16[1024,2048]{1,0:T(8,128)(2,1)} %place_blocks.8.g_ref, bf16[2048,256]{1,0:T(8,128)(2,1)} %place_blocks.7.refs_3_.w_ref, bf16[1024,768]{1,0:T(8,128)(2,1)} %get-tuple-element.189.qkv_ref, f32[1024,2]{1,0:T(8,128)} %get-tuple-element.190.log_ref, ...), custom_call_target="tpu_custom_call" | custom-call | flops 2415919104 | bytes 12582912 | tf_op jit(solution)/shard_map/attend_backward/pallas_call | solution.py:259
  439.4 9.0 %weight_grads.2 = (bf16[4,256,1024]{2,1,0:T(8,128)(2,1)}, bf16[4,256,1024]{2,1,0:T(8,128)(2,1)}) custom-call(bf16[1024,2048]{1,0:T(8,128)(2,1)} %bitcast.190, bf16[1024,768]{1,0:T(8,128)(2,1)} %attend_backward.2.q_ref.refs_0_, bf16[1024,2048]{1,0:T(8,128)(2,1)} %place_blocks.8.g_ref, bf16[1024,256]{1,0:T(8,128)(2,1)} %get-tuple-element.169.refs_2_.h_ref), custom_call_target="tpu_custom_call" | custom-call | flops 4294967296 | bytes 14680064 | tf_op jit(solution)/shard_map/weight_grads/pallas_call | solution.py:330
  459.0 13.1 %attend_backward.3.q_ref.refs_2_ = bf16[1024,768]{1,0:T(8,128)(2,1)} custom-call(bf16[1024,2048]{1,0:T(8,128)(2,1)} %place_blocks.8.g_ref, bf16[2048,256]{1,0:T(8,128)(2,1)} %bitcast.187, bf16[1024,768]{1,0:T(8,128)(2,1)} %get-tuple-element.149.qkv_ref, f32[1024,2]{1,0:T(8,128)} %get-tuple-element.194.log_ref, f32[1024,128]{1,0:T(8,128)} %get-tuple-element.142.cos_ref, ...), custom_call_target="tpu_custom_call" | custom-call | flops 2415919104 | bytes 12582912 | tf_op jit(solution)/shard_map/attend_backward/pallas_call | solution.py:259
  479.0 9.0 %weight_grads.3 = (bf16[4,256,1024]{2,1,0:T(8,128)(2,1)}, bf16[4,256,1024]{2,1,0:T(8,128)(2,1)}) custom-call(bf16[1024,2048]{1,0:T(8,128)(2,1)} %bitcast.191, bf16[1024,768]{1,0:T(8,128)(2,1)} %attend_backward.3.q_ref.refs_2_, bf16[1024,2048]{1,0:T(8,128)(2,1)} %place_blocks.8.g_ref, bf16[1024,256]{1,0:T(8,128)(2,1)} %get-tuple-element.167.refs_0_.h_ref), custom_call_target="tpu_custom_call" | custom-call | flops 4294967296 | bytes 14680064 | tf_op jit(solution)/shard_map/weight_grads/pallas_call | solution.py:330
  493.5 7.8 %share_of.6 = bf16[2,256,2048]{2,1,0:T(8,128)(2,1)} custom-call(s32[1]{0:T(128)} %bitcast.22.side_ref, bf16[1024,768]{1,0:T(8,128)(2,1)} %attend_backward.2.q_ref.refs_0_, bf16[2048,768]{1,0:T(8,128)(2,1)} %place_blocks.6.w_ref.refs_1_, bf16[1024,768]{1,0:T(8,128)(2,1)} %attend_backward.3.q_ref.refs_2_, bf16[2048,768]{1,0:T(8,128)(2,1)} %pad_maximum_fusion.w_ref.refs_3_), custom_call_target="tpu_custom_call" | custom-call | flops 3221225472 | bytes 12582912 | tf_op jit(solution)/shard_map/share_of/pallas_call | solution.py:283
  507.7 20.2 %collective-permute-done.41 = bf16[256,1024]{1,0:T(8,128)(2,1)S(1)} collective-permute-done((bf16[256,1024]{1,0:T(8,128)(2,1)S(1)}, bf16[256,1024]{1,0:T(8,128)(2,1)S(1)}, u32[]{:S(2)}, u32[]{:S(2)}) %collective-permute-start.41) | collective-permute-done | bytes 524320 | tf_op jit(solution)/shard_map/ppermute | solution.py:423
  538.0 8.5 %collective-permute-done.38.refs_2_ = bf16[256,2048]{1,0:T(8,128)(2,1)S(1)} collective-permute-done((bf16[256,2048]{1,0:T(8,128)(2,1)S(1)}, bf16[256,2048]{1,0:T(8,128)(2,1)S(1)}, u32[]{:S(2)}, u32[]{:S(2)}) %collective-permute-start.38) | collective-permute-done | bytes 1048608 | tf_op jit(solution)/shard_map/ppermute | solution.py:458
  556.2 7.8 %share_of.7 = bf16[2,256,2048]{2,1,0:T(8,128)(2,1)} custom-call(s32[1]{0:T(128)} %bitcast.3.side_ref, bf16[1024,768]{1,0:T(8,128)(2,1)} %attend_backward.2.q_ref.refs_0_, bf16[2048,768]{1,0:T(8,128)(2,1)} %place_blocks.6.w_ref.refs_1_, bf16[1024,768]{1,0:T(8,128)(2,1)} %attend_backward.3.q_ref.refs_2_, bf16[2048,768]{1,0:T(8,128)(2,1)} %pad_maximum_fusion.w_ref.refs_3_), custom_call_target="tpu_custom_call" | custom-call | flops 3221225472 | bytes 12582912 | tf_op jit(solution)/shard_map/share_of/pallas_call | solution.py:283
  575.6 11.4 %collective-permute-done.55.refs_3_ = bf16[256,2048]{1,0:T(8,128)(2,1)S(1)} collective-permute-done((bf16[256,2048]{1,0:T(8,128)(2,1)}, bf16[256,2048]{1,0:T(8,128)(2,1)S(1)}, u32[]{:S(2)}, u32[]{:S(2)}) %collective-permute-start.55) | collective-permute-done | bytes 1048608 | tf_op jit(solution)/shard_map/ppermute | solution.py:458
  (362 shorter events, 269.2 us)
Async XLA Ops:
  7.2 172.0 %all-gather.3.cloned.1.call-start = ((), (), s32[]{:S(2)}) async-start(), calls=%async_computation.2 | async-start | bytes 9437184 | tf_op jit(solution)/shard_map/all_gather | solution.py:539
  13.1 43.1 %collective-permute-start = (bf16[256,2048]{1,0:T(8,128)(2,1)S(1)}, bf16[256,2048]{1,0:T(8,128)(2,1)}, u32[]{:S(2)}, u32[]{:S(2)}) collective-permute-start(bf16[256,2048]{1,0:T(8,128)(2,1)S(1)} %fusion.11), channel_id=1, source_target_pairs={{0,2},{1,3},{2,0},{3,1},{4,6},{5,7},{6,4},{7,5},{8,10},{9,11},{10,... | collective-permute-start | bytes 3145736 | tf_op jit(solution)/shard_map/ppermute | solution.py:402
  16.1 32.1 %collective-permute-start.1 = (bf16[256,768]{1,0:T(8,128)(2,1)}, bf16[256,768]{1,0:T(8,128)(2,1)}, u32[]{:S(2)}, u32[]{:S(2)}) collective-permute-start(bf16[256,768]{1,0:T(8,128)(2,1)} %get-tuple-element.137), channel_id=1, source_target_pairs={{0,4},{1,5},{2,6},{3,7},{4,0},{5,1},{6,2},{7,3},{8,12},{9,13},{10,... | collective-permute-start | bytes 1179656 | tf_op jit(solution)/shard_map/ppermute | solution.py:526
  18.7 36.8 %collective-permute-start.2 = (bf16[256,768]{1,0:T(8,128)(2,1)}, bf16[256,768]{1,0:T(8,128)(2,1)}, u32[]{:S(2)}, u32[]{:S(2)}) collective-permute-start(bf16[256,768]{1,0:T(8,128)(2,1)} %get-tuple-element.138), channel_id=1, source_target_pairs={{0,4},{1,5},{2,6},{3,7},{4,0},{5,1},{6,2},{7,3},{8,12},{9,13},{10,... | collective-permute-start | bytes 1179656 | tf_op jit(solution)/shard_map/ppermute | solution.py:526
  56.2 212.3 %all-gather.5.cloned.1.call-start = ((), (), s32[]{:S(2)}) async-start(), calls=%async_computation.3 | async-start | bytes 9437184 | tf_op jit(solution)/shard_map/all_gather | solution.py:562
  81.2 25.8 %collective-permute-start.10 = (bf16[256,768]{1,0:T(8,128)(2,1)}, bf16[256,768]{1,0:T(8,128)(2,1)S(1)}, u32[]{:S(2)}, u32[]{:S(2)}) collective-permute-start(bf16[256,768]{1,0:T(8,128)(2,1)} %collective-permute-done.2.refs_4_), channel_id=1, source_target_pairs={{0,8},{8,0},{16,24},{24,16},{1,9},{9,1},{17,25},{25,17},{2,10},{10... | collective-permute-start | bytes 1179656 | tf_op jit(solution)/shard_map/ppermute | solution.py:402
  143.7 32.3 %collective-permute-start.16 = (bf16[256,2048]{1,0:T(8,128)(2,1)S(1)}, bf16[256,2048]{1,0:T(8,128)(2,1)S(1)}, u32[]{:S(2)}, u32[]{:S(2)}) collective-permute-start(bf16[256,2048]{1,0:T(8,128)(2,1)S(1)} %fusion.25), channel_id=1, source_target_pairs={{0,2},{1,3},{2,0},{3,1},{4,6},{5,7},{6,4},{7,5},{8,10},{9,11},{10,... | collective-permute-start | bytes 3145736 | tf_op jit(solution)/shard_map/ppermute | solution.py:423
  184.0 198.4 %reduce-scatter.3.cloned.1.call-start = ((), (), s32[]{:S(2)}) async-start(), calls=%async_computation.4 | async-start | bytes 9437184 | tf_op jit(solution)/shard_map/reduce_scatter | solution.py:571
  293.9 346.1 %reduce-scatter.5.cloned.1.call-start = ((), (), s32[]{:S(2)}) async-start(), calls=%async_computation.5 | async-start | bytes 9437184 | tf_op jit(solution)/shard_map/reduce_scatter | solution.py:589
  309.7 48.1 %collective-permute-start.25 = (bf16[2,512,1024]{2,1,0:T(8,128)(2,1)}, bf16[2,512,1024]{2,1,0:T(8,128)(2,1)}, u32[]{:S(2)}, u32[]{:S(2)}) collective-permute-start(bf16[2,512,1024]{2,1,0:T(8,128)(2,1)} %dynamic-slice_bitcast_fusion), channel_id=1, source_target_pairs={{0,16},{8,24},{16,0},{24,8},{1,17},{9,25},{17,1},{25,9},{2,18},{10... | collective-permute-start | bytes 6291464 | tf_op jit(solution)/shard_map/ppermute | solution.py:423
  326.6 48.3 %collective-permute-start.24 = (bf16[2,256,2048]{2,1,0:T(8,128)(2,1)}, bf16[2,256,2048]{2,1,0:T(8,128)(2,1)}, u32[]{:S(2)}, u32[]{:S(2)}) collective-permute-start(bf16[2,256,2048]{2,1,0:T(8,128)(2,1)} %dynamic-slice_bitcast_fusion.1), channel_id=1, source_target_pairs={{0,8},{8,0},{16,24},{24,16},{1,9},{9,1},{17,25},{25,17},{2,10},{10... | collective-permute-start | bytes 6291464 | tf_op jit(solution)/shard_map/ppermute | solution.py:423
  422.9 25.5 %collective-permute-start.35 = (bf16[512,1024]{1,0:T(8,128)(2,1)}, bf16[512,1024]{1,0:T(8,128)(2,1)S(1)}, u32[]{:S(2)}, u32[]{:S(2)}) collective-permute-start(bf16[512,1024]{1,0:T(8,128)(2,1)} %fusion.22.refs_0_), channel_id=1, source_target_pairs={{0,16},{8,24},{16,0},{24,8},{1,17},{9,25},{17,1},{25,9},{2,18},{10... | collective-permute-start | bytes 3145736 | tf_op jit(solution)/shard_map/ppermute | solution.py:402
  490.3 39.0 %collective-permute-start.53 = (bf16[2,256,1024]{2,1,0:T(8,128)(2,1)}, bf16[2,256,1024]{2,1,0:T(8,128)(2,1)}, u32[]{:S(2)}, u32[]{:S(2)}) collective-permute-start(bf16[2,256,1024]{2,1,0:T(8,128)(2,1)} %dynamic-slice_bitcast_fusion.2), channel_id=1, source_target_pairs={{0,16},{8,24},{16,0},{24,8},{1,17},{9,25},{17,1},{25,9},{2,18},{10... | collective-permute-start | bytes 3145736 | tf_op jit(solution)/shard_map/ppermute | solution.py:423
  501.4 63.0 %collective-permute-start.40 = (bf16[2,256,2048]{2,1,0:T(8,128)(2,1)}, bf16[2,256,2048]{2,1,0:T(8,128)(2,1)}, u32[]{:S(2)}, u32[]{:S(2)}) collective-permute-start(bf16[2,256,2048]{2,1,0:T(8,128)(2,1)} %share_of.6), channel_id=1, source_target_pairs={{0,1},{1,0},{2,3},{3,2},{4,5},{5,4},{6,7},{7,6},{8,9},{9,8},{10,11... | collective-permute-start | bytes 6291464 | tf_op jit(solution)/shard_map/ppermute | solution.py:500
  501.5 33.5 %collective-permute-start.51 = (bf16[2,256,1024]{2,1,0:T(8,128)(2,1)S(1)}, bf16[2,256,1024]{2,1,0:T(8,128)(2,1)S(1)}, u32[]{:S(2)}, u32[]{:S(2)}) collective-permute-start(bf16[2,256,1024]{2,1,0:T(8,128)(2,1)S(1)} %dynamic-slice_bitcast_fusion.3), channel_id=1, source_target_pairs={{0,8},{8,0},{16,24},{24,16},{1,9},{9,1},{17,25},{25,17},{2,10},{10... | collective-permute-start | bytes 3145736 | tf_op jit(solution)/shard_map/ppermute | solution.py:423
  505.2 41.2 %collective-permute-start.38 = (bf16[256,2048]{1,0:T(8,128)(2,1)S(1)}, bf16[256,2048]{1,0:T(8,128)(2,1)S(1)}, u32[]{:S(2)}, u32[]{:S(2)}) collective-permute-start(bf16[256,2048]{1,0:T(8,128)(2,1)S(1)} %copy-done.15), channel_id=1, source_target_pairs={{0,16},{8,24},{16,0},{24,8},{1,17},{9,25},{17,1},{25,9},{2,18},{10... | collective-permute-start | bytes 3145736 | tf_op jit(solution)/shard_map/ppermute | solution.py:458
  527.8 25.7 %collective-permute-start.39 = (bf16[512,1024]{1,0:T(8,128)(2,1)S(1)}, bf16[512,1024]{1,0:T(8,128)(2,1)S(1)}, u32[]{:S(2)}, u32[]{:S(2)}) collective-permute-start(bf16[512,1024]{1,0:T(8,128)(2,1)S(1)} %copy-done.14), channel_id=1, source_target_pairs={{0,8},{8,0},{16,24},{24,16},{1,9},{9,1},{17,25},{25,17},{2,10},{10... | collective-permute-start | bytes 3145736 | tf_op jit(solution)/shard_map/ppermute | solution.py:458
  529.3 34.7 %collective-permute-start.44 = (bf16[256,1024]{1,0:T(8,128)(2,1)}, bf16[256,1024]{1,0:T(8,128)(2,1)}, u32[]{:S(2)}, u32[]{:S(2)}) collective-permute-start(bf16[256,1024]{1,0:T(8,128)(2,1)} %fusion.29), channel_id=1, source_target_pairs={{0,4},{1,5},{2,6},{3,7},{4,0},{5,1},{6,2},{7,3},{8,12},{9,13},{10,... | collective-permute-start | bytes 1572872 | tf_op jit(solution)/shard_map/ppermute | solution.py:612
  535.0 38.0 %collective-permute-start.42 = (bf16[256,1024]{1,0:T(8,128)(2,1)S(1)}, bf16[256,1024]{1,0:T(8,128)(2,1)}, u32[]{:S(2)}, u32[]{:S(2)}) collective-permute-start(bf16[256,1024]{1,0:T(8,128)(2,1)S(1)} %fusion.30), channel_id=1, source_target_pairs={{0,4},{1,5},{2,6},{3,7},{4,0},{5,1},{6,2},{7,3},{8,12},{9,13},{10,... | collective-permute-start | bytes 1572872 | tf_op jit(solution)/shard_map/ppermute | solution.py:612
  546.5 26.7 %collective-permute-start.54 = (bf16[256,1024]{1,0:T(8,128)(2,1)}, bf16[256,1024]{1,0:T(8,128)(2,1)}, u32[]{:S(2)}, u32[]{:S(2)}) collective-permute-start(bf16[256,1024]{1,0:T(8,128)(2,1)} %fusion.40), channel_id=1, source_target_pairs={{0,8},{8,0},{16,24},{24,16},{1,9},{9,1},{17,25},{25,17},{2,10},{10... | collective-permute-start | bytes 1572872 | tf_op jit(solution)/shard_map/ppermute | solution.py:423
  603.1 29.1 %collective-permute-start.59 = (bf16[256,1024]{1,0:T(8,128)(2,1)}, bf16[256,1024]{1,0:T(8,128)(2,1)}, u32[]{:S(2)}, u32[]{:S(2)}) collective-permute-start(bf16[256,1024]{1,0:T(8,128)(2,1)} %add_convert_fusion.2.refs_0_), channel_id=1, source_target_pairs={{0,16},{8,24},{16,0},{24,8},{1,17},{9,25},{17,1},{25,9},{2,18},{10... | collective-permute-start | bytes 1572872 | tf_op jit(solution)/shard_map/ppermute | solution.py:402
  603.5 28.7 %collective-permute-start.60 = (bf16[256,1024]{1,0:T(8,128)(2,1)}, bf16[256,1024]{1,0:T(8,128)(2,1)}, u32[]{:S(2)}, u32[]{:S(2)}) collective-permute-start(bf16[256,1024]{1,0:T(8,128)(2,1)} %collective-permute-done.57.refs_1_), channel_id=1, source_target_pairs={{0,16},{8,24},{16,0},{24,8},{1,17},{9,25},{17,1},{25,9},{2,18},{10... | collective-permute-start | bytes 1572872 | tf_op jit(solution)/shard_map/ppermute | solution.py:402
  605.1 27.1 %collective-permute-start.61 = (bf16[256,1024]{1,0:T(8,128)(2,1)S(1)}, bf16[256,1024]{1,0:T(8,128)(2,1)}, u32[]{:S(2)}, u32[]{:S(2)}) collective-permute-start(bf16[256,1024]{1,0:T(8,128)(2,1)S(1)} %add_convert_fusion.1.refs_4_), channel_id=1, source_target_pairs={{0,8},{8,0},{16,24},{24,16},{1,9},{9,1},{17,25},{25,17},{2,10},{10... | collective-permute-start | bytes 1572872 | tf_op jit(solution)/shard_map/ppermute | solution.py:402
  605.4 26.8 %collective-permute-start.62 = (bf16[256,1024]{1,0:T(8,128)(2,1)}, bf16[256,1024]{1,0:T(8,128)(2,1)}, u32[]{:S(2)}, u32[]{:S(2)}) collective-permute-start(bf16[256,1024]{1,0:T(8,128)(2,1)} %collective-permute-done.58.refs_6_), channel_id=1, source_target_pairs={{0,8},{8,0},{16,24},{24,16},{1,9},{9,1},{17,25},{25,17},{2,10},{10... | collective-permute-start | bytes 1572872 | tf_op jit(solution)/shard_map/ppermute | solution.py:402
  (100 other events, 1305.1 us)
Sparse Core Ops, SparseCore 0:
  56.4 85.8 all-gather.2
  184.2 84.2 all-gather.4
  294.0 88.3 reduce-scatter.2
  423.0 89.4 reduce-scatter.4

commit v18 on v14

--- a/solution.py
+++ b/solution.py
@@ -614,17 +614,17 @@
                 gate_grad_one = jnp.sum(middle_late * mixer_branch, axis=1)
         helds, sent = lax.optimization_barrier((helds, sent))
         sent = [[narrow(x) for x in column_scatter(lanes, columns, column, start=1)] for lanes in sent]
+        pairs, part, sent = lax.optimization_barrier((pairs, part, sent))
         there = [
             [lax.ppermute(x, "mp", shift_pairs(ranks, -k * group)) for x in lanes]
             for k, lanes in zip(range(1, sequences)[::-1], sent)
         ]
-        pairs, part = lax.optimization_barrier((pairs, part))
-        blocks, helds = core_sum(pairs, gather_part(helds, columns, 0))
-        blocks, there = lax.optimization_barrier((blocks, there))
+        pieces = column_scatter(part, columns, column, cut=1)
+        pieces, there = lax.optimization_barrier((pieces, there))
+        pieces = column_scatter(pieces, columns, column, start=1)
+        blocks, (helds, pieces) = core_sum(pairs, (gather_part(helds, columns, 0), pieces))
         normed_grad_one = chip_sum(blocks)
         helds = gather_part(helds, columns, 1)
-        pieces = column_scatter(part, columns, column)
-        pieces, helds = lax.optimization_barrier((pieces, helds))
         for lanes in there:
             pieces = [p + wide(t) for p, t in zip(pieces, lanes)]
         spread = column_gather([narrow(p) for p in pieces], columns, cut=1)

time: 654 us -> 682 us (1.043)
  waiting for transfers between devices: 245 us -> 263 us
  other arithmetic: 60.6 us -> 68.2 us
    ppermute x2, waiting for transfers between devices: 3.49 us -> 30.3 us  [local(): lax.ppermute(x, 'mp', shift_pairs(ranks, -k * group))]
    ppermute x4, waiting for transfers between devices: 26.7 us -> 0.01 us  [gather_part(): held[far ^ bit] = lax.ppermute(held[far], 'dp', swap_pairs(size, bit))]
    ppermute x33, waiting for transfers between devices: 50.4 us -> 61 us  [xor_gather(): held[far ^ bit] = lax.ppermute(held[far], axis, swap_pairs(size, bit))]
    ppermute x14, waiting for transfers between devices: 77.5 us -> 87.1 us  [xor_scatter(): lax.ppermute(narrow(pick(blocks, 1 - side, at)), axis_name, swap_pairs(si...]
    unnamed x116 -> x114, local copies, waits for them, and re-layouts: 13.4 us -> 14.1 us
  transfers between devices with their start and end apart: 71 -> 71, of which waited for: 29 -> 27; matrix products, arithmetic and copies ran while one was open for 21% -> 21% of each run, Pallas kernels for 18% -> 18%
where the time goes in v18:
time: 682 us; the launch traced here: 677 us
  waiting for transfers between devices  263 us (39%)
  Pallas kernels  145 us (21%)
  starting transfers between devices  78.8 us (12%)
  other arithmetic  68.2 us (10%)
  matrix products  64 us (9%)
  local copies, waits for them, and re-layouts  43 us (6%)
  between operations  15.2 us (2%)
    ppermute x14, waiting for transfers between devices, xor_scatter(): lax.ppermute(narrow(pick(blocks, 1 - side, at)), axis_name, swap_pairs(si...  87.1 us
    ppermute x33, waiting for transfers between devices, xor_gather(): held[far ^ bit] = lax.ppermute(held[far], axis, swap_pairs(size, bit))  61 us
    dot_general x4, matrix products, product(): lax.dot_general(a, b, ((dims[:1], dims[1:]), ((), ())), preferred_element...  51.2 us
    all_gather x1, waiting for transfers between devices, local(): inputs_two = lax.all_gather(narrow(normed_two), 'mp', axis=0, tiled=True)  46.6 us
    ppermute x33, starting transfers between devices, xor_gather(): held[far ^ bit] = lax.ppermute(held[far], axis, swap_pairs(size, bit))  37.3 us
    ppermute x2, waiting for transfers between devices, local(): lax.ppermute(x, 'mp', shift_pairs(ranks, -k * group))  30.3 us
    pallas_call x2, Pallas kernels, attend_backward(): pl.pallas_call(backward_kernel, out_shape=jax.ShapeDtypeStruct((tokens, 3...  27 us
    ppermute x4, waiting for transfers between devices, local(): lax.ppermute(x, 'mp', shift_pairs(ranks, k * group))  26.8 us
  transfers between devices with their start and end apart: 71, of which 27 were waited for; matrix products, arithmetic and copies ran while one was open for 21% of the time, Pallas kernels for 18%

profile of v18, /device:TPU:0, one launch (start us, length us, event | category | flops | bytes accessed | tf_op | source)
XLA Modules:
  0.0 677.4 jit_solution(17329232474377795251)
XLA Ops:
  28.5 19.5 %collective-permute-done.1.refs_0_ = bf16[256,768]{1,0:T(8,128)(2,1)} collective-permute-done((bf16[256,768]{1,0:T(8,128)(2,1)}, bf16[256,768]{1,0:T(8,128)(2,1)}, u32[]{:S(2)}, u32[]{:S(2)}) %collective-permute-start.1) | collective-permute-done | bytes 393248 | tf_op jit(solution)/shard_map/ppermute | solution.py:529
  66.8 12.8 %attend_forward.2 = (bf16[1024,768]{1,0:T(8,128)(2,1)}, bf16[1024,256]{1,0:T(8,128)(2,1)}, f32[1024,2]{1,0:T(8,128)}) custom-call(bf16[1024,2048]{1,0:T(8,128)(2,1)} %bitcast.198, bf16[2048,768]{1,0:T(8,128)(2,1)} %pad_maximum_fusion.w_ref.refs_3_, f32[1024,128]{1,0:T(8,128)} %get-tuple-element.143.cos_ref, f32[1024,128]{1,0:T(8,128)} %get-tuple-element.144.sin_ref, ...), custom_call_target="tpu_custom_call" | custom-call | flops 3758096384 | bytes 12582912 | tf_op jit(solution)/shard_map/attend_forward/pallas_call | solution.py:237
  85.5 17.6 %collective-permute-done.13.refs_1_ = bf16[256,256]{1,0:T(8,128)(2,1)S(1)} collective-permute-done((bf16[256,256]{1,0:T(8,128)(2,1)S(1)}, bf16[256,256]{1,0:T(8,128)(2,1)S(1)}, u32[]{:S(2)}, u32[]{:S(2)}) %collective-permute-start.13) | collective-permute-done | bytes 131104 | tf_op jit(solution)/shard_map/ppermute | solution.py:402
  116.6 12.4 %attend_forward.3 = (bf16[1024,768]{1,0:T(8,128)(2,1)}, bf16[1024,256]{1,0:T(8,128)(2,1)}, f32[1024,2]{1,0:T(8,128)}) custom-call(bf16[1024,2048]{1,0:T(8,128)(2,1)} %bitcast.199, bf16[2048,768]{1,0:T(8,128)(2,1)} %place_blocks.5.w_ref.refs_1_, f32[1024,128]{1,0:T(8,128)} %get-tuple-element.143.cos_ref, f32[1024,128]{1,0:T(8,128)} %get-tuple-element.144.sin_ref, ...), custom_call_target="tpu_custom_call" | custom-call | flops 3758096384 | bytes 12582912 | tf_op jit(solution)/shard_map/attend_forward/pallas_call | solution.py:237
  156.4 21.0 %collective-permute-done.20 = bf16[256,2048]{1,0:T(8,128)(2,1)S(1)} collective-permute-done((bf16[256,2048]{1,0:T(8,128)(2,1)S(1)}, bf16[256,2048]{1,0:T(8,128)(2,1)S(1)}, u32[]{:S(2)}, u32[]{:S(2)}) %collective-permute-start.20) | collective-permute-done | bytes 1048608 | tf_op jit(solution)/shard_map/ppermute | solution.py:423
  198.7 14.6 %fusion.81.top_ref = f32[2048,1024]{1,0:T(8,128)} fusion(bf16[2048,2048]{1,0:T(8,128)(2,1)} %all-gather.3.cloned.1.call-done, bf16[1024,2048]{1,0:T(8,128)(2,1)} %param.22), kind=kOutput, calls=%fused_computation.192 | convolution fusion | flops 8589934592 | bytes 20971520 | tf_op jit(solution)/shard_map/dot_general | solution.py:94
  224.4 46.6 %all-gather.5.cloned.1.call-done.x_ref = bf16[2048,2048]{1,0:T(8,128)(2,1)} async-done(((bf16[256,2048]{1,0:T(8,128)(2,1)}), bf16[2048,2048]{1,0:T(8,128)(2,1)}) %all-gather.5.cloned.1.call-update) | async-done | bytes 8388624 | tf_op jit(solution)/shard_map/all_gather | solution.py:565
  271.0 25.4 %hidden_pass.1 = (bf16[2048,2048]{1,0:T(8,128)(2,1)}, bf16[2048,1024]{1,0:T(8,128)(2,1)}, bf16[2048,1024]{1,0:T(8,128)(2,1)}, f32[1,2048]{1,0:T(1,128)}) custom-call(s32[1]{0:T(128)} %bitcast.29.offset_ref, bf16[2048,2048]{1,0:T(8,128)(2,1)} %all-gather.5.cloned.1.call-done.x_ref, bf16[2048,1024]{1,0:T(8,128)(2,1)} %up_ref.1, f32[2048,1024]{1,0:T(8,128)} %fusion.81.top_ref, ...), custom_call_target="tpu_custom_call" | custom-call | flops 17179869184 | bytes 41943040 | tf_op jit(solution)/shard_map/hidden_pass/pallas_call | solution.py:305
  296.5 13.0 %convolution_convert_fusion.1 = bf16[2048,1024]{1,0:T(8,128)(2,1)S(1)} fusion(bf16[2048,2048]{1,0:T(8,128)(2,1)} %all-gather.5.cloned.1.call-done.x_ref, bf16[2048,1024]{1,0:T(8,128)(2,1)} %get-tuple-element.187), kind=kOutput, calls=%fused_computation.9 | convolution fusion | flops 8592031744 | bytes 16777216 | tf_op jit(solution)/shard_map/dot_general | solution.py:94
  313.6 12.3 %fusion.2 = bf16[1024,2048]{1,0:T(8,128)(2,1)S(1)} fusion(bf16[2048,1024]{1,0:T(8,128)(2,1)S(1)} %copy-done.55, bf16[2048,2048]{1,0:T(8,128)(2,1)} %all-gather.3.cloned.1.call-done, f32[2048]{0:T(1024)S(1)} %bitcast.220), kind=kOutput, calls=%fused_computation.8 | convolution fusion | flops 8604614656 | bytes 16785408 | tf_op jit(solution)/shard_map/dot_general | solution.py:94
  331.0 11.3 %convolution_convert_fusion = bf16[2048,2048]{1,0:T(8,128)(2,1)} fusion(bf16[2048,1024]{1,0:T(8,128)(2,1)S(1)} %copy-done.55, bf16[1024,2048]{1,0:T(8,128)(2,1)S(1)} %copy-done.54), kind=kOutput, calls=%fused_computation.3 | convolution fusion | flops 8594128896 | bytes 16777216 | tf_op jit(solution)/shard_map/dot_general | solution.py:94
  345.6 14.6 %collective-permute-done.29 = bf16[2,512,1024]{2,1,0:T(8,128)(2,1)} collective-permute-done((bf16[2,512,1024]{2,1,0:T(8,128)(2,1)}, bf16[2,512,1024]{2,1,0:T(8,128)(2,1)}, u32[]{:S(2)}, u32[]{:S(2)}) %collective-permute-start.29) | collective-permute-done | bytes 2097184 | tf_op jit(solution)/shard_map/ppermute | solution.py:423
  365.4 12.0 %collective-permute-done.28 = bf16[2,256,2048]{2,1,0:T(8,128)(2,1)} collective-permute-done((bf16[2,256,2048]{2,1,0:T(8,128)(2,1)}, bf16[2,256,2048]{2,1,0:T(8,128)(2,1)}, u32[]{:S(2)}, u32[]{:S(2)}) %collective-permute-start.28) | collective-permute-done | bytes 2097184 | tf_op jit(solution)/shard_map/ppermute | solution.py:423
  396.6 19.4 %collective-permute-done.33 = bf16[256,2048]{1,0:T(8,128)(2,1)S(1)} collective-permute-done((bf16[256,2048]{1,0:T(8,128)(2,1)S(1)}, bf16[256,2048]{1,0:T(8,128)(2,1)S(1)}, u32[]{:S(2)}, u32[]{:S(2)}) %collective-permute-start.33) | collective-permute-done | bytes 1048608 | tf_op jit(solution)/shard_map/ppermute | solution.py:402
  426.6 13.9 %attend_backward.2.q_ref.refs_0_ = bf16[1024,768]{1,0:T(8,128)(2,1)} custom-call(bf16[1024,2048]{1,0:T(8,128)(2,1)} %bitcast.58.g_ref, bf16[2048,256]{1,0:T(8,128)(2,1)} %place_blocks.6.refs_3_.w_ref, bf16[1024,768]{1,0:T(8,128)(2,1)} %get-tuple-element.196.qkv_ref, f32[1024,2]{1,0:T(8,128)} %get-tuple-element.197.log_ref, ...), custom_call_target="tpu_custom_call" | custom-call | flops 2415919104 | bytes 12582912 | tf_op jit(solution)/shard_map/attend_backward/pallas_call | solution.py:259
  440.5 8.9 %weight_grads.2 = (bf16[4,256,1024]{2,1,0:T(8,128)(2,1)}, bf16[4,256,1024]{2,1,0:T(8,128)(2,1)}) custom-call(bf16[1024,2048]{1,0:T(8,128)(2,1)} %bitcast.200, bf16[1024,768]{1,0:T(8,128)(2,1)} %attend_backward.2.q_ref.refs_0_, bf16[1024,2048]{1,0:T(8,128)(2,1)} %bitcast.58.g_ref, bf16[1024,256]{1,0:T(8,128)(2,1)} %get-tuple-element.175.refs_2_.h_ref), custom_call_target="tpu_custom_call" | custom-call | flops 4294967296 | bytes 14680064 | tf_op jit(solution)/shard_map/weight_grads/pallas_call | solution.py:330
  454.8 13.2 %attend_backward.3.q_ref.refs_2_ = bf16[1024,768]{1,0:T(8,128)(2,1)} custom-call(bf16[1024,2048]{1,0:T(8,128)(2,1)} %bitcast.58.g_ref, bf16[2048,256]{1,0:T(8,128)(2,1)} %bitcast.197, bf16[1024,768]{1,0:T(8,128)(2,1)} %get-tuple-element.152.qkv_ref, f32[1024,2]{1,0:T(8,128)} %get-tuple-element.201.log_ref, f32[1024,128]{1,0:T(8,128)} %get-tuple-element.143.cos_ref, ...), custom_call_target="tpu_custom_call" | custom-call | flops 2415919104 | bytes 12582912 | tf_op jit(solution)/shard_map/attend_backward/pallas_call | solution.py:259
  482.1 8.8 %weight_grads.3 = (bf16[4,256,1024]{2,1,0:T(8,128)(2,1)}, bf16[4,256,1024]{2,1,0:T(8,128)(2,1)}) custom-call(bf16[1024,2048]{1,0:T(8,128)(2,1)} %bitcast.201, bf16[1024,768]{1,0:T(8,128)(2,1)} %attend_backward.3.q_ref.refs_2_, bf16[1024,2048]{1,0:T(8,128)(2,1)} %bitcast.58.g_ref, bf16[1024,256]{1,0:T(8,128)(2,1)} %get-tuple-element.173.refs_0_.h_ref), custom_call_target="tpu_custom_call" | custom-call | flops 4294967296 | bytes 14680064 | tf_op jit(solution)/shard_map/weight_grads/pallas_call | solution.py:330
  512.5 9.4 %collective-permute-done.47 = bf16[2,256,1024]{2,1,0:T(8,128)(2,1)} collective-permute-done((bf16[2,256,1024]{2,1,0:T(8,128)(2,1)}, bf16[2,256,1024]{2,1,0:T(8,128)(2,1)}, u32[]{:S(2)}, u32[]{:S(2)}) %collective-permute-start.47) | collective-permute-done | bytes 1048608 | tf_op jit(solution)/shard_map/ppermute | solution.py:423
  526.3 19.9 %collective-permute-done.48 = bf16[256,1024]{1,0:T(8,128)(2,1)} collective-permute-done((bf16[256,1024]{1,0:T(8,128)(2,1)}, bf16[256,1024]{1,0:T(8,128)(2,1)}, u32[]{:S(2)}, u32[]{:S(2)}) %collective-permute-start.48) | collective-permute-done | bytes 524320 | tf_op jit(solution)/shard_map/ppermute | solution.py:619
  546.3 10.3 %collective-permute-done.49 = bf16[256,1024]{1,0:T(8,128)(2,1)} collective-permute-done((bf16[256,1024]{1,0:T(8,128)(2,1)S(1)}, bf16[256,1024]{1,0:T(8,128)(2,1)}, u32[]{:S(2)}, u32[]{:S(2)}) %collective-permute-start.49) | collective-permute-done | bytes 524320 | tf_op jit(solution)/shard_map/ppermute | solution.py:619
  562.4 8.4 %collective-permute-done.51 = bf16[256,1024]{1,0:T(8,128)(2,1)} collective-permute-done((bf16[256,1024]{1,0:T(8,128)(2,1)}, bf16[256,1024]{1,0:T(8,128)(2,1)}, u32[]{:S(2)}, u32[]{:S(2)}) %collective-permute-start.51) | collective-permute-done | bytes 524320 | tf_op jit(solution)/shard_map/ppermute | solution.py:423
  600.8 12.4 %collective-permute-done.53 = bf16[256,2048]{1,0:T(8,128)(2,1)} collective-permute-done((bf16[256,2048]{1,0:T(8,128)(2,1)}, bf16[256,2048]{1,0:T(8,128)(2,1)}, u32[]{:S(2)}, u32[]{:S(2)}) %collective-permute-start.53) | collective-permute-done | bytes 1048608 | tf_op jit(solution)/shard_map/ppermute | solution.py:423
  617.1 13.7 %collective-permute-done.59.refs_1_ = bf16[256,1024]{1,0:T(8,128)(2,1)} collective-permute-done((bf16[256,1024]{1,0:T(8,128)(2,1)}, bf16[256,1024]{1,0:T(8,128)(2,1)}, u32[]{:S(2)}, u32[]{:S(2)}) %collective-permute-start.59) | collective-permute-done | bytes 524320 | tf_op jit(solution)/shard_map/ppermute | solution.py:402
  (373 shorter events, 290.8 us)
Async XLA Ops:
  7.2 173.5 %all-gather.3.cloned.1.call-start = ((), (), s32[]{:S(2)}) async-start(), calls=%async_computation.2 | async-start | bytes 9437184 | tf_op jit(solution)/shard_map/all_gather | solution.py:542
  12.9 43.1 %collective-permute-start = (bf16[256,2048]{1,0:T(8,128)(2,1)S(1)}, bf16[256,2048]{1,0:T(8,128)(2,1)}, u32[]{:S(2)}, u32[]{:S(2)}) collective-permute-start(bf16[256,2048]{1,0:T(8,128)(2,1)S(1)} %fusion.11), channel_id=1, source_target_pairs={{0,2},{1,3},{2,0},{3,1},{4,6},{5,7},{6,4},{7,5},{8,10},{9,11},{10,... | collective-permute-start | bytes 3145736 | tf_op jit(solution)/shard_map/ppermute | solution.py:402
  15.9 32.1 %collective-permute-start.1 = (bf16[256,768]{1,0:T(8,128)(2,1)}, bf16[256,768]{1,0:T(8,128)(2,1)}, u32[]{:S(2)}, u32[]{:S(2)}) collective-permute-start(bf16[256,768]{1,0:T(8,128)(2,1)} %get-tuple-element.138), channel_id=1, source_target_pairs={{0,4},{1,5},{2,6},{3,7},{4,0},{5,1},{6,2},{7,3},{8,12},{9,13},{10,... | collective-permute-start | bytes 1179656 | tf_op jit(solution)/shard_map/ppermute | solution.py:529
  18.5 36.8 %collective-permute-start.2 = (bf16[256,768]{1,0:T(8,128)(2,1)}, bf16[256,768]{1,0:T(8,128)(2,1)}, u32[]{:S(2)}, u32[]{:S(2)}) collective-permute-start(bf16[256,768]{1,0:T(8,128)(2,1)} %get-tuple-element.139), channel_id=1, source_target_pairs={{0,4},{1,5},{2,6},{3,7},{4,0},{5,1},{6,2},{7,3},{8,12},{9,13},{10,... | collective-permute-start | bytes 1179656 | tf_op jit(solution)/shard_map/ppermute | solution.py:529
  56.0 214.9 %all-gather.5.cloned.1.call-start = ((), (), s32[]{:S(2)}) async-start(), calls=%async_computation.3 | async-start | bytes 9437184 | tf_op jit(solution)/shard_map/all_gather | solution.py:565
  79.7 28.4 %collective-permute-start.10 = (bf16[256,768]{1,0:T(8,128)(2,1)}, bf16[256,768]{1,0:T(8,128)(2,1)S(1)}, u32[]{:S(2)}, u32[]{:S(2)}) collective-permute-start(bf16[256,768]{1,0:T(8,128)(2,1)} %collective-permute-done.5.refs_1_), channel_id=1, source_target_pairs={{0,16},{8,24},{16,0},{24,8},{1,17},{9,25},{17,1},{25,9},{2,18},{10... | collective-permute-start | bytes 1179656 | tf_op jit(solution)/shard_map/ppermute | solution.py:402
  81.5 26.6 %collective-permute-start.11 = (bf16[256,768]{1,0:T(8,128)(2,1)}, bf16[256,768]{1,0:T(8,128)(2,1)S(1)}, u32[]{:S(2)}, u32[]{:S(2)}) collective-permute-start(bf16[256,768]{1,0:T(8,128)(2,1)} %collective-permute-done.2.refs_4_), channel_id=1, source_target_pairs={{0,8},{8,0},{16,24},{24,16},{1,9},{9,1},{17,25},{25,17},{2,10},{10... | collective-permute-start | bytes 1179656 | tf_op jit(solution)/shard_map/ppermute | solution.py:402
  146.7 30.8 %collective-permute-start.20 = (bf16[256,2048]{1,0:T(8,128)(2,1)S(1)}, bf16[256,2048]{1,0:T(8,128)(2,1)S(1)}, u32[]{:S(2)}, u32[]{:S(2)}) collective-permute-start(bf16[256,2048]{1,0:T(8,128)(2,1)S(1)} %fusion.25), channel_id=1, source_target_pairs={{0,2},{1,3},{2,0},{3,1},{4,6},{5,7},{6,4},{7,5},{8,10},{9,11},{10,... | collective-permute-start | bytes 3145736 | tf_op jit(solution)/shard_map/ppermute | solution.py:423
  185.5 199.4 %reduce-scatter.3.cloned.1.call-start = ((), (), s32[]{:S(2)}) async-start(), calls=%async_computation.4 | async-start | bytes 9437184 | tf_op jit(solution)/shard_map/reduce_scatter | solution.py:574
  296.4 371.7 %reduce-scatter.5.cloned.1.call-start = ((), (), s32[]{:S(2)}) async-start(), calls=%async_computation.5 | async-start | bytes 9437184 | tf_op jit(solution)/shard_map/reduce_scatter | solution.py:595
  312.1 48.1 %collective-permute-start.29 = (bf16[2,512,1024]{2,1,0:T(8,128)(2,1)}, bf16[2,512,1024]{2,1,0:T(8,128)(2,1)}, u32[]{:S(2)}, u32[]{:S(2)}) collective-permute-start(bf16[2,512,1024]{2,1,0:T(8,128)(2,1)} %dynamic-slice_bitcast_fusion), channel_id=1, source_target_pairs={{0,16},{8,24},{16,0},{24,8},{1,17},{9,25},{17,1},{25,9},{2,18},{10... | collective-permute-start | bytes 6291464 | tf_op jit(solution)/shard_map/ppermute | solution.py:423
  329.1 48.4 %collective-permute-start.28 = (bf16[2,256,2048]{2,1,0:T(8,128)(2,1)}, bf16[2,256,2048]{2,1,0:T(8,128)(2,1)}, u32[]{:S(2)}, u32[]{:S(2)}) collective-permute-start(bf16[2,256,2048]{2,1,0:T(8,128)(2,1)} %dynamic-slice_bitcast_fusion.1), channel_id=1, source_target_pairs={{0,8},{8,0},{16,24},{24,16},{1,9},{9,1},{17,25},{25,17},{2,10},{10... | collective-permute-start | bytes 6291464 | tf_op jit(solution)/shard_map/ppermute | solution.py:423
  499.5 76.1 %collective-permute-start.44 = (bf16[256,2048]{1,0:T(8,128)(2,1)}, bf16[256,2048]{1,0:T(8,128)(2,1)}, u32[]{:S(2)}, u32[]{:S(2)}) collective-permute-start(bf16[256,2048]{1,0:T(8,128)(2,1)} %fusion.23.refs_0_), channel_id=1, source_target_pairs={{0,16},{8,24},{16,0},{24,8},{1,17},{9,25},{17,1},{25,9},{2,18},{10... | collective-permute-start | bytes 3145736 | tf_op jit(solution)/shard_map/ppermute | solution.py:458
  500.6 45.6 %collective-permute-start.48 = (bf16[256,1024]{1,0:T(8,128)(2,1)}, bf16[256,1024]{1,0:T(8,128)(2,1)}, u32[]{:S(2)}, u32[]{:S(2)}) collective-permute-start(bf16[256,1024]{1,0:T(8,128)(2,1)} %fusion.30), channel_id=1, source_target_pairs={{0,4},{1,5},{2,6},{3,7},{4,0},{5,1},{6,2},{7,3},{8,12},{9,13},{10,... | collective-permute-start | bytes 1572872 | tf_op jit(solution)/shard_map/ppermute | solution.py:619
  504.5 52.1 %collective-permute-start.49 = (bf16[256,1024]{1,0:T(8,128)(2,1)S(1)}, bf16[256,1024]{1,0:T(8,128)(2,1)}, u32[]{:S(2)}, u32[]{:S(2)}) collective-permute-start(bf16[256,1024]{1,0:T(8,128)(2,1)S(1)} %fusion.29), channel_id=1, source_target_pairs={{0,4},{1,5},{2,6},{3,7},{4,0},{5,1},{6,2},{7,3},{8,12},{9,13},{10,... | collective-permute-start | bytes 1572872 | tf_op jit(solution)/shard_map/ppermute | solution.py:619
  521.9 61.4 %collective-permute-start.52 = (bf16[2,256,2048]{2,1,0:T(8,128)(2,1)}, bf16[2,256,2048]{2,1,0:T(8,128)(2,1)}, u32[]{:S(2)}, u32[]{:S(2)}) collective-permute-start(bf16[2,256,2048]{2,1,0:T(8,128)(2,1)} %share_of.6), channel_id=1, source_target_pairs={{0,1},{1,0},{2,3},{3,2},{4,5},{5,4},{6,7},{7,6},{8,9},{9,8},{10,11... | collective-permute-start | bytes 6291464 | tf_op jit(solution)/shard_map/ppermute | solution.py:500
  523.5 52.0 %collective-permute-start.45 = (bf16[512,1024]{1,0:T(8,128)(2,1)}, bf16[512,1024]{1,0:T(8,128)(2,1)}, u32[]{:S(2)}, u32[]{:S(2)}) collective-permute-start(bf16[512,1024]{1,0:T(8,128)(2,1)} %fusion.22.refs_0_), channel_id=1, source_target_pairs={{0,8},{8,0},{16,24},{24,16},{1,9},{9,1},{17,25},{25,17},{2,10},{10... | collective-permute-start | bytes 3145736 | tf_op jit(solution)/shard_map/ppermute | solution.py:458
  595.9 34.9 %collective-permute-start.61 = (bf16[256,2048]{1,0:T(8,128)(2,1)}, bf16[256,2048]{1,0:T(8,128)(2,1)S(1)}, u32[]{:S(2)}, u32[]{:S(2)}) collective-permute-start(bf16[256,2048]{1,0:T(8,128)(2,1)} %copy-done.32), channel_id=1, source_target_pairs={{0,16},{8,24},{16,0},{24,8},{1,17},{9,25},{17,1},{25,9},{2,18},{10... | collective-permute-start | bytes 3145736 | tf_op jit(solution)/shard_map/ppermute | solution.py:458
  596.4 34.4 %collective-permute-start.62 = (bf16[512,1024]{1,0:T(8,128)(2,1)}, bf16[512,1024]{1,0:T(8,128)(2,1)S(1)}, u32[]{:S(2)}, u32[]{:S(2)}) collective-permute-start(bf16[512,1024]{1,0:T(8,128)(2,1)} %copy-done.31), channel_id=1, source_target_pairs={{0,8},{8,0},{16,24},{24,16},{1,9},{9,1},{17,25},{25,17},{2,10},{10... | collective-permute-start | bytes 3145736 | tf_op jit(solution)/shard_map/ppermute | solution.py:458
  600.3 30.5 %collective-permute-start.59 = (bf16[256,1024]{1,0:T(8,128)(2,1)}, bf16[256,1024]{1,0:T(8,128)(2,1)}, u32[]{:S(2)}, u32[]{:S(2)}) collective-permute-start(bf16[256,1024]{1,0:T(8,128)(2,1)} %add_convert_fusion.2.refs_0_), channel_id=1, source_target_pairs={{0,8},{8,0},{16,24},{24,16},{1,9},{9,1},{17,25},{25,17},{2,10},{10... | collective-permute-start | bytes 1572872 | tf_op jit(solution)/shard_map/ppermute | solution.py:402
  616.8 30.2 %collective-permute-start.55 = (f32[160,128]{1,0:T(8,128)S(1)}, f32[160,128]{1,0:T(8,128)S(1)}, u32[]{:S(2)}, u32[]{:S(2)}) collective-permute-start(f32[160,128]{1,0:T(8,128)S(1)} %fusion.69), channel_id=1, source_target_pairs={{0,2},{1,3},{2,0},{3,1},{4,6},{5,7},{6,4},{7,5},{8,10},{9,11},{10,... | collective-permute-start | bytes 245768 | tf_op jit(solution)/shard_map/ppermute | solution.py:473
  630.8 29.4 %collective-permute-start.63 = (bf16[256,1024]{1,0:T(8,128)(2,1)}, bf16[256,1024]{1,0:T(8,128)(2,1)}, u32[]{:S(2)}, u32[]{:S(2)}) collective-permute-start(bf16[256,1024]{1,0:T(8,128)(2,1)} %add_convert_fusion.2.refs_0_), channel_id=1, source_target_pairs={{0,16},{8,24},{16,0},{24,8},{1,17},{9,25},{17,1},{25,9},{2,18},{10... | collective-permute-start | bytes 1572872 | tf_op jit(solution)/shard_map/ppermute | solution.py:402
  632.4 27.9 %collective-permute-start.64 = (bf16[256,1024]{1,0:T(8,128)(2,1)}, bf16[256,1024]{1,0:T(8,128)(2,1)}, u32[]{:S(2)}, u32[]{:S(2)}) collective-permute-start(bf16[256,1024]{1,0:T(8,128)(2,1)} %collective-permute-done.59.refs_1_), channel_id=1, source_target_pairs={{0,16},{8,24},{16,0},{24,8},{1,17},{9,25},{17,1},{25,9},{2,18},{10... | collective-permute-start | bytes 1572872 | tf_op jit(solution)/shard_map/ppermute | solution.py:402
  632.9 27.4 %collective-permute-start.65 = (bf16[256,1024]{1,0:T(8,128)(2,1)S(1)}, bf16[256,1024]{1,0:T(8,128)(2,1)}, u32[]{:S(2)}, u32[]{:S(2)}) collective-permute-start(bf16[256,1024]{1,0:T(8,128)(2,1)S(1)} %add_convert_fusion.1.refs_4_), channel_id=1, source_target_pairs={{0,8},{8,0},{16,24},{24,16},{1,9},{9,1},{17,25},{25,17},{2,10},{10... | collective-permute-start | bytes 1572872 | tf_op jit(solution)/shard_map/ppermute | solution.py:402
  (103 other events, 1567.0 us)
Sparse Core Ops, SparseCore 0:
  56.1 85.8 all-gather.2
  185.6 85.2 all-gather.4
  296.5 88.3 reduce-scatter.2
  423.9 96.8 reduce-scatter.4
